TPU v7x, 32 devices: a whole 2x2x4 slice. The times are simulated.
32 devices in a mesh: seq: 8 (over z, y), head: 4 (over x, core).
Axes of the slice: x: 2, y: 2, z: 4, core: 2. Of those that a mesh axis runs over, the one named last changes fastest.
Arguments:
- queries: bfloat16 [12288, 2048], P('seq', 'head'), may hold values from -200 to 200
- keys_values: bfloat16 [2, 12288, 2048], P(None, 'seq', 'head'), may hold values from -6 to 6
- global_ids: int32 [2], replicated, may hold values from 0 to 191
- rand_ids: int32 [192, 3], replicated, may hold values from 0 to 191, as said below
- out_weight: bfloat16 [2048, 4096], P(None, 'head'), may hold values from -2 to 2
Outputs:
- projected: bfloat16 [12288, 4096], P('seq', 'head')
Inputs may be any that keep to these rules, and one draw needn't show every extreme that they name: `rand_ids`: row i lists the 3 random key blocks of query block i. Among the 24 rows of one seq shard, at most 9 listed blocks lie on any one shard, and at most 3 of one column do; both bounds are reached.
All inputs are finite; a program needn't handle non-finite values.
Results may differ from a plain program's by a relative error of at most 0.0057.
Values may be sent and summed in bfloat16 or wider, within the bound.
No kernel may reach another device: no remote copies, remote signals or barrier semaphores. Data moves between devices by JAX's collectives and lax.ppermute only.
A program may use at most 128 MiB of HBM per device.

v0:
```python
import jax
import jax.numpy as jnp
from jax import lax
from jax.sharding import PartitionSpec as P

HEAD_DIM = 128
BLOCK = 64
NGLOBAL = 2
NRANDOM = 3


group_blocks = 8


def padded_2(block, sides, width):
    for axis, dim in sides:
        count = lax.axis_size(axis)
        forward = [(i, i + 1) for i in range(count - 1)]
        backward = [(target, source) for source, target in forward]
        low = lax.ppermute(
            lax.slice_in_dim(block, block.shape[dim] - width, None, axis=dim), axis, forward
        )
        high = lax.ppermute(lax.slice_in_dim(block, 0, width, axis=dim), axis, backward)
        block = jnp.concatenate([low, block, high], axis=dim)
    return block


def broadcast(block, axis, owner):
    block = jnp.where(lax.axis_index(axis) == owner, block, jnp.zeros_like(block))
    return lax.psum(block, axis)


def plan_slots(requests, myself, capacity, per_shard):
    sources = requests // per_shard
    offsets = requests % per_shard
    count = requests.shape[1]
    order = jnp.arange(count, dtype=jnp.int32)
    earlier = (order[:, None] < order[None, :]).astype(jnp.int32)
    matches = (sources[:, :, None] == sources[:, None, :]).astype(jnp.int32)
    ranks = jnp.sum(matches * earlier[None], axis=1)
    slot_range = jnp.arange(capacity, dtype=jnp.int32)
    wanted = (
        (sources == myself)[:, None, :] & (ranks[:, None, :] == slot_range[None, :, None])
    ).astype(jnp.int32)
    chosen = jnp.sum(wanted * offsets[:, None, :], axis=2).reshape(-1)
    own_sources = lax.dynamic_index_in_dim(sources, myself, 0, keepdims=False)
    own_ranks = lax.dynamic_index_in_dim(ranks, myself, 0, keepdims=False)
    return (chosen, own_sources * capacity + own_ranks)


def attend_blocks(query_part, local_keys, local_values, glob_keys, glob_values, valid):
    scale = 1.0 / HEAD_DIM**0.5
    near_scores = (
        jnp.einsum("bqhd,bkhd->bhqk", query_part, local_keys, preferred_element_type=jnp.float32)
        * scale
    )
    near_scores = jnp.where(valid[:, None, None, :], near_scores, -jnp.inf)
    glob_scores = (
        jnp.einsum("bqhd,khd->bhqk", query_part, glob_keys, preferred_element_type=jnp.float32)
        * scale
    )
    highest = jnp.maximum(jnp.max(near_scores, axis=-1), jnp.max(glob_scores, axis=-1))
    near_exp = jnp.exp(near_scores - highest[..., None])
    glob_exp = jnp.exp(glob_scores - highest[..., None])
    total = jnp.sum(near_exp, axis=-1) + jnp.sum(glob_exp, axis=-1)
    near_weights = (near_exp / total[..., None]).astype(jnp.bfloat16)
    glob_weights = (glob_exp / total[..., None]).astype(jnp.bfloat16)
    mixed = jnp.einsum(
        "bhqk,bkhd->bqhd", near_weights, local_values, preferred_element_type=jnp.float32
    )
    mixed = mixed + jnp.einsum(
        "bhqk,khd->bqhd", glob_weights, glob_values, preferred_element_type=jnp.float32
    )
    return mixed.astype(jnp.bfloat16)


def body(queries, keys_values, global_ids, rand_ids, out_weight):
    rows = queries.shape[0]
    width = queries.shape[1]
    heads_here = width // HEAD_DIM
    local_blocks = rows // BLOCK
    shards = lax.axis_size("seq")
    myself = lax.axis_index("seq")
    total_blocks = local_blocks * shards
    pair_blocks = keys_values.reshape(2, local_blocks, BLOCK, width)
    padded = padded_2(keys_values, (("seq", 1),), BLOCK)
    padded = padded.reshape(2, local_blocks + 2, BLOCK, width)
    panel_list = []
    for which in range(NGLOBAL):
        target = global_ids[which]
        owner = target // local_blocks
        local_panel = lax.dynamic_index_in_dim(
            pair_blocks, target % local_blocks, 1, keepdims=False
        )
        panel_list.append(broadcast(local_panel, "seq", owner))
    glob = jnp.stack(panel_list, axis=1).reshape(2, NGLOBAL * BLOCK, heads_here, HEAD_DIM)
    requests = rand_ids.reshape(shards, local_blocks, NRANDOM)
    capacity = (local_blocks + shards - 1) // shards
    fetched = []
    for column in range(NRANDOM):
        chosen, slots = plan_slots(requests[:, :, column], myself, capacity, local_blocks)
        outgoing = jnp.take(pair_blocks, chosen, axis=1)
        incoming = lax.all_to_all(outgoing, "seq", split_axis=1, concat_axis=1, tiled=True)
        fetched.append(jnp.take(incoming, slots, axis=1))
    remote = jnp.stack(fetched, axis=2)
    segment = jnp.arange((3 + NRANDOM) * BLOCK, dtype=jnp.int32) // BLOCK

    def one_group(index):
        first = index * group_blocks
        query_part = lax.dynamic_slice_in_dim(queries, first * BLOCK, group_blocks * BLOCK, 0)
        query_part = query_part.reshape(group_blocks, BLOCK, heads_here, HEAD_DIM)
        window = lax.dynamic_slice_in_dim(padded, first, group_blocks + 2, 1)
        farther = lax.dynamic_slice_in_dim(remote, first, group_blocks, 1)
        farther = farther.reshape(2, group_blocks, NRANDOM * BLOCK, width)
        local = jnp.concatenate(
            [
                window[:, 0:group_blocks],
                window[:, 1 : group_blocks + 1],
                window[:, 2 : group_blocks + 2],
                farther,
            ],
            axis=2,
        )
        local = local.reshape(2, group_blocks, (3 + NRANDOM) * BLOCK, heads_here, HEAD_DIM)
        block_ids = myself * local_blocks + first + jnp.arange(group_blocks, dtype=jnp.int32)
        drop_before = (segment[None, :] == 0) & (block_ids[:, None] == 0)
        drop_after = (segment[None, :] == 2) & (block_ids[:, None] == total_blocks - 1)
        valid = jnp.logical_not(drop_before | drop_after)
        mixed = attend_blocks(query_part, local[0], local[1], glob[0], glob[1], valid)
        return mixed.reshape(group_blocks * BLOCK, width)

    attended = lax.map(
        one_group, jnp.arange(local_blocks // group_blocks, dtype=jnp.int32)
    ).reshape(rows, width)
    summed = jnp.dot(
        lax.all_gather(attended, "head", axis=1, tiled=True),
        out_weight,
        preferred_element_type=jnp.float32,
    )
    return summed.astype(jnp.bfloat16)


def solution(mesh):
    in_specs = (P("seq", "head"), P(None, "seq", "head"), P(), P(), P(None, "head"))
    out_specs = P("seq", "head")
    return jax.shard_map(body, mesh=mesh, in_specs=in_specs, out_specs=out_specs, check_vma=False)
```

profile of v0, /device:TPU:0, one launch (start us, length us, event | category | flops | bytes accessed | tf_op | source)
XLA Modules:
  0.0 521.8 jit_solution(13546856056546497656)
XLA Ops:
  8.3 2.6 gather_fusion.4
  12.9 7.5 %all-to-all-start.2 = ((bf16[2,24,64,512]{3,2,0,1:T(8,128)(2,1)}), bf16[2,24,64,512]{3,2,0,1:T(8,128)(2,1)}, u32[]{:S(2)}, u32[]{:S(2)}) async-start(bf16[2,24,64,512]{3,2,0,1:T(8,128)(2,1)} %select_bitcast_fusion.1), calls=%async_computation.2 | async-start | bytes 6291456 | tf_op jit(solution)/shard_map/all_to_all | solution.py:103
  20.5 2.5 gather_fusion.2
  23.0 3.9 select_bitcast_fusion.3
  26.9 64.4 %all-to-all-done.2 = bf16[2,24,64,512]{3,2,0,1:T(8,128)(2,1)} async-done(((bf16[2,24,64,512]{3,2,0,1:T(8,128)(2,1)}), bf16[2,24,64,512]{3,2,0,1:T(8,128)(2,1)}, u32[]{:S(2)}, u32[]{:S(2)}) %all-to-all-start.2) | async-done | bytes 3145760 | tf_op jit(solution)/shard_map/all_to_all | solution.py:103
  91.3 4.5 all-to-all-start.1
  96.1 2.5 gather_fusion
  98.6 3.9 select_bitcast_fusion.5
  102.6 63.4 %all-to-all-done.1 = bf16[2,24,64,512]{3,2,0,1:T(8,128)(2,1)} async-done(((bf16[2,24,64,512]{3,2,0,1:T(8,128)(2,1)}), bf16[2,24,64,512]{3,2,0,1:T(8,128)(2,1)}, u32[]{:S(2)}, u32[]{:S(2)}) %all-to-all-start.1) | async-done | bytes 3145760 | tf_op jit(solution)/shard_map/all_to_all | solution.py:103
  166.0 4.4 all-to-all-start
  170.5 3.8 collective-permute-start
  184.5 15.8 %collective-permute-done = bf16[2,64,512]{2,1,0:T(8,128)(2,1)S(1)} collective-permute-done((bf16[2,64,512]{2,1,0:T(8,128)(2,1)S(1)}, bf16[2,64,512]{2,1,0:T(8,128)(2,1)S(1)}, u32[]{:S(2)}, u32[]{:S(2)}) %collective-permute-start) | collective-permute-done | bytes 131104 | tf_op jit(solution)/shard_map/ppermute | solution.py:20
  200.3 2.1 pad_maximum_fusion.2
  202.4 81.9 %all-reduce.3.cloned.1.call-done = (bf16[2,1,64,512]{3,2,1,0:T(8,128)(2,1)}, bf16[2,1,64,512]{3,2,1,0:T(8,128)(2,1)}) async-done(((bf16[2,1,64,512]{3,2,1,0:T(8,128)(2,1)}, bf16[2,1,64,512]{3,2,1,0:T(8,128)(2,1)}), (bf16[2,1,64,512]{3,2,1,0:T(8,128)(2,1)}, bf16[2,1,64,512]{3,2,1,0:T(8,128)(2,1)})) %all-reduce.3.cloned.1.call-update) | async-done | bytes 262160 | tf_op jit(solution)/shard_map/psum | solution.py:30
  289.4 3.9 copy.104
  293.3 4.4 gather_fusion.5
  297.8 3.9 copy.102
  301.7 4.4 gather_fusion.3
  306.1 4.1 select_bitcast_fusion
  310.2 2.1 select_bitcast_fusion.2
  312.2 3.9 copy.100
  316.2 4.4 gather_fusion.1
  320.5 2.4 select_bitcast_fusion.4
  324.3 4.2 pad_maximum_fusion.1
  328.6 129.5 %while.14 = (s32[]{:T(128)}, bf16[3,512,512]{2,1,0:T(8,128)(2,1)}, s32[3]{0:T(128)S(1)}, bf16[2,26,64,512]{3,2,1,0:T(8,128)(2,1)S(1)}, bf16[2,24,3,64,512]{4,3,0...) while((s32[]{:T(128)}, bf16[3,512,512]{2,1,0:T(8,128)(2,1)}, ...), condition=%wide.region_13.15_spmd.clone.clone, body=%wide.region_8.14_spmd.clone.clone.sunk | while | flops 573845248 | bytes 162462448 | solution.py:132
  331.7 2.2 constant_dynamic-slice_fusion.14
  335.8 4.8 pad_maximum_fusion.5
  340.5 3.3 fusion.69
  343.8 3.4 copy.141
  357.4 4.8 copy.140
  362.2 3.4 fusion.76
  367.8 2.1 broadcast_in_dim.123
  374.8 2.2 constant_dynamic-slice_fusion.14
  378.9 4.8 pad_maximum_fusion.5
  383.7 3.3 fusion.69
  387.0 3.4 copy.141
  400.6 4.8 copy.140
  405.4 3.4 fusion.76
  410.9 2.1 broadcast_in_dim.123
  418.0 2.2 constant_dynamic-slice_fusion.14
  422.1 4.8 pad_maximum_fusion.5
  426.8 3.3 fusion.69
  430.1 3.4 copy.141
  443.7 4.8 copy.140
  448.5 3.4 fusion.76
  454.1 2.1 broadcast_in_dim.123
  458.0 45.8 %all-gather.2.cloned.1.call-done = bf16[1536,2048]{1,0:T(8,128)(2,1)} async-done(((bf16[1536,512]{1,0:T(8,128)(2,1)}), bf16[1536,2048]{1,0:T(8,128)(2,1)}) %all-gather.2.cloned.1.call-update) | async-done | bytes 6291472 | tf_op jit(solution)/shard_map/all_gather | solution.py:136
  503.9 11.1 %convolution_convert_fusion = bf16[1536,1024]{1,0:T(8,128)(2,1)} fusion(bf16[1536,2048]{1,0:T(8,128)(2,1)} %all-gather.2.cloned.1.call-done, bf16[2048,1024]{1,0:T(8,128)(2,1)} %param.13), kind=kOutput, calls=%fused_computation.56 | convolution fusion | flops 6444023808 | bytes 13631488 | tf_op jit(solution)/shard_map/dot_general | solution.py:135
  (191 shorter events, 70.2 us)
Async XLA Ops:
  12.9 7.6 %copy-start.10 = (bf16[2,1536,512]{2,1,0:T(8,128)(2,1)S(1)}, bf16[2,1536,512]{2,1,0:T(8,128)(2,1)}, u32[]{:S(2)}) copy-start(bf16[2,1536,512]{2,1,0:T(8,128)(2,1)} %param.10) | copy-start | bytes 9437188
  12.9 78.4 %all-to-all-start.2 = ((bf16[2,24,64,512]{3,2,0,1:T(8,128)(2,1)}), bf16[2,24,64,512]{3,2,0,1:T(8,128)(2,1)}, u32[]{:S(2)}, u32[]{:S(2)}) async-start(bf16[2,24,64,512]{3,2,0,1:T(8,128)(2,1)} %select_bitcast_fusion.1), calls=%async_computation.2 | async-start | bytes 6291456 | tf_op jit(solution)/shard_map/all_to_all | solution.py:103
  91.3 74.6 %all-to-all-start.1 = ((bf16[2,24,64,512]{3,2,0,1:T(8,128)(2,1)}), bf16[2,24,64,512]{3,2,0,1:T(8,128)(2,1)}, u32[]{:S(2)}, u32[]{:S(2)}) async-start(bf16[2,24,64,512]{3,2,0,1:T(8,128)(2,1)} %select_bitcast_fusion.3), calls=%async_computation.1 | async-start | bytes 6291456 | tf_op jit(solution)/shard_map/all_to_all | solution.py:103
  166.0 146.3 %all-to-all-start = ((bf16[2,24,64,512]{3,2,0,1:T(8,128)(2,1)}), bf16[2,24,64,512]{3,2,0,1:T(8,128)(2,1)}, u32[]{:S(2)}, u32[]{:S(2)}) async-start(bf16[2,24,64,512]{3,2,0,1:T(8,128)(2,1)} %select_bitcast_fusion.5), calls=%async_computation | async-start | bytes 6291456 | tf_op jit(solution)/shard_map/all_to_all | solution.py:103
  170.4 113.9 %all-reduce.3.cloned.1.call-start = ((), (), s32[]{:S(2)}) async-start(), calls=%async_computation.4 | async-start | bytes 524288 | tf_op jit(solution)/shard_map/psum | solution.py:30
  170.5 29.8 %collective-permute-start = (bf16[2,64,512]{2,1,0:T(8,128)(2,1)S(1)}, bf16[2,64,512]{2,1,0:T(8,128)(2,1)S(1)}, u32[]{:S(2)}, u32[]{:S(2)}) collective-permute-start(bf16[2,64,512]{2,1,0:T(8,128)(2,1)S(1)} %get-tuple-element.267), channel_id=1, source_target_pairs={{0,4},{4,8},{8,12},{12,16},{16,20},{20,24},{24,28},{1,5},{5,9},{9,... | collective-permute-start | bytes 393224 | tf_op jit(solution)/shard_map/ppermute | solution.py:20
  174.2 26.1 %collective-permute-start.1 = (bf16[2,64,512]{2,1,0:T(8,128)(2,1)S(1)}, bf16[2,64,512]{2,1,0:T(8,128)(2,1)}, u32[]{:S(2)}, u32[]{:S(2)}) collective-permute-start(bf16[2,64,512]{2,1,0:T(8,128)(2,1)S(1)} %get-tuple-element.268), channel_id=1, source_target_pairs={{4,0},{8,4},{12,8},{16,12},{20,16},{24,20},{28,24},{5,1},{9,5},{13... | collective-permute-start | bytes 393224 | tf_op jit(solution)/shard_map/ppermute | solution.py:23
  181.5 322.4 %all-gather.2.cloned.1.call-start = ((), (), s32[]{:S(2)}) async-start(), calls=%async_computation.3 | async-start | bytes 7864320 | tf_op jit(solution)/shard_map/all_gather | solution.py:136
  301.7 4.4 copy-start.19
  306.1 4.1 copy-start.13
  306.1 4.1 copy-start.20
  316.1 4.4 copy-start.18
  320.5 2.8 copy-start.11
  320.5 3.8 copy-start.12
  328.6 3.1 copy-start.3
  333.9 1.2 copy-start.7
  333.9 1.5 copy-start.8
  333.9 1.8 copy-start.9
  351.9 2.0 copy-start.2
  351.9 2.0 copy-start.14
  353.8 1.7 copy-start
  354.4 3.0 copy-start.5
  357.4 4.8 copy-start.1
  362.2 3.4 copy-start.6
  362.2 3.4 copy-start.15
  365.6 6.1 %copy-start.4 = (bf16[2,26,64,512]{3,2,1,0:T(8,128)(2,1)S(1)}, bf16[2,26,64,512]{3,2,1,0:T(8,128)(2,1)}, u32[]{:S(2)}) copy-start(bf16[2,26,64,512]{3,2,1,0:T(8,128)(2,1)} %copy-done.3) | copy-start | bytes 10223620 | tf_op jit(solution)/shard_map/while
  371.7 3.1 copy-start.3
  377.1 1.5 copy-start.8
  377.1 1.8 copy-start.9
  395.0 2.0 copy-start.2
  395.0 2.0 copy-start.14
  397.0 1.7 copy-start
  397.6 3.0 copy-start.5
  400.6 4.8 copy-start.1
  405.4 3.4 copy-start.6
  405.4 3.4 copy-start.15
  408.8 6.1 %copy-start.4 = (bf16[2,26,64,512]{3,2,1,0:T(8,128)(2,1)S(1)}, bf16[2,26,64,512]{3,2,1,0:T(8,128)(2,1)}, u32[]{:S(2)}) copy-start(bf16[2,26,64,512]{3,2,1,0:T(8,128)(2,1)} %copy-done.3) | copy-start | bytes 10223620 | tf_op jit(solution)/shard_map/while
  414.9 3.1 copy-start.3
  420.2 1.5 copy-start.8
  420.2 1.8 copy-start.9
  438.2 2.0 copy-start.2
  438.2 2.0 copy-start.14
  440.1 1.7 copy-start
  440.7 3.0 copy-start.5
  443.7 4.8 copy-start.1
  448.5 3.4 copy-start.6
  448.5 3.4 copy-start.15
  451.9 6.1 %copy-start.4 = (bf16[2,26,64,512]{3,2,1,0:T(8,128)(2,1)S(1)}, bf16[2,26,64,512]{3,2,1,0:T(8,128)(2,1)}, u32[]{:S(2)}) copy-start(bf16[2,26,64,512]{3,2,1,0:T(8,128)(2,1)} %copy-done.3) | copy-start | bytes 10223620 | tf_op jit(solution)/shard_map/while
  (4 other events, 3.9 us)
Sparse Core Ops, SparseCore 0:
  181.6 102.6 all-reduce.2
  458.2 45.6 all-gather.1
where the time goes:
time: 524 us; the launch traced here: 522 us
  waiting for transfers between devices  271 us (52%)
  local copies, waits for them, and re-layouts  125 us (24%)
  other arithmetic  51 us (10%)
  matrix products  31.5 us (6%)
  starting transfers between devices  21.6 us (4%)
  between operations  17.4 us (3%)
    all_to_all x3, waiting for transfers between devices, body(): lax.all_to_all(outgoing, 'seq', split_axis=1, concat_axis=1, tiled=True)  128 us
    psum x1, waiting for transfers between devices, broadcast(): return lax.psum(block, axis)  81.9 us
    all_gather x1, waiting for transfers between devices, body(): lax.all_gather(attended, 'head', axis=1, tiled=True)  45.8 us
    slice x6, local copies, waits for them, and re-layouts, one_group(): local[0]  20.3 us
    all_to_all x3, starting transfers between devices, body(): lax.all_to_all(outgoing, 'seq', split_axis=1, concat_axis=1, tiled=True)  16.5 us
    ppermute x1, waiting for transfers between devices, padded_2(): lax.ppermute(lax.slice_in_dim(block, block.shape[dim] - width, None, axis...  15.8 us
    slice x3, local copies, waits for them, and re-layouts, one_group(): local[1]  14.4 us
    concatenate x3, other arithmetic, one_group(): jnp.concatenate([window[:, 0:group_blocks], window[:, 1:group_blocks + 1]...  14.3 us
  transfers between devices with their start and end apart: 7, of which 5 were waited for; matrix products, arithmetic and copies ran while one was open for 9% of the time, Pallas kernels for 0%

commit v1 on v0

--- a/solution.py
+++ b/solution.py
@@ -1,15 +1,272 @@
+import functools
+
 import jax
 import jax.numpy as jnp
 from jax import lax
+from jax.experimental import pallas as pl
+from jax.experimental.pallas import tpu as pltpu
 from jax.sharding import PartitionSpec as P
 
 HEAD_DIM = 128
 BLOCK = 64
 NGLOBAL = 2
 NRANDOM = 3
+NLIST = 3 + NGLOBAL + NRANDOM
+MASKED = -1e30
+EXP2_SCALE = 1.4426950408889634 / HEAD_DIM**0.5
+STAT_ROWS = 32
+VMEM_LIMIT = 32 * 1024 * 1024
 
 
 group_blocks = 8
+
+
+def eye_mask():
+    rows = lax.broadcasted_iota(jnp.int32, (BLOCK, BLOCK), 0)
+    columns = lax.broadcasted_iota(jnp.int32, (BLOCK, BLOCK), 1)
+    return rows == columns
+
+
+def attend_one(i, starts_ref, bias_ref, q_ref, pool):
+    rows = pl.ds(pl.multiple_of(i * BLOCK, BLOCK), BLOCK)
+    query = q_ref[rows, :]
+    where_ = [
+        pl.ds(pl.multiple_of(starts_ref[i * NLIST + e], BLOCK), BLOCK) for e in range(NLIST)
+    ]
+    keys = jnp.concatenate([pool[0, w, :] for w in where_], axis=0)
+    scores = lax.dot_general(
+        query, keys, (((1,), (1,)), ((), ())), preferred_element_type=jnp.float32
+    )
+    scores = scores + bias_ref[pl.ds(i, 1), :]
+    highest = jnp.max(scores, axis=1, keepdims=True)
+    weights = jnp.exp2((scores - highest) * EXP2_SCALE)
+    total = jnp.sum(weights, axis=1, keepdims=True)
+    values = jnp.concatenate([pool[1, w, :] for w in where_], axis=0)
+    mixed = jnp.dot(weights.astype(jnp.bfloat16), values, preferred_element_type=jnp.float32)
+    return rows, mixed, highest, total
+
+
+def put_stats(i, stats_ref, highest, total):
+    eye = eye_mask()
+    high_row = jnp.sum(jnp.where(eye, highest, 0.0), axis=0, keepdims=True)
+    total_row = jnp.sum(jnp.where(eye, total, 0.0), axis=0, keepdims=True)
+    stats_ref[pl.ds(i, 1), :] = jnp.concatenate([high_row, total_row], axis=1)
+
+
+def load_pool(parts, pool, sems):
+    size = parts[0].shape[1]
+    copies = [
+        pltpu.make_async_copy(part, pool.at[:, pl.ds(n * size, size), :], sems.at[n])
+        for n, part in enumerate(parts)
+    ]
+    for copy in copies:
+        copy.start()
+    for copy in copies:
+        copy.wait()
+
+
+def guest_kernel(
+    unroll, starts_ref, bias_ref, q_ref, p0, p1, p2, p3, message_ref, pool, stats, sems
+):
+    load_pool((p0, p1, p2, p3), pool, sems)
+    blocks = q_ref.shape[0] // BLOCK
+    stats[...] = jnp.zeros_like(stats)
+
+    def step(n, _):
+        for u in range(unroll):
+            i = n * unroll + u
+            rows, mixed, highest, total = attend_one(i, starts_ref, bias_ref, q_ref, pool)
+            message_ref[rows, :] = (mixed / total).astype(jnp.bfloat16)
+            put_stats(i, stats, highest, total)
+        return 0
+
+    lax.fori_loop(0, blocks // unroll, step, 0)
+    rest = stats[...]
+    base = q_ref.shape[0]
+    for n in range(3):
+        piece = rest.astype(jnp.bfloat16)
+        message_ref[pl.ds(base + n * STAT_ROWS, STAT_ROWS), :] = piece
+        rest = rest - piece.astype(jnp.float32)
+
+
+def home_kernel(
+    unroll, starts_ref, bias_ref, q_ref, p0, p1, p2, p3, mixed_ref, stats_ref, pool, sems
+):
+    load_pool((p0, p1, p2, p3), pool, sems)
+    blocks = q_ref.shape[0] // BLOCK
+    stats_ref[...] = jnp.zeros_like(stats_ref)
+
+    def step(n, _):
+        for u in range(unroll):
+            i = n * unroll + u
+            rows, mixed, highest, total = attend_one(i, starts_ref, bias_ref, q_ref, pool)
+            mixed_ref[rows, :] = mixed
+            put_stats(i, stats_ref, highest, total)
+        return 0
+
+    lax.fori_loop(0, blocks // unroll, step, 0)
+
+
+def merge_kernel(mixed_ref, stats_ref, message_ref, out_ref, home_scale, guest_scale):
+    base = mixed_ref.shape[0]
+    blocks = base // BLOCK
+    other = message_ref[pl.ds(base, STAT_ROWS), :].astype(jnp.float32)
+    for n in (1, 2):
+        other = other + message_ref[pl.ds(base + n * STAT_ROWS, STAT_ROWS), :].astype(jnp.float32)
+    here = stats_ref[...]
+    high_h, total_h = here[:, :BLOCK], here[:, BLOCK:]
+    high_g, total_g = other[:, :BLOCK], other[:, BLOCK:]
+    highest = jnp.maximum(high_h, high_g)
+    factor_h = jnp.exp2((high_h - highest) * EXP2_SCALE)
+    factor_g = jnp.exp2((high_g - highest) * EXP2_SCALE) * total_g
+    total = factor_h * total_h + factor_g
+    total = jnp.where(total > 0, total, 1.0)
+    home_scale[...] = factor_h / total
+    guest_scale[...] = factor_g / total
+    eye = eye_mask()
+
+    def step(i, _):
+        rows = pl.ds(pl.multiple_of(i * BLOCK, BLOCK), BLOCK)
+        scale_h = jnp.sum(jnp.where(eye, home_scale[pl.ds(i, 1), :], 0.0), axis=1, keepdims=True)
+        scale_g = jnp.sum(jnp.where(eye, guest_scale[pl.ds(i, 1), :], 0.0), axis=1, keepdims=True)
+        mixed = mixed_ref[rows, :] * scale_h + message_ref[rows, :].astype(jnp.float32) * scale_g
+        out_ref[rows, :] = mixed.astype(jnp.bfloat16)
+        return 0
+
+    lax.fori_loop(0, blocks, step, 0, unroll=4)
+
+
+VMEM = pl.BlockSpec(memory_space=pltpu.VMEM)
+SMEM = pl.BlockSpec(memory_space=pltpu.SMEM)
+ANY = pl.BlockSpec(memory_space=pl.ANY)
+
+
+def pool_scratch(rows):
+    return pltpu.VMEM((2, 4 * rows, HEAD_DIM), jnp.bfloat16)
+
+
+def attend_cost(rows):
+    area = rows * NLIST * BLOCK
+    return pl.CostEstimate(
+        flops=4 * area * HEAD_DIM, bytes_accessed=20 * rows * HEAD_DIM, transcendentals=area
+    )
+
+
+def guest_call(starts, bias, query, parts):
+    rows = query.shape[0]
+    return pl.pallas_call(
+        functools.partial(guest_kernel, 4),
+        out_shape=jax.ShapeDtypeStruct((rows + 3 * STAT_ROWS, HEAD_DIM), jnp.bfloat16),
+        in_specs=[SMEM, VMEM, VMEM, ANY, ANY, ANY, ANY],
+        out_specs=VMEM,
+        scratch_shapes=[
+            pool_scratch(rows),
+            pltpu.VMEM((STAT_ROWS, 2 * BLOCK), jnp.float32),
+            pltpu.SemaphoreType.DMA((4,)),
+        ],
+        compiler_params=pltpu.CompilerParams(vmem_limit_bytes=VMEM_LIMIT),
+        cost_estimate=attend_cost(rows),
+        name="guest_attention",
+    )(starts, bias, query, *parts)
+
+
+def home_call(starts, bias, query, parts):
+    rows = query.shape[0]
+    return pl.pallas_call(
+        functools.partial(home_kernel, 4),
+        out_shape=(
+            jax.ShapeDtypeStruct((rows, HEAD_DIM), jnp.float32),
+            jax.ShapeDtypeStruct((STAT_ROWS, 2 * BLOCK), jnp.float32),
+        ),
+        in_specs=[SMEM, VMEM, VMEM, ANY, ANY, ANY, ANY],
+        out_specs=(VMEM, VMEM),
+        scratch_shapes=[pool_scratch(rows), pltpu.SemaphoreType.DMA((4,))],
+        compiler_params=pltpu.CompilerParams(vmem_limit_bytes=VMEM_LIMIT),
+        cost_estimate=attend_cost(rows),
+        name="home_attention",
+    )(starts, bias, query, *parts)
+
+
+def merge_call(mixed, stats, message):
+    rows = mixed.shape[0]
+    return pl.pallas_call(
+        merge_kernel,
+        out_shape=jax.ShapeDtypeStruct((rows, HEAD_DIM), jnp.bfloat16),
+        in_specs=[VMEM, VMEM, VMEM],
+        out_specs=VMEM,
+        scratch_shapes=[
+            pltpu.VMEM((STAT_ROWS, BLOCK), jnp.float32),
+            pltpu.VMEM((STAT_ROWS, BLOCK), jnp.float32),
+        ],
+        compiler_params=pltpu.CompilerParams(vmem_limit_bytes=VMEM_LIMIT),
+        cost_estimate=pl.CostEstimate(
+            flops=4 * rows * HEAD_DIM, bytes_accessed=8 * rows * HEAD_DIM, transcendentals=0
+        ),
+        name="merge_halves",
+    )(mixed, stats, message)
+
+
+def key_places(shard, myself, global_ids, rand_ids, local_blocks, shards):
+    half = shards // 2
+    total_blocks = local_blocks * shards
+    block_ids = shard * local_blocks + jnp.arange(local_blocks, dtype=jnp.int32)
+    near = block_ids[:, None] + jnp.arange(-1, 2, dtype=jnp.int32)[None, :]
+    inside = (near >= 0) & (near < total_blocks)
+    listed = lax.dynamic_slice_in_dim(rand_ids, shard * local_blocks, local_blocks, 0)
+    glob = jnp.broadcast_to(global_ids[None, :], (local_blocks, NGLOBAL))
+    ids = jnp.concatenate([jnp.clip(near, 0, total_blocks - 1), glob, listed], axis=1)
+    owner = ids // local_blocks
+    here = (owner // half) == (myself // half)
+    here = here & jnp.concatenate(
+        [inside, jnp.ones((local_blocks, NGLOBAL + NRANDOM), jnp.bool_)], axis=1
+    )
+    relative = (owner ^ myself) & (half - 1)
+    starts = jnp.where(here, (relative * local_blocks + ids % local_blocks) * BLOCK, 0)
+    bias = jnp.repeat(jnp.where(here, 0.0, MASKED).astype(jnp.float32), BLOCK, axis=1)
+    return starts.reshape(-1).astype(jnp.int32), bias
+
+
+def swap(value, distance, shards):
+    return lax.ppermute(value, "seq", [(i, i ^ distance) for i in range(shards)])
+
+
+def halves_body(queries, keys_values, global_ids, rand_ids, out_weight):
+    rows, width = queries.shape
+    heads_here = width // HEAD_DIM
+    local_blocks = rows // BLOCK
+    shards = lax.axis_size("seq")
+    myself = lax.axis_index("seq")
+    groups = lax.axis_size("head")
+    opposite = shards // 2
+
+    def column(array, head):
+        return lax.slice_in_dim(array, head * HEAD_DIM, (head + 1) * HEAD_DIM, axis=array.ndim - 1)
+
+    own_pairs = [column(keys_values, h) for h in range(heads_here)]
+    own_queries = [column(queries, h) for h in range(heads_here)]
+    home = key_places(myself, myself, global_ids, rand_ids, local_blocks, shards)
+    guest = key_places(myself ^ opposite, myself, global_ids, rand_ids, local_blocks, shards)
+
+    parts, visitors = [], []
+    for h in range(heads_here):
+        along_z = swap(own_pairs[h], 2, shards)
+        along_y = swap(own_pairs[h], 1, shards)
+        visitors.append(swap(own_queries[h], opposite, shards))
+        diagonal = swap(along_z, 1, shards)
+        parts.append((own_pairs[h], along_y, along_z, diagonal))
+
+    weights = out_weight.reshape(groups, heads_here, HEAD_DIM, out_weight.shape[1])
+    summed = None
+    for h in range(heads_here):
+        message = guest_call(*guest, visitors[h], parts[h])
+        answer = swap(message, opposite, shards)
+        mixed, stats = home_call(*home, own_queries[h], parts[h])
+        attended = merge_call(mixed, stats, answer)
+        gathered = lax.all_gather(attended, "head", axis=1, tiled=True)
+        weight = weights[:, h].reshape(groups * HEAD_DIM, -1)
+        term = jnp.dot(gathered, weight, preferred_element_type=jnp.float32)
+        summed = term if summed is None else summed + term
+    return summed.astype(jnp.bfloat16)
 
 
 def padded_2(block, sides, width):
@@ -74,7 +331,7 @@
     return mixed.astype(jnp.bfloat16)
 
 
-def body(queries, keys_values, global_ids, rand_ids, out_weight):
+def exchange_body(queries, keys_values, global_ids, rand_ids, out_weight):
     rows = queries.shape[0]
     width = queries.shape[1]
     heads_here = width // HEAD_DIM
@@ -141,6 +398,7 @@
 
 
 def solution(mesh):
+    body = halves_body if mesh.shape["seq"] == 8 else exchange_body
     in_specs = (P("seq", "head"), P(None, "seq", "head"), P(), P(), P(None, "head"))
     out_specs = P("seq", "head")
     return jax.shard_map(body, mesh=mesh, in_specs=in_specs, out_specs=out_specs, check_vma=False)

time: 524 us -> 339 us (0.65)
  waiting for transfers between devices: 271 us -> 166 us
  local copies, waits for them, and re-layouts: 125 us -> 24.8 us
  Pallas kernels: 0 us -> 75.9 us
  other arithmetic: 51 us -> 4.14 us
    ppermute x2 -> x20, waiting for transfers between devices: 15.8 us -> 166 us  [swap(): lax.ppermute(value, 'seq', [(i, i ^ distance) for i in range(shards)])]
    all_to_all x3 -> x0, waiting for transfers between devices: 128 us -> none  [body(): lax.all_to_all(outgoing, 'seq', split_axis=1, concat_axis=1, tiled=True)]
    psum x1 -> x0, waiting for transfers between devices: 81.9 us -> none  [broadcast(): return lax.psum(block, axis)]
    pallas_call x0 -> x12, Pallas kernels: none -> 75.9 us  [the longest x4 34.4 us: guest_call(): pl.pallas_call(functools.partial(guest_kernel, 4), out_shape=jax.ShapeDty...]
    all_gather x1 -> x4, waiting for transfers between devices: 45.8 us -> 0.01 us  [halves_body(): gathered = lax.all_gather(attended, 'head', axis=1, tiled=True)]
    slice x14 -> x3, local copies, waits for them, and re-layouts: 41.3 us -> 7.57 us  [the longest x1 4.18 us: halves_body(): weight = weights[:, h].reshape(groups * HEAD_DIM, -1)]
    gather x6 -> x0, local copies, waits for them, and re-layouts: 20.9 us -> none  [the longest x3 13.2 us: body(): fetched.append(jnp.take(incoming, slots, axis=1))]
    ppermute x2 -> x20, starting transfers between devices: 5.05 us -> 25.2 us  [swap(): lax.ppermute(value, 'seq', [(i, i ^ distance) for i in range(shards)])]
  transfers between devices with their start and end apart: 7 -> 24, of which waited for: 5 -> 12; matrix products, arithmetic and copies ran while one was open for 9% -> 12% of each run, Pallas kernels for 0% -> 19%
where the time goes in v1:
time: 339 us; the launch traced here: 338 us
  waiting for transfers between devices  166 us (49%)
  Pallas kernels  75.9 us (22%)
  matrix products  29 us (9%)
  starting transfers between devices  25.6 us (8%)
  local copies, waits for them, and re-layouts  24.8 us (7%)
  between operations  13.3 us (4%)
  other arithmetic  4.14 us (1%)
    ppermute x20, waiting for transfers between devices, swap(): lax.ppermute(value, 'seq', [(i, i ^ distance) for i in range(shards)])  166 us
    pallas_call x4, Pallas kernels, guest_call(): pl.pallas_call(functools.partial(guest_kernel, 4), out_shape=jax.ShapeDty...  34.4 us
    pallas_call x4, Pallas kernels, home_call(): pl.pallas_call(functools.partial(home_kernel, 4), out_shape=(jax.ShapeDty...  33.6 us
    dot_general x4, matrix products, halves_body(): term = jnp.dot(gathered, weight, preferred_element_type=jnp.float32)  29 us
    ppermute x20, starting transfers between devices, swap(): lax.ppermute(value, 'seq', [(i, i ^ distance) for i in range(shards)])  25.2 us
    pallas_call x4, Pallas kernels, merge_call(): pl.pallas_call(merge_kernel, out_shape=jax.ShapeDtypeStruct((rows, HEAD_D...  7.88 us
  transfers between devices with their start and end apart: 24, of which 12 were waited for; matrix products, arithmetic and copies ran while one was open for 12% of the time, Pallas kernels for 19%

profile of v1, /device:TPU:0, one launch (start us, length us, event | category | flops | bytes accessed | tf_op | source)
XLA Modules:
  0.0 338.3 jit_solution(8755601998134616321)
XLA Ops:
  6.5 2.2 fusion.17
  8.8 3.1 collective-permute-start.6
  11.9 1.5 collective-permute-start.5
  14.6 2.6 collective-permute-start.8
  17.8 20.1 %collective-permute-done.6.p2 = bf16[2,1536,128]{2,1,0:T(8,128)(2,1)} collective-permute-done((bf16[2,1536,128]{2,1,0:T(8,128)(2,1)S(1)}, bf16[2,1536,128]{2,1,0:T(8,128)(2,1)}, u32[]{:S(2)}, u32[]{:S(2)}) %collective-permute-start.6) | collective-permute-done | bytes 786464 | tf_op jit(solution)/shard_map/ppermute | solution.py:230
  37.9 1.7 collective-permute-start.7
  41.9 1.4 broadcast_select_fusion
  43.2 1.3 fusion.9
  44.6 1.4 copy.10
  46.7 1.4 copy.11
  48.1 1.4 broadcast_in_dim.37
  49.5 1.6 reshape.31.bias_ref
  51.1 5.9 %collective-permute-done.7.p3 = bf16[2,1536,128]{2,1,0:T(8,128)(2,1)} collective-permute-done((bf16[2,1536,128]{2,1,0:T(8,128)(2,1)}, bf16[2,1536,128]{2,1,0:T(8,128)(2,1)}, u32[]{:S(2)}, u32[]{:S(2)}) %collective-permute-start.7) | collective-permute-done | bytes 786464 | tf_op jit(solution)/shard_map/ppermute | solution.py:230
  57.8 10.6 %guest_attention.5 = bf16[1632,128]{1,0:T(8,128)(2,1)} custom-call(s32[192]{0:T(256)S(1)} %reshape.30.starts_ref, f32[24,512]{1,0:T(8,128)S(1)} %copy-done.2, bf16[1536,128]{1,0:T(8,128)(2,1)} %collective-permute-done.8.q_ref, bf16[2,1536,128]{2,1,0:T(8,128)(2,1)S(1)} %get-tuple-element.29.p0, bf16[2,1536,128]{2,1,0:T(8,128)(2,1)} %collective-permute-done.5.p1, ...), custom_call_target="tpu_custom_call" | custom-call | flops 402653184 | bytes 3932160 | tf_op jit(solution)/shard_map/guest_attention/pallas_call | solution.py:157
  68.4 1.5 collective-permute-start.9
  72.0 1.4 broadcast_in_dim.36
  73.4 1.6 reshape.29.bias_ref
  75.8 9.8 %home_attention.5 = (f32[1536,128]{1,0:T(8,128)S(1)}, f32[32,128]{1,0:T(8,128)S(1)}) custom-call(s32[192]{0:T(256)S(1)} %reshape.28.starts_ref, f32[24,512]{1,0:T(8,128)S(1)} %copy-done.6, bf16[1536,128]{1,0:T(8,128)(2,1)} %get-tuple-element.33.q_ref, bf16[2,1536,128]{2,1,0:T(8,128)(2,1)S(1)} %get-tuple-element.29.p0, ...), custom_call_target="tpu_custom_call" | custom-call | flops 402653184 | bytes 3932160 | tf_op jit(solution)/shard_map/home_attention/pallas_call | solution.py:175
  85.7 2.9 collective-permute-done.9.message_ref
  88.5 2.7 merge_halves.5
  91.4 1.3 collective-permute-start.10
  92.7 17.6 %collective-permute-done.11.p2 = bf16[2,1536,128]{2,1,0:T(8,128)(2,1)S(1)} collective-permute-done((bf16[2,1536,128]{2,1,0:T(8,128)(2,1)S(1)}, bf16[2,1536,128]{2,1,0:T(8,128)(2,1)S(1)}, u32[]{:S(2)}, u32[]{:S(2)}) %collective-permute-start.11) | collective-permute-done | bytes 786464 | tf_op jit(solution)/shard_map/ppermute | solution.py:230
  110.9 2.3 collective-permute-start.13
  113.2 17.2 %collective-permute-done.13.q_ref = bf16[1536,128]{1,0:T(8,128)(2,1)S(1)} collective-permute-done((bf16[1536,128]{1,0:T(8,128)(2,1)}, bf16[1536,128]{1,0:T(8,128)(2,1)S(1)}, u32[]{:S(2)}, u32[]{:S(2)}) %collective-permute-start.13) | collective-permute-done | bytes 393248 | tf_op jit(solution)/shard_map/ppermute | solution.py:230
  131.2 7.9 %guest_attention.6 = bf16[1632,128]{1,0:T(8,128)(2,1)S(1)} custom-call(s32[192]{0:T(256)S(1)} %reshape.30.starts_ref, f32[24,512]{1,0:T(8,128)S(1)} %copy-done.3, bf16[1536,128]{1,0:T(8,128)(2,1)S(1)} %collective-permute-done.13.q_ref, bf16[2,1536,128]{2,1,0:T(8,128)(2,1)S(1)} %get-tuple-element.32.p0, bf16[2,1536,128]{2,1,0:T(8,128)(2,1)S(1)} %collective-permute-done.10.p1, ...), custom_call_target="tpu_custom_call" | custom-call | flops 402653184 | bytes 3932160 | tf_op jit(solution)/shard_map/guest_attention/pallas_call | solution.py:157
  140.4 7.9 %home_attention.6 = (f32[1536,128]{1,0:T(8,128)S(1)}, f32[32,128]{1,0:T(8,128)S(1)}) custom-call(s32[192]{0:T(256)S(1)} %reshape.28.starts_ref, f32[24,512]{1,0:T(8,128)S(1)} %copy-done.7, bf16[1536,128]{1,0:T(8,128)(2,1)S(1)} %copy-done.1, bf16[2,1536,128]{2,1,0:T(8,128)(2,1)S(1)} %get-tuple-element.32.p0, ...), custom_call_target="tpu_custom_call" | custom-call | flops 402653184 | bytes 3932160 | tf_op jit(solution)/shard_map/home_attention/pallas_call | solution.py:175
  148.3 11.4 %collective-permute-done.14.message_ref = bf16[1632,128]{1,0:T(8,128)(2,1)S(1)} collective-permute-done((bf16[1632,128]{1,0:T(8,128)(2,1)S(1)}, bf16[1632,128]{1,0:T(8,128)(2,1)S(1)}, u32[]{:S(2)}, u32[]{:S(2)}) %collective-permute-start.14) | collective-permute-done | bytes 417824 | tf_op jit(solution)/shard_map/ppermute | solution.py:230
  159.8 1.7 merge_halves.6
  162.8 16.5 %collective-permute-done.1.p2 = bf16[2,1536,128]{2,1,0:T(8,128)(2,1)S(1)} collective-permute-done((bf16[2,1536,128]{2,1,0:T(8,128)(2,1)S(1)}, bf16[2,1536,128]{2,1,0:T(8,128)(2,1)S(1)}, u32[]{:S(2)}, u32[]{:S(2)}) %collective-permute-start.1) | collective-permute-done | bytes 786464 | tf_op jit(solution)/shard_map/ppermute | solution.py:230
  179.3 1.7 collective-permute-start.2
  181.0 1.2 collective-permute-start.3
  182.2 17.0 %collective-permute-done.3.q_ref = bf16[1536,128]{1,0:T(8,128)(2,1)S(1)} collective-permute-done((bf16[1536,128]{1,0:T(8,128)(2,1)S(1)}, bf16[1536,128]{1,0:T(8,128)(2,1)S(1)}, u32[]{:S(2)}, u32[]{:S(2)}) %collective-permute-start.3) | collective-permute-done | bytes 393248 | tf_op jit(solution)/shard_map/ppermute | solution.py:230
  200.0 7.9 %guest_attention.4 = bf16[1632,128]{1,0:T(8,128)(2,1)S(1)} custom-call(s32[192]{0:T(256)S(1)} %reshape.30.starts_ref, f32[24,512]{1,0:T(8,128)S(1)} %copy-done.4, bf16[1536,128]{1,0:T(8,128)(2,1)S(1)} %collective-permute-done.3.q_ref, bf16[2,1536,128]{2,1,0:T(8,128)(2,1)S(1)} %get-tuple-element.30.p0, bf16[2,1536,128]{2,1,0:T(8,128)(2,1)S(1)} %collective-permute-done.p1, ...), custom_call_target="tpu_custom_call" | custom-call | flops 402653184 | bytes 3932160 | tf_op jit(solution)/shard_map/guest_attention/pallas_call | solution.py:157
  209.0 7.9 %home_attention.4 = (f32[1536,128]{1,0:T(8,128)S(1)}, f32[32,128]{1,0:T(8,128)S(1)}) custom-call(s32[192]{0:T(256)S(1)} %reshape.28.starts_ref, f32[24,512]{1,0:T(8,128)S(1)} %copy-done.8, bf16[1536,128]{1,0:T(8,128)(2,1)S(1)} %copy-done, bf16[2,1536,128]{2,1,0:T(8,128)(2,1)S(1)} %get-tuple-element.30.p0, bf16[2,1536,128]{2,1,0:T(8,128)(2,1)S(1)} %collective-permute-done.p1, ...), custom_call_target="tpu_custom_call" | custom-call | flops 402653184 | bytes 3932160 | tf_op jit(solution)/shard_map/home_attention/pallas_call | solution.py:175
  216.9 11.6 %collective-permute-done.4.message_ref = bf16[1632,128]{1,0:T(8,128)(2,1)S(1)} collective-permute-done((bf16[1632,128]{1,0:T(8,128)(2,1)S(1)}, bf16[1632,128]{1,0:T(8,128)(2,1)S(1)}, u32[]{:S(2)}, u32[]{:S(2)}) %collective-permute-start.4) | collective-permute-done | bytes 417824 | tf_op jit(solution)/shard_map/ppermute | solution.py:230
  228.6 1.7 merge_halves.4
  231.6 16.7 %collective-permute-done.16.p2 = bf16[2,1536,128]{2,1,0:T(8,128)(2,1)S(1)} collective-permute-done((bf16[2,1536,128]{2,1,0:T(8,128)(2,1)S(1)}, bf16[2,1536,128]{2,1,0:T(8,128)(2,1)S(1)}, u32[]{:S(2)}, u32[]{:S(2)}) %collective-permute-start.16) | collective-permute-done | bytes 786464 | tf_op jit(solution)/shard_map/ppermute | solution.py:230
  249.2 2.2 collective-permute-start.18
  251.4 17.0 %collective-permute-done.18.q_ref = bf16[1536,128]{1,0:T(8,128)(2,1)S(1)} collective-permute-done((bf16[1536,128]{1,0:T(8,128)(2,1)S(1)}, bf16[1536,128]{1,0:T(8,128)(2,1)S(1)}, u32[]{:S(2)}, u32[]{:S(2)}) %collective-permute-start.18) | collective-permute-done | bytes 393248 | tf_op jit(solution)/shard_map/ppermute | solution.py:230
  268.4 7.9 %guest_attention.7 = bf16[1632,128]{1,0:T(8,128)(2,1)S(1)} custom-call(s32[192]{0:T(256)S(1)} %reshape.30.starts_ref, f32[24,512]{1,0:T(8,128)S(1)} %copy-done.5, bf16[1536,128]{1,0:T(8,128)(2,1)S(1)} %collective-permute-done.18.q_ref, bf16[2,1536,128]{2,1,0:T(8,128)(2,1)S(1)} %get-tuple-element.31.p0, bf16[2,1536,128]{2,1,0:T(8,128)(2,1)S(1)} %collective-permute-done.15.p1, ...), custom_call_target="tpu_custom_call" | custom-call | flops 402653184 | bytes 3932160 | tf_op jit(solution)/shard_map/guest_attention/pallas_call | solution.py:157
  277.3 7.9 %home_attention.7 = (f32[1536,128]{1,0:T(8,128)S(1)}, f32[32,128]{1,0:T(8,128)S(1)}) custom-call(s32[192]{0:T(256)S(1)} %reshape.28.starts_ref, f32[24,512]{1,0:T(8,128)S(1)} %copy-done.8, bf16[1536,128]{1,0:T(8,128)(2,1)S(1)} %get-tuple-element.35.q_ref, bf16[2,1536,128]{2,1,0:T(8,128)(2,1)S(1)} %get-tuple-element.31.p0, ...), custom_call_target="tpu_custom_call" | custom-call | flops 402653184 | bytes 3932160 | tf_op jit(solution)/shard_map/home_attention/pallas_call | solution.py:175
  285.2 11.7 %collective-permute-done.19.message_ref = bf16[1632,128]{1,0:T(8,128)(2,1)S(1)} collective-permute-done((bf16[1632,128]{1,0:T(8,128)(2,1)S(1)}, bf16[1632,128]{1,0:T(8,128)(2,1)S(1)}, u32[]{:S(2)}, u32[]{:S(2)}) %collective-permute-start.19) | collective-permute-done | bytes 417824 | tf_op jit(solution)/shard_map/ppermute | solution.py:230
  296.9 1.7 merge_halves.7
  298.6 4.2 %fusion.16 = (bf16[4,1,128,1024]{3,2,1,0:T(8,128)(2,1)}, bf16[4,1,128,1024]{3,2,1,0:T(8,128)(2,1)S(1)}, bf16[4,1,128,1024]{3,2,1,0:T(8,128)(2,1)}, bf16[4,1,128,1024]{3,2,1,0:T(8,128)(2,1)S(1)}) fusion(bf16[4,4,128,1024]{3,2,1,0:T(8,128)(2,1)} %bitcast.13), kind=kLoop, calls=%fused_computation.52 | loop fusion | bytes 8388608 | tf_op jit(solution)/shard_map/slice | solution.py:266
  302.8 6.3 %fusion.20 = f32[1536,1024]{1,0:T(8,128)} fusion(bf16[1536,512]{1,0:T(8,128)(2,1)} %all-gather.7.cloned.1.call-done, bf16[512,1024]{1,0:T(8,128)(2,1)} %bitcast.17), kind=kOutput, calls=%fused_computation.56 | convolution fusion | flops 1610612736 | bytes 8912896 | tf_op jit(solution)/shard_map/dot_general | solution.py:267
  309.1 6.2 %fusion.21 = f32[1536,1024]{1,0:T(8,128)} fusion(bf16[1536,512]{1,0:T(8,128)(2,1)} %all-gather.9.cloned.1.call-done, bf16[512,1024]{1,0:T(8,128)(2,1)} %bitcast.16), kind=kOutput, calls=%fused_computation.57 | convolution fusion | flops 1610612736 | bytes 8912896 | tf_op jit(solution)/shard_map/dot_general | solution.py:267
  315.3 5.9 %fusion.19 = f32[1536,1024]{1,0:T(8,128)} fusion(bf16[1536,512]{1,0:T(8,128)(2,1)} %all-gather.5.cloned.1.call-done, bf16[512,1024]{1,0:T(8,128)(2,1)S(1)} %bitcast.15), kind=kOutput, calls=%fused_computation.55 | convolution fusion | flops 1610612736 | bytes 8912896 | tf_op jit(solution)/shard_map/dot_general | solution.py:267
  321.2 10.6 %add_convert_fusion = bf16[1536,1024]{1,0:T(8,128)(2,1)} fusion(f32[1536,1024]{1,0:T(8,128)} %fusion.21, f32[1536,1024]{1,0:T(8,128)} %fusion.19, f32[1536,1024]{1,0:T(8,128)} %fusion.20, bf16[1536,512]{1,0:T(8,128)(2,1)} %all-gather.11.cloned.1.call-done, bf16[512,1024]{1,0:T(8,128)(2,1)S(1)} %bitcast.14), kind=kOutput, calls=%fused_computation | convolution fusion | flops 1616904192 | bytes 24641536 | tf_op jit(solution)/shard_map/dot_general | solution.py:267
  (65 shorter events, 17.5 us)
Async XLA Ops:
  6.5 296.3 %all-gather.7.cloned.1.call-start = ((), (), s32[]{:S(2)}) async-start(), calls=%async_computation.1 | async-start | bytes 1966080 | tf_op jit(solution)/shard_map/all_gather | solution.py:265
  6.5 6.9 %copy-start.9 = (bf16[1536,512]{1,0:T(8,128)(2,1)S(1)}, bf16[1536,512]{1,0:T(8,128)(2,1)}, u32[]{:S(2)}) copy-start(bf16[1536,512]{1,0:T(8,128)(2,1)} %param.5) | copy-start | bytes 4718596
  8.8 30.9 %copy-start.11 = (s32[2]{0:T(128)S(1)}, s32[2]{0:T(128)}, u32[]{:S(2)}) copy-start(s32[2]{0:T(128)} %param.7) | copy-start | bytes 28
  8.8 29.2 %collective-permute-start.6 = (bf16[2,1536,128]{2,1,0:T(8,128)(2,1)S(1)}, bf16[2,1536,128]{2,1,0:T(8,128)(2,1)}, u32[]{:S(2)}, u32[]{:S(2)}) collective-permute-start(bf16[2,1536,128]{2,1,0:T(8,128)(2,1)S(1)} %get-tuple-element.29.p0), channel_id=1, source_target_pairs={{0,8},{4,12},{8,0},{12,4},{16,24},{20,28},{24,16},{28,20},{1,9},{5... | collective-permute-start | bytes 2359304 | tf_op jit(solution)/shard_map/ppermute | solution.py:230
  11.9 39.3 %collective-permute-start.5 = (bf16[2,1536,128]{2,1,0:T(8,128)(2,1)S(1)}, bf16[2,1536,128]{2,1,0:T(8,128)(2,1)}, u32[]{:S(2)}, u32[]{:S(2)}) collective-permute-start(bf16[2,1536,128]{2,1,0:T(8,128)(2,1)S(1)} %get-tuple-element.29.p0), channel_id=1, source_target_pairs={{0,4},{4,0},{8,12},{12,8},{16,20},{20,16},{24,28},{28,24},{1,5},{5... | collective-permute-start | bytes 2359304 | tf_op jit(solution)/shard_map/ppermute | solution.py:230
  14.6 36.6 %collective-permute-start.8 = (bf16[1536,128]{1,0:T(8,128)(2,1)}, bf16[1536,128]{1,0:T(8,128)(2,1)}, u32[]{:S(2)}, u32[]{:S(2)}) collective-permute-start(bf16[1536,128]{1,0:T(8,128)(2,1)} %get-tuple-element.33.q_ref), channel_id=1, source_target_pairs={{0,16},{4,20},{8,24},{12,28},{16,0},{20,4},{24,8},{28,12},{1,17},{... | collective-permute-start | bytes 1179656 | tf_op jit(solution)/shard_map/ppermute | solution.py:230
  17.2 23.1 %copy-start.10 = (s32[3]{0:T(128)}, s32[3]{0:T(128)S(1)}, u32[]{:S(2)}) copy-start(s32[3]{0:T(128)S(1)} %iota_add_fusion.1) | copy-start | bytes 40
  37.9 19.0 %collective-permute-start.7 = (bf16[2,1536,128]{2,1,0:T(8,128)(2,1)}, bf16[2,1536,128]{2,1,0:T(8,128)(2,1)}, u32[]{:S(2)}, u32[]{:S(2)}) collective-permute-start(bf16[2,1536,128]{2,1,0:T(8,128)(2,1)} %collective-permute-done.6.p2), channel_id=1, source_target_pairs={{0,4},{4,0},{8,12},{12,8},{16,20},{20,16},{24,28},{28,24},{1,5},{5... | collective-permute-start | bytes 2359304 | tf_op jit(solution)/shard_map/ppermute | solution.py:230
  57.0 0.8 copy-start.2
  68.4 20.1 %collective-permute-start.9 = (bf16[1632,128]{1,0:T(8,128)(2,1)}, bf16[1632,128]{1,0:T(8,128)(2,1)}, u32[]{:S(2)}, u32[]{:S(2)}) collective-permute-start(bf16[1632,128]{1,0:T(8,128)(2,1)} %guest_attention.5), channel_id=1, source_target_pairs={{0,16},{4,20},{8,24},{12,28},{16,0},{20,4},{24,8},{28,12},{1,17},{... | collective-permute-start | bytes 1253384 | tf_op jit(solution)/shard_map/ppermute | solution.py:230
  75.0 0.8 copy-start.6
  85.7 53.9 %copy-start.1 = (bf16[1536,128]{1,0:T(8,128)(2,1)S(1)}, bf16[1536,128]{1,0:T(8,128)(2,1)}, u32[]{:S(2)}) copy-start(bf16[1536,128]{1,0:T(8,128)(2,1)} %get-tuple-element.36.q_ref) | copy-start | bytes 1179652
  91.3 217.8 %all-gather.9.cloned.1.call-start = ((), (), s32[]{:S(2)}) async-start(), calls=%async_computation.2 | async-start | bytes 1966080 | tf_op jit(solution)/shard_map/all_gather | solution.py:265
  91.3 19.0 %collective-permute-start.11 = (bf16[2,1536,128]{2,1,0:T(8,128)(2,1)S(1)}, bf16[2,1536,128]{2,1,0:T(8,128)(2,1)S(1)}, u32[]{:S(2)}, u32[]{:S(2)}) collective-permute-start(bf16[2,1536,128]{2,1,0:T(8,128)(2,1)S(1)} %get-tuple-element.32.p0), channel_id=1, source_target_pairs={{0,8},{4,12},{8,0},{12,4},{16,24},{20,28},{24,16},{28,20},{1,9},{5... | collective-permute-start | bytes 2359304 | tf_op jit(solution)/shard_map/ppermute | solution.py:230
  91.4 39.0 %collective-permute-start.10 = (bf16[2,1536,128]{2,1,0:T(8,128)(2,1)S(1)}, bf16[2,1536,128]{2,1,0:T(8,128)(2,1)S(1)}, u32[]{:S(2)}, u32[]{:S(2)}) collective-permute-start(bf16[2,1536,128]{2,1,0:T(8,128)(2,1)S(1)} %get-tuple-element.32.p0), channel_id=1, source_target_pairs={{0,4},{4,0},{8,12},{12,8},{16,20},{20,16},{24,28},{28,24},{1,5},{5... | collective-permute-start | bytes 2359304 | tf_op jit(solution)/shard_map/ppermute | solution.py:230
  110.3 20.1 %collective-permute-start.12 = (bf16[2,1536,128]{2,1,0:T(8,128)(2,1)S(1)}, bf16[2,1536,128]{2,1,0:T(8,128)(2,1)S(1)}, u32[]{:S(2)}, u32[]{:S(2)}) collective-permute-start(bf16[2,1536,128]{2,1,0:T(8,128)(2,1)S(1)} %collective-permute-done.11.p2), channel_id=1, source_target_pairs={{0,4},{4,0},{8,12},{12,8},{16,20},{20,16},{24,28},{28,24},{1,5},{5... | collective-permute-start | bytes 2359304 | tf_op jit(solution)/shard_map/ppermute | solution.py:230
  110.9 19.6 %collective-permute-start.13 = (bf16[1536,128]{1,0:T(8,128)(2,1)}, bf16[1536,128]{1,0:T(8,128)(2,1)S(1)}, u32[]{:S(2)}, u32[]{:S(2)}) collective-permute-start(bf16[1536,128]{1,0:T(8,128)(2,1)} %get-tuple-element.36.q_ref), channel_id=1, source_target_pairs={{0,16},{4,20},{8,24},{12,28},{16,0},{20,4},{24,8},{28,12},{1,17},{... | collective-permute-start | bytes 1179656 | tf_op jit(solution)/shard_map/ppermute | solution.py:230
  130.4 0.8 copy-start.3
  139.2 41.8 %copy-start = (bf16[1536,128]{1,0:T(8,128)(2,1)S(1)}, bf16[1536,128]{1,0:T(8,128)(2,1)}, u32[]{:S(2)}) copy-start(bf16[1536,128]{1,0:T(8,128)(2,1)} %get-tuple-element.34.q_ref) | copy-start | bytes 1179652
  139.2 20.6 %collective-permute-start.14 = (bf16[1632,128]{1,0:T(8,128)(2,1)S(1)}, bf16[1632,128]{1,0:T(8,128)(2,1)S(1)}, u32[]{:S(2)}, u32[]{:S(2)}) collective-permute-start(bf16[1632,128]{1,0:T(8,128)(2,1)S(1)} %guest_attention.6), channel_id=1, source_target_pairs={{0,16},{4,20},{8,24},{12,28},{16,0},{20,4},{24,8},{28,12},{1,17},{... | collective-permute-start | bytes 1253384 | tf_op jit(solution)/shard_map/ppermute | solution.py:230
  139.6 0.8 copy-start.7
  148.3 60.7 %copy-start.8 = (f32[24,512]{1,0:T(8,128)S(1)}, f32[24,512]{1,0:T(8,128)}, u32[]{:S(2)}) copy-start(f32[24,512]{1,0:T(8,128)} %reshape.29.bias_ref) | copy-start | bytes 147460
  161.5 153.8 %all-gather.5.cloned.1.call-start = ((), (), s32[]{:S(2)}) async-start(), calls=%async_computation | async-start | bytes 1966080 | tf_op jit(solution)/shard_map/all_gather | solution.py:265
  161.6 17.7 %collective-permute-start.1 = (bf16[2,1536,128]{2,1,0:T(8,128)(2,1)S(1)}, bf16[2,1536,128]{2,1,0:T(8,128)(2,1)S(1)}, u32[]{:S(2)}, u32[]{:S(2)}) collective-permute-start(bf16[2,1536,128]{2,1,0:T(8,128)(2,1)S(1)} %get-tuple-element.30.p0), channel_id=1, source_target_pairs={{0,8},{4,12},{8,0},{12,4},{16,24},{20,28},{24,16},{28,20},{1,9},{5... | collective-permute-start | bytes 2359304 | tf_op jit(solution)/shard_map/ppermute | solution.py:230
  161.6 37.6 %collective-permute-start = (bf16[2,1536,128]{2,1,0:T(8,128)(2,1)S(1)}, bf16[2,1536,128]{2,1,0:T(8,128)(2,1)S(1)}, u32[]{:S(2)}, u32[]{:S(2)}) collective-permute-start(bf16[2,1536,128]{2,1,0:T(8,128)(2,1)S(1)} %get-tuple-element.30.p0), channel_id=1, source_target_pairs={{0,4},{4,0},{8,12},{12,8},{16,20},{20,16},{24,28},{28,24},{1,5},{5... | collective-permute-start | bytes 2359304 | tf_op jit(solution)/shard_map/ppermute | solution.py:230
  179.3 20.0 %collective-permute-start.2 = (bf16[2,1536,128]{2,1,0:T(8,128)(2,1)S(1)}, bf16[2,1536,128]{2,1,0:T(8,128)(2,1)S(1)}, u32[]{:S(2)}, u32[]{:S(2)}) collective-permute-start(bf16[2,1536,128]{2,1,0:T(8,128)(2,1)S(1)} %collective-permute-done.1.p2), channel_id=1, source_target_pairs={{0,4},{4,0},{8,12},{12,8},{16,20},{20,16},{24,28},{28,24},{1,5},{5... | collective-permute-start | bytes 2359304 | tf_op jit(solution)/shard_map/ppermute | solution.py:230
  181.0 18.3 %collective-permute-start.3 = (bf16[1536,128]{1,0:T(8,128)(2,1)S(1)}, bf16[1536,128]{1,0:T(8,128)(2,1)S(1)}, u32[]{:S(2)}, u32[]{:S(2)}) collective-permute-start(bf16[1536,128]{1,0:T(8,128)(2,1)S(1)} %copy-done), channel_id=1, source_target_pairs={{0,16},{4,20},{8,24},{12,28},{16,0},{20,4},{24,8},{28,12},{1,17},{... | collective-permute-start | bytes 1179656 | tf_op jit(solution)/shard_map/ppermute | solution.py:230
  199.2 0.8 copy-start.4
  208.0 60.4 %copy-start.5 = (f32[24,512]{1,0:T(8,128)S(1)}, f32[24,512]{1,0:T(8,128)}, u32[]{:S(2)}) copy-start(f32[24,512]{1,0:T(8,128)} %reshape.31.bias_ref) | copy-start | bytes 147460
  208.0 20.6 %collective-permute-start.4 = (bf16[1632,128]{1,0:T(8,128)(2,1)S(1)}, bf16[1632,128]{1,0:T(8,128)(2,1)S(1)}, u32[]{:S(2)}, u32[]{:S(2)}) collective-permute-start(bf16[1632,128]{1,0:T(8,128)(2,1)S(1)} %guest_attention.4), channel_id=1, source_target_pairs={{0,16},{4,20},{8,24},{12,28},{16,0},{20,4},{24,8},{28,12},{1,17},{... | collective-permute-start | bytes 1253384 | tf_op jit(solution)/shard_map/ppermute | solution.py:230
  230.3 90.9 %all-gather.11.cloned.1.call-start = ((), (), s32[]{:S(2)}) async-start(), calls=%async_computation.3 | async-start | bytes 1966080 | tf_op jit(solution)/shard_map/all_gather | solution.py:265
  230.5 17.7 %collective-permute-start.16 = (bf16[2,1536,128]{2,1,0:T(8,128)(2,1)S(1)}, bf16[2,1536,128]{2,1,0:T(8,128)(2,1)S(1)}, u32[]{:S(2)}, u32[]{:S(2)}) collective-permute-start(bf16[2,1536,128]{2,1,0:T(8,128)(2,1)S(1)} %get-tuple-element.31.p0), channel_id=1, source_target_pairs={{0,8},{4,12},{8,0},{12,4},{16,24},{20,28},{24,16},{28,20},{1,9},{5... | collective-permute-start | bytes 2359304 | tf_op jit(solution)/shard_map/ppermute | solution.py:230
  230.6 37.8 %collective-permute-start.15 = (bf16[2,1536,128]{2,1,0:T(8,128)(2,1)S(1)}, bf16[2,1536,128]{2,1,0:T(8,128)(2,1)S(1)}, u32[]{:S(2)}, u32[]{:S(2)}) collective-permute-start(bf16[2,1536,128]{2,1,0:T(8,128)(2,1)S(1)} %get-tuple-element.31.p0), channel_id=1, source_target_pairs={{0,4},{4,0},{8,12},{12,8},{16,20},{20,16},{24,28},{28,24},{1,5},{5... | collective-permute-start | bytes 2359304 | tf_op jit(solution)/shard_map/ppermute | solution.py:230
  248.2 20.1 %collective-permute-start.17 = (bf16[2,1536,128]{2,1,0:T(8,128)(2,1)S(1)}, bf16[2,1536,128]{2,1,0:T(8,128)(2,1)S(1)}, u32[]{:S(2)}, u32[]{:S(2)}) collective-permute-start(bf16[2,1536,128]{2,1,0:T(8,128)(2,1)S(1)} %collective-permute-done.16.p2), channel_id=1, source_target_pairs={{0,4},{4,0},{8,12},{12,8},{16,20},{20,16},{24,28},{28,24},{1,5},{5... | collective-permute-start | bytes 2359304 | tf_op jit(solution)/shard_map/ppermute | solution.py:230
  249.2 19.2 %collective-permute-start.18 = (bf16[1536,128]{1,0:T(8,128)(2,1)S(1)}, bf16[1536,128]{1,0:T(8,128)(2,1)S(1)}, u32[]{:S(2)}, u32[]{:S(2)}) collective-permute-start(bf16[1536,128]{1,0:T(8,128)(2,1)S(1)} %get-tuple-element.35.q_ref), channel_id=1, source_target_pairs={{0,16},{4,20},{8,24},{12,28},{16,0},{20,4},{24,8},{28,12},{1,17},{... | collective-permute-start | bytes 1179656 | tf_op jit(solution)/shard_map/ppermute | solution.py:230
  276.3 20.5 %collective-permute-start.19 = (bf16[1632,128]{1,0:T(8,128)(2,1)S(1)}, bf16[1632,128]{1,0:T(8,128)(2,1)S(1)}, u32[]{:S(2)}, u32[]{:S(2)}) collective-permute-start(bf16[1632,128]{1,0:T(8,128)(2,1)S(1)} %guest_attention.7), channel_id=1, source_target_pairs={{0,16},{4,20},{8,24},{12,28},{16,0},{20,4},{24,8},{28,12},{1,17},{... | collective-permute-start | bytes 1253384 | tf_op jit(solution)/shard_map/ppermute | solution.py:230
Sparse Core Ops, SparseCore 0:
  91.4 19.4 all-gather.6
  161.6 18.0 all-gather.8
  230.4 18.0 all-gather.4
  298.7 17.8 all-gather.10

commit v2 on v1

--- a/solution.py
+++ b/solution.py
@@ -27,30 +27,45 @@
     return rows == columns
 
 
-def attend_one(i, starts_ref, bias_ref, q_ref, pool):
-    rows = pl.ds(pl.multiple_of(i * BLOCK, BLOCK), BLOCK)
-    query = q_ref[rows, :]
-    where_ = [
-        pl.ds(pl.multiple_of(starts_ref[i * NLIST + e], BLOCK), BLOCK) for e in range(NLIST)
+def attend_group(blocks, head, starts_ref, bias_ref, q_ref, pool):
+    lanes = pl.ds(head * HEAD_DIM, HEAD_DIM)
+    listed = [
+        [
+            pl.ds(pl.multiple_of(starts_ref[i * NLIST + e], BLOCK), BLOCK)
+            for e in range(NLIST)
+        ]
+        for i in blocks
     ]
-    keys = jnp.concatenate([pool[0, w, :] for w in where_], axis=0)
-    scores = lax.dot_general(
-        query, keys, (((1,), (1,)), ((), ())), preferred_element_type=jnp.float32
-    )
-    scores = scores + bias_ref[pl.ds(i, 1), :]
-    highest = jnp.max(scores, axis=1, keepdims=True)
-    weights = jnp.exp2((scores - highest) * EXP2_SCALE)
-    total = jnp.sum(weights, axis=1, keepdims=True)
-    values = jnp.concatenate([pool[1, w, :] for w in where_], axis=0)
-    mixed = jnp.dot(weights.astype(jnp.bfloat16), values, preferred_element_type=jnp.float32)
-    return rows, mixed, highest, total
-
-
-def put_stats(i, stats_ref, highest, total):
+    places = [pl.ds(pl.multiple_of(i * BLOCK, BLOCK), BLOCK) for i in blocks]
+    scores = []
+    for i, rows, listing in zip(blocks, places, listed):
+        keys = jnp.concatenate([pool[0, w, lanes] for w in listing], axis=0)
+        product = lax.dot_general(
+            q_ref[rows, lanes],
+            keys,
+            (((1,), (1,)), ((), ())),
+            preferred_element_type=jnp.float32,
+        )
+        scores.append(product + bias_ref[pl.ds(i, 1), :])
+    weighed = []
+    for score in scores:
+        highest = jnp.max(score, axis=1, keepdims=True)
+        weights = jnp.exp2((score - highest) * EXP2_SCALE)
+        total = jnp.sum(weights, axis=1, keepdims=True)
+        weighed.append((weights.astype(jnp.bfloat16), highest, total))
+    results = []
+    for rows, listing, (weights, highest, total) in zip(places, listed, weighed):
+        values = jnp.concatenate([pool[1, w, lanes] for w in listing], axis=0)
+        mixed = jnp.dot(weights, values, preferred_element_type=jnp.float32)
+        results.append((rows, lanes, mixed, highest, total))
+    return results
+
+
+def put_stats(i, head, stats_ref, highest, total):
     eye = eye_mask()
     high_row = jnp.sum(jnp.where(eye, highest, 0.0), axis=0, keepdims=True)
     total_row = jnp.sum(jnp.where(eye, total, 0.0), axis=0, keepdims=True)
-    stats_ref[pl.ds(i, 1), :] = jnp.concatenate([high_row, total_row], axis=1)
+    stats_ref[head, pl.ds(i, 1), :] = jnp.concatenate([high_row, total_row], axis=1)
 
 
 def load_pool(parts, pool, sems):
@@ -72,21 +87,25 @@
     blocks = q_ref.shape[0] // BLOCK
     stats[...] = jnp.zeros_like(stats)
 
-    def step(n, _):
-        for u in range(unroll):
-            i = n * unroll + u
-            rows, mixed, highest, total = attend_one(i, starts_ref, bias_ref, q_ref, pool)
-            message_ref[rows, :] = (mixed / total).astype(jnp.bfloat16)
-            put_stats(i, stats, highest, total)
-        return 0
-
-    lax.fori_loop(0, blocks // unroll, step, 0)
-    rest = stats[...]
+    for head in range(q_ref.shape[1] // HEAD_DIM):
+
+        def step(n, _):
+            ids = [n * unroll + u for u in range(unroll)]
+            results = attend_group(ids, head, starts_ref, bias_ref, q_ref, pool)
+            for i, (rows, lanes, mixed, highest, total) in zip(ids, results):
+                message_ref[rows, lanes] = (mixed / total).astype(jnp.bfloat16)
+                put_stats(i, head, stats, highest, total)
+            return 0
+
+        lax.fori_loop(0, blocks // unroll, step, 0)
     base = q_ref.shape[0]
-    for n in range(3):
-        piece = rest.astype(jnp.bfloat16)
-        message_ref[pl.ds(base + n * STAT_ROWS, STAT_ROWS), :] = piece
-        rest = rest - piece.astype(jnp.float32)
+    for head in range(q_ref.shape[1] // HEAD_DIM):
+        rest = stats[head]
+        for n in range(3):
+            piece = rest.astype(jnp.bfloat16)
+            rows = pl.ds(base + n * STAT_ROWS, STAT_ROWS)
+            message_ref[rows, pl.ds(head * HEAD_DIM, HEAD_DIM)] = piece
+            rest = rest - piece.astype(jnp.float32)
 
 
 def home_kernel(
@@ -96,44 +115,75 @@
     blocks = q_ref.shape[0] // BLOCK
     stats_ref[...] = jnp.zeros_like(stats_ref)
 
-    def step(n, _):
-        for u in range(unroll):
-            i = n * unroll + u
-            rows, mixed, highest, total = attend_one(i, starts_ref, bias_ref, q_ref, pool)
-            mixed_ref[rows, :] = mixed
-            put_stats(i, stats_ref, highest, total)
-        return 0
-
-    lax.fori_loop(0, blocks // unroll, step, 0)
+    for head in range(q_ref.shape[1] // HEAD_DIM):
+
+        def step(n, _):
+            ids = [n * unroll + u for u in range(unroll)]
+            results = attend_group(ids, head, starts_ref, bias_ref, q_ref, pool)
+            for i, (rows, lanes, mixed, highest, total) in zip(ids, results):
+                mixed_ref[rows, lanes] = mixed
+                put_stats(i, head, stats_ref, highest, total)
+            return 0
+
+        lax.fori_loop(0, blocks // unroll, step, 0)
 
 
 def merge_kernel(mixed_ref, stats_ref, message_ref, out_ref, home_scale, guest_scale):
-    base = mixed_ref.shape[0]
+    base, width = mixed_ref.shape
     blocks = base // BLOCK
     other = message_ref[pl.ds(base, STAT_ROWS), :].astype(jnp.float32)
     for n in (1, 2):
         other = other + message_ref[pl.ds(base + n * STAT_ROWS, STAT_ROWS), :].astype(jnp.float32)
-    here = stats_ref[...]
-    high_h, total_h = here[:, :BLOCK], here[:, BLOCK:]
-    high_g, total_g = other[:, :BLOCK], other[:, BLOCK:]
-    highest = jnp.maximum(high_h, high_g)
-    factor_h = jnp.exp2((high_h - highest) * EXP2_SCALE)
-    factor_g = jnp.exp2((high_g - highest) * EXP2_SCALE) * total_g
-    total = factor_h * total_h + factor_g
-    total = jnp.where(total > 0, total, 1.0)
-    home_scale[...] = factor_h / total
-    guest_scale[...] = factor_g / total
     eye = eye_mask()
-
-    def step(i, _):
-        rows = pl.ds(pl.multiple_of(i * BLOCK, BLOCK), BLOCK)
-        scale_h = jnp.sum(jnp.where(eye, home_scale[pl.ds(i, 1), :], 0.0), axis=1, keepdims=True)
-        scale_g = jnp.sum(jnp.where(eye, guest_scale[pl.ds(i, 1), :], 0.0), axis=1, keepdims=True)
-        mixed = mixed_ref[rows, :] * scale_h + message_ref[rows, :].astype(jnp.float32) * scale_g
-        out_ref[rows, :] = mixed.astype(jnp.bfloat16)
-        return 0
-
-    lax.fori_loop(0, blocks, step, 0, unroll=4)
+    for head in range(width // HEAD_DIM):
+        low = head * HEAD_DIM
+        lanes = pl.ds(low, HEAD_DIM)
+        high_h = stats_ref[head, :, :BLOCK]
+        total_h = stats_ref[head, :, BLOCK:]
+        high_g = other[:, low : low + BLOCK]
+        total_g = other[:, low + BLOCK : low + HEAD_DIM]
+        highest = jnp.maximum(high_h, high_g)
+        factor_h = jnp.exp2((high_h - highest) * EXP2_SCALE)
+        factor_g = jnp.exp2((high_g - highest) * EXP2_SCALE) * total_g
+        total = factor_h * total_h + factor_g
+        total = jnp.where(total > 0, total, 1.0)
+        home_scale[...] = factor_h / total
+        guest_scale[...] = factor_g / total
+
+        def step(i, _):
+            rows = pl.ds(pl.multiple_of(i * BLOCK, BLOCK), BLOCK)
+            scale_h = jnp.sum(
+                jnp.where(eye, home_scale[pl.ds(i, 1), :], 0.0), axis=1, keepdims=True
+            )
+            scale_g = jnp.sum(
+                jnp.where(eye, guest_scale[pl.ds(i, 1), :], 0.0), axis=1, keepdims=True
+            )
+            mixed = (
+                mixed_ref[rows, lanes] * scale_h
+                + message_ref[rows, lanes].astype(jnp.float32) * scale_g
+            )
+            out_ref[rows, lanes] = mixed.astype(jnp.bfloat16)
+            return 0
+
+        lax.fori_loop(0, blocks, step, 0, unroll=4)
+
+
+def products(x_refs, w_refs):
+    total = None
+    for x_ref, w_ref in zip(x_refs, w_refs):
+        weight = w_ref[...].reshape(-1, w_ref.shape[-1])
+        term = jnp.dot(x_ref[...], weight, preferred_element_type=jnp.float32)
+        total = term if total is None else total + term
+    return total
+
+
+def first_terms_kernel(count, _, *refs):
+    refs[-1][...] = products(refs[:count], refs[count : 2 * count])
+
+
+def last_term_kernel(count, _, sum_ref, *refs):
+    total = sum_ref[...] + products(refs[:count], refs[count : 2 * count])
+    refs[-1][...] = total.astype(refs[-1].dtype)
 
 
 VMEM = pl.BlockSpec(memory_space=pltpu.VMEM)
@@ -141,69 +191,112 @@
 ANY = pl.BlockSpec(memory_space=pl.ANY)
 
 
-def pool_scratch(rows):
-    return pltpu.VMEM((2, 4 * rows, HEAD_DIM), jnp.bfloat16)
-
-
-def attend_cost(rows):
-    area = rows * NLIST * BLOCK
-    return pl.CostEstimate(
-        flops=4 * area * HEAD_DIM, bytes_accessed=20 * rows * HEAD_DIM, transcendentals=area
-    )
+def params():
+    return pltpu.CompilerParams(vmem_limit_bytes=VMEM_LIMIT)
+
+
+def pool_scratch(query):
+    return pltpu.VMEM((2, 4 * query.shape[0], query.shape[1]), jnp.bfloat16)
+
+
+def stats_shape(query, kind):
+    return kind((query.shape[1] // HEAD_DIM, STAT_ROWS, 2 * BLOCK), jnp.float32)
+
+
+def cost(micros):
+    return pl.CostEstimate(flops=int(micros * 1.15e9), bytes_accessed=0, transcendentals=0)
 
 
 def guest_call(starts, bias, query, parts):
-    rows = query.shape[0]
+    rows, width = query.shape
     return pl.pallas_call(
-        functools.partial(guest_kernel, 4),
-        out_shape=jax.ShapeDtypeStruct((rows + 3 * STAT_ROWS, HEAD_DIM), jnp.bfloat16),
+        functools.partial(guest_kernel, UNROLL),
+        out_shape=jax.ShapeDtypeStruct((rows + 3 * STAT_ROWS, width), jnp.bfloat16),
         in_specs=[SMEM, VMEM, VMEM, ANY, ANY, ANY, ANY],
         out_specs=VMEM,
         scratch_shapes=[
-            pool_scratch(rows),
-            pltpu.VMEM((STAT_ROWS, 2 * BLOCK), jnp.float32),
+            pool_scratch(query),
+            stats_shape(query, pltpu.VMEM),
             pltpu.SemaphoreType.DMA((4,)),
         ],
-        compiler_params=pltpu.CompilerParams(vmem_limit_bytes=VMEM_LIMIT),
-        cost_estimate=attend_cost(rows),
+        compiler_params=params(),
+        cost_estimate=cost(ATTEND_US * width // HEAD_DIM),
         name="guest_attention",
     )(starts, bias, query, *parts)
 
 
 def home_call(starts, bias, query, parts):
-    rows = query.shape[0]
+    rows, width = query.shape
     return pl.pallas_call(
-        functools.partial(home_kernel, 4),
+        functools.partial(home_kernel, UNROLL),
         out_shape=(
-            jax.ShapeDtypeStruct((rows, HEAD_DIM), jnp.float32),
-            jax.ShapeDtypeStruct((STAT_ROWS, 2 * BLOCK), jnp.float32),
+            jax.ShapeDtypeStruct((rows, width), jnp.float32),
+            stats_shape(query, jax.ShapeDtypeStruct),
         ),
         in_specs=[SMEM, VMEM, VMEM, ANY, ANY, ANY, ANY],
         out_specs=(VMEM, VMEM),
-        scratch_shapes=[pool_scratch(rows), pltpu.SemaphoreType.DMA((4,))],
-        compiler_params=pltpu.CompilerParams(vmem_limit_bytes=VMEM_LIMIT),
-        cost_estimate=attend_cost(rows),
+        scratch_shapes=[pool_scratch(query), pltpu.SemaphoreType.DMA((4,))],
+        compiler_params=params(),
+        cost_estimate=cost(ATTEND_US * width // HEAD_DIM),
         name="home_attention",
     )(starts, bias, query, *parts)
 
 
 def merge_call(mixed, stats, message):
-    rows = mixed.shape[0]
     return pl.pallas_call(
         merge_kernel,
-        out_shape=jax.ShapeDtypeStruct((rows, HEAD_DIM), jnp.bfloat16),
+        out_shape=jax.ShapeDtypeStruct(mixed.shape, jnp.bfloat16),
         in_specs=[VMEM, VMEM, VMEM],
         out_specs=VMEM,
         scratch_shapes=[
             pltpu.VMEM((STAT_ROWS, BLOCK), jnp.float32),
             pltpu.VMEM((STAT_ROWS, BLOCK), jnp.float32),
         ],
-        compiler_params=pltpu.CompilerParams(vmem_limit_bytes=VMEM_LIMIT),
-        cost_estimate=pl.CostEstimate(
-            flops=4 * rows * HEAD_DIM, bytes_accessed=8 * rows * HEAD_DIM, transcendentals=0
-        ),
+        compiler_params=params(),
+        cost_estimate=cost(MERGE_US),
         name="merge_halves",
     )(mixed, stats, message)
+
+
+ROW_TILE = 256
+
+
+def weight_spec(weights, chunk, relation):
+    first, count = chunk
+    _, _, depth, columns = weights.shape
+    return pl.BlockSpec(
+        (1, count, depth, columns), lambda i, me: (me[0] ^ relation, first // count, 0, 0)
+    )
+
+
+def row_spec(array):
+    return pl.BlockSpec((ROW_TILE, array.shape[1]), lambda i, me: (i, 0))
+
+
+def project(kernel, name, summed, gathered, chunks, weights, result):
+    rows = gathered[0][0].shape[0]
+    columns = weights.shape[3]
+    pieces = [piece for group in gathered for piece in group]
+    specs = [
+        weight_spec(weights, chunk, relation)
+        for chunk, group in zip(chunks, gathered)
+        for relation in range(len(group))
+    ]
+    sums = [] if summed is None else [summed]
+    myself = lax.axis_index("head").astype(jnp.int32).reshape(1)
+    return pl.pallas_call(
+        functools.partial(kernel, len(pieces)),
+        out_shape=jax.ShapeDtypeStruct((rows, columns), result),
+        grid_spec=pltpu.PrefetchScalarGridSpec(
+            num_scalar_prefetch=1,
+            grid=(rows // ROW_TILE,),
+            in_specs=[row_spec(v) for v in sums + pieces] + specs,
+            out_specs=pl.BlockSpec((ROW_TILE, columns), lambda i, me: (i, 0)),
+        ),
+        compiler_params=params(),
+        cost_estimate=cost(0),
+        name=name,
+    )(myself, *sums, *pieces, *[weights for _ in specs])
 
 
 def key_places(shard, myself, global_ids, rand_ids, local_blocks, shards):
@@ -230,6 +323,24 @@
     return lax.ppermute(value, "seq", [(i, i ^ distance) for i in range(shards)])
 
 
+def after(value, *tokens):
+    return lax.optimization_barrier((value, *tokens))[0]
+
+
+def gather_heads(value):
+    def hop(v, distance):
+        return lax.ppermute(v, "head", [(i, i ^ distance) for i in range(4)])
+
+    across = hop(value, 2)
+    return value, hop(value, 1), across, hop(across, 1)
+
+
+CHUNKS = ((0, 2), (2, 1), (3, 1))
+UNROLL = 8
+ATTEND_US = 0
+MERGE_US = 0
+
+
 def halves_body(queries, keys_values, global_ids, rand_ids, out_weight):
     rows, width = queries.shape
     heads_here = width // HEAD_DIM
@@ -239,34 +350,57 @@
     groups = lax.axis_size("head")
     opposite = shards // 2
 
-    def column(array, head):
-        return lax.slice_in_dim(array, head * HEAD_DIM, (head + 1) * HEAD_DIM, axis=array.ndim - 1)
-
-    own_pairs = [column(keys_values, h) for h in range(heads_here)]
-    own_queries = [column(queries, h) for h in range(heads_here)]
+    def column(array, chunk):
+        low, count = chunk
+        return lax.slice_in_dim(
+            array, low * HEAD_DIM, (low + count) * HEAD_DIM, axis=array.ndim - 1
+        )
+
+    own_pairs = [column(keys_values, c) for c in CHUNKS]
+    own_queries = [column(queries, c) for c in CHUNKS]
+
+    along_y = [swap(own_pairs[0], 1, shards)]
+    along_z = [swap(own_pairs[0], 2, shards)]
+    diagonal = [swap(along_z[0], 1, shards)]
+    visitors = [swap(after(own_queries[0], along_z[0]), opposite, shards)]
+    for n in (1, 2):
+        along_z.append(swap(after(own_pairs[n], along_z[n - 1]), 2, shards))
+        along_y.append(swap(after(own_pairs[n], along_z[n - 1]), 1, shards))
+        diagonal.append(swap(along_z[n], 1, shards))
+        visitors.append(swap(after(own_queries[n], along_z[n]), opposite, shards))
+
     home = key_places(myself, myself, global_ids, rand_ids, local_blocks, shards)
     guest = key_places(myself ^ opposite, myself, global_ids, rand_ids, local_blocks, shards)
-
-    parts, visitors = [], []
-    for h in range(heads_here):
-        along_z = swap(own_pairs[h], 2, shards)
-        along_y = swap(own_pairs[h], 1, shards)
-        visitors.append(swap(own_queries[h], opposite, shards))
-        diagonal = swap(along_z, 1, shards)
-        parts.append((own_pairs[h], along_y, along_z, diagonal))
-
     weights = out_weight.reshape(groups, heads_here, HEAD_DIM, out_weight.shape[1])
-    summed = None
-    for h in range(heads_here):
-        message = guest_call(*guest, visitors[h], parts[h])
+    gathered = []
+    for n in range(len(CHUNKS)):
+        parts = (own_pairs[n], along_y[n], along_z[n], diagonal[n])
+        visitor = visitors[n]
+        message = guest_call(*guest, visitor, parts)
         answer = swap(message, opposite, shards)
-        mixed, stats = home_call(*home, own_queries[h], parts[h])
+        mixed, stats = home_call(*home, after(own_queries[n], message), parts)
+        if n == 2:
+            summed = project(
+                first_terms_kernel,
+                "first_terms",
+                None,
+                gathered,
+                CHUNKS[:2],
+                after(weights, mixed),
+                jnp.float32,
+            )
+            answer = after(answer, summed)
         attended = merge_call(mixed, stats, answer)
-        gathered = lax.all_gather(attended, "head", axis=1, tiled=True)
-        weight = weights[:, h].reshape(groups * HEAD_DIM, -1)
-        term = jnp.dot(gathered, weight, preferred_element_type=jnp.float32)
-        summed = term if summed is None else summed + term
-    return summed.astype(jnp.bfloat16)
+        gathered.append(gather_heads(attended))
+    return project(
+        last_term_kernel,
+        "last_term",
+        summed,
+        gathered[2:],
+        CHUNKS[2:],
+        weights,
+        jnp.bfloat16,
+    )
 
 
 def padded_2(block, sides, width):
@@ -398,7 +532,7 @@
 
 
 def solution(mesh):
-    body = halves_body if mesh.shape["seq"] == 8 else exchange_body
+    body = halves_body if dict(mesh.shape) == {"seq": 8, "head": 4} else exchange_body
     in_specs = (P("seq", "head"), P(None, "seq", "head"), P(), P(), P(None, "head"))
     out_specs = P("seq", "head")
     return jax.shard_map(body, mesh=mesh, in_specs=in_specs, out_specs=out_specs, check_vma=False)

time: 339 us -> 232 us (0.68)
  waiting for transfers between devices: 166 us -> 132 us
  matrix products: 29 us -> 0 us
  Pallas kernels: 75.9 us -> 57.9 us
  between operations: 13.3 us -> 0.26 us
  local copies, waits for them, and re-layouts: 24.8 us -> 13.7 us
  other arithmetic: 4.14 us -> 0.34 us
    ppermute x20 -> x15, waiting for transfers between devices: 166 us -> 121 us  [swap(): lax.ppermute(value, 'seq', [(i, i ^ distance) for i in range(shards)])]
    dot_general x4 -> x0, matrix products: 29 us -> none  [halves_body(): term = jnp.dot(gathered, weight, preferred_element_type=jnp.float32)]
    pallas_call x12 -> x11, Pallas kernels: 75.9 us -> 57.9 us  [the longest x3 19.3 us: guest_call(): pl.pallas_call(functools.partial(guest_kernel, UNROLL), out_shape=jax.Sha...]
    ppermute x0 -> x9, waiting for transfers between devices: none -> 11.3 us  [hop(): return lax.ppermute(v, 'head', [(i, i ^ distance) for i in range(4)])]
    ppermute x0 -> x9, starting transfers between devices: none -> 5.71 us  [hop(): return lax.ppermute(v, 'head', [(i, i ^ distance) for i in range(4)])]
    ppermute x20 -> x15, starting transfers between devices: 25.2 us -> 21.3 us  [swap(): lax.ppermute(value, 'seq', [(i, i ^ distance) for i in range(shards)])]
    slice x3 -> x4, local copies, waits for them, and re-layouts: 7.57 us -> 4.93 us  [column(): lax.slice_in_dim(array, low * HEAD_DIM, (low + count) * HEAD_DIM, axis=ar...]
  transfers between devices with their start and end apart: 24 -> 24, of which waited for: 12 -> 9; matrix products, arithmetic and copies ran while one was open for 12% -> 4% of each run, Pallas kernels for 19% -> 22%
where the time goes in v2:
time: 232 us; the launch traced here: 231 us
  waiting for transfers between devices  132 us (57%)
  Pallas kernels  57.9 us (25%)
  starting transfers between devices  27 us (12%)
  local copies, waits for them, and re-layouts  13.7 us (6%)
    ppermute x15, waiting for transfers between devices, swap(): lax.ppermute(value, 'seq', [(i, i ^ distance) for i in range(shards)])  121 us
    ppermute x15, starting transfers between devices, swap(): lax.ppermute(value, 'seq', [(i, i ^ distance) for i in range(shards)])  21.3 us
    pallas_call x3, Pallas kernels, guest_call(): pl.pallas_call(functools.partial(guest_kernel, UNROLL), out_shape=jax.Sha...  19.3 us
    pallas_call x3, Pallas kernels, home_call(): pl.pallas_call(functools.partial(home_kernel, UNROLL), out_shape=(jax.Sha...  17.6 us
    pallas_call x2, Pallas kernels, project(): pl.pallas_call(functools.partial(kernel, len(pieces)), out_shape=jax.Shap...  14.2 us
    ppermute x9, waiting for transfers between devices, hop(): return lax.ppermute(v, 'head', [(i, i ^ distance) for i in range(4)])  11.3 us
    pallas_call x3, Pallas kernels, merge_call(): pl.pallas_call(merge_kernel, out_shape=jax.ShapeDtypeStruct(mixed.shape,...  6.86 us
    ppermute x9, starting transfers between devices, hop(): return lax.ppermute(v, 'head', [(i, i ^ distance) for i in range(4)])  5.71 us
  transfers between devices with their start and end apart: 24, of which 9 were waited for; matrix products, arithmetic and copies ran while one was open for 4% of the time, Pallas kernels for 22%

profile of v2, /device:TPU:0, one launch (start us, length us, event | category | flops | bytes accessed | tf_op | source)
XLA Modules:
  0.0 231.3 jit_solution(6517629174601097258)
XLA Ops:
  0.0 1.6 slice.19.p0
  1.6 3.1 %collective-permute-start = (bf16[2,1536,256]{2,1,0:T(8,128)(2,1)S(1)}, bf16[2,1536,256]{2,1,0:T(8,128)(2,1)}, u32[]{:S(2)}, u32[]{:S(2)}) collective-permute-start(bf16[2,1536,256]{2,1,0:T(8,128)(2,1)S(1)} %slice.19.p0), channel_id=1, source_target_pairs={{0,8},{4,12},{8,0},{12,4},{16,24},{20,28},{24,16},{28,20},{1,9},{5... | collective-permute-start | bytes 4718600 | tf_op jit(solution)/shard_map/ppermute | solution.py:323
  4.7 1.5 collective-permute-start.2
  6.2 33.0 %collective-permute-done.p2 = bf16[2,1536,256]{2,1,0:T(8,128)(2,1)} collective-permute-done((bf16[2,1536,256]{2,1,0:T(8,128)(2,1)S(1)}, bf16[2,1536,256]{2,1,0:T(8,128)(2,1)}, u32[]{:S(2)}, u32[]{:S(2)}) %collective-permute-start) | collective-permute-done | bytes 1572896 | tf_op jit(solution)/shard_map/ppermute | solution.py:323
  39.2 1.7 collective-permute-start.3
  40.9 1.0 slice.18.q_ref
  42.0 1.5 fusion.16
  43.5 2.7 %collective-permute-start.1 = (bf16[1536,256]{1,0:T(8,128)(2,1)}, bf16[1536,256]{1,0:T(8,128)(2,1)}, u32[]{:S(2)}, u32[]{:S(2)}) collective-permute-start(bf16[1536,256]{1,0:T(8,128)(2,1)} %slice.18.q_ref), channel_id=1, source_target_pairs={{0,16},{4,20},{8,24},{12,28},{16,0},{20,4},{24,8},{28,12},{1,17},{... | collective-permute-start | bytes 2359304 | tf_op jit(solution)/shard_map/ppermute | solution.py:323
  46.2 1.6 collective-permute-start.8
  48.0 0.1 broadcast_select_fusion
  48.6 31.3 %collective-permute-done.1.q_ref = bf16[1536,256]{1,0:T(8,128)(2,1)} collective-permute-done((bf16[1536,256]{1,0:T(8,128)(2,1)}, bf16[1536,256]{1,0:T(8,128)(2,1)}, u32[]{:S(2)}, u32[]{:S(2)}) %collective-permute-start.1) | collective-permute-done | bytes 786464 | tf_op jit(solution)/shard_map/ppermute | solution.py:323
  79.9 9.3 %guest_attention.3 = bf16[1632,256]{1,0:T(8,128)(2,1)} custom-call(s32[192]{0:T(256)S(1)} %reshape.35.starts_ref, f32[24,512]{1,0:T(8,128)S(1)} %reshape.36.bias_ref, bf16[1536,256]{1,0:T(8,128)(2,1)} %collective-permute-done.1.q_ref, bf16[2,1536,256]{2,1,0:T(8,128)(2,1)S(1)} %slice.19.p0, bf16[2,1536,256]{2,1,0:T(8,128)(2,1)} %collective-permute-done.2.p1, ...), custom_call_target="tpu_custom_call" | custom-call | tf_op jit(solution)/shard_map/guest_attention/pallas_call | solution.py:212
  89.3 0.7 collective-permute-start.10
  90.0 3.7 %collective-permute-start.16 = (bf16[2,1536,128]{2,1,0:T(8,128)(2,1)S(1)}, bf16[2,1536,128]{2,1,0:T(8,128)(2,1)}, u32[]{:S(2)}, u32[]{:S(2)}) collective-permute-start(bf16[2,1536,128]{2,1,0:T(8,128)(2,1)S(1)} %get-tuple-element.30.p0), channel_id=1, source_target_pairs={{0,8},{4,12},{8,0},{12,4},{16,24},{20,28},{24,16},{28,20},{1,9},{5... | collective-permute-start | bytes 2359304 | tf_op jit(solution)/shard_map/ppermute | solution.py:323
  93.7 1.5 collective-permute-start.11
  95.2 0.8 fusion.17
  96.1 0.7 copy.8
  96.8 0.8 reshape.33.starts_ref
  97.6 0.7 copy.9
  98.2 1.4 broadcast_in_dim.36
  99.7 1.6 reshape.34.bias_ref
  101.3 0.8 copy-done.4
  102.1 8.3 %home_attention.3 = (f32[1536,256]{1,0:T(8,128)S(1)}, f32[2,32,128]{2,1,0:T(8,128)S(1)}) custom-call(s32[192]{0:T(256)S(1)} %reshape.33.starts_ref, f32[24,512]{1,0:T(8,128)S(1)} %copy-done.4, bf16[1536,256]{1,0:T(8,128)(2,1)} %slice.18.q_ref, bf16[2,1536,256]{2,1,0:T(8,128)(2,1)S(1)} %slice.19.p0, bf16[2,1536,256]{2,1,0:T(8,128)(2,1)} %collective-permute-done.2.p1, ...), custom_call_target="tpu_custom_call" | custom-call | tf_op jit(solution)/shard_map/home_attention/pallas_call | solution.py:230
  110.4 27.8 %collective-permute-done.4.message_ref = bf16[1632,256]{1,0:T(8,128)(2,1)} collective-permute-done((bf16[1632,256]{1,0:T(8,128)(2,1)}, bf16[1632,256]{1,0:T(8,128)(2,1)}, u32[]{:S(2)}, u32[]{:S(2)}) %collective-permute-start.4) | collective-permute-done | bytes 835616 | tf_op jit(solution)/shard_map/ppermute | solution.py:323
  138.2 0.5 collective-permute-start.18
  138.8 3.9 %merge_halves.3.refs_0_ = bf16[1536,256]{1,0:T(8,128)(2,1)} custom-call(f32[1536,256]{1,0:T(8,128)S(1)} %get-tuple-element.23.mixed_ref, f32[2,32,128]{2,1,0:T(8,128)S(1)} %get-tuple-element.24.stats_ref, bf16[1632,256]{1,0:T(8,128)(2,1)} %collective-permute-done.4.message_ref), custom_call_target="tpu_custom_call" | custom-call | tf_op jit(solution)/shard_map/merge_halves/pallas_call | solution.py:246
  142.7 1.5 collective-permute-start.6
  144.2 0.4 collective-permute-done.9.q_ref
  144.6 5.1 %guest_attention.4 = bf16[1632,128]{1,0:T(8,128)(2,1)S(1)} custom-call(s32[192]{0:T(256)S(1)} %reshape.35.starts_ref, f32[24,512]{1,0:T(8,128)S(1)} %copy-done.3, bf16[1536,128]{1,0:T(8,128)(2,1)} %collective-permute-done.9.q_ref, bf16[2,1536,128]{2,1,0:T(8,128)(2,1)S(1)} %get-tuple-element.25.p0, bf16[2,1536,128]{2,1,0:T(8,128)(2,1)} %collective-permute-done.10.p1, ...), custom_call_target="tpu_custom_call" | custom-call | tf_op jit(solution)/shard_map/guest_attention/pallas_call | solution.py:212
  149.8 1.2 collective-permute-start.19
  150.9 2.8 %collective-permute-start.17 = (bf16[1536,128]{1,0:T(8,128)(2,1)S(1)}, bf16[1536,128]{1,0:T(8,128)(2,1)S(1)}, u32[]{:S(2)}, u32[]{:S(2)}) collective-permute-start(bf16[1536,128]{1,0:T(8,128)(2,1)S(1)} %get-tuple-element.32.q_ref), channel_id=1, source_target_pairs={{0,16},{4,20},{8,24},{12,28},{16,0},{20,4},{24,8},{28,12},{1,17},{... | collective-permute-start | bytes 1179656 | tf_op jit(solution)/shard_map/ppermute | solution.py:323
  153.8 5.0 %home_attention.4 = (f32[1536,128]{1,0:T(8,128)S(1)}, f32[1,32,128]{2,1,0:T(8,128)S(1)}) custom-call(s32[192]{0:T(256)S(1)} %reshape.33.starts_ref, f32[24,512]{1,0:T(8,128)S(1)} %copy-done.4, bf16[1536,128]{1,0:T(8,128)(2,1)} %get-tuple-element.27.q_ref, bf16[2,1536,128]{2,1,0:T(8,128)(2,1)S(1)} %get-tuple-element.25.p0, ...), custom_call_target="tpu_custom_call" | custom-call | tf_op jit(solution)/shard_map/home_attention/pallas_call | solution.py:230
  158.8 19.5 %collective-permute-done.12.message_ref = bf16[1632,128]{1,0:T(8,128)(2,1)S(1)} collective-permute-done((bf16[1632,128]{1,0:T(8,128)(2,1)S(1)}, bf16[1632,128]{1,0:T(8,128)(2,1)S(1)}, u32[]{:S(2)}, u32[]{:S(2)}) %collective-permute-start.12) | collective-permute-done | bytes 417824 | tf_op jit(solution)/shard_map/ppermute | solution.py:323
  178.3 1.0 merge_halves.4.refs_4_
  179.3 1.6 collective-permute-start.14
  180.9 0.5 collective-permute-start.7
  181.4 4.6 %collective-permute-done.17.q_ref = bf16[1536,128]{1,0:T(8,128)(2,1)S(1)} collective-permute-done((bf16[1536,128]{1,0:T(8,128)(2,1)S(1)}, bf16[1536,128]{1,0:T(8,128)(2,1)S(1)}, u32[]{:S(2)}, u32[]{:S(2)}) %collective-permute-start.17) | collective-permute-done | bytes 393248 | tf_op jit(solution)/shard_map/ppermute | solution.py:323
  186.0 4.9 %guest_attention.5 = bf16[1632,128]{1,0:T(8,128)(2,1)} custom-call(s32[192]{0:T(256)S(1)} %reshape.35.starts_ref, f32[24,512]{1,0:T(8,128)S(1)} %copy-done.3, bf16[1536,128]{1,0:T(8,128)(2,1)S(1)} %collective-permute-done.17.q_ref, bf16[2,1536,128]{2,1,0:T(8,128)(2,1)S(1)} %get-tuple-element.30.p0, bf16[2,1536,128]{2,1,0:T(8,128)(2,1)S(1)} %collective-permute-done.18.p1, ...), custom_call_target="tpu_custom_call" | custom-call | tf_op jit(solution)/shard_map/guest_attention/pallas_call | solution.py:212
  191.1 0.5 collective-permute-start.15
  191.6 4.2 %home_attention.5 = (f32[1536,128]{1,0:T(8,128)S(1)}, f32[1,32,128]{2,1,0:T(8,128)S(1)}) custom-call(s32[192]{0:T(256)S(1)} %reshape.33.starts_ref, f32[24,512]{1,0:T(8,128)S(1)} %copy-done.5, bf16[1536,128]{1,0:T(8,128)(2,1)S(1)} %get-tuple-element.32.q_ref, bf16[2,1536,128]{2,1,0:T(8,128)(2,1)S(1)} %get-tuple-element.30.p0, ...), custom_call_target="tpu_custom_call" | custom-call | tf_op jit(solution)/shard_map/home_attention/pallas_call | solution.py:230
  195.9 2.2 copy-done
  198.1 9.0 %first_terms.1.sum_ref = f32[1536,1024]{1,0:T(8,128)S(1)} custom-call(s32[1]{0:T(128)} %bitcast._, bf16[1536,256]{1,0:T(8,128)(2,1)} %merge_halves.3.refs_0_, bf16[1536,256]{1,0:T(8,128)(2,1)} %collective-permute-done.5.refs_1_, bf16[1536,256]{1,0:T(8,128)(2,1)} %collective-permute-done.6.refs_2_, bf16[1536,256]{1,0:T(8,128)(2,1)} %collective-permute-done.7.refs_3_, ...), custom_call_target="tpu_custom_call" | custom-call | tf_op jit(solution)/shard_map/first_terms/pallas_call | solution.py:287
  207.1 4.2 %collective-permute-done.20.message_ref = bf16[1632,128]{1,0:T(8,128)(2,1)} collective-permute-done((bf16[1632,128]{1,0:T(8,128)(2,1)}, bf16[1632,128]{1,0:T(8,128)(2,1)}, u32[]{:S(2)}, u32[]{:S(2)}) %collective-permute-start.20) | collective-permute-done | bytes 417824 | tf_op jit(solution)/shard_map/ppermute | solution.py:323
  211.3 2.0 merge_halves.5.refs_0_
  213.3 1.6 collective-permute-start.22
  214.9 9.5 %collective-permute-done.22.refs_2_ = bf16[1536,128]{1,0:T(8,128)(2,1)S(1)} collective-permute-done((bf16[1536,128]{1,0:T(8,128)(2,1)S(1)}, bf16[1536,128]{1,0:T(8,128)(2,1)S(1)}, u32[]{:S(2)}, u32[]{:S(2)}) %collective-permute-start.22) | collective-permute-done | bytes 393248 | tf_op jit(solution)/shard_map/ppermute | solution.py:332
  224.4 1.7 collective-permute-done.23.refs_3_
  226.1 5.1 %last_term.1 = bf16[1536,1024]{1,0:T(8,128)(2,1)} custom-call(s32[1]{0:T(128)} %bitcast._, f32[1536,1024]{1,0:T(8,128)S(1)} %first_terms.1.sum_ref, bf16[1536,128]{1,0:T(8,128)(2,1)S(1)} %merge_halves.5.refs_0_, bf16[1536,128]{1,0:T(8,128)(2,1)S(1)} %collective-permute-done.21.refs_1_, bf16[1536,128]{1,0:T(8,128)(2,1)S(1)} %collective-permute-done.22.refs_2_, ...), custom_call_target="tpu_custom_call" | custom-call | tf_op jit(solution)/shard_map/last_term/pallas_call | solution.py:287
  (53 shorter events, 1.3 us)
Async XLA Ops:
  0.0 40.9 %copy-start.6 = (bf16[1536,512]{1,0:T(8,128)(2,1)S(1)}, bf16[1536,512]{1,0:T(8,128)(2,1)}, u32[]{:S(2)}) copy-start(bf16[1536,512]{1,0:T(8,128)(2,1)} %param.5) | copy-start | bytes 4718596
  1.6 37.6 %collective-permute-start = (bf16[2,1536,256]{2,1,0:T(8,128)(2,1)S(1)}, bf16[2,1536,256]{2,1,0:T(8,128)(2,1)}, u32[]{:S(2)}, u32[]{:S(2)}) collective-permute-start(bf16[2,1536,256]{2,1,0:T(8,128)(2,1)S(1)} %slice.19.p0), channel_id=1, source_target_pairs={{0,8},{4,12},{8,0},{12,4},{16,24},{20,28},{24,16},{28,20},{1,9},{5... | collective-permute-start | bytes 4718600 | tf_op jit(solution)/shard_map/ppermute | solution.py:323
  4.7 43.9 %collective-permute-start.2 = (bf16[2,1536,256]{2,1,0:T(8,128)(2,1)S(1)}, bf16[2,1536,256]{2,1,0:T(8,128)(2,1)}, u32[]{:S(2)}, u32[]{:S(2)}) collective-permute-start(bf16[2,1536,256]{2,1,0:T(8,128)(2,1)S(1)} %slice.19.p0), channel_id=1, source_target_pairs={{0,4},{4,0},{8,12},{12,8},{16,20},{20,16},{24,28},{28,24},{1,5},{5... | collective-permute-start | bytes 4718600 | tf_op jit(solution)/shard_map/ppermute | solution.py:323
  39.2 40.7 %collective-permute-start.3 = (bf16[2,1536,256]{2,1,0:T(8,128)(2,1)}, bf16[2,1536,256]{2,1,0:T(8,128)(2,1)}, u32[]{:S(2)}, u32[]{:S(2)}) collective-permute-start(bf16[2,1536,256]{2,1,0:T(8,128)(2,1)} %collective-permute-done.p2), channel_id=1, source_target_pairs={{0,4},{4,0},{8,12},{12,8},{16,20},{20,16},{24,28},{28,24},{1,5},{5... | collective-permute-start | bytes 4718600 | tf_op jit(solution)/shard_map/ppermute | solution.py:323
  42.0 5.8 %copy-start.8 = (s32[192,3]{0,1:T(4,128)S(1)}, s32[192,3]{0,1:T(4,128)}, u32[]{:S(2)}) copy-start(s32[192,3]{0,1:T(4,128)} %param.8) | copy-start | bytes 6916
  42.0 5.9 %copy-start.9 = (s32[2]{0:T(128)S(1)}, s32[2]{0:T(128)}, u32[]{:S(2)}) copy-start(s32[2]{0:T(128)} %param.7) | copy-start | bytes 28
  43.5 36.4 %collective-permute-start.1 = (bf16[1536,256]{1,0:T(8,128)(2,1)}, bf16[1536,256]{1,0:T(8,128)(2,1)}, u32[]{:S(2)}, u32[]{:S(2)}) collective-permute-start(bf16[1536,256]{1,0:T(8,128)(2,1)} %slice.18.q_ref), channel_id=1, source_target_pairs={{0,16},{4,20},{8,24},{12,28},{16,0},{20,4},{24,8},{28,12},{1,17},{... | collective-permute-start | bytes 2359304 | tf_op jit(solution)/shard_map/ppermute | solution.py:323
  46.2 43.8 %collective-permute-start.8 = (bf16[2,1536,128]{2,1,0:T(8,128)(2,1)S(1)}, bf16[2,1536,128]{2,1,0:T(8,128)(2,1)}, u32[]{:S(2)}, u32[]{:S(2)}) collective-permute-start(bf16[2,1536,128]{2,1,0:T(8,128)(2,1)S(1)} %get-tuple-element.25.p0), channel_id=1, source_target_pairs={{0,8},{4,12},{8,0},{12,4},{16,24},{20,28},{24,16},{28,20},{1,9},{5... | collective-permute-start | bytes 2359304 | tf_op jit(solution)/shard_map/ppermute | solution.py:323
  48.6 40.6 %copy-start.2 = (f32[24,512]{1,0:T(8,128)}, f32[24,512]{1,0:T(8,128)S(1)}, u32[]{:S(2)}) copy-start(f32[24,512]{1,0:T(8,128)S(1)} %reshape.36.bias_ref) | copy-start | bytes 147460
  48.6 46.6 %copy-start.7 = (bf16[1536,512]{1,0:T(8,128)(2,1)S(1)}, bf16[1536,512]{1,0:T(8,128)(2,1)}, u32[]{:S(2)}) copy-start(bf16[1536,512]{1,0:T(8,128)(2,1)} %param.5) | copy-start | bytes 4718596
  89.2 49.0 %collective-permute-start.4 = (bf16[1632,256]{1,0:T(8,128)(2,1)}, bf16[1632,256]{1,0:T(8,128)(2,1)}, u32[]{:S(2)}, u32[]{:S(2)}) collective-permute-start(bf16[1632,256]{1,0:T(8,128)(2,1)} %guest_attention.3), channel_id=1, source_target_pairs={{0,16},{4,20},{8,24},{12,28},{16,0},{20,4},{24,8},{28,12},{1,17},{... | collective-permute-start | bytes 2506760 | tf_op jit(solution)/shard_map/ppermute | solution.py:323
  89.3 53.4 %collective-permute-start.10 = (bf16[2,1536,128]{2,1,0:T(8,128)(2,1)S(1)}, bf16[2,1536,128]{2,1,0:T(8,128)(2,1)}, u32[]{:S(2)}, u32[]{:S(2)}) collective-permute-start(bf16[2,1536,128]{2,1,0:T(8,128)(2,1)S(1)} %get-tuple-element.25.p0), channel_id=1, source_target_pairs={{0,4},{4,0},{8,12},{12,8},{16,20},{20,16},{24,28},{28,24},{1,5},{5... | collective-permute-start | bytes 2359304 | tf_op jit(solution)/shard_map/ppermute | solution.py:323
  90.0 59.8 %collective-permute-start.16 = (bf16[2,1536,128]{2,1,0:T(8,128)(2,1)S(1)}, bf16[2,1536,128]{2,1,0:T(8,128)(2,1)}, u32[]{:S(2)}, u32[]{:S(2)}) collective-permute-start(bf16[2,1536,128]{2,1,0:T(8,128)(2,1)S(1)} %get-tuple-element.30.p0), channel_id=1, source_target_pairs={{0,8},{4,12},{8,0},{12,4},{16,24},{20,28},{24,16},{28,20},{1,9},{5... | collective-permute-start | bytes 2359304 | tf_op jit(solution)/shard_map/ppermute | solution.py:323
  93.7 50.9 %collective-permute-start.11 = (bf16[2,1536,128]{2,1,0:T(8,128)(2,1)}, bf16[2,1536,128]{2,1,0:T(8,128)(2,1)}, u32[]{:S(2)}, u32[]{:S(2)}) collective-permute-start(bf16[2,1536,128]{2,1,0:T(8,128)(2,1)} %collective-permute-done.8.p2), channel_id=1, source_target_pairs={{0,4},{4,0},{8,12},{12,8},{16,20},{20,16},{24,28},{28,24},{1,5},{5... | collective-permute-start | bytes 2359304 | tf_op jit(solution)/shard_map/ppermute | solution.py:323
  96.0 48.6 %collective-permute-start.9 = (bf16[1536,128]{1,0:T(8,128)(2,1)}, bf16[1536,128]{1,0:T(8,128)(2,1)}, u32[]{:S(2)}, u32[]{:S(2)}) collective-permute-start(bf16[1536,128]{1,0:T(8,128)(2,1)} %get-tuple-element.27.q_ref), channel_id=1, source_target_pairs={{0,16},{4,20},{8,24},{12,28},{16,0},{20,4},{24,8},{28,12},{1,17},{... | collective-permute-start | bytes 1179656 | tf_op jit(solution)/shard_map/ppermute | solution.py:323
  101.3 0.8 copy-start.4
  138.2 42.7 %collective-permute-start.18 = (bf16[2,1536,128]{2,1,0:T(8,128)(2,1)S(1)}, bf16[2,1536,128]{2,1,0:T(8,128)(2,1)S(1)}, u32[]{:S(2)}, u32[]{:S(2)}) collective-permute-start(bf16[2,1536,128]{2,1,0:T(8,128)(2,1)S(1)} %get-tuple-element.30.p0), channel_id=1, source_target_pairs={{0,4},{4,0},{8,12},{12,8},{16,20},{20,16},{24,28},{28,24},{1,5},{5... | collective-permute-start | bytes 2359304 | tf_op jit(solution)/shard_map/ppermute | solution.py:323
  138.8 5.8 %copy-start.3 = (f32[24,512]{1,0:T(8,128)S(1)}, f32[24,512]{1,0:T(8,128)}, u32[]{:S(2)}) copy-start(f32[24,512]{1,0:T(8,128)} %copy-done.2) | copy-start | bytes 147460
  142.7 38.2 %collective-permute-start.6 = (bf16[1536,256]{1,0:T(8,128)(2,1)}, bf16[1536,256]{1,0:T(8,128)(2,1)}, u32[]{:S(2)}, u32[]{:S(2)}) collective-permute-start(bf16[1536,256]{1,0:T(8,128)(2,1)} %merge_halves.3.refs_0_), channel_id=1, source_target_pairs={{0,2},{1,3},{2,0},{3,1},{4,6},{5,7},{6,4},{7,5},{8,10},{9,11},{10,... | collective-permute-start | bytes 2359304 | tf_op jit(solution)/shard_map/ppermute | solution.py:332
  149.7 28.7 %collective-permute-start.12 = (bf16[1632,128]{1,0:T(8,128)(2,1)S(1)}, bf16[1632,128]{1,0:T(8,128)(2,1)S(1)}, u32[]{:S(2)}, u32[]{:S(2)}) collective-permute-start(bf16[1632,128]{1,0:T(8,128)(2,1)S(1)} %guest_attention.4), channel_id=1, source_target_pairs={{0,16},{4,20},{8,24},{12,28},{16,0},{20,4},{24,8},{28,12},{1,17},{... | collective-permute-start | bytes 1253384 | tf_op jit(solution)/shard_map/ppermute | solution.py:323
  149.8 36.3 %collective-permute-start.19 = (bf16[2,1536,128]{2,1,0:T(8,128)(2,1)}, bf16[2,1536,128]{2,1,0:T(8,128)(2,1)S(1)}, u32[]{:S(2)}, u32[]{:S(2)}) collective-permute-start(bf16[2,1536,128]{2,1,0:T(8,128)(2,1)} %collective-permute-done.16.p2), channel_id=1, source_target_pairs={{0,4},{4,0},{8,12},{12,8},{16,20},{20,16},{24,28},{28,24},{1,5},{5... | collective-permute-start | bytes 2359304 | tf_op jit(solution)/shard_map/ppermute | solution.py:323
  150.9 35.1 %collective-permute-start.17 = (bf16[1536,128]{1,0:T(8,128)(2,1)S(1)}, bf16[1536,128]{1,0:T(8,128)(2,1)S(1)}, u32[]{:S(2)}, u32[]{:S(2)}) collective-permute-start(bf16[1536,128]{1,0:T(8,128)(2,1)S(1)} %get-tuple-element.32.q_ref), channel_id=1, source_target_pairs={{0,16},{4,20},{8,24},{12,28},{16,0},{20,4},{24,8},{28,12},{1,17},{... | collective-permute-start | bytes 1179656 | tf_op jit(solution)/shard_map/ppermute | solution.py:323
  179.3 12.3 %copy-start.5 = (f32[24,512]{1,0:T(8,128)S(1)}, f32[24,512]{1,0:T(8,128)}, u32[]{:S(2)}) copy-start(f32[24,512]{1,0:T(8,128)} %reshape.34.bias_ref) | copy-start | bytes 147460
  179.3 11.8 %collective-permute-start.14 = (bf16[1536,128]{1,0:T(8,128)(2,1)S(1)}, bf16[1536,128]{1,0:T(8,128)(2,1)}, u32[]{:S(2)}, u32[]{:S(2)}) collective-permute-start(bf16[1536,128]{1,0:T(8,128)(2,1)S(1)} %merge_halves.4.refs_4_), channel_id=1, source_target_pairs={{0,2},{1,3},{2,0},{3,1},{4,6},{5,7},{6,4},{7,5},{8,10},{9,11},{10,... | collective-permute-start | bytes 1179656 | tf_op jit(solution)/shard_map/ppermute | solution.py:332
  180.9 15.0 %collective-permute-start.5 = (bf16[1536,256]{1,0:T(8,128)(2,1)}, bf16[1536,256]{1,0:T(8,128)(2,1)}, u32[]{:S(2)}, u32[]{:S(2)}) collective-permute-start(bf16[1536,256]{1,0:T(8,128)(2,1)} %merge_halves.3.refs_0_), channel_id=1, source_target_pairs={{0,1},{1,0},{2,3},{3,2},{4,5},{5,4},{6,7},{7,6},{8,9},{9,8},{10,11... | collective-permute-start | bytes 2359304 | tf_op jit(solution)/shard_map/ppermute | solution.py:332
  180.9 15.0 %collective-permute-start.7 = (bf16[1536,256]{1,0:T(8,128)(2,1)}, bf16[1536,256]{1,0:T(8,128)(2,1)}, u32[]{:S(2)}, u32[]{:S(2)}) collective-permute-start(bf16[1536,256]{1,0:T(8,128)(2,1)} %collective-permute-done.6.refs_2_), channel_id=1, source_target_pairs={{0,1},{1,0},{2,3},{3,2},{4,5},{5,4},{6,7},{7,6},{8,9},{9,8},{10,11... | collective-permute-start | bytes 2359304 | tf_op jit(solution)/shard_map/ppermute | solution.py:332
  191.0 20.4 %collective-permute-start.20 = (bf16[1632,128]{1,0:T(8,128)(2,1)}, bf16[1632,128]{1,0:T(8,128)(2,1)}, u32[]{:S(2)}, u32[]{:S(2)}) collective-permute-start(bf16[1632,128]{1,0:T(8,128)(2,1)} %guest_attention.5), channel_id=1, source_target_pairs={{0,16},{4,20},{8,24},{12,28},{16,0},{20,4},{24,8},{28,12},{1,17},{... | collective-permute-start | bytes 1253384 | tf_op jit(solution)/shard_map/ppermute | solution.py:323
  191.1 4.8 %collective-permute-start.13 = (bf16[1536,128]{1,0:T(8,128)(2,1)S(1)}, bf16[1536,128]{1,0:T(8,128)(2,1)}, u32[]{:S(2)}, u32[]{:S(2)}) collective-permute-start(bf16[1536,128]{1,0:T(8,128)(2,1)S(1)} %merge_halves.4.refs_4_), channel_id=1, source_target_pairs={{0,1},{1,0},{2,3},{3,2},{4,5},{5,4},{6,7},{7,6},{8,9},{9,8},{10,11... | collective-permute-start | bytes 1179656 | tf_op jit(solution)/shard_map/ppermute | solution.py:332
  191.1 4.7 %collective-permute-start.15 = (bf16[1536,128]{1,0:T(8,128)(2,1)}, bf16[1536,128]{1,0:T(8,128)(2,1)}, u32[]{:S(2)}, u32[]{:S(2)}) collective-permute-start(bf16[1536,128]{1,0:T(8,128)(2,1)} %collective-permute-done.14.refs_6_), channel_id=1, source_target_pairs={{0,1},{1,0},{2,3},{3,2},{4,5},{5,4},{6,7},{7,6},{8,9},{9,8},{10,11... | collective-permute-start | bytes 1179656 | tf_op jit(solution)/shard_map/ppermute | solution.py:332
  195.9 2.2 copy-start
  198.1 28.1 %copy-start.1 = (bf16[2048,1024]{1,0:T(8,128)(2,1)S(1)}, bf16[2048,1024]{1,0:T(8,128)(2,1)}, u32[]{:S(2)}) copy-start(bf16[2048,1024]{1,0:T(8,128)(2,1)} %param.9) | copy-start | bytes 12582916
  213.3 11.1 %collective-permute-start.22 = (bf16[1536,128]{1,0:T(8,128)(2,1)S(1)}, bf16[1536,128]{1,0:T(8,128)(2,1)S(1)}, u32[]{:S(2)}, u32[]{:S(2)}) collective-permute-start(bf16[1536,128]{1,0:T(8,128)(2,1)S(1)} %merge_halves.5.refs_0_), channel_id=1, source_target_pairs={{0,2},{1,3},{2,0},{3,1},{4,6},{5,7},{6,4},{7,5},{8,10},{9,11},{10,... | collective-permute-start | bytes 1179656 | tf_op jit(solution)/shard_map/ppermute | solution.py:332
  214.9 9.5 %collective-permute-start.21 = (bf16[1536,128]{1,0:T(8,128)(2,1)S(1)}, bf16[1536,128]{1,0:T(8,128)(2,1)S(1)}, u32[]{:S(2)}, u32[]{:S(2)}) collective-permute-start(bf16[1536,128]{1,0:T(8,128)(2,1)S(1)} %merge_halves.5.refs_0_), channel_id=1, source_target_pairs={{0,1},{1,0},{2,3},{3,2},{4,5},{5,4},{6,7},{7,6},{8,9},{9,8},{10,11... | collective-permute-start | bytes 1179656 | tf_op jit(solution)/shard_map/ppermute | solution.py:332
  224.4 1.7 collective-permute-start.23

commit v3 on v2

--- a/solution.py
+++ b/solution.py
@@ -14,8 +14,9 @@
 NLIST = 3 + NGLOBAL + NRANDOM
 MASKED = -1e30
 EXP2_SCALE = 1.4426950408889634 / HEAD_DIM**0.5
-STAT_ROWS = 32
+STAT_TILE = 16
 VMEM_LIMIT = 32 * 1024 * 1024
+PROJECT_LIMIT = 32 * 1024 * 1024
 
 
 group_blocks = 8
@@ -54,10 +55,10 @@
         total = jnp.sum(weights, axis=1, keepdims=True)
         weighed.append((weights.astype(jnp.bfloat16), highest, total))
     results = []
-    for rows, listing, (weights, highest, total) in zip(places, listed, weighed):
+    for listing, (weights, highest, total) in zip(listed, weighed):
         values = jnp.concatenate([pool[1, w, lanes] for w in listing], axis=0)
         mixed = jnp.dot(weights, values, preferred_element_type=jnp.float32)
-        results.append((rows, lanes, mixed, highest, total))
+        results.append((lanes, mixed, highest, total))
     return results
 
 
@@ -80,60 +81,58 @@
         copy.wait()
 
 
-def guest_kernel(
-    unroll, starts_ref, bias_ref, q_ref, p0, p1, p2, p3, message_ref, pool, stats, sems
-):
-    load_pool((p0, p1, p2, p3), pool, sems)
-    blocks = q_ref.shape[0] // BLOCK
-    stats[...] = jnp.zeros_like(stats)
+def attend_part(part, parts, starts_ref, bias_ref, q_ref, pool, mixed_ref, stats_ref, normalise):
+    blocks = q_ref.shape[0] // BLOCK // parts
+    unroll = UNROLL if blocks % UNROLL == 0 else blocks
+    stats_ref[...] = jnp.zeros_like(stats_ref)
 
     for head in range(q_ref.shape[1] // HEAD_DIM):
 
         def step(n, _):
             ids = [n * unroll + u for u in range(unroll)]
-            results = attend_group(ids, head, starts_ref, bias_ref, q_ref, pool)
-            for i, (rows, lanes, mixed, highest, total) in zip(ids, results):
-                message_ref[rows, lanes] = (mixed / total).astype(jnp.bfloat16)
-                put_stats(i, head, stats, highest, total)
-            return 0
-
-        lax.fori_loop(0, blocks // unroll, step, 0)
-    base = q_ref.shape[0]
-    for head in range(q_ref.shape[1] // HEAD_DIM):
-        rest = stats[head]
-        for n in range(3):
-            piece = rest.astype(jnp.bfloat16)
-            rows = pl.ds(base + n * STAT_ROWS, STAT_ROWS)
-            message_ref[rows, pl.ds(head * HEAD_DIM, HEAD_DIM)] = piece
-            rest = rest - piece.astype(jnp.float32)
-
-
-def home_kernel(
-    unroll, starts_ref, bias_ref, q_ref, p0, p1, p2, p3, mixed_ref, stats_ref, pool, sems
-):
-    load_pool((p0, p1, p2, p3), pool, sems)
-    blocks = q_ref.shape[0] // BLOCK
-    stats_ref[...] = jnp.zeros_like(stats_ref)
-
-    for head in range(q_ref.shape[1] // HEAD_DIM):
-
-        def step(n, _):
-            ids = [n * unroll + u for u in range(unroll)]
-            results = attend_group(ids, head, starts_ref, bias_ref, q_ref, pool)
-            for i, (rows, lanes, mixed, highest, total) in zip(ids, results):
-                mixed_ref[rows, lanes] = mixed
+            results = attend_group(
+                [part * blocks + i for i in ids], head, starts_ref, bias_ref, q_ref, pool
+            )
+            for i, (lanes, mixed, highest, total) in zip(ids, results):
+                rows = pl.ds(pl.multiple_of(i * BLOCK, BLOCK), BLOCK)
+                mixed = mixed / total if normalise else mixed
+                mixed_ref[rows, lanes] = mixed.astype(mixed_ref.dtype)
                 put_stats(i, head, stats_ref, highest, total)
             return 0
 
         lax.fori_loop(0, blocks // unroll, step, 0)
+
+
+def guest_kernel(parts, starts_ref, bias_ref, q_ref, p0, p1, p2, p3, *refs):
+    *message_refs, pool, stats, sems = refs
+    load_pool((p0, p1, p2, p3), pool, sems)
+    base = q_ref.shape[0] // parts
+    for part, message_ref in enumerate(message_refs):
+        attend_part(part, parts, starts_ref, bias_ref, q_ref, pool, message_ref, stats, True)
+        for head in range(q_ref.shape[1] // HEAD_DIM):
+            rest = stats[head]
+            for n in range(3):
+                piece = rest.astype(jnp.bfloat16)
+                rows = pl.ds(base + n * rest.shape[0], rest.shape[0])
+                message_ref[rows, pl.ds(head * HEAD_DIM, HEAD_DIM)] = piece
+                rest = rest - piece.astype(jnp.float32)
+
+
+def home_kernel(parts, starts_ref, bias_ref, q_ref, p0, p1, p2, p3, *refs):
+    *result_refs, pool, sems = refs
+    load_pool((p0, p1, p2, p3), pool, sems)
+    for part in range(parts):
+        mixed_ref, stats_ref = result_refs[2 * part : 2 * part + 2]
+        attend_part(part, parts, starts_ref, bias_ref, q_ref, pool, mixed_ref, stats_ref, False)
 
 
 def merge_kernel(mixed_ref, stats_ref, message_ref, out_ref, home_scale, guest_scale):
     base, width = mixed_ref.shape
     blocks = base // BLOCK
-    other = message_ref[pl.ds(base, STAT_ROWS), :].astype(jnp.float32)
+    size = stats_ref.shape[1]
+    other = message_ref[pl.ds(base, size), :].astype(jnp.float32)
     for n in (1, 2):
-        other = other + message_ref[pl.ds(base + n * STAT_ROWS, STAT_ROWS), :].astype(jnp.float32)
+        other = other + message_ref[pl.ds(base + n * size, size), :].astype(jnp.float32)
     eye = eye_mask()
     for head in range(width // HEAD_DIM):
         low = head * HEAD_DIM
@@ -168,22 +167,18 @@
         lax.fori_loop(0, blocks, step, 0, unroll=4)
 
 
-def products(x_refs, w_refs):
+def project_kernel(heads, me_ref, w_ref, *refs):
+    groups = w_ref.shape[0]
+    *x_refs, out_ref = refs
     total = None
-    for x_ref, w_ref in zip(x_refs, w_refs):
-        weight = w_ref[...].reshape(-1, w_ref.shape[-1])
-        term = jnp.dot(x_ref[...], weight, preferred_element_type=jnp.float32)
+    for relation in range(groups):
+        pieces = [x_refs[head * groups + relation][...] for head in range(heads)]
+        weight = w_ref[me_ref[0] ^ relation].reshape(-1, w_ref.shape[-1])
+        term = jnp.dot(
+            jnp.concatenate(pieces, axis=1), weight, preferred_element_type=jnp.float32
+        )
         total = term if total is None else total + term
-    return total
-
-
-def first_terms_kernel(count, _, *refs):
-    refs[-1][...] = products(refs[:count], refs[count : 2 * count])
-
-
-def last_term_kernel(count, _, sum_ref, *refs):
-    total = sum_ref[...] + products(refs[:count], refs[count : 2 * count])
-    refs[-1][...] = total.astype(refs[-1].dtype)
+    out_ref[...] = total.astype(out_ref.dtype)
 
 
 VMEM = pl.BlockSpec(memory_space=pltpu.VMEM)
@@ -199,47 +194,52 @@
     return pltpu.VMEM((2, 4 * query.shape[0], query.shape[1]), jnp.bfloat16)
 
 
-def stats_shape(query, kind):
-    return kind((query.shape[1] // HEAD_DIM, STAT_ROWS, 2 * BLOCK), jnp.float32)
+def stats_shape(query, parts, kind):
+    blocks = query.shape[0] // BLOCK // parts
+    size = -(-blocks // STAT_TILE) * STAT_TILE
+    return kind((query.shape[1] // HEAD_DIM, size, 2 * BLOCK), jnp.float32)
 
 
 def cost(micros):
     return pl.CostEstimate(flops=int(micros * 1.15e9), bytes_accessed=0, transcendentals=0)
 
 
-def guest_call(starts, bias, query, parts):
+def guest_call(starts, bias, query, pieces, parts=1):
     rows, width = query.shape
+    size = stats_shape(query, parts, jax.ShapeDtypeStruct).shape[1]
+    message = jax.ShapeDtypeStruct((rows // parts + 3 * size, width), jnp.bfloat16)
     return pl.pallas_call(
-        functools.partial(guest_kernel, UNROLL),
-        out_shape=jax.ShapeDtypeStruct((rows + 3 * STAT_ROWS, width), jnp.bfloat16),
+        functools.partial(guest_kernel, parts),
+        out_shape=[message] * parts,
         in_specs=[SMEM, VMEM, VMEM, ANY, ANY, ANY, ANY],
-        out_specs=VMEM,
+        out_specs=[VMEM] * parts,
         scratch_shapes=[
             pool_scratch(query),
-            stats_shape(query, pltpu.VMEM),
+            stats_shape(query, parts, pltpu.VMEM),
             pltpu.SemaphoreType.DMA((4,)),
         ],
         compiler_params=params(),
-        cost_estimate=cost(ATTEND_US * width // HEAD_DIM),
+        cost_estimate=cost(GUEST_US),
         name="guest_attention",
-    )(starts, bias, query, *parts)
-
-
-def home_call(starts, bias, query, parts):
+    )(starts, bias, query, *pieces)
+
+
+def home_call(starts, bias, query, pieces, parts=1):
     rows, width = query.shape
+    results = [
+        jax.ShapeDtypeStruct((rows // parts, width), jnp.float32),
+        stats_shape(query, parts, jax.ShapeDtypeStruct),
+    ]
     return pl.pallas_call(
-        functools.partial(home_kernel, UNROLL),
-        out_shape=(
-            jax.ShapeDtypeStruct((rows, width), jnp.float32),
-            stats_shape(query, jax.ShapeDtypeStruct),
-        ),
+        functools.partial(home_kernel, parts),
+        out_shape=results * parts,
         in_specs=[SMEM, VMEM, VMEM, ANY, ANY, ANY, ANY],
-        out_specs=(VMEM, VMEM),
+        out_specs=[VMEM] * (2 * parts),
         scratch_shapes=[pool_scratch(query), pltpu.SemaphoreType.DMA((4,))],
         compiler_params=params(),
-        cost_estimate=cost(ATTEND_US * width // HEAD_DIM),
+        cost_estimate=cost(0),
         name="home_attention",
-    )(starts, bias, query, *parts)
+    )(starts, bias, query, *pieces)
 
 
 def merge_call(mixed, stats, message):
@@ -249,11 +249,11 @@
         in_specs=[VMEM, VMEM, VMEM],
         out_specs=VMEM,
         scratch_shapes=[
-            pltpu.VMEM((STAT_ROWS, BLOCK), jnp.float32),
-            pltpu.VMEM((STAT_ROWS, BLOCK), jnp.float32),
+            pltpu.VMEM((stats.shape[1], BLOCK), jnp.float32),
+            pltpu.VMEM((stats.shape[1], BLOCK), jnp.float32),
         ],
         compiler_params=params(),
-        cost_estimate=cost(MERGE_US),
+        cost_estimate=cost(0),
         name="merge_halves",
     )(mixed, stats, message)
 
@@ -261,42 +261,37 @@
 ROW_TILE = 256
 
 
-def weight_spec(weights, chunk, relation):
-    first, count = chunk
-    _, _, depth, columns = weights.shape
-    return pl.BlockSpec(
-        (1, count, depth, columns), lambda i, me: (me[0] ^ relation, first // count, 0, 0)
-    )
-
-
-def row_spec(array):
-    return pl.BlockSpec((ROW_TILE, array.shape[1]), lambda i, me: (i, 0))
-
-
-def project(kernel, name, summed, gathered, chunks, weights, result):
-    rows = gathered[0][0].shape[0]
-    columns = weights.shape[3]
-    pieces = [piece for group in gathered for piece in group]
-    specs = [
-        weight_spec(weights, chunk, relation)
-        for chunk, group in zip(chunks, gathered)
-        for relation in range(len(group))
-    ]
-    sums = [] if summed is None else [summed]
+def project(pieces, weights, part, filled=None):
+    groups, heads, _, columns = weights.shape
+    number, parts = part
+    rows = pieces[0].shape[0]
+    tiles = rows // parts // ROW_TILE
+
+    def row_spec(height, width):
+        first = number * tiles if height == rows else 0
+        return pl.BlockSpec((ROW_TILE, width), lambda i, me: (i + first, 0))
+
+    others = [] if filled is None else [filled]
     myself = lax.axis_index("head").astype(jnp.int32).reshape(1)
+
+    def kernel(me_ref, w_ref, *refs):
+        x_refs = refs[: len(pieces)]
+        project_kernel(heads, me_ref, w_ref, *x_refs, refs[-1])
+
     return pl.pallas_call(
-        functools.partial(kernel, len(pieces)),
-        out_shape=jax.ShapeDtypeStruct((rows, columns), result),
+        kernel,
+        out_shape=jax.ShapeDtypeStruct((rows, columns), jnp.bfloat16),
         grid_spec=pltpu.PrefetchScalarGridSpec(
             num_scalar_prefetch=1,
-            grid=(rows // ROW_TILE,),
-            in_specs=[row_spec(v) for v in sums + pieces] + specs,
-            out_specs=pl.BlockSpec((ROW_TILE, columns), lambda i, me: (i, 0)),
+            grid=(tiles,),
+            in_specs=[VMEM] + [row_spec(*v.shape) for v in pieces] + [ANY] * len(others),
+            out_specs=row_spec(rows, columns),
         ),
+        input_output_aliases={2 + len(pieces): 0} if others else {},
         compiler_params=params(),
-        cost_estimate=cost(0),
-        name=name,
-    )(myself, *sums, *pieces, *[weights for _ in specs])
+        cost_estimate=cost(PROJECT_US),
+        name="project_rows",
+    )(myself, weights, *pieces, *others)
 
 
 def key_places(shard, myself, global_ids, rand_ids, local_blocks, shards):
@@ -327,18 +322,17 @@
     return lax.optimization_barrier((value, *tokens))[0]
 
 
-def gather_heads(value):
-    def hop(v, distance):
-        return lax.ppermute(v, "head", [(i, i ^ distance) for i in range(4)])
-
-    across = hop(value, 2)
-    return value, hop(value, 1), across, hop(across, 1)
-
-
-CHUNKS = ((0, 2), (2, 1), (3, 1))
+def hop(value, distance, groups):
+    return lax.ppermute(value, "head", [(i, i ^ distance) for i in range(groups)])
+
+
+def together(*values):
+    return lax.optimization_barrier(values)
+
+
 UNROLL = 8
-ATTEND_US = 0
-MERGE_US = 0
+GUEST_US = 0.1
+PROJECT_US = 4
 
 
 def halves_body(queries, keys_values, global_ids, rand_ids, out_weight):
@@ -350,57 +344,69 @@
     groups = lax.axis_size("head")
     opposite = shards // 2
 
-    def column(array, chunk):
-        low, count = chunk
-        return lax.slice_in_dim(
-            array, low * HEAD_DIM, (low + count) * HEAD_DIM, axis=array.ndim - 1
-        )
-
-    own_pairs = [column(keys_values, c) for c in CHUNKS]
-    own_queries = [column(queries, c) for c in CHUNKS]
-
-    along_y = [swap(own_pairs[0], 1, shards)]
-    along_z = [swap(own_pairs[0], 2, shards)]
-    diagonal = [swap(along_z[0], 1, shards)]
-    visitors = [swap(after(own_queries[0], along_z[0]), opposite, shards)]
-    for n in (1, 2):
-        along_z.append(swap(after(own_pairs[n], along_z[n - 1]), 2, shards))
-        along_y.append(swap(after(own_pairs[n], along_z[n - 1]), 1, shards))
-        diagonal.append(swap(along_z[n], 1, shards))
-        visitors.append(swap(after(own_queries[n], along_z[n]), opposite, shards))
+    def column(array, head):
+        return lax.slice_in_dim(array, head * HEAD_DIM, (head + 1) * HEAD_DIM, axis=array.ndim - 1)
+
+    def over_y(value):
+        return swap(value, 1, shards)
+
+    def over_z(value):
+        return swap(value, 2, shards)
+
+    def across(value):
+        return swap(value, opposite, shards)
 
     home = key_places(myself, myself, global_ids, rand_ids, local_blocks, shards)
     guest = key_places(myself ^ opposite, myself, global_ids, rand_ids, local_blocks, shards)
     weights = out_weight.reshape(groups, heads_here, HEAD_DIM, out_weight.shape[1])
-    gathered = []
-    for n in range(len(CHUNKS)):
-        parts = (own_pairs[n], along_y[n], along_z[n], diagonal[n])
-        visitor = visitors[n]
-        message = guest_call(*guest, visitor, parts)
-        answer = swap(message, opposite, shards)
-        mixed, stats = home_call(*home, after(own_queries[n], message), parts)
-        if n == 2:
-            summed = project(
-                first_terms_kernel,
-                "first_terms",
-                None,
-                gathered,
-                CHUNKS[:2],
-                after(weights, mixed),
-                jnp.float32,
-            )
-            answer = after(answer, summed)
-        attended = merge_call(mixed, stats, answer)
-        gathered.append(gather_heads(attended))
-    return project(
-        last_term_kernel,
-        "last_term",
-        summed,
-        gathered[2:],
-        CHUNKS[2:],
-        weights,
-        jnp.bfloat16,
-    )
+    k0, k1, k2, k3 = [column(keys_values, h) for h in range(heads_here)]
+    q0, q1, q2, q3 = [column(queries, h) for h in range(heads_here)]
+
+    y0, z0 = over_y(k0), over_z(k0)
+    y0, z0, k1_, v0, v1, home, guest = together(y0, z0, k1, q0, q1, home, guest)
+
+    d0, y1, z1, v0, v1 = over_y(z0), over_y(k1_), over_z(k1_), across(v0), across(v1)
+    p0 = (k0, y0, z0, d0)
+    (s0,) = guest_call(*guest, v0, p0)
+    s0, y1, z1, v1, k2_, v2 = together(s0, y1, z1, v1, k2, q2)
+
+    d1, y2, z2, v2, g0 = over_y(z1), over_y(k2_), over_z(k2_), across(v2), across(s0)
+    m0 = home_call(*home, after(q0, s0), p0)
+    p1 = (k1, y1, z1, d1)
+    (s1,) = guest_call(*guest, after(v1, m0[1], v2), p1)
+    s1, y2, z2, v2, g0, k3_, v3 = together(s1, y2, z2, v2, g0, k3, q3)
+
+    d2, y3, z3, v3, g1 = over_y(z2), over_y(k3_), over_z(k3_), across(v3), across(s1)
+    m1 = home_call(*home, after(q1, s1), p1)
+    a0 = merge_call(*m0, after(g0, m1[1]))
+    a0x, a0c = hop(a0, 2, groups), hop(a0, 1, groups)
+    p2 = (k2, y2, z2, d2)
+    (s2,) = guest_call(*guest, after(v2, m1[1], v3), p2)
+    s2, y3, z3, v3, g1, a0x, a0c = together(s2, y3, z3, v3, g1, a0x, a0c)
+
+    d3, g2 = over_y(z3), across(s2)
+    m2 = home_call(*home, after(q2, s2), p2)
+    a1 = merge_call(*m1, after(g1, m2[1]))
+    a1x, a1c, a0d = hop(a1, 2, groups), hop(a1, 1, groups), hop(a0x, 1, groups)
+    p3 = (k3, y3, z3, d3)
+    s3a, s3b = guest_call(*guest, after(v3, a1), p3, 2)
+    s3a, s3b, g2, a1x, a1c, a0d = together(s3a, s3b, g2, a1x, a1c, a0d)
+
+    g3a, g3b = across(s3a), across(s3b)
+    m3 = home_call(*home, after(q3, s3a), p3, 2)
+    a2 = merge_call(*m2, after(g2, s3a))
+    a1d = hop(a1x, 1, groups)
+    a2x, a2c = hop(a2, 2, groups), hop(a2, 1, groups)
+    a2d = hop(a2x, 1, groups)
+    whole = (a0, a0c, a0x, a0d, a1, a1c, a1x, a1d, a2, a2c, a2x, a2d)
+    a3a = merge_call(*m3[:2], after(g3a, a2))
+    a3ax, a3ac = hop(a3a, 2, groups), hop(a3a, 1, groups)
+    a3b = merge_call(*m3[2:], after(g3b, a3a))
+    a3bx, a3bc = hop(a3b, 2, groups), hop(a3b, 1, groups)
+    a3ad = hop(a3ax, 1, groups)
+    upper = project((*whole, after(a3a, a3b), a3ac, a3ax, a3ad), weights, (0, 2))
+    a3bd = hop(after(a3bx, upper), 1, groups)
+    return project((*whole, a3b, a3bc, a3bx, a3bd), weights, (1, 2), upper)
 
 
 def padded_2(block, sides, width):

time: 232 us -> 202 us (0.87)
  waiting for transfers between devices: 132 us -> 112 us
  Pallas kernels: 57.9 us -> 41.7 us
  starting transfers between devices: 27 us -> 35.3 us
    ppermute x15 -> x21, waiting for transfers between devices: 121 us -> 101 us  [swap(): lax.ppermute(value, 'seq', [(i, i ^ distance) for i in range(shards)])]
    pallas_call x8 -> x10, Pallas kernels: 51 us -> 37.8 us  [the longest x4 13.3 us: guest_call(): pl.pallas_call(functools.partial(guest_kernel, parts), out_shape=[message...]
    ppermute x15 -> x21, starting transfers between devices: 21.3 us -> 28.3 us  [swap(): lax.ppermute(value, 'seq', [(i, i ^ distance) for i in range(shards)])]
    unnamed x20 -> x26, local copies, waits for them, and re-layouts: 3.01 us -> 7.71 us
    pallas_call x3 -> x5, Pallas kernels: 6.86 us -> 3.92 us  [merge_call(): pl.pallas_call(merge_kernel, out_shape=jax.ShapeDtypeStruct(mixed.shape,...]
    ppermute x9 -> x15, starting transfers between devices: 5.71 us -> 7.05 us  [hop(): lax.ppermute(value, 'head', [(i, i ^ distance) for i in range(groups)])]
    slice x4 -> x2, local copies, waits for them, and re-layouts: 4.93 us -> 3.64 us  [column(): lax.slice_in_dim(array, head * HEAD_DIM, (head + 1) * HEAD_DIM, axis=arra...]
    ppermute x9 -> x15, waiting for transfers between devices: 11.3 us -> 10.3 us  [hop(): lax.ppermute(value, 'head', [(i, i ^ distance) for i in range(groups)])]
  transfers between devices with their start and end apart: 24 -> 36, of which waited for: 9 -> 14; matrix products, arithmetic and copies ran while one was open for 4% -> 1% of each run, Pallas kernels for 22% -> 17%
where the time goes in v3:
time: 202 us
  waiting for transfers between devices  112 us (55%)
  Pallas kernels  41.7 us (21%)
  starting transfers between devices  35.3 us (17%)
  local copies, waits for them, and re-layouts  12.3 us (6%)
    ppermute x21, waiting for transfers between devices, swap(): lax.ppermute(value, 'seq', [(i, i ^ distance) for i in range(shards)])  101 us
    ppermute x21, starting transfers between devices, swap(): lax.ppermute(value, 'seq', [(i, i ^ distance) for i in range(shards)])  28.3 us
    pallas_call x4, Pallas kernels, guest_call(): pl.pallas_call(functools.partial(guest_kernel, parts), out_shape=[message...  13.3 us
    pallas_call x4, Pallas kernels, home_call(): pl.pallas_call(functools.partial(home_kernel, parts), out_shape=results *...  13.3 us
    pallas_call x2, Pallas kernels, project(): pl.pallas_call(kernel, out_shape=jax.ShapeDtypeStruct((rows, columns), jn...  11.2 us
    ppermute x15, waiting for transfers between devices, hop(): lax.ppermute(value, 'head', [(i, i ^ distance) for i in range(groups)])  10.3 us
    unnamed x26, local copies, waits for them, and re-layouts  7.71 us
    ppermute x15, starting transfers between devices, hop(): lax.ppermute(value, 'head', [(i, i ^ distance) for i in range(groups)])  7.05 us
  transfers between devices with their start and end apart: 36, of which 14 were waited for; matrix products, arithmetic and copies ran while one was open for 1% of the time, Pallas kernels for 17%

profile of v3, /device:TPU:0, one launch (start us, length us, event | category | flops | bytes accessed | tf_op | source)
XLA Modules:
  0.0 201.5 jit_solution(6278593066562214566)
XLA Ops:
  0.0 2.1 %fusion.16 = (bf16[2,1536,128]{2,1,0:T(8,128)(2,1)S(1)}, bf16[2,1536,128]{2,1,0:T(8,128)(2,1)S(1)}, bf16[2,1536,128]{2,1,0:T(8,128)(2,1)S(1)}, bf16[2,1536,128]{2,1,0:T(8,128)(2,1)S(1)}) fusion(bf16[2,1536,512]{2,1,0:T(8,128)(2,1)} %param.6), kind=kLoop, calls=%fused_computation.51 | loop fusion | bytes 6291456 | tf_op jit(solution)/shard_map/slice | solution.py:348
  2.2 3.1 %collective-permute-start.1 = (bf16[2,1536,128]{2,1,0:T(8,128)(2,1)S(1)}, bf16[2,1536,128]{2,1,0:T(8,128)(2,1)}, u32[]{:S(2)}, u32[]{:S(2)}) collective-permute-start(bf16[2,1536,128]{2,1,0:T(8,128)(2,1)S(1)} %get-tuple-element.133.p0), channel_id=1, source_target_pairs={{0,8},{4,12},{8,0},{12,4},{16,24},{20,28},{24,16},{28,20},{1,9},{5... | collective-permute-start | bytes 2359304 | tf_op jit(solution)/shard_map/ppermute | solution.py:318
  5.2 1.5 collective-permute-start
  8.1 1.5 fusion.17
  9.6 13.3 %collective-permute-done.1.p2 = bf16[2,1536,128]{2,1,0:T(8,128)(2,1)} collective-permute-done((bf16[2,1536,128]{2,1,0:T(8,128)(2,1)S(1)}, bf16[2,1536,128]{2,1,0:T(8,128)(2,1)}, u32[]{:S(2)}, u32[]{:S(2)}) %collective-permute-start.1) | collective-permute-done | bytes 786464 | tf_op jit(solution)/shard_map/ppermute | solution.py:318
  22.9 1.5 collective-permute-done.p1
  24.4 1.5 collective-permute-start.3
  26.7 2.7 %collective-permute-start.2 = (bf16[1536,128]{1,0:T(8,128)(2,1)S(1)}, bf16[1536,128]{1,0:T(8,128)(2,1)S(1)}, u32[]{:S(2)}, u32[]{:S(2)}) collective-permute-start(bf16[1536,128]{1,0:T(8,128)(2,1)S(1)} %get-tuple-element.76.q_ref), channel_id=1, source_target_pairs={{0,16},{4,20},{8,24},{12,28},{16,0},{20,4},{24,8},{28,12},{1,17},{... | collective-permute-start | bytes 1179656 | tf_op jit(solution)/shard_map/ppermute | solution.py:318
  29.7 23.1 %collective-permute-done.2.q_ref = bf16[1536,128]{1,0:T(8,128)(2,1)S(1)} collective-permute-done((bf16[1536,128]{1,0:T(8,128)(2,1)S(1)}, bf16[1536,128]{1,0:T(8,128)(2,1)S(1)}, u32[]{:S(2)}, u32[]{:S(2)}) %collective-permute-start.2) | collective-permute-done | bytes 393248 | tf_op jit(solution)/shard_map/ppermute | solution.py:318
  52.8 4.4 %guest_attention.4 = bf16[1632,128]{1,0:T(8,128)(2,1)S(1)} custom-call(s32[192]{0:T(256)S(1)} %reshape.36.starts_ref, f32[24,512]{1,0:T(8,128)S(1)} %reshape.37.bias_ref, bf16[1536,128]{1,0:T(8,128)(2,1)S(1)} %collective-permute-done.2.q_ref, bf16[2,1536,128]{2,1,0:T(8,128)(2,1)S(1)} %get-tuple-element.133.p0, ...), custom_call_target="tpu_custom_call" | custom-call | flops 115000000 | tf_op jit(solution)/shard_map/guest_attention/pallas_call | solution.py:211
  57.2 1.5 collective-permute-done.6.q_ref
  58.7 1.8 collective-permute-done.5.p2
  60.5 3.0 %collective-permute-start.8 = (bf16[2,1536,128]{2,1,0:T(8,128)(2,1)S(1)}, bf16[2,1536,128]{2,1,0:T(8,128)(2,1)S(1)}, u32[]{:S(2)}, u32[]{:S(2)}) collective-permute-start(bf16[2,1536,128]{2,1,0:T(8,128)(2,1)S(1)} %collective-permute-done.5.p2), channel_id=1, source_target_pairs={{0,4},{4,0},{8,12},{12,8},{16,20},{20,16},{24,28},{28,24},{1,5},{5... | collective-permute-start | bytes 2359304 | tf_op jit(solution)/shard_map/ppermute | solution.py:318
  64.2 1.0 collective-permute-start.9
  65.2 2.9 %collective-permute-start.11 = (bf16[1632,128]{1,0:T(8,128)(2,1)S(1)}, bf16[1632,128]{1,0:T(8,128)(2,1)S(1)}, u32[]{:S(2)}, u32[]{:S(2)}) collective-permute-start(bf16[1632,128]{1,0:T(8,128)(2,1)S(1)} %guest_attention.4), channel_id=1, source_target_pairs={{0,16},{4,20},{8,24},{12,28},{16,0},{20,4},{24,8},{28,12},{1,17},{... | collective-permute-start | bytes 1253384 | tf_op jit(solution)/shard_map/ppermute | solution.py:318
  68.1 4.4 %home_attention.4 = (f32[1536,128]{1,0:T(8,128)S(1)}, f32[1,32,128]{2,1,0:T(8,128)S(1)}) custom-call(s32[192]{0:T(256)S(1)} %reshape.34.starts_ref, f32[24,512]{1,0:T(8,128)S(1)} %reshape.35.bias_ref, bf16[1536,128]{1,0:T(8,128)(2,1)S(1)} %get-tuple-element.76.q_ref, bf16[2,1536,128]{2,1,0:T(8,128)(2,1)S(1)} %get-tuple-element.133.p0, ...), custom_call_target="tpu_custom_call" | custom-call | tf_op jit(solution)/shard_map/home_attention/pallas_call | solution.py:233
  72.5 27.6 %collective-permute-done.7.q_ref = bf16[1536,128]{1,0:T(8,128)(2,1)S(1)} collective-permute-done((bf16[1536,128]{1,0:T(8,128)(2,1)S(1)}, bf16[1536,128]{1,0:T(8,128)(2,1)S(1)}, u32[]{:S(2)}, u32[]{:S(2)}) %collective-permute-start.7) | collective-permute-done | bytes 393248 | tf_op jit(solution)/shard_map/ppermute | solution.py:318
  100.1 3.2 %guest_attention.5 = bf16[1632,128]{1,0:T(8,128)(2,1)S(1)} custom-call(s32[192]{0:T(256)S(1)} %reshape.36.starts_ref, f32[24,512]{1,0:T(8,128)S(1)} %reshape.37.bias_ref, bf16[1536,128]{1,0:T(8,128)(2,1)S(1)} %collective-permute-done.6.q_ref, bf16[2,1536,128]{2,1,0:T(8,128)(2,1)S(1)} %get-tuple-element.73.p0, ...), custom_call_target="tpu_custom_call" | custom-call | flops 115000000 | tf_op jit(solution)/shard_map/guest_attention/pallas_call | solution.py:211
  103.3 2.1 %collective-permute-start.13 = (bf16[2,1536,128]{2,1,0:T(8,128)(2,1)S(1)}, bf16[2,1536,128]{2,1,0:T(8,128)(2,1)S(1)}, u32[]{:S(2)}, u32[]{:S(2)}) collective-permute-start(bf16[2,1536,128]{2,1,0:T(8,128)(2,1)S(1)} %collective-permute-done.10.p2), channel_id=1, source_target_pairs={{0,4},{4,0},{8,12},{12,8},{16,20},{20,16},{24,28},{28,24},{1,5},{5... | collective-permute-start | bytes 2359304 | tf_op jit(solution)/shard_map/ppermute | solution.py:318
  105.3 2.3 %collective-permute-start.15 = (bf16[2,1536,128]{2,1,0:T(8,128)(2,1)S(1)}, bf16[2,1536,128]{2,1,0:T(8,128)(2,1)S(1)}, u32[]{:S(2)}, u32[]{:S(2)}) collective-permute-start(bf16[2,1536,128]{2,1,0:T(8,128)(2,1)S(1)} %get-tuple-element.95.p0), channel_id=1, source_target_pairs={{0,8},{4,12},{8,0},{12,4},{16,24},{20,28},{24,16},{28,20},{1,9},{5... | collective-permute-start | bytes 2359304 | tf_op jit(solution)/shard_map/ppermute | solution.py:318
  108.3 3.2 %home_attention.5 = (f32[1536,128]{1,0:T(8,128)S(1)}, f32[1,32,128]{2,1,0:T(8,128)S(1)}) custom-call(s32[192]{0:T(256)S(1)} %reshape.34.starts_ref, f32[24,512]{1,0:T(8,128)S(1)} %reshape.35.bias_ref, bf16[1536,128]{1,0:T(8,128)(2,1)S(1)} %get-tuple-element.87.q_ref, bf16[2,1536,128]{2,1,0:T(8,128)(2,1)S(1)} %get-tuple-element.73.p0, ...), custom_call_target="tpu_custom_call" | custom-call | tf_op jit(solution)/shard_map/home_attention/pallas_call | solution.py:233
  111.5 1.0 merge_halves.5.refs_0_
  112.5 10.8 %collective-permute-done.12.q_ref = bf16[1536,128]{1,0:T(8,128)(2,1)S(1)} collective-permute-done((bf16[1536,128]{1,0:T(8,128)(2,1)S(1)}, bf16[1536,128]{1,0:T(8,128)(2,1)S(1)}, u32[]{:S(2)}, u32[]{:S(2)}) %collective-permute-start.12) | collective-permute-done | bytes 393248 | tf_op jit(solution)/shard_map/ppermute | solution.py:318
  123.3 1.5 collective-permute-start.17
  124.7 3.2 %guest_attention.6 = bf16[1632,128]{1,0:T(8,128)(2,1)S(1)} custom-call(s32[192]{0:T(256)S(1)} %reshape.36.starts_ref, f32[24,512]{1,0:T(8,128)S(1)} %reshape.37.bias_ref, bf16[1536,128]{1,0:T(8,128)(2,1)S(1)} %collective-permute-done.7.q_ref, bf16[2,1536,128]{2,1,0:T(8,128)(2,1)S(1)} %get-tuple-element.84.p0, ...), custom_call_target="tpu_custom_call" | custom-call | flops 115000000 | tf_op jit(solution)/shard_map/guest_attention/pallas_call | solution.py:211
  128.7 6.1 %collective-permute-done.17.refs_2_ = bf16[1536,128]{1,0:T(8,128)(2,1)S(1)} collective-permute-done((bf16[1536,128]{1,0:T(8,128)(2,1)S(1)}, bf16[1536,128]{1,0:T(8,128)(2,1)S(1)}, u32[]{:S(2)}, u32[]{:S(2)}) %collective-permute-start.17) | collective-permute-done | bytes 393248 | tf_op jit(solution)/shard_map/ppermute | solution.py:326
  134.8 0.8 collective-permute-start.19
  135.6 2.0 collective-permute-start.20
  137.6 3.2 %home_attention.6 = (f32[1536,128]{1,0:T(8,128)S(1)}, f32[1,32,128]{2,1,0:T(8,128)S(1)}) custom-call(s32[192]{0:T(256)S(1)} %reshape.34.starts_ref, f32[24,512]{1,0:T(8,128)S(1)} %reshape.35.bias_ref, bf16[1536,128]{1,0:T(8,128)(2,1)S(1)} %get-tuple-element.102.q_ref, bf16[2,1536,128]{2,1,0:T(8,128)(2,1)S(1)} %get-tuple-element.84.p0, ...), custom_call_target="tpu_custom_call" | custom-call | tf_op jit(solution)/shard_map/home_attention/pallas_call | solution.py:233
  140.8 1.0 merge_halves.6.refs_4_
  141.8 1.6 collective-permute-start.21
  143.5 10.5 %collective-permute-done.19.p3 = bf16[2,1536,128]{2,1,0:T(8,128)(2,1)S(1)} collective-permute-done((bf16[2,1536,128]{2,1,0:T(8,128)(2,1)S(1)}, bf16[2,1536,128]{2,1,0:T(8,128)(2,1)S(1)}, u32[]{:S(2)}, u32[]{:S(2)}) %collective-permute-start.19) | collective-permute-done | bytes 786464 | tf_op jit(solution)/shard_map/ppermute | solution.py:318
  154.0 2.6 %guest_attention.7 = (bf16[816,128]{1,0:T(8,128)(2,1)S(1)}, bf16[816,128]{1,0:T(8,128)(2,1)S(1)}) custom-call(s32[192]{0:T(256)S(1)} %reshape.36.starts_ref, f32[24,512]{1,0:T(8,128)S(1)} %reshape.37.bias_ref, bf16[1536,128]{1,0:T(8,128)(2,1)S(1)} %collective-permute-done.12.q_ref, bf16[2,1536,128]{2,1,0:T(8,128)(2,1)S(1)} %get-tuple-element.95.p0, ...), custom_call_target="tpu_custom_call" | custom-call | flops 115000000 | tf_op jit(solution)/shard_map/guest_attention/pallas_call | solution.py:211
  157.5 1.0 merge_halves.7.refs_8_
  158.4 1.5 collective-permute-start.26
  160.0 2.9 %collective-permute-start.28 = (bf16[816,128]{1,0:T(8,128)(2,1)S(1)}, bf16[816,128]{1,0:T(8,128)(2,1)S(1)}, u32[]{:S(2)}, u32[]{:S(2)}) collective-permute-start(bf16[816,128]{1,0:T(8,128)(2,1)S(1)} %get-tuple-element.120), channel_id=1, source_target_pairs={{0,16},{4,20},{8,24},{12,28},{16,0},{20,4},{24,8},{28,12},{1,17},{... | collective-permute-start | bytes 626696 | tf_op jit(solution)/shard_map/ppermute | solution.py:318
  163.4 2.6 %home_attention.7 = (f32[768,128]{1,0:T(8,128)S(1)}, f32[1,16,128]{2,1,0:T(8,128)S(1)}, f32[768,128]{1,0:T(8,128)S(1)}, f32[1,16,128]{2,1,0:T(8,128)S(1)}) custom-call(s32[192]{0:T(256)S(1)} %reshape.34.starts_ref, f32[24,512]{1,0:T(8,128)S(1)} %reshape.35.bias_ref, bf16[1536,128]{1,0:T(8,128)(2,1)S(1)} %get-tuple-element.117.q_ref, ...), custom_call_target="tpu_custom_call" | custom-call | tf_op jit(solution)/shard_map/home_attention/pallas_call | solution.py:233
  166.0 7.9 %collective-permute-done.29.message_ref = bf16[816,128]{1,0:T(8,128)(2,1)S(1)} collective-permute-done((bf16[816,128]{1,0:T(8,128)(2,1)S(1)}, bf16[816,128]{1,0:T(8,128)(2,1)S(1)}, u32[]{:S(2)}, u32[]{:S(2)}) %collective-permute-start.29) | collective-permute-done | bytes 208928 | tf_op jit(solution)/shard_map/ppermute | solution.py:318
  175.0 3.2 %collective-permute-done.28.message_ref = bf16[816,128]{1,0:T(8,128)(2,1)S(1)} collective-permute-done((bf16[816,128]{1,0:T(8,128)(2,1)S(1)}, bf16[816,128]{1,0:T(8,128)(2,1)S(1)}, u32[]{:S(2)}, u32[]{:S(2)}) %collective-permute-start.28) | collective-permute-done | bytes 208928 | tf_op jit(solution)/shard_map/ppermute | solution.py:318
  178.3 2.9 %collective-permute-done.33.refs_14_ = bf16[768,128]{1,0:T(8,128)(2,1)S(1)} collective-permute-done((bf16[768,128]{1,0:T(8,128)(2,1)S(1)}, bf16[768,128]{1,0:T(8,128)(2,1)S(1)}, u32[]{:S(2)}, u32[]{:S(2)}) %collective-permute-start.33) | collective-permute-done | bytes 196640 | tf_op jit(solution)/shard_map/ppermute | solution.py:326
  182.7 2.2 %copy-done.2 = bf16[2048,1024]{1,0:T(8,128)(2,1)S(1)} copy-done((bf16[2048,1024]{1,0:T(8,128)(2,1)S(1)}, bf16[2048,1024]{1,0:T(8,128)(2,1)}, u32[]{:S(2)}) %copy-start.2) | copy-done | bytes 4194328
  184.9 1.0 copy-done.4
  185.8 1.0 copy-done.6
  186.8 1.0 copy-done.8
  187.8 1.0 copy-done.10
  188.8 5.6 %project_rows.2.refs_16_ = bf16[1536,1024]{1,0:T(8,128)(2,1)} custom-call(s32[1]{0:T(128)} %bitcast.me_ref, bf16[4,4,128,1024]{3,2,1,0:T(8,128)(2,1)S(1)} %bitcast.2, bf16[1536,128]{1,0:T(8,128)(2,1)S(1)} %copy-done.1, bf16[1536,128]{1,0:T(8,128)(2,1)S(1)} %copy-done.4, bf16[1536,128]{1,0:T(8,128)(2,1)S(1)} %copy-done.6, bf16[1536,128]{1,0:T(8,128)(2,1)S(1)} %copy-done.10, ...), custom_call_target="tpu_custom_call" | custom-call | flops 4600000000 | tf_op jit(solution)/shard_map/project_rows/pallas_call | solution.py:281
  194.7 1.2 collective-permute-done.35.refs_15_
  195.9 5.6 %project_rows.3 = bf16[1536,1024]{1,0:T(8,128)(2,1)} custom-call(s32[1]{0:T(128)} %bitcast.me_ref, bf16[4,4,128,1024]{3,2,1,0:T(8,128)(2,1)S(1)} %bitcast.3, bf16[1536,128]{1,0:T(8,128)(2,1)S(1)} %copy-done.1, bf16[1536,128]{1,0:T(8,128)(2,1)S(1)} %copy-done.4, bf16[1536,128]{1,0:T(8,128)(2,1)S(1)} %copy-done.6, ...), custom_call_target="tpu_custom_call", output_to_operand_aliasing={{}: (18, {})} | custom-call | flops 4600000000 | tf_op jit(solution)/shard_map/project_rows/pallas_call | solution.py:281
  (85 shorter events, 8.9 us)
Async XLA Ops:
  0.0 6.9 %copy-start.12 = (s32[2]{0:T(128)S(1)}, s32[2]{0:T(128)}, u32[]{:S(2)}) copy-start(s32[2]{0:T(128)} %param.7) | copy-start | bytes 28
  0.0 7.0 %copy-start.11 = (s32[192,3]{0,1:T(4,128)S(1)}, s32[192,3]{0,1:T(4,128)}, u32[]{:S(2)}) copy-start(s32[192,3]{0,1:T(4,128)} %param.8) | copy-start | bytes 6916
  2.2 20.7 %collective-permute-start.1 = (bf16[2,1536,128]{2,1,0:T(8,128)(2,1)S(1)}, bf16[2,1536,128]{2,1,0:T(8,128)(2,1)}, u32[]{:S(2)}, u32[]{:S(2)}) collective-permute-start(bf16[2,1536,128]{2,1,0:T(8,128)(2,1)S(1)} %get-tuple-element.133.p0), channel_id=1, source_target_pairs={{0,8},{4,12},{8,0},{12,4},{16,24},{20,28},{24,16},{28,20},{1,9},{5... | collective-permute-start | bytes 2359304 | tf_op jit(solution)/shard_map/ppermute | solution.py:318
  5.2 19.1 %collective-permute-start = (bf16[2,1536,128]{2,1,0:T(8,128)(2,1)S(1)}, bf16[2,1536,128]{2,1,0:T(8,128)(2,1)}, u32[]{:S(2)}, u32[]{:S(2)}) collective-permute-start(bf16[2,1536,128]{2,1,0:T(8,128)(2,1)S(1)} %get-tuple-element.133.p0), channel_id=1, source_target_pairs={{0,4},{4,0},{8,12},{12,8},{16,20},{20,16},{24,28},{28,24},{1,5},{5... | collective-permute-start | bytes 2359304 | tf_op jit(solution)/shard_map/ppermute | solution.py:318
  24.4 28.4 %collective-permute-start.3 = (bf16[2,1536,128]{2,1,0:T(8,128)(2,1)}, bf16[2,1536,128]{2,1,0:T(8,128)(2,1)S(1)}, u32[]{:S(2)}, u32[]{:S(2)}) collective-permute-start(bf16[2,1536,128]{2,1,0:T(8,128)(2,1)} %collective-permute-done.1.p2), channel_id=1, source_target_pairs={{0,4},{4,0},{8,12},{12,8},{16,20},{20,16},{24,28},{28,24},{1,5},{5... | collective-permute-start | bytes 2359304 | tf_op jit(solution)/shard_map/ppermute | solution.py:318
  25.9 34.7 %collective-permute-start.5 = (bf16[2,1536,128]{2,1,0:T(8,128)(2,1)S(1)}, bf16[2,1536,128]{2,1,0:T(8,128)(2,1)S(1)}, u32[]{:S(2)}, u32[]{:S(2)}) collective-permute-start(bf16[2,1536,128]{2,1,0:T(8,128)(2,1)S(1)} %get-tuple-element.73.p0), channel_id=1, source_target_pairs={{0,8},{4,12},{8,0},{12,4},{16,24},{20,28},{24,16},{28,20},{1,9},{5... | collective-permute-start | bytes 2359304 | tf_op jit(solution)/shard_map/ppermute | solution.py:318
  26.3 34.2 %collective-permute-start.4 = (bf16[2,1536,128]{2,1,0:T(8,128)(2,1)S(1)}, bf16[2,1536,128]{2,1,0:T(8,128)(2,1)S(1)}, u32[]{:S(2)}, u32[]{:S(2)}) collective-permute-start(bf16[2,1536,128]{2,1,0:T(8,128)(2,1)S(1)} %get-tuple-element.73.p0), channel_id=1, source_target_pairs={{0,4},{4,0},{8,12},{12,8},{16,20},{20,16},{24,28},{28,24},{1,5},{5... | collective-permute-start | bytes 2359304 | tf_op jit(solution)/shard_map/ppermute | solution.py:318
  26.7 26.1 %collective-permute-start.2 = (bf16[1536,128]{1,0:T(8,128)(2,1)S(1)}, bf16[1536,128]{1,0:T(8,128)(2,1)S(1)}, u32[]{:S(2)}, u32[]{:S(2)}) collective-permute-start(bf16[1536,128]{1,0:T(8,128)(2,1)S(1)} %get-tuple-element.76.q_ref), channel_id=1, source_target_pairs={{0,16},{4,20},{8,24},{12,28},{16,0},{20,4},{24,8},{28,12},{1,17},{... | collective-permute-start | bytes 1179656 | tf_op jit(solution)/shard_map/ppermute | solution.py:318
  29.4 29.3 %collective-permute-start.6 = (bf16[1536,128]{1,0:T(8,128)(2,1)S(1)}, bf16[1536,128]{1,0:T(8,128)(2,1)S(1)}, u32[]{:S(2)}, u32[]{:S(2)}) collective-permute-start(bf16[1536,128]{1,0:T(8,128)(2,1)S(1)} %get-tuple-element.87.q_ref), channel_id=1, source_target_pairs={{0,16},{4,20},{8,24},{12,28},{16,0},{20,4},{24,8},{28,12},{1,17},{... | collective-permute-start | bytes 1179656 | tf_op jit(solution)/shard_map/ppermute | solution.py:318
  60.5 39.5 %collective-permute-start.8 = (bf16[2,1536,128]{2,1,0:T(8,128)(2,1)S(1)}, bf16[2,1536,128]{2,1,0:T(8,128)(2,1)S(1)}, u32[]{:S(2)}, u32[]{:S(2)}) collective-permute-start(bf16[2,1536,128]{2,1,0:T(8,128)(2,1)S(1)} %collective-permute-done.5.p2), channel_id=1, source_target_pairs={{0,4},{4,0},{8,12},{12,8},{16,20},{20,16},{24,28},{28,24},{1,5},{5... | collective-permute-start | bytes 2359304 | tf_op jit(solution)/shard_map/ppermute | solution.py:318
  63.6 39.7 %collective-permute-start.10 = (bf16[2,1536,128]{2,1,0:T(8,128)(2,1)S(1)}, bf16[2,1536,128]{2,1,0:T(8,128)(2,1)S(1)}, u32[]{:S(2)}, u32[]{:S(2)}) collective-permute-start(bf16[2,1536,128]{2,1,0:T(8,128)(2,1)S(1)} %get-tuple-element.84.p0), channel_id=1, source_target_pairs={{0,8},{4,12},{8,0},{12,4},{16,24},{20,28},{24,16},{28,20},{1,9},{5... | collective-permute-start | bytes 2359304 | tf_op jit(solution)/shard_map/ppermute | solution.py:318
  64.2 39.1 %collective-permute-start.9 = (bf16[2,1536,128]{2,1,0:T(8,128)(2,1)S(1)}, bf16[2,1536,128]{2,1,0:T(8,128)(2,1)S(1)}, u32[]{:S(2)}, u32[]{:S(2)}) collective-permute-start(bf16[2,1536,128]{2,1,0:T(8,128)(2,1)S(1)} %get-tuple-element.84.p0), channel_id=1, source_target_pairs={{0,4},{4,0},{8,12},{12,8},{16,20},{20,16},{24,28},{28,24},{1,5},{5... | collective-permute-start | bytes 2359304 | tf_op jit(solution)/shard_map/ppermute | solution.py:318
  65.2 38.1 %collective-permute-start.11 = (bf16[1632,128]{1,0:T(8,128)(2,1)S(1)}, bf16[1632,128]{1,0:T(8,128)(2,1)S(1)}, u32[]{:S(2)}, u32[]{:S(2)}) collective-permute-start(bf16[1632,128]{1,0:T(8,128)(2,1)S(1)} %guest_attention.4), channel_id=1, source_target_pairs={{0,16},{4,20},{8,24},{12,28},{16,0},{20,4},{24,8},{28,12},{1,17},{... | collective-permute-start | bytes 1253384 | tf_op jit(solution)/shard_map/ppermute | solution.py:318
  68.1 32.0 %collective-permute-start.7 = (bf16[1536,128]{1,0:T(8,128)(2,1)S(1)}, bf16[1536,128]{1,0:T(8,128)(2,1)S(1)}, u32[]{:S(2)}, u32[]{:S(2)}) collective-permute-start(bf16[1536,128]{1,0:T(8,128)(2,1)S(1)} %get-tuple-element.102.q_ref), channel_id=1, source_target_pairs={{0,16},{4,20},{8,24},{12,28},{16,0},{20,4},{24,8},{28,12},{1,17},{... | collective-permute-start | bytes 1179656 | tf_op jit(solution)/shard_map/ppermute | solution.py:318
  103.3 20.0 %collective-permute-start.13 = (bf16[2,1536,128]{2,1,0:T(8,128)(2,1)S(1)}, bf16[2,1536,128]{2,1,0:T(8,128)(2,1)S(1)}, u32[]{:S(2)}, u32[]{:S(2)}) collective-permute-start(bf16[2,1536,128]{2,1,0:T(8,128)(2,1)S(1)} %collective-permute-done.10.p2), channel_id=1, source_target_pairs={{0,4},{4,0},{8,12},{12,8},{16,20},{20,16},{24,28},{28,24},{1,5},{5... | collective-permute-start | bytes 2359304 | tf_op jit(solution)/shard_map/ppermute | solution.py:318
  105.3 17.9 %collective-permute-start.12 = (bf16[1536,128]{1,0:T(8,128)(2,1)S(1)}, bf16[1536,128]{1,0:T(8,128)(2,1)S(1)}, u32[]{:S(2)}, u32[]{:S(2)}) collective-permute-start(bf16[1536,128]{1,0:T(8,128)(2,1)S(1)} %get-tuple-element.117.q_ref), channel_id=1, source_target_pairs={{0,16},{4,20},{8,24},{12,28},{16,0},{20,4},{24,8},{28,12},{1,17},{... | collective-permute-start | bytes 1179656 | tf_op jit(solution)/shard_map/ppermute | solution.py:318
  105.3 29.5 %collective-permute-start.15 = (bf16[2,1536,128]{2,1,0:T(8,128)(2,1)S(1)}, bf16[2,1536,128]{2,1,0:T(8,128)(2,1)S(1)}, u32[]{:S(2)}, u32[]{:S(2)}) collective-permute-start(bf16[2,1536,128]{2,1,0:T(8,128)(2,1)S(1)} %get-tuple-element.95.p0), channel_id=1, source_target_pairs={{0,8},{4,12},{8,0},{12,4},{16,24},{20,28},{24,16},{28,20},{1,9},{5... | collective-permute-start | bytes 2359304 | tf_op jit(solution)/shard_map/ppermute | solution.py:318
  107.6 27.2 %collective-permute-start.14 = (bf16[2,1536,128]{2,1,0:T(8,128)(2,1)S(1)}, bf16[2,1536,128]{2,1,0:T(8,128)(2,1)S(1)}, u32[]{:S(2)}, u32[]{:S(2)}) collective-permute-start(bf16[2,1536,128]{2,1,0:T(8,128)(2,1)S(1)} %get-tuple-element.95.p0), channel_id=1, source_target_pairs={{0,4},{4,0},{8,12},{12,8},{16,20},{20,16},{24,28},{28,24},{1,5},{5... | collective-permute-start | bytes 2359304 | tf_op jit(solution)/shard_map/ppermute | solution.py:318
  108.1 26.7 %collective-permute-start.16 = (bf16[1632,128]{1,0:T(8,128)(2,1)S(1)}, bf16[1632,128]{1,0:T(8,128)(2,1)S(1)}, u32[]{:S(2)}, u32[]{:S(2)}) collective-permute-start(bf16[1632,128]{1,0:T(8,128)(2,1)S(1)} %guest_attention.5), channel_id=1, source_target_pairs={{0,16},{4,20},{8,24},{12,28},{16,0},{20,4},{24,8},{28,12},{1,17},{... | collective-permute-start | bytes 1253384 | tf_op jit(solution)/shard_map/ppermute | solution.py:318
  112.5 28.3 %copy-start = (bf16[1536,128]{1,0:T(8,128)(2,1)}, bf16[1536,128]{1,0:T(8,128)(2,1)S(1)}, u32[]{:S(2)}) copy-start(bf16[1536,128]{1,0:T(8,128)(2,1)S(1)} %merge_halves.5.refs_0_) | copy-start | bytes 1179652
  123.3 4.7 %collective-permute-start.18 = (bf16[1536,128]{1,0:T(8,128)(2,1)S(1)}, bf16[1536,128]{1,0:T(8,128)(2,1)S(1)}, u32[]{:S(2)}, u32[]{:S(2)}) collective-permute-start(bf16[1536,128]{1,0:T(8,128)(2,1)S(1)} %merge_halves.5.refs_0_), channel_id=1, source_target_pairs={{0,1},{1,0},{2,3},{3,2},{4,5},{5,4},{6,7},{7,6},{8,9},{9,8},{10,11... | collective-permute-start | bytes 1179656 | tf_op jit(solution)/shard_map/ppermute | solution.py:326
  123.3 11.5 %collective-permute-start.17 = (bf16[1536,128]{1,0:T(8,128)(2,1)S(1)}, bf16[1536,128]{1,0:T(8,128)(2,1)S(1)}, u32[]{:S(2)}, u32[]{:S(2)}) collective-permute-start(bf16[1536,128]{1,0:T(8,128)(2,1)S(1)} %merge_halves.5.refs_0_), channel_id=1, source_target_pairs={{0,2},{1,3},{2,0},{3,1},{4,6},{5,7},{6,4},{7,5},{8,10},{9,11},{10,... | collective-permute-start | bytes 1179656 | tf_op jit(solution)/shard_map/ppermute | solution.py:326
  127.9 0.8 copy-start.3
  134.8 21.9 %copy-start.5 = (bf16[1536,128]{1,0:T(8,128)(2,1)}, bf16[1536,128]{1,0:T(8,128)(2,1)S(1)}, u32[]{:S(2)}) copy-start(bf16[1536,128]{1,0:T(8,128)(2,1)S(1)} %collective-permute-done.17.refs_2_) | copy-start | bytes 1179652
  134.8 19.2 %collective-permute-start.19 = (bf16[2,1536,128]{2,1,0:T(8,128)(2,1)S(1)}, bf16[2,1536,128]{2,1,0:T(8,128)(2,1)S(1)}, u32[]{:S(2)}, u32[]{:S(2)}) collective-permute-start(bf16[2,1536,128]{2,1,0:T(8,128)(2,1)S(1)} %collective-permute-done.15.p2), channel_id=1, source_target_pairs={{0,4},{4,0},{8,12},{12,8},{16,20},{20,16},{24,28},{28,24},{1,5},{5... | collective-permute-start | bytes 2359304 | tf_op jit(solution)/shard_map/ppermute | solution.py:318
  135.6 21.9 %collective-permute-start.20 = (bf16[1632,128]{1,0:T(8,128)(2,1)S(1)}, bf16[1632,128]{1,0:T(8,128)(2,1)S(1)}, u32[]{:S(2)}, u32[]{:S(2)}) collective-permute-start(bf16[1632,128]{1,0:T(8,128)(2,1)S(1)} %guest_attention.6), channel_id=1, source_target_pairs={{0,16},{4,20},{8,24},{12,28},{16,0},{20,4},{24,8},{28,12},{1,17},{... | collective-permute-start | bytes 1253384 | tf_op jit(solution)/shard_map/ppermute | solution.py:318
  141.7 14.9 %collective-permute-start.22 = (bf16[1536,128]{1,0:T(8,128)(2,1)S(1)}, bf16[1536,128]{1,0:T(8,128)(2,1)S(1)}, u32[]{:S(2)}, u32[]{:S(2)}) collective-permute-start(bf16[1536,128]{1,0:T(8,128)(2,1)S(1)} %merge_halves.6.refs_4_), channel_id=1, source_target_pairs={{0,1},{1,0},{2,3},{3,2},{4,5},{5,4},{6,7},{7,6},{8,9},{9,8},{10,11... | collective-permute-start | bytes 1179656 | tf_op jit(solution)/shard_map/ppermute | solution.py:326
  141.8 15.6 %collective-permute-start.21 = (bf16[1536,128]{1,0:T(8,128)(2,1)S(1)}, bf16[1536,128]{1,0:T(8,128)(2,1)}, u32[]{:S(2)}, u32[]{:S(2)}) collective-permute-start(bf16[1536,128]{1,0:T(8,128)(2,1)S(1)} %merge_halves.6.refs_4_), channel_id=1, source_target_pairs={{0,2},{1,3},{2,0},{3,1},{4,6},{5,7},{6,4},{7,5},{8,10},{9,11},{10,... | collective-permute-start | bytes 1179656 | tf_op jit(solution)/shard_map/ppermute | solution.py:326
  143.4 14.1 %collective-permute-start.23 = (bf16[1536,128]{1,0:T(8,128)(2,1)S(1)}, bf16[1536,128]{1,0:T(8,128)(2,1)S(1)}, u32[]{:S(2)}, u32[]{:S(2)}) collective-permute-start(bf16[1536,128]{1,0:T(8,128)(2,1)S(1)} %collective-permute-done.17.refs_2_), channel_id=1, source_target_pairs={{0,1},{1,0},{2,3},{3,2},{4,5},{5,4},{6,7},{7,6},{8,9},{9,8},{10,11... | collective-permute-start | bytes 1179656 | tf_op jit(solution)/shard_map/ppermute | solution.py:326
  157.4 23.8 %copy-start.9 = (bf16[1536,128]{1,0:T(8,128)(2,1)}, bf16[1536,128]{1,0:T(8,128)(2,1)S(1)}, u32[]{:S(2)}) copy-start(bf16[1536,128]{1,0:T(8,128)(2,1)S(1)} %collective-permute-done.23.refs_3_) | copy-start | bytes 1179652
  157.5 25.2 %copy-start.1 = (bf16[1536,128]{1,0:T(8,128)(2,1)S(1)}, bf16[1536,128]{1,0:T(8,128)(2,1)}, u32[]{:S(2)}) copy-start(bf16[1536,128]{1,0:T(8,128)(2,1)} %copy-done) | copy-start | bytes 1179652
  158.4 16.6 %collective-permute-start.26 = (bf16[1536,128]{1,0:T(8,128)(2,1)S(1)}, bf16[1536,128]{1,0:T(8,128)(2,1)}, u32[]{:S(2)}, u32[]{:S(2)}) collective-permute-start(bf16[1536,128]{1,0:T(8,128)(2,1)S(1)} %merge_halves.7.refs_8_), channel_id=1, source_target_pairs={{0,2},{1,3},{2,0},{3,1},{4,6},{5,7},{6,4},{7,5},{8,10},{9,11},{10,... | collective-permute-start | bytes 1179656 | tf_op jit(solution)/shard_map/ppermute | solution.py:326
  160.0 13.9 %collective-permute-start.29 = (bf16[816,128]{1,0:T(8,128)(2,1)S(1)}, bf16[816,128]{1,0:T(8,128)(2,1)S(1)}, u32[]{:S(2)}, u32[]{:S(2)}) collective-permute-start(bf16[816,128]{1,0:T(8,128)(2,1)S(1)} %get-tuple-element.115), channel_id=1, source_target_pairs={{0,16},{4,20},{8,24},{12,28},{16,0},{20,4},{24,8},{28,12},{1,17},{... | collective-permute-start | bytes 626696 | tf_op jit(solution)/shard_map/ppermute | solution.py:318
  160.0 18.3 %collective-permute-start.28 = (bf16[816,128]{1,0:T(8,128)(2,1)S(1)}, bf16[816,128]{1,0:T(8,128)(2,1)S(1)}, u32[]{:S(2)}, u32[]{:S(2)}) collective-permute-start(bf16[816,128]{1,0:T(8,128)(2,1)S(1)} %get-tuple-element.120), channel_id=1, source_target_pairs={{0,16},{4,20},{8,24},{12,28},{16,0},{20,4},{24,8},{28,12},{1,17},{... | collective-permute-start | bytes 626696 | tf_op jit(solution)/shard_map/ppermute | solution.py:318
  162.9 18.8 %collective-permute-start.25 = (bf16[1536,128]{1,0:T(8,128)(2,1)S(1)}, bf16[1536,128]{1,0:T(8,128)(2,1)}, u32[]{:S(2)}, u32[]{:S(2)}) collective-permute-start(bf16[1536,128]{1,0:T(8,128)(2,1)S(1)} %merge_halves.7.refs_8_), channel_id=1, source_target_pairs={{0,1},{1,0},{2,3},{3,2},{4,5},{5,4},{6,7},{7,6},{8,9},{9,8},{10,11... | collective-permute-start | bytes 1179656 | tf_op jit(solution)/shard_map/ppermute | solution.py:326
  162.9 19.5 %collective-permute-start.24 = (bf16[1536,128]{1,0:T(8,128)(2,1)}, bf16[1536,128]{1,0:T(8,128)(2,1)}, u32[]{:S(2)}, u32[]{:S(2)}) collective-permute-start(bf16[1536,128]{1,0:T(8,128)(2,1)} %collective-permute-done.21.refs_6_), channel_id=1, source_target_pairs={{0,1},{1,0},{2,3},{3,2},{4,5},{5,4},{6,7},{7,6},{8,9},{9,8},{10,11... | collective-permute-start | bytes 1179656 | tf_op jit(solution)/shard_map/ppermute | solution.py:326
  174.4 6.8 %collective-permute-start.33 = (bf16[768,128]{1,0:T(8,128)(2,1)S(1)}, bf16[768,128]{1,0:T(8,128)(2,1)S(1)}, u32[]{:S(2)}, u32[]{:S(2)}) collective-permute-start(bf16[768,128]{1,0:T(8,128)(2,1)S(1)} %merge_halves.8.refs_12_), channel_id=1, source_target_pairs={{0,2},{1,3},{2,0},{3,1},{4,6},{5,7},{6,4},{7,5},{8,10},{9,11},{10,... | collective-permute-start | bytes 589832 | tf_op jit(solution)/shard_map/ppermute | solution.py:326
  175.0 7.6 %collective-permute-start.27 = (bf16[1536,128]{1,0:T(8,128)(2,1)}, bf16[1536,128]{1,0:T(8,128)(2,1)S(1)}, u32[]{:S(2)}, u32[]{:S(2)}) collective-permute-start(bf16[1536,128]{1,0:T(8,128)(2,1)} %collective-permute-done.26.refs_10_), channel_id=1, source_target_pairs={{0,1},{1,0},{2,3},{3,2},{4,5},{5,4},{6,7},{7,6},{8,9},{9,8},{10,11... | collective-permute-start | bytes 1179656 | tf_op jit(solution)/shard_map/ppermute | solution.py:326
  178.3 4.3 %collective-permute-start.32 = (bf16[768,128]{1,0:T(8,128)(2,1)S(1)}, bf16[768,128]{1,0:T(8,128)(2,1)S(1)}, u32[]{:S(2)}, u32[]{:S(2)}) collective-permute-start(bf16[768,128]{1,0:T(8,128)(2,1)S(1)} %merge_halves.8.refs_12_), channel_id=1, source_target_pairs={{0,1},{1,0},{2,3},{3,2},{4,5},{5,4},{6,7},{7,6},{8,9},{9,8},{10,11... | collective-permute-start | bytes 589832 | tf_op jit(solution)/shard_map/ppermute | solution.py:326
  181.2 1.4 collective-permute-start.34
  181.7 12.7 %collective-permute-start.31 = (bf16[768,128]{1,0:T(8,128)(2,1)S(1)}, bf16[768,128]{1,0:T(8,128)(2,1)S(1)}, u32[]{:S(2)}, u32[]{:S(2)}) collective-permute-start(bf16[768,128]{1,0:T(8,128)(2,1)S(1)} %merge_halves.9.refs_12_), channel_id=1, source_target_pairs={{0,2},{1,3},{2,0},{3,1},{4,6},{5,7},{6,4},{7,5},{8,10},{9,11},{10,... | collective-permute-start | bytes 589832 | tf_op jit(solution)/shard_map/ppermute | solution.py:326
  182.4 12.3 %collective-permute-start.30 = (bf16[768,128]{1,0:T(8,128)(2,1)S(1)}, bf16[768,128]{1,0:T(8,128)(2,1)S(1)}, u32[]{:S(2)}, u32[]{:S(2)}) collective-permute-start(bf16[768,128]{1,0:T(8,128)(2,1)S(1)} %merge_halves.9.refs_12_), channel_id=1, source_target_pairs={{0,1},{1,0},{2,3},{3,2},{4,5},{5,4},{6,7},{7,6},{8,9},{9,8},{10,11... | collective-permute-start | bytes 589832 | tf_op jit(solution)/shard_map/ppermute | solution.py:326
  182.7 2.2 %copy-start.2 = (bf16[2048,1024]{1,0:T(8,128)(2,1)S(1)}, bf16[2048,1024]{1,0:T(8,128)(2,1)}, u32[]{:S(2)}) copy-start(bf16[2048,1024]{1,0:T(8,128)(2,1)} %param.9) | copy-start | bytes 12582916
  184.8 1.0 copy-start.4
  185.8 1.0 copy-start.6
  186.8 1.0 copy-start.8
  187.8 1.0 copy-start.10
  194.5 1.4 collective-permute-start.35
  (1 other events, 0.8 us)

commit v4 on v3

--- a/solution.py
+++ b/solution.py
@@ -15,7 +15,7 @@
 MASKED = -1e30
 EXP2_SCALE = 1.4426950408889634 / HEAD_DIM**0.5
 STAT_TILE = 16
-VMEM_LIMIT = 32 * 1024 * 1024
+VMEM_LIMIT = 14 * 1024 * 1024
 PROJECT_LIMIT = 32 * 1024 * 1024
 
 
@@ -70,11 +70,13 @@
 
 
 def load_pool(parts, pool, sems):
-    size = parts[0].shape[1]
-    copies = [
-        pltpu.make_async_copy(part, pool.at[:, pl.ds(n * size, size), :], sems.at[n])
-        for n, part in enumerate(parts)
-    ]
+    copies, low = [], 0
+    for n, part in enumerate(parts):
+        size = part.shape[1]
+        copies.append(
+            pltpu.make_async_copy(part, pool.at[:, pl.ds(low, size), :], sems.at[n])
+        )
+        low += size
     for copy in copies:
         copy.start()
     for copy in copies:
@@ -103,9 +105,9 @@
         lax.fori_loop(0, blocks // unroll, step, 0)
 
 
-def guest_kernel(parts, starts_ref, bias_ref, q_ref, p0, p1, p2, p3, *refs):
-    *message_refs, pool, stats, sems = refs
-    load_pool((p0, p1, p2, p3), pool, sems)
+def guest_kernel(parts, count, starts_ref, bias_ref, q_ref, *refs):
+    *message_refs, pool, stats, sems = refs[count:]
+    load_pool(refs[:count], pool, sems)
     base = q_ref.shape[0] // parts
     for part, message_ref in enumerate(message_refs):
         attend_part(part, parts, starts_ref, bias_ref, q_ref, pool, message_ref, stats, True)
@@ -118,15 +120,16 @@
                 rest = rest - piece.astype(jnp.float32)
 
 
-def home_kernel(parts, starts_ref, bias_ref, q_ref, p0, p1, p2, p3, *refs):
-    *result_refs, pool, sems = refs
-    load_pool((p0, p1, p2, p3), pool, sems)
+def home_kernel(parts, count, starts_ref, bias_ref, q_ref, *refs):
+    *result_refs, pool, sems = refs[count:]
+    load_pool(refs[:count], pool, sems)
     for part in range(parts):
         mixed_ref, stats_ref = result_refs[2 * part : 2 * part + 2]
         attend_part(part, parts, starts_ref, bias_ref, q_ref, pool, mixed_ref, stats_ref, False)
 
 
-def merge_kernel(mixed_ref, stats_ref, message_ref, out_ref, home_scale, guest_scale):
+def merge_kernel(mixed_ref, stats_ref, message_ref, *refs):
+    *out_refs, home_scale, guest_scale = refs
     base, width = mixed_ref.shape
     blocks = base // BLOCK
     size = stats_ref.shape[1]
@@ -149,7 +152,8 @@
         home_scale[...] = factor_h / total
         guest_scale[...] = factor_g / total
 
-        def step(i, _):
+        def step(n, part):
+            i = part * (blocks // len(out_refs)) + n
             rows = pl.ds(pl.multiple_of(i * BLOCK, BLOCK), BLOCK)
             scale_h = jnp.sum(
                 jnp.where(eye, home_scale[pl.ds(i, 1), :], 0.0), axis=1, keepdims=True
@@ -161,29 +165,54 @@
                 mixed_ref[rows, lanes] * scale_h
                 + message_ref[rows, lanes].astype(jnp.float32) * scale_g
             )
-            out_ref[rows, lanes] = mixed.astype(jnp.bfloat16)
-            return 0
-
-        lax.fori_loop(0, blocks, step, 0, unroll=4)
-
-
-def project_kernel(heads, me_ref, w_ref, *refs):
+            rows = pl.ds(pl.multiple_of(n * BLOCK, BLOCK), BLOCK)
+            out_refs[part][rows, lanes] = mixed.astype(jnp.bfloat16)
+
+        for part in range(len(out_refs)):
+
+            def body(n, _, part=part):
+                step(n, part)
+                return 0
+
+            lax.fori_loop(0, blocks // len(out_refs), body, 0, unroll=4)
+
+
+def project_kernel(heads, given, filled, me_ref, w_ref, *refs):
+    *x_refs, out_ref, held, sem = refs
     groups = w_ref.shape[0]
-    *x_refs, out_ref = refs
-    total = None
-    for relation in range(groups):
-        pieces = [x_refs[head * groups + relation][...] for head in range(heads)]
-        weight = w_ref[me_ref[0] ^ relation].reshape(-1, w_ref.shape[-1])
-        term = jnp.dot(
-            jnp.concatenate(pieces, axis=1), weight, preferred_element_type=jnp.float32
-        )
-        total = term if total is None else total + term
+    sum_ref = x_refs.pop(0) if given else None
+    if filled:
+        x_refs.pop()
+
+    @pl.when(pl.program_id(0) == 0)
+    def _():
+        copies = [
+            pltpu.make_async_copy(
+                w_ref.at[me_ref[0] ^ relation, pl.ds(heads[0], len(heads))],
+                held.at[relation],
+                sem.at[relation],
+            )
+            for relation in range(groups)
+        ]
+        for copy in copies:
+            copy.start()
+        for copy in copies:
+            copy.wait()
+
+    ordered = [x_refs[h * groups + r][...] for r in range(groups) for h in range(len(heads))]
+    weight = held[...].reshape(-1, held.shape[-1])
+    total = jnp.dot(
+        jnp.concatenate(ordered, axis=1), weight, preferred_element_type=jnp.float32
+    )
+    if given:
+        total = total + sum_ref[...]
     out_ref[...] = total.astype(out_ref.dtype)
 
 
 VMEM = pl.BlockSpec(memory_space=pltpu.VMEM)
 SMEM = pl.BlockSpec(memory_space=pltpu.SMEM)
 ANY = pl.BlockSpec(memory_space=pl.ANY)
+HBM = pl.BlockSpec(memory_space=pltpu.HBM)
 
 
 def params():
@@ -209,14 +238,14 @@
     size = stats_shape(query, parts, jax.ShapeDtypeStruct).shape[1]
     message = jax.ShapeDtypeStruct((rows // parts + 3 * size, width), jnp.bfloat16)
     return pl.pallas_call(
-        functools.partial(guest_kernel, parts),
+        functools.partial(guest_kernel, parts, len(pieces)),
         out_shape=[message] * parts,
-        in_specs=[SMEM, VMEM, VMEM, ANY, ANY, ANY, ANY],
+        in_specs=[SMEM, VMEM, VMEM] + [ANY] * len(pieces),
         out_specs=[VMEM] * parts,
         scratch_shapes=[
             pool_scratch(query),
             stats_shape(query, parts, pltpu.VMEM),
-            pltpu.SemaphoreType.DMA((4,)),
+            pltpu.SemaphoreType.DMA((len(pieces),)),
         ],
         compiler_params=params(),
         cost_estimate=cost(GUEST_US),
@@ -231,23 +260,25 @@
         stats_shape(query, parts, jax.ShapeDtypeStruct),
     ]
     return pl.pallas_call(
-        functools.partial(home_kernel, parts),
+        functools.partial(home_kernel, parts, len(pieces)),
         out_shape=results * parts,
-        in_specs=[SMEM, VMEM, VMEM, ANY, ANY, ANY, ANY],
+        in_specs=[SMEM, VMEM, VMEM] + [ANY] * len(pieces),
         out_specs=[VMEM] * (2 * parts),
-        scratch_shapes=[pool_scratch(query), pltpu.SemaphoreType.DMA((4,))],
+        scratch_shapes=[pool_scratch(query), pltpu.SemaphoreType.DMA((len(pieces),))],
         compiler_params=params(),
         cost_estimate=cost(0),
         name="home_attention",
     )(starts, bias, query, *pieces)
 
 
-def merge_call(mixed, stats, message):
+def merge_call(mixed, stats, message, parts=1):
+    rows, width = mixed.shape
+    result = jax.ShapeDtypeStruct((rows // parts, width), jnp.bfloat16)
     return pl.pallas_call(
         merge_kernel,
-        out_shape=jax.ShapeDtypeStruct(mixed.shape, jnp.bfloat16),
+        out_shape=[result] * parts,
         in_specs=[VMEM, VMEM, VMEM],
-        out_specs=VMEM,
+        out_specs=[VMEM] * parts,
         scratch_shapes=[
             pltpu.VMEM((stats.shape[1], BLOCK), jnp.float32),
             pltpu.VMEM((stats.shape[1], BLOCK), jnp.float32),
@@ -261,41 +292,98 @@
 ROW_TILE = 256
 
 
-def project(pieces, weights, part, filled=None):
-    groups, heads, _, columns = weights.shape
+def project(name, summed, gathered, heads, weights, result, rows, part=(0, 1), filled=None):
+    groups, _, depth, columns = weights.shape
     number, parts = part
-    rows = pieces[0].shape[0]
     tiles = rows // parts // ROW_TILE
 
     def row_spec(height, width):
         first = number * tiles if height == rows else 0
         return pl.BlockSpec((ROW_TILE, width), lambda i, me: (i + first, 0))
 
+    pieces = [piece for group in gathered for piece in group]
+    sums = [] if summed is None else [summed]
     others = [] if filled is None else [filled]
     myself = lax.axis_index("head").astype(jnp.int32).reshape(1)
-
-    def kernel(me_ref, w_ref, *refs):
-        x_refs = refs[: len(pieces)]
-        project_kernel(heads, me_ref, w_ref, *x_refs, refs[-1])
-
     return pl.pallas_call(
-        kernel,
-        out_shape=jax.ShapeDtypeStruct((rows, columns), jnp.bfloat16),
+        functools.partial(project_kernel, heads, summed is not None, filled is not None),
+        out_shape=jax.ShapeDtypeStruct((rows, columns), result),
         grid_spec=pltpu.PrefetchScalarGridSpec(
             num_scalar_prefetch=1,
             grid=(tiles,),
-            in_specs=[VMEM] + [row_spec(*v.shape) for v in pieces] + [ANY] * len(others),
+            in_specs=[HBM] + [row_spec(*v.shape) for v in sums + pieces] + [ANY] * len(others),
             out_specs=row_spec(rows, columns),
+            scratch_shapes=[
+                pltpu.VMEM((groups, len(heads), depth, columns), weights.dtype),
+                pltpu.SemaphoreType.DMA((groups,)),
+            ],
         ),
-        input_output_aliases={2 + len(pieces): 0} if others else {},
+        input_output_aliases={2 + len(sums) + len(pieces): 0} if others else {},
         compiler_params=params(),
         cost_estimate=cost(PROJECT_US),
-        name="project_rows",
-    )(myself, weights, *pieces, *others)
-
-
-def key_places(shard, myself, global_ids, rand_ids, local_blocks, shards):
-    half = shards // 2
+        name=name,
+    )(myself, weights, *sums, *pieces, *others)
+
+
+def first_terms_kernel(heads, me_ref, w_ref, *refs):
+    *x_refs, out_ref, held, columns, sems = refs
+    groups = w_ref.shape[0]
+    copies = []
+    for relation in range(groups):
+        copies.append(
+            pltpu.make_async_copy(
+                w_ref.at[me_ref[0] ^ relation, pl.ds(0, heads)], held.at[relation], sems.at[relation]
+            )
+        )
+    for relation in range(groups):
+        for head in range(heads):
+            place = relation * heads + head
+            copies.append(
+                pltpu.make_async_copy(
+                    x_refs[head * groups + relation],
+                    columns.at[:, pl.ds(place * HEAD_DIM, HEAD_DIM)],
+                    sems.at[groups + place],
+                )
+            )
+    for copy in copies:
+        copy.start()
+    for copy in copies:
+        copy.wait()
+    weight = held[...].reshape(-1, held.shape[-1])
+
+    def step(i, _):
+        rows = pl.ds(pl.multiple_of(i * ROW_TILE, ROW_TILE), ROW_TILE)
+        out_ref[rows, :] = jnp.dot(
+            columns[rows, :], weight, preferred_element_type=jnp.float32
+        )
+        return 0
+
+    lax.fori_loop(0, out_ref.shape[0] // ROW_TILE, step, 0)
+
+
+def first_terms(gathered, weights):
+    groups, _, depth, width = weights.shape
+    heads = len(gathered)
+    pieces = [piece for group in gathered for piece in group]
+    rows = pieces[0].shape[0]
+    myself = lax.axis_index("head").astype(jnp.int32).reshape(1)
+    return pl.pallas_call(
+        functools.partial(first_terms_kernel, heads),
+        out_shape=jax.ShapeDtypeStruct((rows, width), jnp.float32),
+        in_specs=[SMEM] + [HBM] * (1 + len(pieces)),
+        out_specs=VMEM,
+        scratch_shapes=[
+            pltpu.VMEM((groups, heads, depth, width), weights.dtype),
+            pltpu.VMEM((rows, heads * groups * HEAD_DIM), jnp.bfloat16),
+            pltpu.SemaphoreType.DMA((groups + len(pieces),)),
+        ],
+        compiler_params=params(),
+        cost_estimate=cost(0),
+        name="first_terms",
+    )(myself, weights, *pieces)
+
+
+def key_list(shard, global_ids, rand_ids, local_blocks, shards):
     total_blocks = local_blocks * shards
     block_ids = shard * local_blocks + jnp.arange(local_blocks, dtype=jnp.int32)
     near = block_ids[:, None] + jnp.arange(-1, 2, dtype=jnp.int32)[None, :]
@@ -303,15 +391,58 @@
     listed = lax.dynamic_slice_in_dim(rand_ids, shard * local_blocks, local_blocks, 0)
     glob = jnp.broadcast_to(global_ids[None, :], (local_blocks, NGLOBAL))
     ids = jnp.concatenate([jnp.clip(near, 0, total_blocks - 1), glob, listed], axis=1)
+    inside = jnp.concatenate(
+        [inside, jnp.ones((local_blocks, NGLOBAL + NRANDOM), jnp.bool_)], axis=1
+    )
+    return ids, inside
+
+
+def guests_first(guests, source, global_ids, rand_ids, local_blocks, shards):
+    ids, inside = key_list(guests, global_ids, rand_ids, local_blocks, shards)
+    order = jnp.arange(local_blocks, dtype=jnp.int32)
+    blocks = source * local_blocks + order
+    hits = (ids[None] == blocks[:, None, None]) & inside[None]
+    listed = jnp.max(hits.astype(jnp.int32), axis=(1, 2))
+    earlier = (order[None, :] < order[:, None]).astype(jnp.int32)
+    among = jnp.sum(earlier * listed[None, :], axis=1)
+    return jnp.where(listed > 0, among, jnp.sum(listed) + order - among)
+
+
+def key_places(shard, myself, global_ids, rand_ids, local_blocks, shards, diagonal=None):
+    half = shards // 2
+    ids, inside = key_list(shard, global_ids, rand_ids, local_blocks, shards)
     owner = ids // local_blocks
-    here = (owner // half) == (myself // half)
-    here = here & jnp.concatenate(
-        [inside, jnp.ones((local_blocks, NGLOBAL + NRANDOM), jnp.bool_)], axis=1
-    )
+    here = ((owner // half) == (myself // half)) & inside
     relative = (owner ^ myself) & (half - 1)
-    starts = jnp.where(here, (relative * local_blocks + ids % local_blocks) * BLOCK, 0)
+    block = ids % local_blocks
+    if diagonal is not None:
+        order = jnp.arange(local_blocks, dtype=jnp.int32)
+        moved = jnp.sum(jnp.where(block[..., None] == order, diagonal, 0), axis=-1)
+        block = jnp.where(relative == half - 1, moved, block)
+    starts = jnp.where(here, (relative * local_blocks + block) * BLOCK, 0)
     bias = jnp.repeat(jnp.where(here, 0.0, MASKED).astype(jnp.float32), BLOCK, axis=1)
     return starts.reshape(-1).astype(jnp.int32), bias
+
+
+def split_kernel(order_ref, pair_ref, first_ref, rest_ref):
+    blocks = first_ref.shape[1] // BLOCK
+    for n in range(pair_ref.shape[1] // BLOCK):
+        source = pl.ds(pl.multiple_of(order_ref[n] * BLOCK, BLOCK), BLOCK)
+        target = first_ref if n < blocks else rest_ref
+        target[:, pl.ds((n % blocks) * BLOCK, BLOCK), :] = pair_ref[:, source, :]
+
+
+def split_call(order, pair):
+    half = jax.ShapeDtypeStruct((2, pair.shape[1] // 2, pair.shape[2]), pair.dtype)
+    return pl.pallas_call(
+        split_kernel,
+        out_shape=[half, half],
+        in_specs=[SMEM, VMEM],
+        out_specs=[VMEM, VMEM],
+        compiler_params=params(),
+        cost_estimate=cost(0),
+        name="guests_first",
+    )(order, pair)
 
 
 def swap(value, distance, shards):
@@ -356,10 +487,20 @@
     def across(value):
         return swap(value, opposite, shards)
 
-    home = key_places(myself, myself, global_ids, rand_ids, local_blocks, shards)
-    guest = key_places(myself ^ opposite, myself, global_ids, rand_ids, local_blocks, shards)
+    lists = (global_ids, rand_ids, local_blocks, shards)
+    mine = guests_first(myself ^ opposite, myself ^ 3, *lists)
+    theirs = guests_first(myself ^ opposite ^ 1, myself ^ 2, *lists)
+    count = jnp.arange(local_blocks, dtype=jnp.int32)
+    order = jnp.sum(jnp.where(theirs[None, :] == count[:, None], count[None, :], 0), axis=1)
+    home = key_places(myself, myself, *lists)
+    guest = key_places(myself ^ opposite, myself, *lists)
+    last_home = key_places(myself, myself, *lists, mine)
+    last_guest = key_places(myself ^ opposite, myself, *lists, mine)
+    home, guest = (*home, *last_home, order), (*guest, *last_guest)
     weights = out_weight.reshape(groups, heads_here, HEAD_DIM, out_weight.shape[1])
-    k0, k1, k2, k3 = [column(keys_values, h) for h in range(heads_here)]
+    k0 = column(keys_values, 0)
+    others = after(keys_values, k0)
+    k1, k2, k3 = [column(others, h) for h in range(1, heads_here)]
     q0, q1, q2, q3 = [column(queries, h) for h in range(heads_here)]
 
     y0, z0 = over_y(k0), over_z(k0)
@@ -367,46 +508,50 @@
 
     d0, y1, z1, v0, v1 = over_y(z0), over_y(k1_), over_z(k1_), across(v0), across(v1)
     p0 = (k0, y0, z0, d0)
-    (s0,) = guest_call(*guest, v0, p0)
+    (s0,) = guest_call(*guest[:2], v0, p0)
     s0, y1, z1, v1, k2_, v2 = together(s0, y1, z1, v1, k2, q2)
 
     d1, y2, z2, v2, g0 = over_y(z1), over_y(k2_), over_z(k2_), across(v2), across(s0)
-    m0 = home_call(*home, after(q0, s0), p0)
+    m0 = home_call(*home[:2], after(q0, s0), p0)
     p1 = (k1, y1, z1, d1)
-    (s1,) = guest_call(*guest, after(v1, m0[1], v2), p1)
+    (s1,) = guest_call(*guest[:2], after(v1, m0[1], v2), p1)
     s1, y2, z2, v2, g0, k3_, v3 = together(s1, y2, z2, v2, g0, k3, q3)
 
     d2, y3, z3, v3, g1 = over_y(z2), over_y(k3_), over_z(k3_), across(v3), across(s1)
-    m1 = home_call(*home, after(q1, s1), p1)
-    a0 = merge_call(*m0, after(g0, m1[1]))
+    m1 = home_call(*home[:2], after(q1, s1), p1)
+    (a0,) = merge_call(*m0, after(g0, m1[1]))
     a0x, a0c = hop(a0, 2, groups), hop(a0, 1, groups)
     p2 = (k2, y2, z2, d2)
-    (s2,) = guest_call(*guest, after(v2, m1[1], v3), p2)
+    (s2,) = guest_call(*guest[:2], after(v2, m1[1], v3), p2)
     s2, y3, z3, v3, g1, a0x, a0c = together(s2, y3, z3, v3, g1, a0x, a0c)
 
-    d3, g2 = over_y(z3), across(s2)
-    m2 = home_call(*home, after(q2, s2), p2)
-    a1 = merge_call(*m1, after(g1, m2[1]))
+    first, rest = split_call(home[4], z3)
+    d3, d3_, g2 = over_y(first), over_y(rest), across(s2)
+    m2 = home_call(*home[:2], after(q2, s2), p2)
+    (a1,) = merge_call(*m1, after(g1, m2[1]))
     a1x, a1c, a0d = hop(a1, 2, groups), hop(a1, 1, groups), hop(a0x, 1, groups)
-    p3 = (k3, y3, z3, d3)
-    s3a, s3b = guest_call(*guest, after(v3, a1), p3, 2)
-    s3a, s3b, g2, a1x, a1c, a0d = together(s3a, s3b, g2, a1x, a1c, a0d)
-
-    g3a, g3b = across(s3a), across(s3b)
-    m3 = home_call(*home, after(q3, s3a), p3, 2)
-    a2 = merge_call(*m2, after(g2, s3a))
-    a1d = hop(a1x, 1, groups)
+    (s3,) = guest_call(*guest[2:4], after(v3, a1), (k3, y3, z3, d3))
+    g3 = across(after(s3, g2))
+    m3 = home_call(*home[2:4], after(q3, s3), (k3, y3, z3, d3, d3_))
+    (a2,) = merge_call(*m2, after(g2, m3[1]))
+    a1d = hop(after(a1x, s3), 1, groups)
     a2x, a2c = hop(a2, 2, groups), hop(a2, 1, groups)
-    a2d = hop(a2x, 1, groups)
-    whole = (a0, a0c, a0x, a0d, a1, a1c, a1x, a1d, a2, a2c, a2x, a2d)
-    a3a = merge_call(*m3[:2], after(g3a, a2))
+    early = ((a0, a0c, a0x, a0d), (a1, a1c, a1x, a1d))
+    summed = first_terms(early, after(weights, m3[1]))
+
+    a3a, a3b = merge_call(*m3, after(g3, summed), 2)
     a3ax, a3ac = hop(a3a, 2, groups), hop(a3a, 1, groups)
-    a3b = merge_call(*m3[2:], after(g3b, a3a))
-    a3bx, a3bc = hop(a3b, 2, groups), hop(a3b, 1, groups)
+    a3bx, a3bc = hop(after(a3b, a3a), 2, groups), hop(a3b, 1, groups)
+    a2d = hop(after(a2x, a3b), 1, groups)
+    a2 = (a2, a2c, a2x, a2d)
     a3ad = hop(a3ax, 1, groups)
-    upper = project((*whole, after(a3a, a3b), a3ac, a3ax, a3ad), weights, (0, 2))
+    late = (a2, (a3a, a3ac, a3ax, a3ad))
+    upper = project("last_terms", summed, late, (2, 3), weights, jnp.bfloat16, rows, (0, 2))
     a3bd = hop(after(a3bx, upper), 1, groups)
-    return project((*whole, a3b, a3bc, a3bx, a3bd), weights, (1, 2), upper)
+    late = (a2, (a3b, a3bc, a3bx, a3bd))
+    return project(
+        "last_terms", summed, late, (2, 3), weights, jnp.bfloat16, rows, (1, 2), upper
+    )
 
 
 def padded_2(block, sides, width):

time: 202 us -> 196 us (0.970)
  waiting for transfers between devices: 112 us -> 99.7 us
  other arithmetic: 0.34 us -> 5.52 us
  local copies, waits for them, and re-layouts: 12.3 us -> 8.46 us
  Pallas kernels: 41.7 us -> 45.4 us
    ppermute x21, waiting for transfers between devices: 101 us -> 85.2 us  [swap(): lax.ppermute(value, 'seq', [(i, i ^ distance) for i in range(shards)])]
    unnamed x26 -> x6, local copies, waits for them, and re-layouts: 7.71 us -> 2.2 us
    ppermute x15, waiting for transfers between devices: 10.3 us -> 14.5 us  [hop(): lax.ppermute(value, 'head', [(i, i ^ distance) for i in range(groups)])]
    pallas_call x15 -> x16, Pallas kernels: 41.7 us -> 45.4 us  [the longest x4 12.9 us: guest_call(): pl.pallas_call(functools.partial(guest_kernel, parts, len(pieces)), out_s...]
    reduce_sum x0 -> x6, other arithmetic: none -> 2.57 us  [the longest x2 1.28 us: guests_first(): return jnp.where(listed > 0, among, jnp.sum(listed) + order - among)]
    ppermute x15, starting transfers between devices: 7.05 us -> 9.17 us  [hop(): lax.ppermute(value, 'head', [(i, i ^ distance) for i in range(groups)])]
  transfers between devices with their start and end apart: 36 -> 36, of which waited for: 14 -> 14; matrix products, arithmetic and copies ran while one was open for 1% -> 5% of each run, Pallas kernels for 17% -> 21%
where the time goes in v4:
time: 196 us
  waiting for transfers between devices  99.7 us (51%)
  Pallas kernels  45.4 us (23%)
  starting transfers between devices  36 us (18%)
  local copies, waits for them, and re-layouts  8.46 us (4%)
  other arithmetic  5.52 us (3%)
    ppermute x21, waiting for transfers between devices, swap(): lax.ppermute(value, 'seq', [(i, i ^ distance) for i in range(shards)])  85.2 us
    ppermute x21, starting transfers between devices, swap(): lax.ppermute(value, 'seq', [(i, i ^ distance) for i in range(shards)])  26.9 us
    ppermute x15, waiting for transfers between devices, hop(): lax.ppermute(value, 'head', [(i, i ^ distance) for i in range(groups)])  14.5 us
    pallas_call x4, Pallas kernels, guest_call(): pl.pallas_call(functools.partial(guest_kernel, parts, len(pieces)), out_s...  12.9 us
    pallas_call x4, Pallas kernels, home_call(): pl.pallas_call(functools.partial(home_kernel, parts, len(pieces)), out_sh...  12.8 us
    ppermute x15, starting transfers between devices, hop(): lax.ppermute(value, 'head', [(i, i ^ distance) for i in range(groups)])  9.17 us
    pallas_call x2, Pallas kernels, project(): pl.pallas_call(functools.partial(project_kernel, heads, summed is not Non...  8.46 us
    pallas_call x1, Pallas kernels, first_terms(): pl.pallas_call(functools.partial(first_terms_kernel, heads), out_shape=ja...  6.77 us
  transfers between devices with their start and end apart: 36, of which 14 were waited for; matrix products, arithmetic and copies ran while one was open for 5% of the time, Pallas kernels for 21%

profile of v4, /device:TPU:0, one launch (start us, length us, event | category | flops | bytes accessed | tf_op | source)
XLA Modules:
  0.0 195.6 jit_solution(3907179119724593661)
XLA Ops:
  0.0 1.2 slice.24.refs_0_
  1.2 3.1 %collective-permute-start.1 = (bf16[2,1536,128]{2,1,0:T(8,128)(2,1)S(1)}, bf16[2,1536,128]{2,1,0:T(8,128)(2,1)S(1)}, u32[]{:S(2)}, u32[]{:S(2)}) collective-permute-start(bf16[2,1536,128]{2,1,0:T(8,128)(2,1)S(1)} %slice.24.refs_0_), channel_id=1, source_target_pairs={{0,8},{4,12},{8,0},{12,4},{16,24},{20,28},{24,16},{28,20},{1,9},{5... | collective-permute-start | bytes 2359304 | tf_op jit(solution)/shard_map/ppermute | solution.py:449
  4.3 1.5 collective-permute-start
  13.7 1.6 fusion.14
  16.5 5.3 %collective-permute-done.1.refs_2_ = bf16[2,1536,128]{2,1,0:T(8,128)(2,1)S(1)} collective-permute-done((bf16[2,1536,128]{2,1,0:T(8,128)(2,1)S(1)}, bf16[2,1536,128]{2,1,0:T(8,128)(2,1)S(1)}, u32[]{:S(2)}, u32[]{:S(2)}) %collective-permute-start.1) | collective-permute-done | bytes 786464 | tf_op jit(solution)/shard_map/ppermute | solution.py:449
  21.8 1.5 collective-permute-done.refs_1_
  23.3 1.5 collective-permute-start.3
  25.7 2.7 %collective-permute-start.2 = (bf16[1536,128]{1,0:T(8,128)(2,1)S(1)}, bf16[1536,128]{1,0:T(8,128)(2,1)S(1)}, u32[]{:S(2)}, u32[]{:S(2)}) collective-permute-start(bf16[1536,128]{1,0:T(8,128)(2,1)S(1)} %get-tuple-element.85.q_ref), channel_id=1, source_target_pairs={{0,16},{4,20},{8,24},{12,28},{16,0},{20,4},{24,8},{28,12},{1,17},{... | collective-permute-start | bytes 1179656 | tf_op jit(solution)/shard_map/ppermute | solution.py:449
  28.6 23.1 %collective-permute-done.2.q_ref = bf16[1536,128]{1,0:T(8,128)(2,1)S(1)} collective-permute-done((bf16[1536,128]{1,0:T(8,128)(2,1)S(1)}, bf16[1536,128]{1,0:T(8,128)(2,1)S(1)}, u32[]{:S(2)}, u32[]{:S(2)}) %collective-permute-start.2) | collective-permute-done | bytes 393248 | tf_op jit(solution)/shard_map/ppermute | solution.py:449
  51.7 3.4 %guest_attention.4 = bf16[1632,128]{1,0:T(8,128)(2,1)S(1)} custom-call(s32[192]{0:T(256)S(1)} %reshape.153.starts_ref, f32[24,512]{1,0:T(8,128)S(1)} %reshape.154.bias_ref, bf16[1536,128]{1,0:T(8,128)(2,1)S(1)} %collective-permute-done.2.q_ref, bf16[2,1536,128]{2,1,0:T(8,128)(2,1)S(1)} %slice.24.refs_0_, ...), custom_call_target="tpu_custom_call" | custom-call | flops 115000000 | tf_op jit(solution)/shard_map/guest_attention/pallas_call | solution.py:240
  55.1 2.5 %collective-permute-done.6.q_ref = bf16[1536,128]{1,0:T(8,128)(2,1)S(1)} collective-permute-done((bf16[1536,128]{1,0:T(8,128)(2,1)S(1)}, bf16[1536,128]{1,0:T(8,128)(2,1)S(1)}, u32[]{:S(2)}, u32[]{:S(2)}) %collective-permute-start.6) | collective-permute-done | bytes 393248 | tf_op jit(solution)/shard_map/ppermute | solution.py:449
  57.6 1.8 collective-permute-done.5.refs_2_
  59.5 3.0 %collective-permute-start.8 = (bf16[2,1536,128]{2,1,0:T(8,128)(2,1)S(1)}, bf16[2,1536,128]{2,1,0:T(8,128)(2,1)S(1)}, u32[]{:S(2)}, u32[]{:S(2)}) collective-permute-start(bf16[2,1536,128]{2,1,0:T(8,128)(2,1)S(1)} %collective-permute-done.5.refs_2_), channel_id=1, source_target_pairs={{0,4},{4,0},{8,12},{12,8},{16,20},{20,16},{24,28},{28,24},{1,5},{5... | collective-permute-start | bytes 2359304 | tf_op jit(solution)/shard_map/ppermute | solution.py:449
  63.1 1.0 collective-permute-start.9
  64.1 2.9 %collective-permute-start.11 = (bf16[1632,128]{1,0:T(8,128)(2,1)S(1)}, bf16[1632,128]{1,0:T(8,128)(2,1)S(1)}, u32[]{:S(2)}, u32[]{:S(2)}) collective-permute-start(bf16[1632,128]{1,0:T(8,128)(2,1)S(1)} %guest_attention.4), channel_id=1, source_target_pairs={{0,16},{4,20},{8,24},{12,28},{16,0},{20,4},{24,8},{28,12},{1,17},{... | collective-permute-start | bytes 1253384 | tf_op jit(solution)/shard_map/ppermute | solution.py:449
  67.0 3.2 %home_attention.4 = (f32[1536,128]{1,0:T(8,128)S(1)}, f32[1,32,128]{2,1,0:T(8,128)S(1)}) custom-call(s32[192]{0:T(256)S(1)} %reshape.150.starts_ref, f32[24,512]{1,0:T(8,128)S(1)} %reshape.151.bias_ref, bf16[1536,128]{1,0:T(8,128)(2,1)S(1)} %get-tuple-element.85.q_ref, bf16[2,1536,128]{2,1,0:T(8,128)(2,1)S(1)} %slice.24.refs_0_, ...), custom_call_target="tpu_custom_call" | custom-call | tf_op jit(solution)/shard_map/home_attention/pallas_call | solution.py:262
  70.2 28.8 %collective-permute-done.7.q_ref = bf16[1536,128]{1,0:T(8,128)(2,1)S(1)} collective-permute-done((bf16[1536,128]{1,0:T(8,128)(2,1)S(1)}, bf16[1536,128]{1,0:T(8,128)(2,1)S(1)}, u32[]{:S(2)}, u32[]{:S(2)}) %collective-permute-start.7) | collective-permute-done | bytes 393248 | tf_op jit(solution)/shard_map/ppermute | solution.py:449
  99.0 3.2 %guest_attention.5 = bf16[1632,128]{1,0:T(8,128)(2,1)S(1)} custom-call(s32[192]{0:T(256)S(1)} %reshape.153.starts_ref, f32[24,512]{1,0:T(8,128)S(1)} %reshape.154.bias_ref, bf16[1536,128]{1,0:T(8,128)(2,1)S(1)} %collective-permute-done.6.q_ref, bf16[2,1536,128]{2,1,0:T(8,128)(2,1)S(1)} %get-tuple-element.79.refs_0_, ...), custom_call_target="tpu_custom_call" | custom-call | flops 115000000 | tf_op jit(solution)/shard_map/guest_attention/pallas_call | solution.py:240
  102.2 2.1 %collective-permute-start.13 = (bf16[2,1536,128]{2,1,0:T(8,128)(2,1)S(1)}, bf16[2,1536,128]{2,1,0:T(8,128)(2,1)S(1)}, u32[]{:S(2)}, u32[]{:S(2)}) collective-permute-start(bf16[2,1536,128]{2,1,0:T(8,128)(2,1)S(1)} %collective-permute-done.10.refs_2_), channel_id=1, source_target_pairs={{0,4},{4,0},{8,12},{12,8},{16,20},{20,16},{24,28},{28,24},{1,5},{5... | collective-permute-start | bytes 2359304 | tf_op jit(solution)/shard_map/ppermute | solution.py:449
  104.3 2.3 %collective-permute-start.15 = (bf16[2,1536,128]{2,1,0:T(8,128)(2,1)S(1)}, bf16[2,1536,128]{2,1,0:T(8,128)(2,1)S(1)}, u32[]{:S(2)}, u32[]{:S(2)}) collective-permute-start(bf16[2,1536,128]{2,1,0:T(8,128)(2,1)S(1)} %get-tuple-element.100.refs_0_), channel_id=1, source_target_pairs={{0,8},{4,12},{8,0},{12,4},{16,24},{20,28},{24,16},{28,20},{1,9},{5... | collective-permute-start | bytes 2359304 | tf_op jit(solution)/shard_map/ppermute | solution.py:449
  107.3 3.2 %home_attention.5 = (f32[1536,128]{1,0:T(8,128)S(1)}, f32[1,32,128]{2,1,0:T(8,128)S(1)}) custom-call(s32[192]{0:T(256)S(1)} %reshape.150.starts_ref, f32[24,512]{1,0:T(8,128)S(1)} %reshape.151.bias_ref, bf16[1536,128]{1,0:T(8,128)(2,1)S(1)} %get-tuple-element.94.q_ref, bf16[2,1536,128]{2,1,0:T(8,128)(2,1)S(1)} %get-tuple-element.79.refs_0_, ...), custom_call_target="tpu_custom_call" | custom-call | tf_op jit(solution)/shard_map/home_attention/pallas_call | solution.py:262
  110.4 1.0 merge_halves.4.refs_0_
  111.4 10.8 %collective-permute-done.12.q_ref = bf16[1536,128]{1,0:T(8,128)(2,1)S(1)} collective-permute-done((bf16[1536,128]{1,0:T(8,128)(2,1)S(1)}, bf16[1536,128]{1,0:T(8,128)(2,1)S(1)}, u32[]{:S(2)}, u32[]{:S(2)}) %collective-permute-start.12) | collective-permute-done | bytes 393248 | tf_op jit(solution)/shard_map/ppermute | solution.py:449
  122.2 1.5 collective-permute-start.17
  123.7 3.2 %guest_attention.6 = bf16[1632,128]{1,0:T(8,128)(2,1)S(1)} custom-call(s32[192]{0:T(256)S(1)} %reshape.153.starts_ref, f32[24,512]{1,0:T(8,128)S(1)} %reshape.154.bias_ref, bf16[1536,128]{1,0:T(8,128)(2,1)S(1)} %collective-permute-done.7.q_ref, bf16[2,1536,128]{2,1,0:T(8,128)(2,1)S(1)} %get-tuple-element.91.refs_0_, ...), custom_call_target="tpu_custom_call" | custom-call | flops 115000000 | tf_op jit(solution)/shard_map/guest_attention/pallas_call | solution.py:240
  126.9 7.0 %collective-permute-done.17.refs_2_ = bf16[1536,128]{1,0:T(8,128)(2,1)} collective-permute-done((bf16[1536,128]{1,0:T(8,128)(2,1)S(1)}, bf16[1536,128]{1,0:T(8,128)(2,1)}, u32[]{:S(2)}, u32[]{:S(2)}) %collective-permute-start.17) | collective-permute-done | bytes 393248 | tf_op jit(solution)/shard_map/ppermute | solution.py:457
  133.8 2.2 %collective-permute-start.25 = (bf16[1632,128]{1,0:T(8,128)(2,1)S(1)}, bf16[1632,128]{1,0:T(8,128)(2,1)S(1)}, u32[]{:S(2)}, u32[]{:S(2)}) collective-permute-start(bf16[1632,128]{1,0:T(8,128)(2,1)S(1)} %guest_attention.6), channel_id=1, source_target_pairs={{0,16},{4,20},{8,24},{12,28},{16,0},{20,4},{24,8},{28,12},{1,17},{... | collective-permute-start | bytes 1253384 | tf_op jit(solution)/shard_map/ppermute | solution.py:449
  136.7 1.3 collective-permute-start.19
  138.0 3.2 %home_attention.6 = (f32[1536,128]{1,0:T(8,128)S(1)}, f32[1,32,128]{2,1,0:T(8,128)S(1)}) custom-call(s32[192]{0:T(256)S(1)} %reshape.150.starts_ref, f32[24,512]{1,0:T(8,128)S(1)} %reshape.151.bias_ref, bf16[1536,128]{1,0:T(8,128)(2,1)S(1)} %get-tuple-element.108.q_ref, bf16[2,1536,128]{2,1,0:T(8,128)(2,1)S(1)} %get-tuple-element.91.refs_0_, ...), custom_call_target="tpu_custom_call" | custom-call | tf_op jit(solution)/shard_map/home_attention/pallas_call | solution.py:262
  141.1 1.0 merge_halves.5.refs_4_
  142.1 1.6 collective-permute-start.23
  144.4 3.8 %collective-permute-done.19.refs_3_ = bf16[2,768,128]{2,1,0:T(8,128)(2,1)S(1)} collective-permute-done((bf16[2,768,128]{2,1,0:T(8,128)(2,1)S(1)}, bf16[2,768,128]{2,1,0:T(8,128)(2,1)S(1)}, u32[]{:S(2)}, u32[]{:S(2)}) %collective-permute-start.19) | collective-permute-done | bytes 393248 | tf_op jit(solution)/shard_map/ppermute | solution.py:449
  148.3 3.2 %guest_attention.7 = bf16[1632,128]{1,0:T(8,128)(2,1)S(1)} custom-call(s32[192]{0:T(256)S(1)} %reshape.155.starts_ref, f32[24,512]{1,0:T(8,128)S(1)} %reshape.154.bias_ref, bf16[1536,128]{1,0:T(8,128)(2,1)S(1)} %collective-permute-done.12.q_ref, bf16[2,1536,128]{2,1,0:T(8,128)(2,1)S(1)} %get-tuple-element.100.refs_0_, ...), custom_call_target="tpu_custom_call" | custom-call | flops 115000000 | tf_op jit(solution)/shard_map/guest_attention/pallas_call | solution.py:240
  151.5 1.9 collective-permute-done.25.message_ref
  153.9 3.3 %home_attention.7 = (f32[1536,128]{1,0:T(8,128)S(1)}, f32[1,32,128]{2,1,0:T(8,128)S(1)}) custom-call(s32[192]{0:T(256)S(1)} %reshape.152.starts_ref, f32[24,512]{1,0:T(8,128)S(1)} %reshape.151.bias_ref, bf16[1536,128]{1,0:T(8,128)(2,1)S(1)} %get-tuple-element.116.q_ref, bf16[2,1536,128]{2,1,0:T(8,128)(2,1)S(1)} %get-tuple-element.100.refs_0_, ...), custom_call_target="tpu_custom_call" | custom-call | tf_op jit(solution)/shard_map/home_attention/pallas_call | solution.py:262
  157.2 1.0 merge_halves.6.refs_1_
  158.2 1.5 collective-permute-start.27
  160.0 2.2 %copy-done = bf16[2048,1024]{1,0:T(8,128)(2,1)S(1)} copy-done((bf16[2048,1024]{1,0:T(8,128)(2,1)S(1)}, bf16[2048,1024]{1,0:T(8,128)(2,1)}, u32[]{:S(2)}) %copy-start) | copy-done | bytes 4194328
  162.1 6.8 %first_terms.1.refs_0_ = f32[1536,1024]{1,0:T(8,128)S(1)} custom-call(s32[1]{0:T(128)} %bitcast.me_ref, bf16[4,4,128,1024]{3,2,1,0:T(8,128)(2,1)S(1)} %bitcast.2, bf16[1536,128]{1,0:T(8,128)(2,1)S(1)} %merge_halves.4.refs_0_, bf16[1536,128]{1,0:T(8,128)(2,1)S(1)} %collective-permute-done.18.refs_1_, bf16[1536,128]{1,0:T(8,128)(2,1)} %collective-permute-done.17.refs_2_, ...), custom_call_target="tpu_custom_call" | custom-call | tf_op jit(solution)/shard_map/first_terms/pallas_call | solution.py:370
  168.9 5.7 %collective-permute-done.28.message_ref = bf16[1632,128]{1,0:T(8,128)(2,1)S(1)} collective-permute-done((bf16[1632,128]{1,0:T(8,128)(2,1)S(1)}, bf16[1632,128]{1,0:T(8,128)(2,1)S(1)}, u32[]{:S(2)}, u32[]{:S(2)}) %collective-permute-start.28) | collective-permute-done | bytes 417824 | tf_op jit(solution)/shard_map/ppermute | solution.py:449
  174.6 1.0 merge_halves.7
  175.6 1.5 collective-permute-start.33
  177.6 4.9 %collective-permute-done.33.refs_7_ = bf16[768,128]{1,0:T(8,128)(2,1)S(1)} collective-permute-done((bf16[768,128]{1,0:T(8,128)(2,1)S(1)}, bf16[768,128]{1,0:T(8,128)(2,1)S(1)}, u32[]{:S(2)}, u32[]{:S(2)}) %collective-permute-start.33) | collective-permute-done | bytes 196640 | tf_op jit(solution)/shard_map/ppermute | solution.py:457
  183.0 1.4 collective-permute-start.31
  184.4 4.2 %last_terms.2.refs_9_ = bf16[1536,1024]{1,0:T(8,128)(2,1)} custom-call(s32[1]{0:T(128)} %bitcast.me_ref, bf16[4,4,128,1024]{3,2,1,0:T(8,128)(2,1)S(1)} %bitcast.3, f32[1536,1024]{1,0:T(8,128)S(1)} %first_terms.1.refs_0_, bf16[1536,128]{1,0:T(8,128)(2,1)S(1)} %merge_halves.6.refs_1_, bf16[1536,128]{1,0:T(8,128)(2,1)S(1)} %collective-permute-done.26.refs_2_, ...), custom_call_target="tpu_custom_call" | custom-call | flops 4600000000 | tf_op jit(solution)/shard_map/last_terms/pallas_call | solution.py:308
  188.7 1.1 collective-permute-done.31.refs_7_
  189.8 1.4 collective-permute-done.35.refs_8_
  191.2 4.2 %last_terms.3 = bf16[1536,1024]{1,0:T(8,128)(2,1)} custom-call(s32[1]{0:T(128)} %bitcast.me_ref, bf16[4,4,128,1024]{3,2,1,0:T(8,128)(2,1)S(1)} %bitcast.4, f32[1536,1024]{1,0:T(8,128)S(1)} %first_terms.1.refs_0_, bf16[1536,128]{1,0:T(8,128)(2,1)S(1)} %merge_halves.6.refs_1_, ...), custom_call_target="tpu_custom_call", output_to_operand_aliasing={{}: (11, {})} | custom-call | flops 4600000000 | tf_op jit(solution)/shard_map/last_terms/pallas_call | solution.py:308
  (95 shorter events, 14.6 us)
Async XLA Ops:
  1.2 20.6 %collective-permute-start.1 = (bf16[2,1536,128]{2,1,0:T(8,128)(2,1)S(1)}, bf16[2,1536,128]{2,1,0:T(8,128)(2,1)S(1)}, u32[]{:S(2)}, u32[]{:S(2)}) collective-permute-start(bf16[2,1536,128]{2,1,0:T(8,128)(2,1)S(1)} %slice.24.refs_0_), channel_id=1, source_target_pairs={{0,8},{4,12},{8,0},{12,4},{16,24},{20,28},{24,16},{28,20},{1,9},{5... | collective-permute-start | bytes 2359304 | tf_op jit(solution)/shard_map/ppermute | solution.py:449
  4.3 19.0 %collective-permute-start = (bf16[2,1536,128]{2,1,0:T(8,128)(2,1)S(1)}, bf16[2,1536,128]{2,1,0:T(8,128)(2,1)S(1)}, u32[]{:S(2)}, u32[]{:S(2)}) collective-permute-start(bf16[2,1536,128]{2,1,0:T(8,128)(2,1)S(1)} %slice.24.refs_0_), channel_id=1, source_target_pairs={{0,4},{4,0},{8,12},{12,8},{16,20},{20,16},{24,28},{28,24},{1,5},{5... | collective-permute-start | bytes 2359304 | tf_op jit(solution)/shard_map/ppermute | solution.py:449
  13.7 2.4 %copy-start.2 = (bf16[2,1536,512]{2,1,0:T(8,128)(2,1)S(1)}, bf16[2,1536,512]{2,1,0:T(8,128)(2,1)}, u32[]{:S(2)}) copy-start(bf16[2,1536,512]{2,1,0:T(8,128)(2,1)} %param.6) | copy-start | bytes 9437188
  23.3 28.4 %collective-permute-start.3 = (bf16[2,1536,128]{2,1,0:T(8,128)(2,1)S(1)}, bf16[2,1536,128]{2,1,0:T(8,128)(2,1)S(1)}, u32[]{:S(2)}, u32[]{:S(2)}) collective-permute-start(bf16[2,1536,128]{2,1,0:T(8,128)(2,1)S(1)} %collective-permute-done.1.refs_2_), channel_id=1, source_target_pairs={{0,4},{4,0},{8,12},{12,8},{16,20},{20,16},{24,28},{28,24},{1,5},{5... | collective-permute-start | bytes 2359304 | tf_op jit(solution)/shard_map/ppermute | solution.py:449
  24.8 34.7 %collective-permute-start.5 = (bf16[2,1536,128]{2,1,0:T(8,128)(2,1)S(1)}, bf16[2,1536,128]{2,1,0:T(8,128)(2,1)S(1)}, u32[]{:S(2)}, u32[]{:S(2)}) collective-permute-start(bf16[2,1536,128]{2,1,0:T(8,128)(2,1)S(1)} %get-tuple-element.79.refs_0_), channel_id=1, source_target_pairs={{0,8},{4,12},{8,0},{12,4},{16,24},{20,28},{24,16},{28,20},{1,9},{5... | collective-permute-start | bytes 2359304 | tf_op jit(solution)/shard_map/ppermute | solution.py:449
  25.2 34.2 %collective-permute-start.4 = (bf16[2,1536,128]{2,1,0:T(8,128)(2,1)S(1)}, bf16[2,1536,128]{2,1,0:T(8,128)(2,1)S(1)}, u32[]{:S(2)}, u32[]{:S(2)}) collective-permute-start(bf16[2,1536,128]{2,1,0:T(8,128)(2,1)S(1)} %get-tuple-element.79.refs_0_), channel_id=1, source_target_pairs={{0,4},{4,0},{8,12},{12,8},{16,20},{20,16},{24,28},{28,24},{1,5},{5... | collective-permute-start | bytes 2359304 | tf_op jit(solution)/shard_map/ppermute | solution.py:449
  25.7 26.1 %collective-permute-start.2 = (bf16[1536,128]{1,0:T(8,128)(2,1)S(1)}, bf16[1536,128]{1,0:T(8,128)(2,1)S(1)}, u32[]{:S(2)}, u32[]{:S(2)}) collective-permute-start(bf16[1536,128]{1,0:T(8,128)(2,1)S(1)} %get-tuple-element.85.q_ref), channel_id=1, source_target_pairs={{0,16},{4,20},{8,24},{12,28},{16,0},{20,4},{24,8},{28,12},{1,17},{... | collective-permute-start | bytes 1179656 | tf_op jit(solution)/shard_map/ppermute | solution.py:449
  28.3 29.3 %collective-permute-start.6 = (bf16[1536,128]{1,0:T(8,128)(2,1)S(1)}, bf16[1536,128]{1,0:T(8,128)(2,1)S(1)}, u32[]{:S(2)}, u32[]{:S(2)}) collective-permute-start(bf16[1536,128]{1,0:T(8,128)(2,1)S(1)} %get-tuple-element.94.q_ref), channel_id=1, source_target_pairs={{0,16},{4,20},{8,24},{12,28},{16,0},{20,4},{24,8},{28,12},{1,17},{... | collective-permute-start | bytes 1179656 | tf_op jit(solution)/shard_map/ppermute | solution.py:449
  59.5 39.5 %collective-permute-start.8 = (bf16[2,1536,128]{2,1,0:T(8,128)(2,1)S(1)}, bf16[2,1536,128]{2,1,0:T(8,128)(2,1)S(1)}, u32[]{:S(2)}, u32[]{:S(2)}) collective-permute-start(bf16[2,1536,128]{2,1,0:T(8,128)(2,1)S(1)} %collective-permute-done.5.refs_2_), channel_id=1, source_target_pairs={{0,4},{4,0},{8,12},{12,8},{16,20},{20,16},{24,28},{28,24},{1,5},{5... | collective-permute-start | bytes 2359304 | tf_op jit(solution)/shard_map/ppermute | solution.py:449
  62.5 39.7 %collective-permute-start.10 = (bf16[2,1536,128]{2,1,0:T(8,128)(2,1)S(1)}, bf16[2,1536,128]{2,1,0:T(8,128)(2,1)S(1)}, u32[]{:S(2)}, u32[]{:S(2)}) collective-permute-start(bf16[2,1536,128]{2,1,0:T(8,128)(2,1)S(1)} %get-tuple-element.91.refs_0_), channel_id=1, source_target_pairs={{0,8},{4,12},{8,0},{12,4},{16,24},{20,28},{24,16},{28,20},{1,9},{5... | collective-permute-start | bytes 2359304 | tf_op jit(solution)/shard_map/ppermute | solution.py:449
  63.1 39.1 %collective-permute-start.9 = (bf16[2,1536,128]{2,1,0:T(8,128)(2,1)S(1)}, bf16[2,1536,128]{2,1,0:T(8,128)(2,1)S(1)}, u32[]{:S(2)}, u32[]{:S(2)}) collective-permute-start(bf16[2,1536,128]{2,1,0:T(8,128)(2,1)S(1)} %get-tuple-element.91.refs_0_), channel_id=1, source_target_pairs={{0,4},{4,0},{8,12},{12,8},{16,20},{20,16},{24,28},{28,24},{1,5},{5... | collective-permute-start | bytes 2359304 | tf_op jit(solution)/shard_map/ppermute | solution.py:449
  64.1 38.1 %collective-permute-start.11 = (bf16[1632,128]{1,0:T(8,128)(2,1)S(1)}, bf16[1632,128]{1,0:T(8,128)(2,1)S(1)}, u32[]{:S(2)}, u32[]{:S(2)}) collective-permute-start(bf16[1632,128]{1,0:T(8,128)(2,1)S(1)} %guest_attention.4), channel_id=1, source_target_pairs={{0,16},{4,20},{8,24},{12,28},{16,0},{20,4},{24,8},{28,12},{1,17},{... | collective-permute-start | bytes 1253384 | tf_op jit(solution)/shard_map/ppermute | solution.py:449
  67.0 32.0 %collective-permute-start.7 = (bf16[1536,128]{1,0:T(8,128)(2,1)S(1)}, bf16[1536,128]{1,0:T(8,128)(2,1)S(1)}, u32[]{:S(2)}, u32[]{:S(2)}) collective-permute-start(bf16[1536,128]{1,0:T(8,128)(2,1)S(1)} %get-tuple-element.108.q_ref), channel_id=1, source_target_pairs={{0,16},{4,20},{8,24},{12,28},{16,0},{20,4},{24,8},{28,12},{1,17},{... | collective-permute-start | bytes 1179656 | tf_op jit(solution)/shard_map/ppermute | solution.py:449
  102.2 20.0 %collective-permute-start.13 = (bf16[2,1536,128]{2,1,0:T(8,128)(2,1)S(1)}, bf16[2,1536,128]{2,1,0:T(8,128)(2,1)S(1)}, u32[]{:S(2)}, u32[]{:S(2)}) collective-permute-start(bf16[2,1536,128]{2,1,0:T(8,128)(2,1)S(1)} %collective-permute-done.10.refs_2_), channel_id=1, source_target_pairs={{0,4},{4,0},{8,12},{12,8},{16,20},{20,16},{24,28},{28,24},{1,5},{5... | collective-permute-start | bytes 2359304 | tf_op jit(solution)/shard_map/ppermute | solution.py:449
  104.3 17.9 %collective-permute-start.12 = (bf16[1536,128]{1,0:T(8,128)(2,1)S(1)}, bf16[1536,128]{1,0:T(8,128)(2,1)S(1)}, u32[]{:S(2)}, u32[]{:S(2)}) collective-permute-start(bf16[1536,128]{1,0:T(8,128)(2,1)S(1)} %get-tuple-element.116.q_ref), channel_id=1, source_target_pairs={{0,16},{4,20},{8,24},{12,28},{16,0},{20,4},{24,8},{28,12},{1,17},{... | collective-permute-start | bytes 1179656 | tf_op jit(solution)/shard_map/ppermute | solution.py:449
  104.3 29.6 %collective-permute-start.15 = (bf16[2,1536,128]{2,1,0:T(8,128)(2,1)S(1)}, bf16[2,1536,128]{2,1,0:T(8,128)(2,1)S(1)}, u32[]{:S(2)}, u32[]{:S(2)}) collective-permute-start(bf16[2,1536,128]{2,1,0:T(8,128)(2,1)S(1)} %get-tuple-element.100.refs_0_), channel_id=1, source_target_pairs={{0,8},{4,12},{8,0},{12,4},{16,24},{20,28},{24,16},{28,20},{1,9},{5... | collective-permute-start | bytes 2359304 | tf_op jit(solution)/shard_map/ppermute | solution.py:449
  106.6 27.3 %collective-permute-start.14 = (bf16[2,1536,128]{2,1,0:T(8,128)(2,1)S(1)}, bf16[2,1536,128]{2,1,0:T(8,128)(2,1)S(1)}, u32[]{:S(2)}, u32[]{:S(2)}) collective-permute-start(bf16[2,1536,128]{2,1,0:T(8,128)(2,1)S(1)} %get-tuple-element.100.refs_0_), channel_id=1, source_target_pairs={{0,4},{4,0},{8,12},{12,8},{16,20},{20,16},{24,28},{28,24},{1,5},{5... | collective-permute-start | bytes 2359304 | tf_op jit(solution)/shard_map/ppermute | solution.py:449
  107.1 26.8 %collective-permute-start.16 = (bf16[1632,128]{1,0:T(8,128)(2,1)S(1)}, bf16[1632,128]{1,0:T(8,128)(2,1)S(1)}, u32[]{:S(2)}, u32[]{:S(2)}) collective-permute-start(bf16[1632,128]{1,0:T(8,128)(2,1)S(1)} %guest_attention.5), channel_id=1, source_target_pairs={{0,16},{4,20},{8,24},{12,28},{16,0},{20,4},{24,8},{28,12},{1,17},{... | collective-permute-start | bytes 1253384 | tf_op jit(solution)/shard_map/ppermute | solution.py:449
  122.2 4.7 %collective-permute-start.18 = (bf16[1536,128]{1,0:T(8,128)(2,1)S(1)}, bf16[1536,128]{1,0:T(8,128)(2,1)S(1)}, u32[]{:S(2)}, u32[]{:S(2)}) collective-permute-start(bf16[1536,128]{1,0:T(8,128)(2,1)S(1)} %merge_halves.4.refs_0_), channel_id=1, source_target_pairs={{0,1},{1,0},{2,3},{3,2},{4,5},{5,4},{6,7},{7,6},{8,9},{9,8},{10,11... | collective-permute-start | bytes 1179656 | tf_op jit(solution)/shard_map/ppermute | solution.py:457
  122.2 11.6 %collective-permute-start.17 = (bf16[1536,128]{1,0:T(8,128)(2,1)S(1)}, bf16[1536,128]{1,0:T(8,128)(2,1)}, u32[]{:S(2)}, u32[]{:S(2)}) collective-permute-start(bf16[1536,128]{1,0:T(8,128)(2,1)S(1)} %merge_halves.4.refs_0_), channel_id=1, source_target_pairs={{0,2},{1,3},{2,0},{3,1},{4,6},{5,7},{6,4},{7,5},{8,10},{9,11},{10,... | collective-permute-start | bytes 1179656 | tf_op jit(solution)/shard_map/ppermute | solution.py:457
  133.8 19.6 %collective-permute-start.25 = (bf16[1632,128]{1,0:T(8,128)(2,1)S(1)}, bf16[1632,128]{1,0:T(8,128)(2,1)S(1)}, u32[]{:S(2)}, u32[]{:S(2)}) collective-permute-start(bf16[1632,128]{1,0:T(8,128)(2,1)S(1)} %guest_attention.6), channel_id=1, source_target_pairs={{0,16},{4,20},{8,24},{12,28},{16,0},{20,4},{24,8},{28,12},{1,17},{... | collective-permute-start | bytes 1253384 | tf_op jit(solution)/shard_map/ppermute | solution.py:449
  136.7 11.6 %collective-permute-start.19 = (bf16[2,768,128]{2,1,0:T(8,128)(2,1)S(1)}, bf16[2,768,128]{2,1,0:T(8,128)(2,1)S(1)}, u32[]{:S(2)}, u32[]{:S(2)}) collective-permute-start(bf16[2,768,128]{2,1,0:T(8,128)(2,1)S(1)} %get-tuple-element.115), channel_id=1, source_target_pairs={{0,4},{4,0},{8,12},{12,8},{16,20},{20,16},{24,28},{28,24},{1,5},{5... | collective-permute-start | bytes 1179656 | tf_op jit(solution)/shard_map/ppermute | solution.py:449
  142.1 11.8 %collective-permute-start.23 = (bf16[1536,128]{1,0:T(8,128)(2,1)S(1)}, bf16[1536,128]{1,0:T(8,128)(2,1)}, u32[]{:S(2)}, u32[]{:S(2)}) collective-permute-start(bf16[1536,128]{1,0:T(8,128)(2,1)S(1)} %merge_halves.5.refs_4_), channel_id=1, source_target_pairs={{0,2},{1,3},{2,0},{3,1},{4,6},{5,7},{6,4},{7,5},{8,10},{9,11},{10,... | collective-permute-start | bytes 1179656 | tf_op jit(solution)/shard_map/ppermute | solution.py:457
  143.7 10.3 %collective-permute-start.20 = (bf16[2,768,128]{2,1,0:T(8,128)(2,1)S(1)}, bf16[2,768,128]{2,1,0:T(8,128)(2,1)S(1)}, u32[]{:S(2)}, u32[]{:S(2)}) collective-permute-start(bf16[2,768,128]{2,1,0:T(8,128)(2,1)S(1)} %get-tuple-element.117), channel_id=1, source_target_pairs={{0,4},{4,0},{8,12},{12,8},{16,20},{20,16},{24,28},{28,24},{1,5},{5... | collective-permute-start | bytes 1179656 | tf_op jit(solution)/shard_map/ppermute | solution.py:449
  153.4 21.2 %collective-permute-start.28 = (bf16[1632,128]{1,0:T(8,128)(2,1)S(1)}, bf16[1632,128]{1,0:T(8,128)(2,1)S(1)}, u32[]{:S(2)}, u32[]{:S(2)}) collective-permute-start(bf16[1632,128]{1,0:T(8,128)(2,1)S(1)} %guest_attention.7), channel_id=1, source_target_pairs={{0,16},{4,20},{8,24},{12,28},{16,0},{20,4},{24,8},{28,12},{1,17},{... | collective-permute-start | bytes 1253384 | tf_op jit(solution)/shard_map/ppermute | solution.py:449
  153.4 6.3 %collective-permute-start.22 = (bf16[1536,128]{1,0:T(8,128)(2,1)S(1)}, bf16[1536,128]{1,0:T(8,128)(2,1)}, u32[]{:S(2)}, u32[]{:S(2)}) collective-permute-start(bf16[1536,128]{1,0:T(8,128)(2,1)S(1)} %merge_halves.5.refs_4_), channel_id=1, source_target_pairs={{0,1},{1,0},{2,3},{3,2},{4,5},{5,4},{6,7},{7,6},{8,9},{9,8},{10,11... | collective-permute-start | bytes 1179656 | tf_op jit(solution)/shard_map/ppermute | solution.py:457
  153.4 6.5 %collective-permute-start.21 = (bf16[1536,128]{1,0:T(8,128)(2,1)}, bf16[1536,128]{1,0:T(8,128)(2,1)}, u32[]{:S(2)}, u32[]{:S(2)}) collective-permute-start(bf16[1536,128]{1,0:T(8,128)(2,1)} %collective-permute-done.17.refs_2_), channel_id=1, source_target_pairs={{0,1},{1,0},{2,3},{3,2},{4,5},{5,4},{6,7},{7,6},{8,9},{9,8},{10,11... | collective-permute-start | bytes 1179656 | tf_op jit(solution)/shard_map/ppermute | solution.py:457
  153.9 6.1 %collective-permute-start.24 = (bf16[1536,128]{1,0:T(8,128)(2,1)}, bf16[1536,128]{1,0:T(8,128)(2,1)}, u32[]{:S(2)}, u32[]{:S(2)}) collective-permute-start(bf16[1536,128]{1,0:T(8,128)(2,1)} %collective-permute-done.23.refs_6_), channel_id=1, source_target_pairs={{0,1},{1,0},{2,3},{3,2},{4,5},{5,4},{6,7},{7,6},{8,9},{9,8},{10,11... | collective-permute-start | bytes 1179656 | tf_op jit(solution)/shard_map/ppermute | solution.py:457
  158.2 17.4 %collective-permute-start.27 = (bf16[1536,128]{1,0:T(8,128)(2,1)S(1)}, bf16[1536,128]{1,0:T(8,128)(2,1)}, u32[]{:S(2)}, u32[]{:S(2)}) collective-permute-start(bf16[1536,128]{1,0:T(8,128)(2,1)S(1)} %merge_halves.6.refs_1_), channel_id=1, source_target_pairs={{0,2},{1,3},{2,0},{3,1},{4,6},{5,7},{6,4},{7,5},{8,10},{9,11},{10,... | collective-permute-start | bytes 1179656 | tf_op jit(solution)/shard_map/ppermute | solution.py:457
  159.7 23.3 %collective-permute-start.26 = (bf16[1536,128]{1,0:T(8,128)(2,1)S(1)}, bf16[1536,128]{1,0:T(8,128)(2,1)S(1)}, u32[]{:S(2)}, u32[]{:S(2)}) collective-permute-start(bf16[1536,128]{1,0:T(8,128)(2,1)S(1)} %merge_halves.6.refs_1_), channel_id=1, source_target_pairs={{0,1},{1,0},{2,3},{3,2},{4,5},{5,4},{6,7},{7,6},{8,9},{9,8},{10,11... | collective-permute-start | bytes 1179656 | tf_op jit(solution)/shard_map/ppermute | solution.py:457
  160.0 2.2 %copy-start = (bf16[2048,1024]{1,0:T(8,128)(2,1)S(1)}, bf16[2048,1024]{1,0:T(8,128)(2,1)}, u32[]{:S(2)}) copy-start(bf16[2048,1024]{1,0:T(8,128)(2,1)} %param.9) | copy-start | bytes 12582916
  162.1 22.3 %copy-start.1 = (bf16[2048,1024]{1,0:T(8,128)(2,1)S(1)}, bf16[2048,1024]{1,0:T(8,128)(2,1)}, u32[]{:S(2)}) copy-start(bf16[2048,1024]{1,0:T(8,128)(2,1)} %param.9) | copy-start | bytes 12582916
  175.6 6.9 %collective-permute-start.33 = (bf16[768,128]{1,0:T(8,128)(2,1)S(1)}, bf16[768,128]{1,0:T(8,128)(2,1)S(1)}, u32[]{:S(2)}, u32[]{:S(2)}) collective-permute-start(bf16[768,128]{1,0:T(8,128)(2,1)S(1)} %get-tuple-element.130.refs_5_), channel_id=1, source_target_pairs={{0,2},{1,3},{2,0},{3,1},{4,6},{5,7},{6,4},{7,5},{8,10},{9,11},{10,... | collective-permute-start | bytes 589832 | tf_op jit(solution)/shard_map/ppermute | solution.py:457
  177.0 7.4 %collective-permute-start.29 = (bf16[1536,128]{1,0:T(8,128)(2,1)}, bf16[1536,128]{1,0:T(8,128)(2,1)S(1)}, u32[]{:S(2)}, u32[]{:S(2)}) collective-permute-start(bf16[1536,128]{1,0:T(8,128)(2,1)} %collective-permute-done.27.refs_3_), channel_id=1, source_target_pairs={{0,1},{1,0},{2,3},{3,2},{4,5},{5,4},{6,7},{7,6},{8,9},{9,8},{10,11... | collective-permute-start | bytes 1179656 | tf_op jit(solution)/shard_map/ppermute | solution.py:457
  177.0 7.3 %collective-permute-start.32 = (bf16[768,128]{1,0:T(8,128)(2,1)S(1)}, bf16[768,128]{1,0:T(8,128)(2,1)S(1)}, u32[]{:S(2)}, u32[]{:S(2)}) collective-permute-start(bf16[768,128]{1,0:T(8,128)(2,1)S(1)} %get-tuple-element.130.refs_5_), channel_id=1, source_target_pairs={{0,1},{1,0},{2,3},{3,2},{4,5},{5,4},{6,7},{7,6},{8,9},{9,8},{10,11... | collective-permute-start | bytes 589832 | tf_op jit(solution)/shard_map/ppermute | solution.py:457
  182.5 1.9 collective-permute-start.34
  182.5 7.3 %collective-permute-start.30 = (bf16[768,128]{1,0:T(8,128)(2,1)S(1)}, bf16[768,128]{1,0:T(8,128)(2,1)S(1)}, u32[]{:S(2)}, u32[]{:S(2)}) collective-permute-start(bf16[768,128]{1,0:T(8,128)(2,1)S(1)} %get-tuple-element.131.refs_5_), channel_id=1, source_target_pairs={{0,1},{1,0},{2,3},{3,2},{4,5},{5,4},{6,7},{7,6},{8,9},{9,8},{10,11... | collective-permute-start | bytes 589832 | tf_op jit(solution)/shard_map/ppermute | solution.py:457
  183.0 6.8 %collective-permute-start.31 = (bf16[768,128]{1,0:T(8,128)(2,1)S(1)}, bf16[768,128]{1,0:T(8,128)(2,1)S(1)}, u32[]{:S(2)}, u32[]{:S(2)}) collective-permute-start(bf16[768,128]{1,0:T(8,128)(2,1)S(1)} %get-tuple-element.131.refs_5_), channel_id=1, source_target_pairs={{0,2},{1,3},{2,0},{3,1},{4,6},{5,7},{6,4},{7,5},{8,10},{9,11},{10,... | collective-permute-start | bytes 589832 | tf_op jit(solution)/shard_map/ppermute | solution.py:457
  189.8 1.4 collective-permute-start.35

commit v5 on v4

--- a/solution.py
+++ b/solution.py
@@ -152,8 +152,8 @@
         home_scale[...] = factor_h / total
         guest_scale[...] = factor_g / total
 
-        def step(n, part):
-            i = part * (blocks // len(out_refs)) + n
+        def step(n, part, low):
+            i = low + n
             rows = pl.ds(pl.multiple_of(i * BLOCK, BLOCK), BLOCK)
             scale_h = jnp.sum(
                 jnp.where(eye, home_scale[pl.ds(i, 1), :], 0.0), axis=1, keepdims=True
@@ -168,45 +168,25 @@
             rows = pl.ds(pl.multiple_of(n * BLOCK, BLOCK), BLOCK)
             out_refs[part][rows, lanes] = mixed.astype(jnp.bfloat16)
 
-        for part in range(len(out_refs)):
-
-            def body(n, _, part=part):
-                step(n, part)
+        low = 0
+        for part, out_ref in enumerate(out_refs):
+
+            def body(n, _, part=part, low=low):
+                step(n, part, low)
                 return 0
 
-            lax.fori_loop(0, blocks // len(out_refs), body, 0, unroll=4)
-
-
-def project_kernel(heads, given, filled, me_ref, w_ref, *refs):
-    *x_refs, out_ref, held, sem = refs
-    groups = w_ref.shape[0]
-    sum_ref = x_refs.pop(0) if given else None
-    if filled:
-        x_refs.pop()
-
-    @pl.when(pl.program_id(0) == 0)
-    def _():
-        copies = [
-            pltpu.make_async_copy(
-                w_ref.at[me_ref[0] ^ relation, pl.ds(heads[0], len(heads))],
-                held.at[relation],
-                sem.at[relation],
-            )
-            for relation in range(groups)
-        ]
-        for copy in copies:
-            copy.start()
-        for copy in copies:
-            copy.wait()
-
-    ordered = [x_refs[h * groups + r][...] for r in range(groups) for h in range(len(heads))]
-    weight = held[...].reshape(-1, held.shape[-1])
-    total = jnp.dot(
-        jnp.concatenate(ordered, axis=1), weight, preferred_element_type=jnp.float32
-    )
-    if given:
-        total = total + sum_ref[...]
-    out_ref[...] = total.astype(out_ref.dtype)
+            count = out_ref.shape[0] // BLOCK
+            lax.fori_loop(0, count, body, 0, unroll=4)
+            low += count
+
+
+def last_terms_kernel(groups, w_ref, sum_ref, *refs):
+    x_refs, out_ref = refs[: 2 * groups], refs[-1]
+    ordered = [x_refs[h * groups + r][...] for r in range(groups) for h in range(2)]
+    term = jnp.dot(
+        jnp.concatenate(ordered, axis=1), w_ref[...], preferred_element_type=jnp.float32
+    )
+    out_ref[...] = (sum_ref[...] + term).astype(out_ref.dtype)
 
 
 VMEM = pl.BlockSpec(memory_space=pltpu.VMEM)
@@ -271,14 +251,14 @@
     )(starts, bias, query, *pieces)
 
 
-def merge_call(mixed, stats, message, parts=1):
+def merge_call(mixed, stats, message, sizes=None):
     rows, width = mixed.shape
-    result = jax.ShapeDtypeStruct((rows // parts, width), jnp.bfloat16)
+    sizes = sizes or [rows]
     return pl.pallas_call(
         merge_kernel,
-        out_shape=[result] * parts,
+        out_shape=[jax.ShapeDtypeStruct((size, width), jnp.bfloat16) for size in sizes],
         in_specs=[VMEM, VMEM, VMEM],
-        out_specs=[VMEM] * parts,
+        out_specs=[VMEM] * len(sizes),
         scratch_shapes=[
             pltpu.VMEM((stats.shape[1], BLOCK), jnp.float32),
             pltpu.VMEM((stats.shape[1], BLOCK), jnp.float32),
@@ -292,95 +272,107 @@
 ROW_TILE = 256
 
 
-def project(name, summed, gathered, heads, weights, result, rows, part=(0, 1), filled=None):
-    groups, _, depth, columns = weights.shape
-    number, parts = part
-    tiles = rows // parts // ROW_TILE
+def last_terms(summed, gathered, weight, part, filled=None):
+    rows, columns = summed.shape
+    first, tiles = part
+    pieces = [piece for group in gathered for piece in group]
 
     def row_spec(height, width):
-        first = number * tiles if height == rows else 0
-        return pl.BlockSpec((ROW_TILE, width), lambda i, me: (i + first, 0))
-
-    pieces = [piece for group in gathered for piece in group]
-    sums = [] if summed is None else [summed]
+        low = first if height == rows else 0
+        return pl.BlockSpec((ROW_TILE, width), lambda i: (i + low, 0))
+
     others = [] if filled is None else [filled]
-    myself = lax.axis_index("head").astype(jnp.int32).reshape(1)
     return pl.pallas_call(
-        functools.partial(project_kernel, heads, summed is not None, filled is not None),
-        out_shape=jax.ShapeDtypeStruct((rows, columns), result),
-        grid_spec=pltpu.PrefetchScalarGridSpec(
-            num_scalar_prefetch=1,
-            grid=(tiles,),
-            in_specs=[HBM] + [row_spec(*v.shape) for v in sums + pieces] + [ANY] * len(others),
-            out_specs=row_spec(rows, columns),
-            scratch_shapes=[
-                pltpu.VMEM((groups, len(heads), depth, columns), weights.dtype),
-                pltpu.SemaphoreType.DMA((groups,)),
-            ],
-        ),
-        input_output_aliases={2 + len(sums) + len(pieces): 0} if others else {},
+        functools.partial(last_terms_kernel, len(pieces) // 2),
+        grid=(tiles,),
+        out_shape=jax.ShapeDtypeStruct((rows, columns), jnp.bfloat16),
+        in_specs=[VMEM]
+        + [row_spec(*v.shape) for v in [summed, *pieces]]
+        + [ANY] * len(others),
+        out_specs=row_spec(rows, columns),
+        input_output_aliases={2 + len(pieces): 0} if others else {},
         compiler_params=params(),
         cost_estimate=cost(PROJECT_US),
-        name=name,
-    )(myself, weights, *sums, *pieces, *others)
-
-
-def first_terms_kernel(heads, me_ref, w_ref, *refs):
-    *x_refs, out_ref, held, columns, sems = refs
-    groups = w_ref.shape[0]
+        name="last_terms",
+    )(weight, summed, *pieces, *others)
+
+
+def first_terms_kernel(groups, w_ref, *refs):
+    x_refs, (out_ref, columns, sems) = refs[: 2 * groups], refs[2 * groups :]
+    copies = [
+        pltpu.make_async_copy(
+            x_refs[head * groups + relation],
+            columns.at[:, pl.ds((2 * relation + head) * HEAD_DIM, HEAD_DIM)],
+            sems.at[2 * relation + head],
+        )
+        for relation in range(groups)
+        for head in range(2)
+    ]
+    for copy in copies:
+        copy.start()
+    for copy in copies:
+        copy.wait()
+
+    def step(i, _):
+        rows = pl.ds(pl.multiple_of(i * ROW_TILE, ROW_TILE), ROW_TILE)
+        out_ref[rows, :] = jnp.dot(
+            columns[rows, :], w_ref[...], preferred_element_type=jnp.float32
+        )
+        return 0
+
+    lax.fori_loop(0, out_ref.shape[0] // ROW_TILE, step, 0)
+
+
+def first_terms(gathered, weight):
+    pieces = [piece for group in gathered for piece in group]
+    rows = pieces[0].shape[0]
+    return pl.pallas_call(
+        functools.partial(first_terms_kernel, len(pieces) // 2),
+        out_shape=jax.ShapeDtypeStruct((rows, weight.shape[1]), jnp.float32),
+        in_specs=[VMEM] + [ANY] * len(pieces),
+        out_specs=VMEM,
+        scratch_shapes=[
+            pltpu.VMEM((rows, weight.shape[0]), jnp.bfloat16),
+            pltpu.SemaphoreType.DMA((len(pieces),)),
+        ],
+        compiler_params=params(),
+        cost_estimate=cost(0),
+        name="first_terms",
+    )(weight, *pieces)
+
+
+def order_kernel(me_ref, w_ref, first_ref, last_ref, sems):
     copies = []
-    for relation in range(groups):
-        copies.append(
-            pltpu.make_async_copy(
-                w_ref.at[me_ref[0] ^ relation, pl.ds(0, heads)], held.at[relation], sems.at[relation]
-            )
-        )
-    for relation in range(groups):
-        for head in range(heads):
-            place = relation * heads + head
+    for relation in range(w_ref.shape[0]):
+        for n, target in enumerate((first_ref, last_ref)):
             copies.append(
                 pltpu.make_async_copy(
-                    x_refs[head * groups + relation],
-                    columns.at[:, pl.ds(place * HEAD_DIM, HEAD_DIM)],
-                    sems.at[groups + place],
+                    w_ref.at[me_ref[0] ^ relation, pl.ds(2 * n, 2)],
+                    target.at[relation],
+                    sems.at[2 * relation + n],
                 )
             )
     for copy in copies:
         copy.start()
     for copy in copies:
         copy.wait()
-    weight = held[...].reshape(-1, held.shape[-1])
-
-    def step(i, _):
-        rows = pl.ds(pl.multiple_of(i * ROW_TILE, ROW_TILE), ROW_TILE)
-        out_ref[rows, :] = jnp.dot(
-            columns[rows, :], weight, preferred_element_type=jnp.float32
-        )
-        return 0
-
-    lax.fori_loop(0, out_ref.shape[0] // ROW_TILE, step, 0)
-
-
-def first_terms(gathered, weights):
-    groups, _, depth, width = weights.shape
-    heads = len(gathered)
-    pieces = [piece for group in gathered for piece in group]
-    rows = pieces[0].shape[0]
+
+
+def order_weights(weights):
+    groups, heads, depth, columns = weights.shape
+    half = jax.ShapeDtypeStruct((groups, heads // 2, depth, columns), weights.dtype)
     myself = lax.axis_index("head").astype(jnp.int32).reshape(1)
-    return pl.pallas_call(
-        functools.partial(first_terms_kernel, heads),
-        out_shape=jax.ShapeDtypeStruct((rows, width), jnp.float32),
-        in_specs=[SMEM] + [HBM] * (1 + len(pieces)),
-        out_specs=VMEM,
-        scratch_shapes=[
-            pltpu.VMEM((groups, heads, depth, width), weights.dtype),
-            pltpu.VMEM((rows, heads * groups * HEAD_DIM), jnp.bfloat16),
-            pltpu.SemaphoreType.DMA((groups + len(pieces),)),
-        ],
+    parts = pl.pallas_call(
+        order_kernel,
+        out_shape=[half, half],
+        in_specs=[SMEM, ANY],
+        out_specs=[ANY, ANY],
+        scratch_shapes=[pltpu.SemaphoreType.DMA((2 * groups,))],
         compiler_params=params(),
         cost_estimate=cost(0),
-        name="first_terms",
-    )(myself, weights, *pieces)
+        name="order_weights",
+    )(myself, weights)
+    return [part.reshape(-1, columns) for part in parts]
 
 
 def key_list(shard, global_ids, rand_ids, local_blocks, shards):
@@ -464,6 +456,7 @@
 UNROLL = 8
 GUEST_US = 0.1
 PROJECT_US = 4
+UPPER_TILES = 4
 
 
 def halves_body(queries, keys_values, global_ids, rand_ids, out_weight):
@@ -497,7 +490,9 @@
     last_home = key_places(myself, myself, *lists, mine)
     last_guest = key_places(myself ^ opposite, myself, *lists, mine)
     home, guest = (*home, *last_home, order), (*guest, *last_guest)
-    weights = out_weight.reshape(groups, heads_here, HEAD_DIM, out_weight.shape[1])
+    weights = order_weights(
+        out_weight.reshape(groups, heads_here, HEAD_DIM, out_weight.shape[1])
+    )
     k0 = column(keys_values, 0)
     others = after(keys_values, k0)
     k1, k2, k3 = [column(others, h) for h in range(1, heads_here)]
@@ -509,7 +504,7 @@
     d0, y1, z1, v0, v1 = over_y(z0), over_y(k1_), over_z(k1_), across(v0), across(v1)
     p0 = (k0, y0, z0, d0)
     (s0,) = guest_call(*guest[:2], v0, p0)
-    s0, y1, z1, v1, k2_, v2 = together(s0, y1, z1, v1, k2, q2)
+    s0, y1, z1, v1, k2_, v2, weights = together(s0, y1, z1, v1, k2, q2, weights)
 
     d1, y2, z2, v2, g0 = over_y(z1), over_y(k2_), over_z(k2_), across(v2), across(s0)
     m0 = home_call(*home[:2], after(q0, s0), p0)
@@ -537,21 +532,21 @@
     a1d = hop(after(a1x, s3), 1, groups)
     a2x, a2c = hop(a2, 2, groups), hop(a2, 1, groups)
     early = ((a0, a0c, a0x, a0d), (a1, a1c, a1x, a1d))
-    summed = first_terms(early, after(weights, m3[1]))
-
-    a3a, a3b = merge_call(*m3, after(g3, summed), 2)
+    summed = first_terms(early, after(weights[0], m3[1]))
+
+    tiles = rows // ROW_TILE
+    tiles_a = UPPER_TILES
+    sizes = [tiles_a * ROW_TILE, (tiles - tiles_a) * ROW_TILE]
+    a3a, a3b = merge_call(*m3, after(g3, summed), sizes)
     a3ax, a3ac = hop(a3a, 2, groups), hop(a3a, 1, groups)
     a3bx, a3bc = hop(after(a3b, a3a), 2, groups), hop(a3b, 1, groups)
     a2d = hop(after(a2x, a3b), 1, groups)
     a2 = (a2, a2c, a2x, a2d)
     a3ad = hop(a3ax, 1, groups)
-    late = (a2, (a3a, a3ac, a3ax, a3ad))
-    upper = project("last_terms", summed, late, (2, 3), weights, jnp.bfloat16, rows, (0, 2))
+    upper = last_terms(summed, (a2, (a3a, a3ac, a3ax, a3ad)), weights[1], (0, tiles_a))
     a3bd = hop(after(a3bx, upper), 1, groups)
     late = (a2, (a3b, a3bc, a3bx, a3bd))
-    return project(
-        "last_terms", summed, late, (2, 3), weights, jnp.bfloat16, rows, (1, 2), upper
-    )
+    return last_terms(summed, late, weights[1], (tiles_a, tiles - tiles_a), upper)
 
 
 def padded_2(block, sides, width):

time: 196 us -> 194 us (0.990)
  waiting for transfers between devices: 99.7 us -> 91.8 us
  Pallas kernels: 45.4 us -> 48.8 us
    ppermute x21, waiting for transfers between devices: 85.2 us -> 77.3 us  [swap(): lax.ppermute(value, 'seq', [(i, i ^ distance) for i in range(shards)])]
    pallas_call x4, Pallas kernels: 12.8 us -> 16.3 us  [home_call(): pl.pallas_call(functools.partial(home_kernel, parts, len(pieces)), out_sh...]
    pallas_call x7 -> x8, Pallas kernels: 19.1 us -> 15.6 us  [the longest x2 6 us: last_terms(): pl.pallas_call(functools.partial(last_terms_kernel, len(pieces) // 2), gr...]
    pallas_call x4, Pallas kernels: 12.9 us -> 16.3 us  [guest_call(): pl.pallas_call(functools.partial(guest_kernel, parts, len(pieces)), out_s...]
  transfers between devices with their start and end apart: 36 -> 36, of which waited for: 14 -> 14; matrix products, arithmetic and copies ran while one was open for 5% -> 6% of each run, Pallas kernels for 21% -> 24%
where the time goes in v5:
time: 194 us; the launch traced here: 193 us
  waiting for transfers between devices  91.8 us (47%)
  Pallas kernels  48.8 us (25%)
  starting transfers between devices  36.7 us (19%)
  local copies, waits for them, and re-layouts  9.37 us (5%)
  other arithmetic  6.31 us (3%)
    ppermute x21, waiting for transfers between devices, swap(): lax.ppermute(value, 'seq', [(i, i ^ distance) for i in range(shards)])  77.3 us
    ppermute x21, starting transfers between devices, swap(): lax.ppermute(value, 'seq', [(i, i ^ distance) for i in range(shards)])  27.5 us
    pallas_call x4, Pallas kernels, home_call(): pl.pallas_call(functools.partial(home_kernel, parts, len(pieces)), out_sh...  16.3 us
    pallas_call x4, Pallas kernels, guest_call(): pl.pallas_call(functools.partial(guest_kernel, parts, len(pieces)), out_s...  16.3 us
    ppermute x15, waiting for transfers between devices, hop(): lax.ppermute(value, 'head', [(i, i ^ distance) for i in range(groups)])  14.5 us
    ppermute x15, starting transfers between devices, hop(): lax.ppermute(value, 'head', [(i, i ^ distance) for i in range(groups)])  9.22 us
    pallas_call x2, Pallas kernels, last_terms(): pl.pallas_call(functools.partial(last_terms_kernel, len(pieces) // 2), gr...  6 us
    pallas_call x1, Pallas kernels, first_terms(): pl.pallas_call(functools.partial(first_terms_kernel, len(pieces) // 2), o...  5.38 us
  transfers between devices with their start and end apart: 36, of which 14 were waited for; matrix products, arithmetic and copies ran while one was open for 6% of the time, Pallas kernels for 24%

profile of v5, /device:TPU:0, one launch (start us, length us, event | category | flops | bytes accessed | tf_op | source)
XLA Modules:
  0.0 193.4 jit_solution(3191315132286022109)
XLA Ops:
  0.0 1.3 slice.24.refs_0_
  1.3 3.1 %collective-permute-start.1 = (bf16[2,1536,128]{2,1,0:T(8,128)(2,1)S(1)}, bf16[2,1536,128]{2,1,0:T(8,128)(2,1)}, u32[]{:S(2)}, u32[]{:S(2)}) collective-permute-start(bf16[2,1536,128]{2,1,0:T(8,128)(2,1)S(1)} %slice.24.refs_0_), channel_id=1, source_target_pairs={{0,8},{4,12},{8,0},{12,4},{16,24},{20,28},{24,16},{28,20},{1,9},{5... | collective-permute-start | bytes 2359304 | tf_op jit(solution)/shard_map/ppermute | solution.py:441
  4.4 1.5 collective-permute-start
  6.8 0.9 constant_dynamic-slice_fusion
  10.0 1.0 select_reduce_fusion
  15.1 1.2 fusion.14
  18.2 3.8 %collective-permute-done.1.refs_2_ = bf16[2,1536,128]{2,1,0:T(8,128)(2,1)} collective-permute-done((bf16[2,1536,128]{2,1,0:T(8,128)(2,1)S(1)}, bf16[2,1536,128]{2,1,0:T(8,128)(2,1)}, u32[]{:S(2)}, u32[]{:S(2)}) %collective-permute-start.1) | collective-permute-done | bytes 786464 | tf_op jit(solution)/shard_map/ppermute | solution.py:441
  22.0 1.5 collective-permute-done.refs_1_
  23.5 1.5 collective-permute-start.3
  25.9 2.7 %collective-permute-start.2 = (bf16[1536,128]{1,0:T(8,128)(2,1)}, bf16[1536,128]{1,0:T(8,128)(2,1)}, u32[]{:S(2)}, u32[]{:S(2)}) collective-permute-start(bf16[1536,128]{1,0:T(8,128)(2,1)} %get-tuple-element.93.q_ref), channel_id=1, source_target_pairs={{0,16},{4,20},{8,24},{12,28},{16,0},{20,4},{24,8},{28,12},{1,17},{... | collective-permute-start | bytes 1179656 | tf_op jit(solution)/shard_map/ppermute | solution.py:441
  28.8 2.2 %copy-done = bf16[2048,1024]{1,0:T(8,128)(2,1)S(1)} copy-done((bf16[2048,1024]{1,0:T(8,128)(2,1)S(1)}, bf16[2048,1024]{1,0:T(8,128)(2,1)}, u32[]{:S(2)}) %copy-start) | copy-done | bytes 4194328
  31.4 20.6 %collective-permute-done.2.q_ref = bf16[1536,128]{1,0:T(8,128)(2,1)} collective-permute-done((bf16[1536,128]{1,0:T(8,128)(2,1)}, bf16[1536,128]{1,0:T(8,128)(2,1)}, u32[]{:S(2)}, u32[]{:S(2)}) %collective-permute-start.2) | collective-permute-done | bytes 393248 | tf_op jit(solution)/shard_map/ppermute | solution.py:441
  52.1 5.1 %guest_attention.4 = bf16[1632,128]{1,0:T(8,128)(2,1)S(1)} custom-call(s32[192]{0:T(256)S(1)} %reshape.155.starts_ref, f32[24,512]{1,0:T(8,128)S(1)} %copy-done.3, bf16[1536,128]{1,0:T(8,128)(2,1)} %collective-permute-done.2.q_ref, bf16[2,1536,128]{2,1,0:T(8,128)(2,1)S(1)} %slice.24.refs_0_, bf16[2,1536,128]{2,1,0:T(8,128)(2,1)} %collective-permute-done.refs_1_, ...), custom_call_target="tpu_custom_call" | custom-call | flops 115000000 | tf_op jit(solution)/shard_map/guest_attention/pallas_call | solution.py:220
  58.0 1.8 collective-permute-done.5.refs_2_
  59.8 3.3 %collective-permute-start.8 = (bf16[2,1536,128]{2,1,0:T(8,128)(2,1)}, bf16[2,1536,128]{2,1,0:T(8,128)(2,1)S(1)}, u32[]{:S(2)}, u32[]{:S(2)}) collective-permute-start(bf16[2,1536,128]{2,1,0:T(8,128)(2,1)} %collective-permute-done.5.refs_2_), channel_id=1, source_target_pairs={{0,4},{4,0},{8,12},{12,8},{16,20},{20,16},{24,28},{28,24},{1,5},{5... | collective-permute-start | bytes 2359304 | tf_op jit(solution)/shard_map/ppermute | solution.py:441
  64.4 3.1 %collective-permute-start.11 = (bf16[1632,128]{1,0:T(8,128)(2,1)S(1)}, bf16[1632,128]{1,0:T(8,128)(2,1)S(1)}, u32[]{:S(2)}, u32[]{:S(2)}) collective-permute-start(bf16[1632,128]{1,0:T(8,128)(2,1)S(1)} %guest_attention.4), channel_id=1, source_target_pairs={{0,16},{4,20},{8,24},{12,28},{16,0},{20,4},{24,8},{28,12},{1,17},{... | collective-permute-start | bytes 1253384 | tf_op jit(solution)/shard_map/ppermute | solution.py:441
  67.6 5.0 %home_attention.4 = (f32[1536,128]{1,0:T(8,128)S(1)}, f32[1,32,128]{2,1,0:T(8,128)S(1)}) custom-call(s32[192]{0:T(256)S(1)} %reshape.152.starts_ref, f32[24,512]{1,0:T(8,128)S(1)} %copy-done.2, bf16[1536,128]{1,0:T(8,128)(2,1)} %get-tuple-element.93.q_ref, bf16[2,1536,128]{2,1,0:T(8,128)(2,1)S(1)} %slice.24.refs_0_, ...), custom_call_target="tpu_custom_call" | custom-call | tf_op jit(solution)/shard_map/home_attention/pallas_call | solution.py:242
  72.6 26.7 %collective-permute-done.7.q_ref = bf16[1536,128]{1,0:T(8,128)(2,1)S(1)} collective-permute-done((bf16[1536,128]{1,0:T(8,128)(2,1)S(1)}, bf16[1536,128]{1,0:T(8,128)(2,1)S(1)}, u32[]{:S(2)}, u32[]{:S(2)}) %collective-permute-start.7) | collective-permute-done | bytes 393248 | tf_op jit(solution)/shard_map/ppermute | solution.py:441
  99.3 4.8 %guest_attention.5 = bf16[1632,128]{1,0:T(8,128)(2,1)S(1)} custom-call(s32[192]{0:T(256)S(1)} %reshape.155.starts_ref, f32[24,512]{1,0:T(8,128)S(1)} %copy-done.3, bf16[1536,128]{1,0:T(8,128)(2,1)} %collective-permute-done.6.q_ref, bf16[2,1536,128]{2,1,0:T(8,128)(2,1)S(1)} %get-tuple-element.79.refs_0_, ...), custom_call_target="tpu_custom_call" | custom-call | flops 115000000 | tf_op jit(solution)/shard_map/guest_attention/pallas_call | solution.py:220
  104.2 1.5 collective-permute-start.13
  105.7 2.9 %collective-permute-start.15 = (bf16[2,1536,128]{2,1,0:T(8,128)(2,1)S(1)}, bf16[2,1536,128]{2,1,0:T(8,128)(2,1)S(1)}, u32[]{:S(2)}, u32[]{:S(2)}) collective-permute-start(bf16[2,1536,128]{2,1,0:T(8,128)(2,1)S(1)} %get-tuple-element.108.refs_0_), channel_id=1, source_target_pairs={{0,8},{4,12},{8,0},{12,4},{16,24},{20,28},{24,16},{28,20},{1,9},{5... | collective-permute-start | bytes 2359304 | tf_op jit(solution)/shard_map/ppermute | solution.py:441
  109.2 4.8 %home_attention.5 = (f32[1536,128]{1,0:T(8,128)S(1)}, f32[1,32,128]{2,1,0:T(8,128)S(1)}) custom-call(s32[192]{0:T(256)S(1)} %reshape.152.starts_ref, f32[24,512]{1,0:T(8,128)S(1)} %copy-done.2, bf16[1536,128]{1,0:T(8,128)(2,1)} %get-tuple-element.102.q_ref, bf16[2,1536,128]{2,1,0:T(8,128)(2,1)S(1)} %get-tuple-element.79.refs_0_, ...), custom_call_target="tpu_custom_call" | custom-call | tf_op jit(solution)/shard_map/home_attention/pallas_call | solution.py:242
  114.0 1.0 merge_halves.4.refs_0_
  115.0 8.8 %collective-permute-done.12.q_ref = bf16[1536,128]{1,0:T(8,128)(2,1)S(1)} collective-permute-done((bf16[1536,128]{1,0:T(8,128)(2,1)S(1)}, bf16[1536,128]{1,0:T(8,128)(2,1)S(1)}, u32[]{:S(2)}, u32[]{:S(2)}) %collective-permute-start.12) | collective-permute-done | bytes 393248 | tf_op jit(solution)/shard_map/ppermute | solution.py:441
  123.9 1.4 collective-permute-start.17
  125.3 3.2 %guest_attention.6 = bf16[1632,128]{1,0:T(8,128)(2,1)S(1)} custom-call(s32[192]{0:T(256)S(1)} %reshape.155.starts_ref, f32[24,512]{1,0:T(8,128)S(1)} %copy-done.3, bf16[1536,128]{1,0:T(8,128)(2,1)S(1)} %collective-permute-done.7.q_ref, bf16[2,1536,128]{2,1,0:T(8,128)(2,1)S(1)} %get-tuple-element.99.refs_0_, ...), custom_call_target="tpu_custom_call" | custom-call | flops 115000000 | tf_op jit(solution)/shard_map/guest_attention/pallas_call | solution.py:220
  128.5 6.9 %collective-permute-done.17.refs_2_ = bf16[1536,128]{1,0:T(8,128)(2,1)S(1)} collective-permute-done((bf16[1536,128]{1,0:T(8,128)(2,1)S(1)}, bf16[1536,128]{1,0:T(8,128)(2,1)S(1)}, u32[]{:S(2)}, u32[]{:S(2)}) %collective-permute-start.17) | collective-permute-done | bytes 393248 | tf_op jit(solution)/shard_map/ppermute | solution.py:449
  135.4 2.7 %collective-permute-start.25 = (bf16[1632,128]{1,0:T(8,128)(2,1)S(1)}, bf16[1632,128]{1,0:T(8,128)(2,1)S(1)}, u32[]{:S(2)}, u32[]{:S(2)}) collective-permute-start(bf16[1632,128]{1,0:T(8,128)(2,1)S(1)} %guest_attention.6), channel_id=1, source_target_pairs={{0,16},{4,20},{8,24},{12,28},{16,0},{20,4},{24,8},{28,12},{1,17},{... | collective-permute-start | bytes 1253384 | tf_op jit(solution)/shard_map/ppermute | solution.py:441
  138.7 0.9 collective-permute-start.19
  139.5 3.2 %home_attention.6 = (f32[1536,128]{1,0:T(8,128)S(1)}, f32[1,32,128]{2,1,0:T(8,128)S(1)}) custom-call(s32[192]{0:T(256)S(1)} %reshape.152.starts_ref, f32[24,512]{1,0:T(8,128)S(1)} %copy-done.2, bf16[1536,128]{1,0:T(8,128)(2,1)S(1)} %copy-done.1, bf16[2,1536,128]{2,1,0:T(8,128)(2,1)S(1)} %get-tuple-element.99.refs_0_, ...), custom_call_target="tpu_custom_call" | custom-call | tf_op jit(solution)/shard_map/home_attention/pallas_call | solution.py:242
  142.7 1.0 merge_halves.5.refs_4_
  143.7 1.5 collective-permute-start.23
  145.2 1.3 collective-permute-start.20
  146.4 3.4 %collective-permute-done.19.refs_3_ = bf16[2,768,128]{2,1,0:T(8,128)(2,1)S(1)} collective-permute-done((bf16[2,768,128]{2,1,0:T(8,128)(2,1)S(1)}, bf16[2,768,128]{2,1,0:T(8,128)(2,1)S(1)}, u32[]{:S(2)}, u32[]{:S(2)}) %collective-permute-start.19) | collective-permute-done | bytes 393248 | tf_op jit(solution)/shard_map/ppermute | solution.py:441
  149.9 3.2 %guest_attention.7 = bf16[1632,128]{1,0:T(8,128)(2,1)S(1)} custom-call(s32[192]{0:T(256)S(1)} %reshape.157.starts_ref, f32[24,512]{1,0:T(8,128)S(1)} %copy-done.3, bf16[1536,128]{1,0:T(8,128)(2,1)S(1)} %collective-permute-done.12.q_ref, bf16[2,1536,128]{2,1,0:T(8,128)(2,1)S(1)} %get-tuple-element.108.refs_0_, ...), custom_call_target="tpu_custom_call" | custom-call | flops 115000000 | tf_op jit(solution)/shard_map/guest_attention/pallas_call | solution.py:220
  153.1 1.8 collective-permute-done.25.message_ref
  155.5 3.3 %home_attention.7 = (f32[1536,128]{1,0:T(8,128)S(1)}, f32[1,32,128]{2,1,0:T(8,128)S(1)}) custom-call(s32[192]{0:T(256)S(1)} %reshape.154.starts_ref, f32[24,512]{1,0:T(8,128)S(1)} %copy-done.2, bf16[1536,128]{1,0:T(8,128)(2,1)S(1)} %get-tuple-element.124.q_ref, bf16[2,1536,128]{2,1,0:T(8,128)(2,1)S(1)} %get-tuple-element.108.refs_0_, ...), custom_call_target="tpu_custom_call" | custom-call | tf_op jit(solution)/shard_map/home_attention/pallas_call | solution.py:242
  158.8 1.0 merge_halves.6.refs_0_
  159.7 1.6 collective-permute-start.27
  161.3 5.4 %first_terms.1.sum_ref = f32[1536,1024]{1,0:T(8,128)S(1)} custom-call(bf16[1024,1024]{1,0:T(8,128)(2,1)S(1)} %bitcast.5, bf16[1536,128]{1,0:T(8,128)(2,1)S(1)} %merge_halves.4.refs_0_, bf16[1536,128]{1,0:T(8,128)(2,1)S(1)} %collective-permute-done.18.refs_1_, bf16[1536,128]{1,0:T(8,128)(2,1)S(1)} %collective-permute-done.17.refs_2_, ...), custom_call_target="tpu_custom_call" | custom-call | tf_op jit(solution)/shard_map/first_terms/pallas_call | solution.py:329
  166.7 7.9 %collective-permute-done.28.message_ref = bf16[1632,128]{1,0:T(8,128)(2,1)S(1)} collective-permute-done((bf16[1632,128]{1,0:T(8,128)(2,1)S(1)}, bf16[1632,128]{1,0:T(8,128)(2,1)S(1)}, u32[]{:S(2)}, u32[]{:S(2)}) %collective-permute-start.28) | collective-permute-done | bytes 417824 | tf_op jit(solution)/shard_map/ppermute | solution.py:441
  174.6 1.0 merge_halves.7
  175.6 1.6 collective-permute-start.33
  177.7 6.2 %collective-permute-done.33.refs_6_ = bf16[1024,128]{1,0:T(8,128)(2,1)S(1)} collective-permute-done((bf16[1024,128]{1,0:T(8,128)(2,1)S(1)}, bf16[1024,128]{1,0:T(8,128)(2,1)S(1)}, u32[]{:S(2)}, u32[]{:S(2)}) %collective-permute-start.33) | collective-permute-done | bytes 262176 | tf_op jit(solution)/shard_map/ppermute | solution.py:449
  184.4 1.5 collective-permute-start.31
  185.9 3.8 %last_terms.2.refs_8_ = bf16[1536,1024]{1,0:T(8,128)(2,1)} custom-call(bf16[1024,1024]{1,0:T(8,128)(2,1)S(1)} %bitcast.6, f32[1536,1024]{1,0:T(8,128)S(1)} %first_terms.1.sum_ref, bf16[1536,128]{1,0:T(8,128)(2,1)S(1)} %merge_halves.6.refs_0_, bf16[1536,128]{1,0:T(8,128)(2,1)S(1)} %collective-permute-done.26.refs_1_, ...), custom_call_target="tpu_custom_call" | custom-call | flops 4600000000 | tf_op jit(solution)/shard_map/last_terms/pallas_call | solution.py:285
  189.8 1.3 collective-permute-done.35.refs_7_
  191.1 2.2 %last_terms.3 = bf16[1536,1024]{1,0:T(8,128)(2,1)} custom-call(bf16[1024,1024]{1,0:T(8,128)(2,1)S(1)} %bitcast.7, f32[1536,1024]{1,0:T(8,128)S(1)} %first_terms.1.sum_ref, bf16[1536,128]{1,0:T(8,128)(2,1)S(1)} %merge_halves.6.refs_0_, bf16[1536,128]{1,0:T(8,128)(2,1)S(1)} %collective-permute-done.26.refs_1_, ...), custom_call_target="tpu_custom_call", output_to_operand_aliasing={{}: (10, {})} | custom-call | flops 4600000000 | tf_op jit(solution)/shard_map/last_terms/pallas_call | solution.py:285
  (104 shorter events, 15.7 us)
Async XLA Ops:
  0.0 15.1 %copy-start.6 = (bf16[1536,512]{1,0:T(8,128)(2,1)S(1)}, bf16[1536,512]{1,0:T(8,128)(2,1)}, u32[]{:S(2)}) copy-start(bf16[1536,512]{1,0:T(8,128)(2,1)} %param.5) | copy-start | bytes 4718596
  1.3 20.7 %collective-permute-start.1 = (bf16[2,1536,128]{2,1,0:T(8,128)(2,1)S(1)}, bf16[2,1536,128]{2,1,0:T(8,128)(2,1)}, u32[]{:S(2)}, u32[]{:S(2)}) collective-permute-start(bf16[2,1536,128]{2,1,0:T(8,128)(2,1)S(1)} %slice.24.refs_0_), channel_id=1, source_target_pairs={{0,8},{4,12},{8,0},{12,4},{16,24},{20,28},{24,16},{28,20},{1,9},{5... | collective-permute-start | bytes 2359304 | tf_op jit(solution)/shard_map/ppermute | solution.py:441
  4.4 19.1 %collective-permute-start = (bf16[2,1536,128]{2,1,0:T(8,128)(2,1)S(1)}, bf16[2,1536,128]{2,1,0:T(8,128)(2,1)}, u32[]{:S(2)}, u32[]{:S(2)}) collective-permute-start(bf16[2,1536,128]{2,1,0:T(8,128)(2,1)S(1)} %slice.24.refs_0_), channel_id=1, source_target_pairs={{0,4},{4,0},{8,12},{12,8},{16,20},{20,16},{24,28},{28,24},{1,5},{5... | collective-permute-start | bytes 2359304 | tf_op jit(solution)/shard_map/ppermute | solution.py:441
  15.1 2.7 %copy-start.5 = (bf16[2,1536,512]{2,1,0:T(8,128)(2,1)S(1)}, bf16[2,1536,512]{2,1,0:T(8,128)(2,1)}, u32[]{:S(2)}) copy-start(bf16[2,1536,512]{2,1,0:T(8,128)(2,1)} %param.6) | copy-start | bytes 9437188
  23.5 28.6 %collective-permute-start.3 = (bf16[2,1536,128]{2,1,0:T(8,128)(2,1)}, bf16[2,1536,128]{2,1,0:T(8,128)(2,1)}, u32[]{:S(2)}, u32[]{:S(2)}) collective-permute-start(bf16[2,1536,128]{2,1,0:T(8,128)(2,1)} %collective-permute-done.1.refs_2_), channel_id=1, source_target_pairs={{0,4},{4,0},{8,12},{12,8},{16,20},{20,16},{24,28},{28,24},{1,5},{5... | collective-permute-start | bytes 2359304 | tf_op jit(solution)/shard_map/ppermute | solution.py:441
  25.0 34.8 %collective-permute-start.5 = (bf16[2,1536,128]{2,1,0:T(8,128)(2,1)S(1)}, bf16[2,1536,128]{2,1,0:T(8,128)(2,1)}, u32[]{:S(2)}, u32[]{:S(2)}) collective-permute-start(bf16[2,1536,128]{2,1,0:T(8,128)(2,1)S(1)} %get-tuple-element.79.refs_0_), channel_id=1, source_target_pairs={{0,8},{4,12},{8,0},{12,4},{16,24},{20,28},{24,16},{28,20},{1,9},{5... | collective-permute-start | bytes 2359304 | tf_op jit(solution)/shard_map/ppermute | solution.py:441
  25.5 34.3 %collective-permute-start.4 = (bf16[2,1536,128]{2,1,0:T(8,128)(2,1)S(1)}, bf16[2,1536,128]{2,1,0:T(8,128)(2,1)}, u32[]{:S(2)}, u32[]{:S(2)}) collective-permute-start(bf16[2,1536,128]{2,1,0:T(8,128)(2,1)S(1)} %get-tuple-element.79.refs_0_), channel_id=1, source_target_pairs={{0,4},{4,0},{8,12},{12,8},{16,20},{20,16},{24,28},{28,24},{1,5},{5... | collective-permute-start | bytes 2359304 | tf_op jit(solution)/shard_map/ppermute | solution.py:441
  25.9 26.2 %collective-permute-start.2 = (bf16[1536,128]{1,0:T(8,128)(2,1)}, bf16[1536,128]{1,0:T(8,128)(2,1)}, u32[]{:S(2)}, u32[]{:S(2)}) collective-permute-start(bf16[1536,128]{1,0:T(8,128)(2,1)} %get-tuple-element.93.q_ref), channel_id=1, source_target_pairs={{0,16},{4,20},{8,24},{12,28},{16,0},{20,4},{24,8},{28,12},{1,17},{... | collective-permute-start | bytes 1179656 | tf_op jit(solution)/shard_map/ppermute | solution.py:441
  28.6 29.4 %collective-permute-start.6 = (bf16[1536,128]{1,0:T(8,128)(2,1)}, bf16[1536,128]{1,0:T(8,128)(2,1)}, u32[]{:S(2)}, u32[]{:S(2)}) collective-permute-start(bf16[1536,128]{1,0:T(8,128)(2,1)} %get-tuple-element.102.q_ref), channel_id=1, source_target_pairs={{0,16},{4,20},{8,24},{12,28},{16,0},{20,4},{24,8},{28,12},{1,17},{... | collective-permute-start | bytes 1179656 | tf_op jit(solution)/shard_map/ppermute | solution.py:441
  28.8 2.2 %copy-start = (bf16[2048,1024]{1,0:T(8,128)(2,1)S(1)}, bf16[2048,1024]{1,0:T(8,128)(2,1)}, u32[]{:S(2)}) copy-start(bf16[2048,1024]{1,0:T(8,128)(2,1)} %param.9) | copy-start | bytes 12582916
  31.0 21.0 %copy-start.3 = (f32[24,512]{1,0:T(8,128)S(1)}, f32[24,512]{1,0:T(8,128)}, u32[]{:S(2)}) copy-start(f32[24,512]{1,0:T(8,128)} %reshape.156.bias_ref) | copy-start | bytes 147460
  31.0 36.5 %copy-start.1 = (bf16[1536,128]{1,0:T(8,128)(2,1)S(1)}, bf16[1536,128]{1,0:T(8,128)(2,1)}, u32[]{:S(2)}) copy-start(bf16[1536,128]{1,0:T(8,128)(2,1)} %get-tuple-element.116.q_ref) | copy-start | bytes 1179652
  31.0 36.6 %copy-start.2 = (f32[24,512]{1,0:T(8,128)S(1)}, f32[24,512]{1,0:T(8,128)}, u32[]{:S(2)}) copy-start(f32[24,512]{1,0:T(8,128)} %reshape.153.bias_ref) | copy-start | bytes 147460
  59.8 39.5 %collective-permute-start.8 = (bf16[2,1536,128]{2,1,0:T(8,128)(2,1)}, bf16[2,1536,128]{2,1,0:T(8,128)(2,1)S(1)}, u32[]{:S(2)}, u32[]{:S(2)}) collective-permute-start(bf16[2,1536,128]{2,1,0:T(8,128)(2,1)} %collective-permute-done.5.refs_2_), channel_id=1, source_target_pairs={{0,4},{4,0},{8,12},{12,8},{16,20},{20,16},{24,28},{28,24},{1,5},{5... | collective-permute-start | bytes 2359304 | tf_op jit(solution)/shard_map/ppermute | solution.py:441
  63.1 41.1 %collective-permute-start.10 = (bf16[2,1536,128]{2,1,0:T(8,128)(2,1)S(1)}, bf16[2,1536,128]{2,1,0:T(8,128)(2,1)S(1)}, u32[]{:S(2)}, u32[]{:S(2)}) collective-permute-start(bf16[2,1536,128]{2,1,0:T(8,128)(2,1)S(1)} %get-tuple-element.99.refs_0_), channel_id=1, source_target_pairs={{0,8},{4,12},{8,0},{12,4},{16,24},{20,28},{24,16},{28,20},{1,9},{5... | collective-permute-start | bytes 2359304 | tf_op jit(solution)/shard_map/ppermute | solution.py:441
  63.7 40.5 %collective-permute-start.9 = (bf16[2,1536,128]{2,1,0:T(8,128)(2,1)S(1)}, bf16[2,1536,128]{2,1,0:T(8,128)(2,1)S(1)}, u32[]{:S(2)}, u32[]{:S(2)}) collective-permute-start(bf16[2,1536,128]{2,1,0:T(8,128)(2,1)S(1)} %get-tuple-element.99.refs_0_), channel_id=1, source_target_pairs={{0,4},{4,0},{8,12},{12,8},{16,20},{20,16},{24,28},{28,24},{1,5},{5... | collective-permute-start | bytes 2359304 | tf_op jit(solution)/shard_map/ppermute | solution.py:441
  64.4 39.7 %collective-permute-start.11 = (bf16[1632,128]{1,0:T(8,128)(2,1)S(1)}, bf16[1632,128]{1,0:T(8,128)(2,1)S(1)}, u32[]{:S(2)}, u32[]{:S(2)}) collective-permute-start(bf16[1632,128]{1,0:T(8,128)(2,1)S(1)} %guest_attention.4), channel_id=1, source_target_pairs={{0,16},{4,20},{8,24},{12,28},{16,0},{20,4},{24,8},{28,12},{1,17},{... | collective-permute-start | bytes 1253384 | tf_op jit(solution)/shard_map/ppermute | solution.py:441
  67.6 31.8 %collective-permute-start.7 = (bf16[1536,128]{1,0:T(8,128)(2,1)S(1)}, bf16[1536,128]{1,0:T(8,128)(2,1)S(1)}, u32[]{:S(2)}, u32[]{:S(2)}) collective-permute-start(bf16[1536,128]{1,0:T(8,128)(2,1)S(1)} %copy-done.1), channel_id=1, source_target_pairs={{0,16},{4,20},{8,24},{12,28},{16,0},{20,4},{24,8},{28,12},{1,17},{... | collective-permute-start | bytes 1179656 | tf_op jit(solution)/shard_map/ppermute | solution.py:441
  104.2 19.7 %collective-permute-start.13 = (bf16[2,1536,128]{2,1,0:T(8,128)(2,1)S(1)}, bf16[2,1536,128]{2,1,0:T(8,128)(2,1)S(1)}, u32[]{:S(2)}, u32[]{:S(2)}) collective-permute-start(bf16[2,1536,128]{2,1,0:T(8,128)(2,1)S(1)} %collective-permute-done.10.refs_2_), channel_id=1, source_target_pairs={{0,4},{4,0},{8,12},{12,8},{16,20},{20,16},{24,28},{28,24},{1,5},{5... | collective-permute-start | bytes 2359304 | tf_op jit(solution)/shard_map/ppermute | solution.py:441
  105.7 18.1 %collective-permute-start.12 = (bf16[1536,128]{1,0:T(8,128)(2,1)S(1)}, bf16[1536,128]{1,0:T(8,128)(2,1)S(1)}, u32[]{:S(2)}, u32[]{:S(2)}) collective-permute-start(bf16[1536,128]{1,0:T(8,128)(2,1)S(1)} %get-tuple-element.124.q_ref), channel_id=1, source_target_pairs={{0,16},{4,20},{8,24},{12,28},{16,0},{20,4},{24,8},{28,12},{1,17},{... | collective-permute-start | bytes 1179656 | tf_op jit(solution)/shard_map/ppermute | solution.py:441
  105.7 29.6 %collective-permute-start.15 = (bf16[2,1536,128]{2,1,0:T(8,128)(2,1)S(1)}, bf16[2,1536,128]{2,1,0:T(8,128)(2,1)S(1)}, u32[]{:S(2)}, u32[]{:S(2)}) collective-permute-start(bf16[2,1536,128]{2,1,0:T(8,128)(2,1)S(1)} %get-tuple-element.108.refs_0_), channel_id=1, source_target_pairs={{0,8},{4,12},{8,0},{12,4},{16,24},{20,28},{24,16},{28,20},{1,9},{5... | collective-permute-start | bytes 2359304 | tf_op jit(solution)/shard_map/ppermute | solution.py:441
  108.7 26.7 %collective-permute-start.14 = (bf16[2,1536,128]{2,1,0:T(8,128)(2,1)S(1)}, bf16[2,1536,128]{2,1,0:T(8,128)(2,1)S(1)}, u32[]{:S(2)}, u32[]{:S(2)}) collective-permute-start(bf16[2,1536,128]{2,1,0:T(8,128)(2,1)S(1)} %get-tuple-element.108.refs_0_), channel_id=1, source_target_pairs={{0,4},{4,0},{8,12},{12,8},{16,20},{20,16},{24,28},{28,24},{1,5},{5... | collective-permute-start | bytes 2359304 | tf_op jit(solution)/shard_map/ppermute | solution.py:441
  109.1 26.3 %collective-permute-start.16 = (bf16[1632,128]{1,0:T(8,128)(2,1)S(1)}, bf16[1632,128]{1,0:T(8,128)(2,1)S(1)}, u32[]{:S(2)}, u32[]{:S(2)}) collective-permute-start(bf16[1632,128]{1,0:T(8,128)(2,1)S(1)} %guest_attention.5), channel_id=1, source_target_pairs={{0,16},{4,20},{8,24},{12,28},{16,0},{20,4},{24,8},{28,12},{1,17},{... | collective-permute-start | bytes 1253384 | tf_op jit(solution)/shard_map/ppermute | solution.py:441
  114.0 24.0 %copy-start.4 = (s32[24]{0:T(128)S(1)}, s32[24]{0:T(128)}, u32[]{:S(2)}) copy-start(s32[24]{0:T(128)} %select_reduce_fusion.2.order_ref) | copy-start | bytes 292
  123.9 4.6 %collective-permute-start.18 = (bf16[1536,128]{1,0:T(8,128)(2,1)S(1)}, bf16[1536,128]{1,0:T(8,128)(2,1)S(1)}, u32[]{:S(2)}, u32[]{:S(2)}) collective-permute-start(bf16[1536,128]{1,0:T(8,128)(2,1)S(1)} %merge_halves.4.refs_0_), channel_id=1, source_target_pairs={{0,1},{1,0},{2,3},{3,2},{4,5},{5,4},{6,7},{7,6},{8,9},{9,8},{10,11... | collective-permute-start | bytes 1179656 | tf_op jit(solution)/shard_map/ppermute | solution.py:449
  123.9 11.5 %collective-permute-start.17 = (bf16[1536,128]{1,0:T(8,128)(2,1)S(1)}, bf16[1536,128]{1,0:T(8,128)(2,1)S(1)}, u32[]{:S(2)}, u32[]{:S(2)}) collective-permute-start(bf16[1536,128]{1,0:T(8,128)(2,1)S(1)} %merge_halves.4.refs_0_), channel_id=1, source_target_pairs={{0,2},{1,3},{2,0},{3,1},{4,6},{5,7},{6,4},{7,5},{8,10},{9,11},{10,... | collective-permute-start | bytes 1179656 | tf_op jit(solution)/shard_map/ppermute | solution.py:449
  135.4 19.5 %collective-permute-start.25 = (bf16[1632,128]{1,0:T(8,128)(2,1)S(1)}, bf16[1632,128]{1,0:T(8,128)(2,1)S(1)}, u32[]{:S(2)}, u32[]{:S(2)}) collective-permute-start(bf16[1632,128]{1,0:T(8,128)(2,1)S(1)} %guest_attention.6), channel_id=1, source_target_pairs={{0,16},{4,20},{8,24},{12,28},{16,0},{20,4},{24,8},{28,12},{1,17},{... | collective-permute-start | bytes 1253384 | tf_op jit(solution)/shard_map/ppermute | solution.py:441
  138.7 11.2 %collective-permute-start.19 = (bf16[2,768,128]{2,1,0:T(8,128)(2,1)S(1)}, bf16[2,768,128]{2,1,0:T(8,128)(2,1)S(1)}, u32[]{:S(2)}, u32[]{:S(2)}) collective-permute-start(bf16[2,768,128]{2,1,0:T(8,128)(2,1)S(1)} %get-tuple-element.123), channel_id=1, source_target_pairs={{0,4},{4,0},{8,12},{12,8},{16,20},{20,16},{24,28},{28,24},{1,5},{5... | collective-permute-start | bytes 1179656 | tf_op jit(solution)/shard_map/ppermute | solution.py:441
  143.7 11.8 %collective-permute-start.23 = (bf16[1536,128]{1,0:T(8,128)(2,1)S(1)}, bf16[1536,128]{1,0:T(8,128)(2,1)S(1)}, u32[]{:S(2)}, u32[]{:S(2)}) collective-permute-start(bf16[1536,128]{1,0:T(8,128)(2,1)S(1)} %merge_halves.5.refs_4_), channel_id=1, source_target_pairs={{0,2},{1,3},{2,0},{3,1},{4,6},{5,7},{6,4},{7,5},{8,10},{9,11},{10,... | collective-permute-start | bytes 1179656 | tf_op jit(solution)/shard_map/ppermute | solution.py:449
  145.2 10.3 %collective-permute-start.20 = (bf16[2,768,128]{2,1,0:T(8,128)(2,1)S(1)}, bf16[2,768,128]{2,1,0:T(8,128)(2,1)S(1)}, u32[]{:S(2)}, u32[]{:S(2)}) collective-permute-start(bf16[2,768,128]{2,1,0:T(8,128)(2,1)S(1)} %get-tuple-element.125), channel_id=1, source_target_pairs={{0,4},{4,0},{8,12},{12,8},{16,20},{20,16},{24,28},{28,24},{1,5},{5... | collective-permute-start | bytes 1179656 | tf_op jit(solution)/shard_map/ppermute | solution.py:441
  154.9 19.7 %collective-permute-start.28 = (bf16[1632,128]{1,0:T(8,128)(2,1)S(1)}, bf16[1632,128]{1,0:T(8,128)(2,1)S(1)}, u32[]{:S(2)}, u32[]{:S(2)}) collective-permute-start(bf16[1632,128]{1,0:T(8,128)(2,1)S(1)} %guest_attention.7), channel_id=1, source_target_pairs={{0,16},{4,20},{8,24},{12,28},{16,0},{20,4},{24,8},{28,12},{1,17},{... | collective-permute-start | bytes 1253384 | tf_op jit(solution)/shard_map/ppermute | solution.py:441
  154.9 6.4 %collective-permute-start.22 = (bf16[1536,128]{1,0:T(8,128)(2,1)S(1)}, bf16[1536,128]{1,0:T(8,128)(2,1)S(1)}, u32[]{:S(2)}, u32[]{:S(2)}) collective-permute-start(bf16[1536,128]{1,0:T(8,128)(2,1)S(1)} %merge_halves.5.refs_4_), channel_id=1, source_target_pairs={{0,1},{1,0},{2,3},{3,2},{4,5},{5,4},{6,7},{7,6},{8,9},{9,8},{10,11... | collective-permute-start | bytes 1179656 | tf_op jit(solution)/shard_map/ppermute | solution.py:449
  154.9 6.4 %collective-permute-start.21 = (bf16[1536,128]{1,0:T(8,128)(2,1)S(1)}, bf16[1536,128]{1,0:T(8,128)(2,1)S(1)}, u32[]{:S(2)}, u32[]{:S(2)}) collective-permute-start(bf16[1536,128]{1,0:T(8,128)(2,1)S(1)} %collective-permute-done.17.refs_2_), channel_id=1, source_target_pairs={{0,1},{1,0},{2,3},{3,2},{4,5},{5,4},{6,7},{7,6},{8,9},{9,8},{10,11... | collective-permute-start | bytes 1179656 | tf_op jit(solution)/shard_map/ppermute | solution.py:449
  155.4 5.9 %collective-permute-start.24 = (bf16[1536,128]{1,0:T(8,128)(2,1)S(1)}, bf16[1536,128]{1,0:T(8,128)(2,1)S(1)}, u32[]{:S(2)}, u32[]{:S(2)}) collective-permute-start(bf16[1536,128]{1,0:T(8,128)(2,1)S(1)} %collective-permute-done.23.refs_6_), channel_id=1, source_target_pairs={{0,1},{1,0},{2,3},{3,2},{4,5},{5,4},{6,7},{7,6},{8,9},{9,8},{10,11... | collective-permute-start | bytes 1179656 | tf_op jit(solution)/shard_map/ppermute | solution.py:449
  159.7 17.4 %collective-permute-start.27 = (bf16[1536,128]{1,0:T(8,128)(2,1)S(1)}, bf16[1536,128]{1,0:T(8,128)(2,1)S(1)}, u32[]{:S(2)}, u32[]{:S(2)}) collective-permute-start(bf16[1536,128]{1,0:T(8,128)(2,1)S(1)} %merge_halves.6.refs_0_), channel_id=1, source_target_pairs={{0,2},{1,3},{2,0},{3,1},{4,6},{5,7},{6,4},{7,5},{8,10},{9,11},{10,... | collective-permute-start | bytes 1179656 | tf_op jit(solution)/shard_map/ppermute | solution.py:449
  175.6 8.3 %collective-permute-start.33 = (bf16[1024,128]{1,0:T(8,128)(2,1)S(1)}, bf16[1024,128]{1,0:T(8,128)(2,1)S(1)}, u32[]{:S(2)}, u32[]{:S(2)}) collective-permute-start(bf16[1024,128]{1,0:T(8,128)(2,1)S(1)} %get-tuple-element.138.refs_4_), channel_id=1, source_target_pairs={{0,2},{1,3},{2,0},{3,1},{4,6},{5,7},{6,4},{7,5},{8,10},{9,11},{10,... | collective-permute-start | bytes 786440 | tf_op jit(solution)/shard_map/ppermute | solution.py:449
  177.2 7.2 %collective-permute-start.26 = (bf16[1536,128]{1,0:T(8,128)(2,1)S(1)}, bf16[1536,128]{1,0:T(8,128)(2,1)S(1)}, u32[]{:S(2)}, u32[]{:S(2)}) collective-permute-start(bf16[1536,128]{1,0:T(8,128)(2,1)S(1)} %merge_halves.6.refs_0_), channel_id=1, source_target_pairs={{0,1},{1,0},{2,3},{3,2},{4,5},{5,4},{6,7},{7,6},{8,9},{9,8},{10,11... | collective-permute-start | bytes 1179656 | tf_op jit(solution)/shard_map/ppermute | solution.py:449
  177.2 8.7 %collective-permute-start.29 = (bf16[1536,128]{1,0:T(8,128)(2,1)S(1)}, bf16[1536,128]{1,0:T(8,128)(2,1)S(1)}, u32[]{:S(2)}, u32[]{:S(2)}) collective-permute-start(bf16[1536,128]{1,0:T(8,128)(2,1)S(1)} %collective-permute-done.27.refs_2_), channel_id=1, source_target_pairs={{0,1},{1,0},{2,3},{3,2},{4,5},{5,4},{6,7},{7,6},{8,9},{9,8},{10,11... | collective-permute-start | bytes 1179656 | tf_op jit(solution)/shard_map/ppermute | solution.py:449
  177.7 8.2 %collective-permute-start.32 = (bf16[1024,128]{1,0:T(8,128)(2,1)S(1)}, bf16[1024,128]{1,0:T(8,128)(2,1)S(1)}, u32[]{:S(2)}, u32[]{:S(2)}) collective-permute-start(bf16[1024,128]{1,0:T(8,128)(2,1)S(1)} %get-tuple-element.138.refs_4_), channel_id=1, source_target_pairs={{0,1},{1,0},{2,3},{3,2},{4,5},{5,4},{6,7},{7,6},{8,9},{9,8},{10,11... | collective-permute-start | bytes 786440 | tf_op jit(solution)/shard_map/ppermute | solution.py:449
  183.9 2.1 %collective-permute-start.34 = (bf16[1024,128]{1,0:T(8,128)(2,1)S(1)}, bf16[1024,128]{1,0:T(8,128)(2,1)S(1)}, u32[]{:S(2)}, u32[]{:S(2)}) collective-permute-start(bf16[1024,128]{1,0:T(8,128)(2,1)S(1)} %collective-permute-done.33.refs_6_), channel_id=1, source_target_pairs={{0,1},{1,0},{2,3},{3,2},{4,5},{5,4},{6,7},{7,6},{8,9},{9,8},{10,11... | collective-permute-start | bytes 786440 | tf_op jit(solution)/shard_map/ppermute | solution.py:449
  183.9 5.9 %collective-permute-start.30 = (bf16[512,128]{1,0:T(8,128)(2,1)S(1)}, bf16[512,128]{1,0:T(8,128)(2,1)S(1)}, u32[]{:S(2)}, u32[]{:S(2)}) collective-permute-start(bf16[512,128]{1,0:T(8,128)(2,1)S(1)} %get-tuple-element.139.refs_4_), channel_id=1, source_target_pairs={{0,1},{1,0},{2,3},{3,2},{4,5},{5,4},{6,7},{7,6},{8,9},{9,8},{10,11... | collective-permute-start | bytes 393224 | tf_op jit(solution)/shard_map/ppermute | solution.py:449
  184.4 5.4 %collective-permute-start.31 = (bf16[512,128]{1,0:T(8,128)(2,1)S(1)}, bf16[512,128]{1,0:T(8,128)(2,1)S(1)}, u32[]{:S(2)}, u32[]{:S(2)}) collective-permute-start(bf16[512,128]{1,0:T(8,128)(2,1)S(1)} %get-tuple-element.139.refs_4_), channel_id=1, source_target_pairs={{0,2},{1,3},{2,0},{3,1},{4,6},{5,7},{6,4},{7,5},{8,10},{9,11},{10,... | collective-permute-start | bytes 393224 | tf_op jit(solution)/shard_map/ppermute | solution.py:449
  189.8 1.3 collective-permute-start.35

commit v6 on v5

--- a/solution.py
+++ b/solution.py
@@ -15,7 +15,7 @@
 MASKED = -1e30
 EXP2_SCALE = 1.4426950408889634 / HEAD_DIM**0.5
 STAT_TILE = 16
-VMEM_LIMIT = 14 * 1024 * 1024
+VMEM_LIMIT = 20 * 1024 * 1024
 PROJECT_LIMIT = 32 * 1024 * 1024
 
 
@@ -453,7 +453,7 @@
     return lax.optimization_barrier(values)
 
 
-UNROLL = 8
+UNROLL = 12
 GUEST_US = 0.1
 PROJECT_US = 4
 UPPER_TILES = 4
@@ -504,25 +504,25 @@
     d0, y1, z1, v0, v1 = over_y(z0), over_y(k1_), over_z(k1_), across(v0), across(v1)
     p0 = (k0, y0, z0, d0)
     (s0,) = guest_call(*guest[:2], v0, p0)
-    s0, y1, z1, v1, k2_, v2, weights = together(s0, y1, z1, v1, k2, q2, weights)
+    t0, y1, z1, v1, k2_, v2, weights = together(s0, y1, z1, v1, k2, q2, weights)
 
     d1, y2, z2, v2, g0 = over_y(z1), over_y(k2_), over_z(k2_), across(v2), across(s0)
-    m0 = home_call(*home[:2], after(q0, s0), p0)
+    m0 = home_call(*home[:2], after(q0, t0), p0)
     p1 = (k1, y1, z1, d1)
     (s1,) = guest_call(*guest[:2], after(v1, m0[1], v2), p1)
-    s1, y2, z2, v2, g0, k3_, v3 = together(s1, y2, z2, v2, g0, k3, q3)
+    t1, y2, z2, v2, g0, k3_, v3 = together(s1, y2, z2, v2, g0, k3, q3)
 
     d2, y3, z3, v3, g1 = over_y(z2), over_y(k3_), over_z(k3_), across(v3), across(s1)
-    m1 = home_call(*home[:2], after(q1, s1), p1)
+    m1 = home_call(*home[:2], after(q1, t1), p1)
     (a0,) = merge_call(*m0, after(g0, m1[1]))
     a0x, a0c = hop(a0, 2, groups), hop(a0, 1, groups)
     p2 = (k2, y2, z2, d2)
     (s2,) = guest_call(*guest[:2], after(v2, m1[1], v3), p2)
-    s2, y3, z3, v3, g1, a0x, a0c = together(s2, y3, z3, v3, g1, a0x, a0c)
+    t2, y3, z3, v3, g1, a0x, a0c = together(s2, y3, z3, v3, g1, a0x, a0c)
 
     first, rest = split_call(home[4], z3)
     d3, d3_, g2 = over_y(first), over_y(rest), across(s2)
-    m2 = home_call(*home[:2], after(q2, s2), p2)
+    m2 = home_call(*home[:2], after(q2, t2), p2)
     (a1,) = merge_call(*m1, after(g1, m2[1]))
     a1x, a1c, a0d = hop(a1, 2, groups), hop(a1, 1, groups), hop(a0x, 1, groups)
     (s3,) = guest_call(*guest[2:4], after(v3, a1), (k3, y3, z3, d3))

time: 194 us -> 192 us (0.990)
  waiting for transfers between devices: 91.8 us -> 96.3 us
  Pallas kernels: 48.8 us -> 45.4 us
  starting transfers between devices: 36.7 us -> 34.2 us
    ppermute x21, waiting for transfers between devices: 77.3 us -> 82.1 us  [swap(): lax.ppermute(value, 'seq', [(i, i ^ distance) for i in range(shards)])]
    ppermute x21, starting transfers between devices: 27.5 us -> 25.4 us  [swap(): lax.ppermute(value, 'seq', [(i, i ^ distance) for i in range(shards)])]
  transfers between devices with their start and end apart: 36 -> 36, of which waited for: 14 -> 14; matrix products, arithmetic and copies ran while one was open for 6% -> 6% of each run, Pallas kernels for 24% -> 23%
where the time goes in v6:
time: 192 us
  waiting for transfers between devices  96.3 us (50%)
  Pallas kernels  45.4 us (24%)
  starting transfers between devices  34.2 us (18%)
  local copies, waits for them, and re-layouts  9.37 us (5%)
  other arithmetic  6.31 us (3%)
    ppermute x21, waiting for transfers between devices, swap(): lax.ppermute(value, 'seq', [(i, i ^ distance) for i in range(shards)])  82.1 us
    ppermute x21, starting transfers between devices, swap(): lax.ppermute(value, 'seq', [(i, i ^ distance) for i in range(shards)])  25.4 us
    pallas_call x4, Pallas kernels, home_call(): pl.pallas_call(functools.partial(home_kernel, parts, len(pieces)), out_sh...  14.6 us
    pallas_call x4, Pallas kernels, guest_call(): pl.pallas_call(functools.partial(guest_kernel, parts, len(pieces)), out_s...  14.6 us
    ppermute x15, waiting for transfers between devices, hop(): lax.ppermute(value, 'head', [(i, i ^ distance) for i in range(groups)])  14.2 us
    ppermute x15, starting transfers between devices, hop(): lax.ppermute(value, 'head', [(i, i ^ distance) for i in range(groups)])  8.81 us
    pallas_call x2, Pallas kernels, last_terms(): pl.pallas_call(functools.partial(last_terms_kernel, len(pieces) // 2), gr...  6 us
    pallas_call x1, Pallas kernels, first_terms(): pl.pallas_call(functools.partial(first_terms_kernel, len(pieces) // 2), o...  5.36 us
  transfers between devices with their start and end apart: 36, of which 14 were waited for; matrix products, arithmetic and copies ran while one was open for 6% of the time, Pallas kernels for 23%

profile of v6, /device:TPU:0, one launch (start us, length us, event | category | flops | bytes accessed | tf_op | source)
XLA Modules:
  0.0 192.0 jit_solution(14201051315667651199)
XLA Ops:
  0.0 1.3 slice.24.refs_0_
  1.3 3.1 %collective-permute-start.1 = (bf16[2,1536,128]{2,1,0:T(8,128)(2,1)S(1)}, bf16[2,1536,128]{2,1,0:T(8,128)(2,1)}, u32[]{:S(2)}, u32[]{:S(2)}) collective-permute-start(bf16[2,1536,128]{2,1,0:T(8,128)(2,1)S(1)} %slice.24.refs_0_), channel_id=1, source_target_pairs={{0,8},{4,12},{8,0},{12,4},{16,24},{20,28},{24,16},{28,20},{1,9},{5... | collective-permute-start | bytes 2359304 | tf_op jit(solution)/shard_map/ppermute | solution.py:441
  4.4 1.5 collective-permute-start
  6.8 0.9 constant_dynamic-slice_fusion
  10.0 1.0 select_reduce_fusion
  15.1 1.2 fusion.14
  16.3 0.8 compare_select_fusion
  18.2 3.8 %collective-permute-done.1.refs_2_ = bf16[2,1536,128]{2,1,0:T(8,128)(2,1)} collective-permute-done((bf16[2,1536,128]{2,1,0:T(8,128)(2,1)S(1)}, bf16[2,1536,128]{2,1,0:T(8,128)(2,1)}, u32[]{:S(2)}, u32[]{:S(2)}) %collective-permute-start.1) | collective-permute-done | bytes 786464 | tf_op jit(solution)/shard_map/ppermute | solution.py:441
  22.0 1.5 collective-permute-done.refs_1_
  23.5 1.5 collective-permute-start.3
  25.9 2.7 %collective-permute-start.2 = (bf16[1536,128]{1,0:T(8,128)(2,1)}, bf16[1536,128]{1,0:T(8,128)(2,1)}, u32[]{:S(2)}, u32[]{:S(2)}) collective-permute-start(bf16[1536,128]{1,0:T(8,128)(2,1)} %get-tuple-element.70.q_ref), channel_id=1, source_target_pairs={{0,16},{4,20},{8,24},{12,28},{16,0},{20,4},{24,8},{28,12},{1,17},{... | collective-permute-start | bytes 1179656 | tf_op jit(solution)/shard_map/ppermute | solution.py:441
  28.8 2.2 %copy-done = bf16[2048,1024]{1,0:T(8,128)(2,1)S(1)} copy-done((bf16[2048,1024]{1,0:T(8,128)(2,1)S(1)}, bf16[2048,1024]{1,0:T(8,128)(2,1)}, u32[]{:S(2)}) %copy-start) | copy-done | bytes 4194328
  31.4 20.6 %collective-permute-done.2.q_ref = bf16[1536,128]{1,0:T(8,128)(2,1)} collective-permute-done((bf16[1536,128]{1,0:T(8,128)(2,1)}, bf16[1536,128]{1,0:T(8,128)(2,1)}, u32[]{:S(2)}, u32[]{:S(2)}) %collective-permute-start.2) | collective-permute-done | bytes 393248 | tf_op jit(solution)/shard_map/ppermute | solution.py:441
  52.1 4.7 %guest_attention.4 = bf16[1632,128]{1,0:T(8,128)(2,1)S(1)} custom-call(s32[192]{0:T(256)S(1)} %reshape.155.starts_ref, f32[24,512]{1,0:T(8,128)S(1)} %copy-done.3, bf16[1536,128]{1,0:T(8,128)(2,1)} %collective-permute-done.2.q_ref, bf16[2,1536,128]{2,1,0:T(8,128)(2,1)S(1)} %slice.24.refs_0_, bf16[2,1536,128]{2,1,0:T(8,128)(2,1)} %collective-permute-done.refs_1_, ...), custom_call_target="tpu_custom_call" | custom-call | flops 115000000 | tf_op jit(solution)/shard_map/guest_attention/pallas_call | solution.py:220
  56.7 1.2 collective-permute-done.6.q_ref
  58.0 1.8 collective-permute-done.5.refs_2_
  59.8 3.3 %collective-permute-start.8 = (bf16[2,1536,128]{2,1,0:T(8,128)(2,1)}, bf16[2,1536,128]{2,1,0:T(8,128)(2,1)S(1)}, u32[]{:S(2)}, u32[]{:S(2)}) collective-permute-start(bf16[2,1536,128]{2,1,0:T(8,128)(2,1)} %collective-permute-done.5.refs_2_), channel_id=1, source_target_pairs={{0,4},{4,0},{8,12},{12,8},{16,20},{20,16},{24,28},{28,24},{1,5},{5... | collective-permute-start | bytes 2359304 | tf_op jit(solution)/shard_map/ppermute | solution.py:441
  64.4 3.1 %collective-permute-start.11 = (bf16[1632,128]{1,0:T(8,128)(2,1)S(1)}, bf16[1632,128]{1,0:T(8,128)(2,1)S(1)}, u32[]{:S(2)}, u32[]{:S(2)}) collective-permute-start(bf16[1632,128]{1,0:T(8,128)(2,1)S(1)} %guest_attention.4), channel_id=1, source_target_pairs={{0,16},{4,20},{8,24},{12,28},{16,0},{20,4},{24,8},{28,12},{1,17},{... | collective-permute-start | bytes 1253384 | tf_op jit(solution)/shard_map/ppermute | solution.py:441
  67.6 4.6 %home_attention.4 = (f32[1536,128]{1,0:T(8,128)S(1)}, f32[1,32,128]{2,1,0:T(8,128)S(1)}) custom-call(s32[192]{0:T(256)S(1)} %reshape.152.starts_ref, f32[24,512]{1,0:T(8,128)S(1)} %copy-done.2, bf16[1536,128]{1,0:T(8,128)(2,1)} %get-tuple-element.70.q_ref, bf16[2,1536,128]{2,1,0:T(8,128)(2,1)S(1)} %slice.24.refs_0_, ...), custom_call_target="tpu_custom_call" | custom-call | tf_op jit(solution)/shard_map/home_attention/pallas_call | solution.py:242
  72.2 27.1 %collective-permute-done.7.q_ref = bf16[1536,128]{1,0:T(8,128)(2,1)S(1)} collective-permute-done((bf16[1536,128]{1,0:T(8,128)(2,1)S(1)}, bf16[1536,128]{1,0:T(8,128)(2,1)S(1)}, u32[]{:S(2)}, u32[]{:S(2)}) %collective-permute-start.7) | collective-permute-done | bytes 393248 | tf_op jit(solution)/shard_map/ppermute | solution.py:441
  99.3 4.4 %guest_attention.5 = bf16[1632,128]{1,0:T(8,128)(2,1)S(1)} custom-call(s32[192]{0:T(256)S(1)} %reshape.155.starts_ref, f32[24,512]{1,0:T(8,128)S(1)} %copy-done.3, bf16[1536,128]{1,0:T(8,128)(2,1)} %collective-permute-done.6.q_ref, bf16[2,1536,128]{2,1,0:T(8,128)(2,1)S(1)} %get-tuple-element.73.refs_0_, ...), custom_call_target="tpu_custom_call" | custom-call | flops 115000000 | tf_op jit(solution)/shard_map/guest_attention/pallas_call | solution.py:220
  103.8 1.6 collective-permute-start.13
  105.3 2.9 %collective-permute-start.15 = (bf16[2,1536,128]{2,1,0:T(8,128)(2,1)S(1)}, bf16[2,1536,128]{2,1,0:T(8,128)(2,1)S(1)}, u32[]{:S(2)}, u32[]{:S(2)}) collective-permute-start(bf16[2,1536,128]{2,1,0:T(8,128)(2,1)S(1)} %get-tuple-element.98.refs_0_), channel_id=1, source_target_pairs={{0,8},{4,12},{8,0},{12,4},{16,24},{20,28},{24,16},{28,20},{1,9},{5... | collective-permute-start | bytes 2359304 | tf_op jit(solution)/shard_map/ppermute | solution.py:441
  108.8 4.4 %home_attention.5 = (f32[1536,128]{1,0:T(8,128)S(1)}, f32[1,32,128]{2,1,0:T(8,128)S(1)}) custom-call(s32[192]{0:T(256)S(1)} %reshape.152.starts_ref, f32[24,512]{1,0:T(8,128)S(1)} %copy-done.2, bf16[1536,128]{1,0:T(8,128)(2,1)} %get-tuple-element.74.q_ref, bf16[2,1536,128]{2,1,0:T(8,128)(2,1)S(1)} %get-tuple-element.73.refs_0_, ...), custom_call_target="tpu_custom_call" | custom-call | tf_op jit(solution)/shard_map/home_attention/pallas_call | solution.py:242
  113.2 1.0 merge_halves.4.refs_0_
  114.2 9.2 %collective-permute-done.12.q_ref = bf16[1536,128]{1,0:T(8,128)(2,1)S(1)} collective-permute-done((bf16[1536,128]{1,0:T(8,128)(2,1)S(1)}, bf16[1536,128]{1,0:T(8,128)(2,1)S(1)}, u32[]{:S(2)}, u32[]{:S(2)}) %collective-permute-start.12) | collective-permute-done | bytes 393248 | tf_op jit(solution)/shard_map/ppermute | solution.py:441
  123.4 1.5 collective-permute-start.17
  124.9 2.8 %guest_attention.6 = bf16[1632,128]{1,0:T(8,128)(2,1)S(1)} custom-call(s32[192]{0:T(256)S(1)} %reshape.155.starts_ref, f32[24,512]{1,0:T(8,128)S(1)} %copy-done.3, bf16[1536,128]{1,0:T(8,128)(2,1)S(1)} %collective-permute-done.7.q_ref, bf16[2,1536,128]{2,1,0:T(8,128)(2,1)S(1)} %get-tuple-element.91.refs_0_, ...), custom_call_target="tpu_custom_call" | custom-call | flops 115000000 | tf_op jit(solution)/shard_map/guest_attention/pallas_call | solution.py:220
  128.2 6.7 %collective-permute-done.17.refs_2_ = bf16[1536,128]{1,0:T(8,128)(2,1)S(1)} collective-permute-done((bf16[1536,128]{1,0:T(8,128)(2,1)S(1)}, bf16[1536,128]{1,0:T(8,128)(2,1)S(1)}, u32[]{:S(2)}, u32[]{:S(2)}) %collective-permute-start.17) | collective-permute-done | bytes 393248 | tf_op jit(solution)/shard_map/ppermute | solution.py:449
  134.9 3.8 %collective-permute-done.16.message_ref = bf16[1632,128]{1,0:T(8,128)(2,1)S(1)} collective-permute-done((bf16[1632,128]{1,0:T(8,128)(2,1)S(1)}, bf16[1632,128]{1,0:T(8,128)(2,1)S(1)}, u32[]{:S(2)}, u32[]{:S(2)}) %collective-permute-start.16) | collective-permute-done | bytes 417824 | tf_op jit(solution)/shard_map/ppermute | solution.py:441
  139.8 2.7 %home_attention.6 = (f32[1536,128]{1,0:T(8,128)S(1)}, f32[1,32,128]{2,1,0:T(8,128)S(1)}) custom-call(s32[192]{0:T(256)S(1)} %reshape.152.starts_ref, f32[24,512]{1,0:T(8,128)S(1)} %copy-done.2, bf16[1536,128]{1,0:T(8,128)(2,1)S(1)} %copy-done.1, bf16[2,1536,128]{2,1,0:T(8,128)(2,1)S(1)} %get-tuple-element.91.refs_0_, ...), custom_call_target="tpu_custom_call" | custom-call | tf_op jit(solution)/shard_map/home_attention/pallas_call | solution.py:242
  142.6 1.0 merge_halves.5.refs_4_
  143.5 1.6 collective-permute-start.23
  145.1 1.7 collective-permute-start.20
  146.7 4.7 %collective-permute-done.19.refs_3_ = bf16[2,768,128]{2,1,0:T(8,128)(2,1)S(1)} collective-permute-done((bf16[2,768,128]{2,1,0:T(8,128)(2,1)S(1)}, bf16[2,768,128]{2,1,0:T(8,128)(2,1)S(1)}, u32[]{:S(2)}, u32[]{:S(2)}) %collective-permute-start.19) | collective-permute-done | bytes 393248 | tf_op jit(solution)/shard_map/ppermute | solution.py:441
  151.4 2.8 %guest_attention.7 = bf16[1632,128]{1,0:T(8,128)(2,1)S(1)} custom-call(s32[192]{0:T(256)S(1)} %reshape.157.starts_ref, f32[24,512]{1,0:T(8,128)S(1)} %copy-done.3, bf16[1536,128]{1,0:T(8,128)(2,1)S(1)} %collective-permute-done.12.q_ref, bf16[2,1536,128]{2,1,0:T(8,128)(2,1)S(1)} %get-tuple-element.98.refs_0_, ...), custom_call_target="tpu_custom_call" | custom-call | flops 115000000 | tf_op jit(solution)/shard_map/guest_attention/pallas_call | solution.py:220
  155.6 2.9 %home_attention.7 = (f32[1536,128]{1,0:T(8,128)S(1)}, f32[1,32,128]{2,1,0:T(8,128)S(1)}) custom-call(s32[192]{0:T(256)S(1)} %reshape.154.starts_ref, f32[24,512]{1,0:T(8,128)S(1)} %copy-done.2, bf16[1536,128]{1,0:T(8,128)(2,1)S(1)} %get-tuple-element.112.q_ref, bf16[2,1536,128]{2,1,0:T(8,128)(2,1)S(1)} %get-tuple-element.98.refs_0_, ...), custom_call_target="tpu_custom_call" | custom-call | tf_op jit(solution)/shard_map/home_attention/pallas_call | solution.py:242
  158.5 1.0 merge_halves.6.refs_0_
  159.5 0.8 collective-permute-start.27
  160.3 5.4 %first_terms.1.sum_ref = f32[1536,1024]{1,0:T(8,128)S(1)} custom-call(bf16[1024,1024]{1,0:T(8,128)(2,1)S(1)} %bitcast.5, bf16[1536,128]{1,0:T(8,128)(2,1)S(1)} %merge_halves.4.refs_0_, bf16[1536,128]{1,0:T(8,128)(2,1)S(1)} %collective-permute-done.18.refs_1_, bf16[1536,128]{1,0:T(8,128)(2,1)S(1)} %collective-permute-done.17.refs_2_, ...), custom_call_target="tpu_custom_call" | custom-call | tf_op jit(solution)/shard_map/first_terms/pallas_call | solution.py:329
  165.6 7.6 %collective-permute-done.28.message_ref = bf16[1632,128]{1,0:T(8,128)(2,1)S(1)} collective-permute-done((bf16[1632,128]{1,0:T(8,128)(2,1)S(1)}, bf16[1632,128]{1,0:T(8,128)(2,1)S(1)}, u32[]{:S(2)}, u32[]{:S(2)}) %collective-permute-start.28) | collective-permute-done | bytes 417824 | tf_op jit(solution)/shard_map/ppermute | solution.py:441
  173.2 1.0 merge_halves.7
  174.2 1.7 collective-permute-start.33
  176.4 6.1 %collective-permute-done.33.refs_6_ = bf16[1024,128]{1,0:T(8,128)(2,1)S(1)} collective-permute-done((bf16[1024,128]{1,0:T(8,128)(2,1)S(1)}, bf16[1024,128]{1,0:T(8,128)(2,1)S(1)}, u32[]{:S(2)}, u32[]{:S(2)}) %collective-permute-start.33) | collective-permute-done | bytes 262176 | tf_op jit(solution)/shard_map/ppermute | solution.py:449
  183.0 1.6 collective-permute-start.31
  184.6 3.8 %last_terms.2.refs_8_ = bf16[1536,1024]{1,0:T(8,128)(2,1)} custom-call(bf16[1024,1024]{1,0:T(8,128)(2,1)S(1)} %bitcast.6, f32[1536,1024]{1,0:T(8,128)S(1)} %first_terms.1.sum_ref, bf16[1536,128]{1,0:T(8,128)(2,1)S(1)} %merge_halves.6.refs_0_, bf16[1536,128]{1,0:T(8,128)(2,1)S(1)} %collective-permute-done.26.refs_1_, ...), custom_call_target="tpu_custom_call" | custom-call | flops 4600000000 | tf_op jit(solution)/shard_map/last_terms/pallas_call | solution.py:285
  188.4 1.3 collective-permute-done.35.refs_7_
  189.7 2.2 %last_terms.3 = bf16[1536,1024]{1,0:T(8,128)(2,1)} custom-call(bf16[1024,1024]{1,0:T(8,128)(2,1)S(1)} %bitcast.7, f32[1536,1024]{1,0:T(8,128)S(1)} %first_terms.1.sum_ref, bf16[1536,128]{1,0:T(8,128)(2,1)S(1)} %merge_halves.6.refs_0_, bf16[1536,128]{1,0:T(8,128)(2,1)S(1)} %collective-permute-done.26.refs_1_, ...), custom_call_target="tpu_custom_call", output_to_operand_aliasing={{}: (10, {})} | custom-call | flops 4600000000 | tf_op jit(solution)/shard_map/last_terms/pallas_call | solution.py:285
  (104 shorter events, 15.8 us)
Async XLA Ops:
  0.0 15.1 %copy-start.6 = (bf16[1536,512]{1,0:T(8,128)(2,1)S(1)}, bf16[1536,512]{1,0:T(8,128)(2,1)}, u32[]{:S(2)}) copy-start(bf16[1536,512]{1,0:T(8,128)(2,1)} %param.5) | copy-start | bytes 4718596
  1.3 20.7 %collective-permute-start.1 = (bf16[2,1536,128]{2,1,0:T(8,128)(2,1)S(1)}, bf16[2,1536,128]{2,1,0:T(8,128)(2,1)}, u32[]{:S(2)}, u32[]{:S(2)}) collective-permute-start(bf16[2,1536,128]{2,1,0:T(8,128)(2,1)S(1)} %slice.24.refs_0_), channel_id=1, source_target_pairs={{0,8},{4,12},{8,0},{12,4},{16,24},{20,28},{24,16},{28,20},{1,9},{5... | collective-permute-start | bytes 2359304 | tf_op jit(solution)/shard_map/ppermute | solution.py:441
  4.4 19.1 %collective-permute-start = (bf16[2,1536,128]{2,1,0:T(8,128)(2,1)S(1)}, bf16[2,1536,128]{2,1,0:T(8,128)(2,1)}, u32[]{:S(2)}, u32[]{:S(2)}) collective-permute-start(bf16[2,1536,128]{2,1,0:T(8,128)(2,1)S(1)} %slice.24.refs_0_), channel_id=1, source_target_pairs={{0,4},{4,0},{8,12},{12,8},{16,20},{20,16},{24,28},{28,24},{1,5},{5... | collective-permute-start | bytes 2359304 | tf_op jit(solution)/shard_map/ppermute | solution.py:441
  15.1 2.7 %copy-start.5 = (bf16[2,1536,512]{2,1,0:T(8,128)(2,1)S(1)}, bf16[2,1536,512]{2,1,0:T(8,128)(2,1)}, u32[]{:S(2)}) copy-start(bf16[2,1536,512]{2,1,0:T(8,128)(2,1)} %param.6) | copy-start | bytes 9437188
  23.5 28.6 %collective-permute-start.3 = (bf16[2,1536,128]{2,1,0:T(8,128)(2,1)}, bf16[2,1536,128]{2,1,0:T(8,128)(2,1)}, u32[]{:S(2)}, u32[]{:S(2)}) collective-permute-start(bf16[2,1536,128]{2,1,0:T(8,128)(2,1)} %collective-permute-done.1.refs_2_), channel_id=1, source_target_pairs={{0,4},{4,0},{8,12},{12,8},{16,20},{20,16},{24,28},{28,24},{1,5},{5... | collective-permute-start | bytes 2359304 | tf_op jit(solution)/shard_map/ppermute | solution.py:441
  25.0 34.8 %collective-permute-start.5 = (bf16[2,1536,128]{2,1,0:T(8,128)(2,1)S(1)}, bf16[2,1536,128]{2,1,0:T(8,128)(2,1)}, u32[]{:S(2)}, u32[]{:S(2)}) collective-permute-start(bf16[2,1536,128]{2,1,0:T(8,128)(2,1)S(1)} %get-tuple-element.73.refs_0_), channel_id=1, source_target_pairs={{0,8},{4,12},{8,0},{12,4},{16,24},{20,28},{24,16},{28,20},{1,9},{5... | collective-permute-start | bytes 2359304 | tf_op jit(solution)/shard_map/ppermute | solution.py:441
  25.5 34.3 %collective-permute-start.4 = (bf16[2,1536,128]{2,1,0:T(8,128)(2,1)S(1)}, bf16[2,1536,128]{2,1,0:T(8,128)(2,1)}, u32[]{:S(2)}, u32[]{:S(2)}) collective-permute-start(bf16[2,1536,128]{2,1,0:T(8,128)(2,1)S(1)} %get-tuple-element.73.refs_0_), channel_id=1, source_target_pairs={{0,4},{4,0},{8,12},{12,8},{16,20},{20,16},{24,28},{28,24},{1,5},{5... | collective-permute-start | bytes 2359304 | tf_op jit(solution)/shard_map/ppermute | solution.py:441
  25.9 26.2 %collective-permute-start.2 = (bf16[1536,128]{1,0:T(8,128)(2,1)}, bf16[1536,128]{1,0:T(8,128)(2,1)}, u32[]{:S(2)}, u32[]{:S(2)}) collective-permute-start(bf16[1536,128]{1,0:T(8,128)(2,1)} %get-tuple-element.70.q_ref), channel_id=1, source_target_pairs={{0,16},{4,20},{8,24},{12,28},{16,0},{20,4},{24,8},{28,12},{1,17},{... | collective-permute-start | bytes 1179656 | tf_op jit(solution)/shard_map/ppermute | solution.py:441
  28.6 29.4 %collective-permute-start.6 = (bf16[1536,128]{1,0:T(8,128)(2,1)}, bf16[1536,128]{1,0:T(8,128)(2,1)}, u32[]{:S(2)}, u32[]{:S(2)}) collective-permute-start(bf16[1536,128]{1,0:T(8,128)(2,1)} %get-tuple-element.74.q_ref), channel_id=1, source_target_pairs={{0,16},{4,20},{8,24},{12,28},{16,0},{20,4},{24,8},{28,12},{1,17},{... | collective-permute-start | bytes 1179656 | tf_op jit(solution)/shard_map/ppermute | solution.py:441
  28.8 2.2 %copy-start = (bf16[2048,1024]{1,0:T(8,128)(2,1)S(1)}, bf16[2048,1024]{1,0:T(8,128)(2,1)}, u32[]{:S(2)}) copy-start(bf16[2048,1024]{1,0:T(8,128)(2,1)} %param.9) | copy-start | bytes 12582916
  31.0 21.0 %copy-start.3 = (f32[24,512]{1,0:T(8,128)S(1)}, f32[24,512]{1,0:T(8,128)}, u32[]{:S(2)}) copy-start(f32[24,512]{1,0:T(8,128)} %reshape.156.bias_ref) | copy-start | bytes 147460
  31.0 36.5 %copy-start.1 = (bf16[1536,128]{1,0:T(8,128)(2,1)S(1)}, bf16[1536,128]{1,0:T(8,128)(2,1)}, u32[]{:S(2)}) copy-start(bf16[1536,128]{1,0:T(8,128)(2,1)} %get-tuple-element.87.q_ref) | copy-start | bytes 1179652
  31.0 36.6 %copy-start.2 = (f32[24,512]{1,0:T(8,128)S(1)}, f32[24,512]{1,0:T(8,128)}, u32[]{:S(2)}) copy-start(f32[24,512]{1,0:T(8,128)} %reshape.153.bias_ref) | copy-start | bytes 147460
  59.8 39.5 %collective-permute-start.8 = (bf16[2,1536,128]{2,1,0:T(8,128)(2,1)}, bf16[2,1536,128]{2,1,0:T(8,128)(2,1)S(1)}, u32[]{:S(2)}, u32[]{:S(2)}) collective-permute-start(bf16[2,1536,128]{2,1,0:T(8,128)(2,1)} %collective-permute-done.5.refs_2_), channel_id=1, source_target_pairs={{0,4},{4,0},{8,12},{12,8},{16,20},{20,16},{24,28},{28,24},{1,5},{5... | collective-permute-start | bytes 2359304 | tf_op jit(solution)/shard_map/ppermute | solution.py:441
  63.1 40.7 %collective-permute-start.10 = (bf16[2,1536,128]{2,1,0:T(8,128)(2,1)S(1)}, bf16[2,1536,128]{2,1,0:T(8,128)(2,1)S(1)}, u32[]{:S(2)}, u32[]{:S(2)}) collective-permute-start(bf16[2,1536,128]{2,1,0:T(8,128)(2,1)S(1)} %get-tuple-element.91.refs_0_), channel_id=1, source_target_pairs={{0,8},{4,12},{8,0},{12,4},{16,24},{20,28},{24,16},{28,20},{1,9},{5... | collective-permute-start | bytes 2359304 | tf_op jit(solution)/shard_map/ppermute | solution.py:441
  63.7 40.1 %collective-permute-start.9 = (bf16[2,1536,128]{2,1,0:T(8,128)(2,1)S(1)}, bf16[2,1536,128]{2,1,0:T(8,128)(2,1)S(1)}, u32[]{:S(2)}, u32[]{:S(2)}) collective-permute-start(bf16[2,1536,128]{2,1,0:T(8,128)(2,1)S(1)} %get-tuple-element.91.refs_0_), channel_id=1, source_target_pairs={{0,4},{4,0},{8,12},{12,8},{16,20},{20,16},{24,28},{28,24},{1,5},{5... | collective-permute-start | bytes 2359304 | tf_op jit(solution)/shard_map/ppermute | solution.py:441
  64.4 39.3 %collective-permute-start.11 = (bf16[1632,128]{1,0:T(8,128)(2,1)S(1)}, bf16[1632,128]{1,0:T(8,128)(2,1)S(1)}, u32[]{:S(2)}, u32[]{:S(2)}) collective-permute-start(bf16[1632,128]{1,0:T(8,128)(2,1)S(1)} %guest_attention.4), channel_id=1, source_target_pairs={{0,16},{4,20},{8,24},{12,28},{16,0},{20,4},{24,8},{28,12},{1,17},{... | collective-permute-start | bytes 1253384 | tf_op jit(solution)/shard_map/ppermute | solution.py:441
  67.6 31.8 %collective-permute-start.7 = (bf16[1536,128]{1,0:T(8,128)(2,1)S(1)}, bf16[1536,128]{1,0:T(8,128)(2,1)S(1)}, u32[]{:S(2)}, u32[]{:S(2)}) collective-permute-start(bf16[1536,128]{1,0:T(8,128)(2,1)S(1)} %copy-done.1), channel_id=1, source_target_pairs={{0,16},{4,20},{8,24},{12,28},{16,0},{20,4},{24,8},{28,12},{1,17},{... | collective-permute-start | bytes 1179656 | tf_op jit(solution)/shard_map/ppermute | solution.py:441
  103.8 19.6 %collective-permute-start.13 = (bf16[2,1536,128]{2,1,0:T(8,128)(2,1)S(1)}, bf16[2,1536,128]{2,1,0:T(8,128)(2,1)S(1)}, u32[]{:S(2)}, u32[]{:S(2)}) collective-permute-start(bf16[2,1536,128]{2,1,0:T(8,128)(2,1)S(1)} %collective-permute-done.10.refs_2_), channel_id=1, source_target_pairs={{0,4},{4,0},{8,12},{12,8},{16,20},{20,16},{24,28},{28,24},{1,5},{5... | collective-permute-start | bytes 2359304 | tf_op jit(solution)/shard_map/ppermute | solution.py:441
  105.3 18.1 %collective-permute-start.12 = (bf16[1536,128]{1,0:T(8,128)(2,1)S(1)}, bf16[1536,128]{1,0:T(8,128)(2,1)S(1)}, u32[]{:S(2)}, u32[]{:S(2)}) collective-permute-start(bf16[1536,128]{1,0:T(8,128)(2,1)S(1)} %get-tuple-element.112.q_ref), channel_id=1, source_target_pairs={{0,16},{4,20},{8,24},{12,28},{16,0},{20,4},{24,8},{28,12},{1,17},{... | collective-permute-start | bytes 1179656 | tf_op jit(solution)/shard_map/ppermute | solution.py:441
  105.3 33.4 %collective-permute-start.15 = (bf16[2,1536,128]{2,1,0:T(8,128)(2,1)S(1)}, bf16[2,1536,128]{2,1,0:T(8,128)(2,1)S(1)}, u32[]{:S(2)}, u32[]{:S(2)}) collective-permute-start(bf16[2,1536,128]{2,1,0:T(8,128)(2,1)S(1)} %get-tuple-element.98.refs_0_), channel_id=1, source_target_pairs={{0,8},{4,12},{8,0},{12,4},{16,24},{20,28},{24,16},{28,20},{1,9},{5... | collective-permute-start | bytes 2359304 | tf_op jit(solution)/shard_map/ppermute | solution.py:441
  108.3 30.5 %collective-permute-start.14 = (bf16[2,1536,128]{2,1,0:T(8,128)(2,1)S(1)}, bf16[2,1536,128]{2,1,0:T(8,128)(2,1)S(1)}, u32[]{:S(2)}, u32[]{:S(2)}) collective-permute-start(bf16[2,1536,128]{2,1,0:T(8,128)(2,1)S(1)} %get-tuple-element.98.refs_0_), channel_id=1, source_target_pairs={{0,4},{4,0},{8,12},{12,8},{16,20},{20,16},{24,28},{28,24},{1,5},{5... | collective-permute-start | bytes 2359304 | tf_op jit(solution)/shard_map/ppermute | solution.py:441
  108.7 30.1 %collective-permute-start.16 = (bf16[1632,128]{1,0:T(8,128)(2,1)S(1)}, bf16[1632,128]{1,0:T(8,128)(2,1)S(1)}, u32[]{:S(2)}, u32[]{:S(2)}) collective-permute-start(bf16[1632,128]{1,0:T(8,128)(2,1)S(1)} %guest_attention.5), channel_id=1, source_target_pairs={{0,16},{4,20},{8,24},{12,28},{16,0},{20,4},{24,8},{28,12},{1,17},{... | collective-permute-start | bytes 1253384 | tf_op jit(solution)/shard_map/ppermute | solution.py:441
  113.2 25.6 %copy-start.4 = (s32[24]{0:T(128)S(1)}, s32[24]{0:T(128)}, u32[]{:S(2)}) copy-start(s32[24]{0:T(128)} %select_reduce_fusion.2.order_ref) | copy-start | bytes 292
  123.4 4.3 %collective-permute-start.18 = (bf16[1536,128]{1,0:T(8,128)(2,1)S(1)}, bf16[1536,128]{1,0:T(8,128)(2,1)S(1)}, u32[]{:S(2)}, u32[]{:S(2)}) collective-permute-start(bf16[1536,128]{1,0:T(8,128)(2,1)S(1)} %merge_halves.4.refs_0_), channel_id=1, source_target_pairs={{0,1},{1,0},{2,3},{3,2},{4,5},{5,4},{6,7},{7,6},{8,9},{9,8},{10,11... | collective-permute-start | bytes 1179656 | tf_op jit(solution)/shard_map/ppermute | solution.py:449
  123.4 11.5 %collective-permute-start.17 = (bf16[1536,128]{1,0:T(8,128)(2,1)S(1)}, bf16[1536,128]{1,0:T(8,128)(2,1)S(1)}, u32[]{:S(2)}, u32[]{:S(2)}) collective-permute-start(bf16[1536,128]{1,0:T(8,128)(2,1)S(1)} %merge_halves.4.refs_0_), channel_id=1, source_target_pairs={{0,2},{1,3},{2,0},{3,1},{4,6},{5,7},{6,4},{7,5},{8,10},{9,11},{10,... | collective-permute-start | bytes 1179656 | tf_op jit(solution)/shard_map/ppermute | solution.py:449
  127.7 26.5 %collective-permute-start.25 = (bf16[1632,128]{1,0:T(8,128)(2,1)S(1)}, bf16[1632,128]{1,0:T(8,128)(2,1)S(1)}, u32[]{:S(2)}, u32[]{:S(2)}) collective-permute-start(bf16[1632,128]{1,0:T(8,128)(2,1)S(1)} %guest_attention.6), channel_id=1, source_target_pairs={{0,16},{4,20},{8,24},{12,28},{16,0},{20,4},{24,8},{28,12},{1,17},{... | collective-permute-start | bytes 1253384 | tf_op jit(solution)/shard_map/ppermute | solution.py:441
  139.4 12.0 %collective-permute-start.19 = (bf16[2,768,128]{2,1,0:T(8,128)(2,1)S(1)}, bf16[2,768,128]{2,1,0:T(8,128)(2,1)S(1)}, u32[]{:S(2)}, u32[]{:S(2)}) collective-permute-start(bf16[2,768,128]{2,1,0:T(8,128)(2,1)S(1)} %get-tuple-element.111), channel_id=1, source_target_pairs={{0,4},{4,0},{8,12},{12,8},{16,20},{20,16},{24,28},{28,24},{1,5},{5... | collective-permute-start | bytes 1179656 | tf_op jit(solution)/shard_map/ppermute | solution.py:441
  143.5 11.4 %collective-permute-start.23 = (bf16[1536,128]{1,0:T(8,128)(2,1)S(1)}, bf16[1536,128]{1,0:T(8,128)(2,1)S(1)}, u32[]{:S(2)}, u32[]{:S(2)}) collective-permute-start(bf16[1536,128]{1,0:T(8,128)(2,1)S(1)} %merge_halves.5.refs_4_), channel_id=1, source_target_pairs={{0,2},{1,3},{2,0},{3,1},{4,6},{5,7},{6,4},{7,5},{8,10},{9,11},{10,... | collective-permute-start | bytes 1179656 | tf_op jit(solution)/shard_map/ppermute | solution.py:449
  145.1 10.5 %collective-permute-start.20 = (bf16[2,768,128]{2,1,0:T(8,128)(2,1)S(1)}, bf16[2,768,128]{2,1,0:T(8,128)(2,1)S(1)}, u32[]{:S(2)}, u32[]{:S(2)}) collective-permute-start(bf16[2,768,128]{2,1,0:T(8,128)(2,1)S(1)} %get-tuple-element.113), channel_id=1, source_target_pairs={{0,4},{4,0},{8,12},{12,8},{16,20},{20,16},{24,28},{28,24},{1,5},{5... | collective-permute-start | bytes 1179656 | tf_op jit(solution)/shard_map/ppermute | solution.py:441
  154.2 19.0 %collective-permute-start.28 = (bf16[1632,128]{1,0:T(8,128)(2,1)S(1)}, bf16[1632,128]{1,0:T(8,128)(2,1)S(1)}, u32[]{:S(2)}, u32[]{:S(2)}) collective-permute-start(bf16[1632,128]{1,0:T(8,128)(2,1)S(1)} %guest_attention.7), channel_id=1, source_target_pairs={{0,16},{4,20},{8,24},{12,28},{16,0},{20,4},{24,8},{28,12},{1,17},{... | collective-permute-start | bytes 1253384 | tf_op jit(solution)/shard_map/ppermute | solution.py:441
  154.3 5.9 %collective-permute-start.22 = (bf16[1536,128]{1,0:T(8,128)(2,1)S(1)}, bf16[1536,128]{1,0:T(8,128)(2,1)S(1)}, u32[]{:S(2)}, u32[]{:S(2)}) collective-permute-start(bf16[1536,128]{1,0:T(8,128)(2,1)S(1)} %merge_halves.5.refs_4_), channel_id=1, source_target_pairs={{0,1},{1,0},{2,3},{3,2},{4,5},{5,4},{6,7},{7,6},{8,9},{9,8},{10,11... | collective-permute-start | bytes 1179656 | tf_op jit(solution)/shard_map/ppermute | solution.py:449
  154.4 5.9 %collective-permute-start.21 = (bf16[1536,128]{1,0:T(8,128)(2,1)S(1)}, bf16[1536,128]{1,0:T(8,128)(2,1)S(1)}, u32[]{:S(2)}, u32[]{:S(2)}) collective-permute-start(bf16[1536,128]{1,0:T(8,128)(2,1)S(1)} %collective-permute-done.17.refs_2_), channel_id=1, source_target_pairs={{0,1},{1,0},{2,3},{3,2},{4,5},{5,4},{6,7},{7,6},{8,9},{9,8},{10,11... | collective-permute-start | bytes 1179656 | tf_op jit(solution)/shard_map/ppermute | solution.py:449
  154.9 5.4 %collective-permute-start.24 = (bf16[1536,128]{1,0:T(8,128)(2,1)S(1)}, bf16[1536,128]{1,0:T(8,128)(2,1)S(1)}, u32[]{:S(2)}, u32[]{:S(2)}) collective-permute-start(bf16[1536,128]{1,0:T(8,128)(2,1)S(1)} %collective-permute-done.23.refs_6_), channel_id=1, source_target_pairs={{0,1},{1,0},{2,3},{3,2},{4,5},{5,4},{6,7},{7,6},{8,9},{9,8},{10,11... | collective-permute-start | bytes 1179656 | tf_op jit(solution)/shard_map/ppermute | solution.py:449
  159.5 16.4 %collective-permute-start.27 = (bf16[1536,128]{1,0:T(8,128)(2,1)S(1)}, bf16[1536,128]{1,0:T(8,128)(2,1)S(1)}, u32[]{:S(2)}, u32[]{:S(2)}) collective-permute-start(bf16[1536,128]{1,0:T(8,128)(2,1)S(1)} %merge_halves.6.refs_0_), channel_id=1, source_target_pairs={{0,2},{1,3},{2,0},{3,1},{4,6},{5,7},{6,4},{7,5},{8,10},{9,11},{10,... | collective-permute-start | bytes 1179656 | tf_op jit(solution)/shard_map/ppermute | solution.py:449
  174.2 8.3 %collective-permute-start.33 = (bf16[1024,128]{1,0:T(8,128)(2,1)S(1)}, bf16[1024,128]{1,0:T(8,128)(2,1)S(1)}, u32[]{:S(2)}, u32[]{:S(2)}) collective-permute-start(bf16[1024,128]{1,0:T(8,128)(2,1)S(1)} %get-tuple-element.126.refs_4_), channel_id=1, source_target_pairs={{0,2},{1,3},{2,0},{3,1},{4,6},{5,7},{6,4},{7,5},{8,10},{9,11},{10,... | collective-permute-start | bytes 786440 | tf_op jit(solution)/shard_map/ppermute | solution.py:449
  175.9 7.1 %collective-permute-start.26 = (bf16[1536,128]{1,0:T(8,128)(2,1)S(1)}, bf16[1536,128]{1,0:T(8,128)(2,1)S(1)}, u32[]{:S(2)}, u32[]{:S(2)}) collective-permute-start(bf16[1536,128]{1,0:T(8,128)(2,1)S(1)} %merge_halves.6.refs_0_), channel_id=1, source_target_pairs={{0,1},{1,0},{2,3},{3,2},{4,5},{5,4},{6,7},{7,6},{8,9},{9,8},{10,11... | collective-permute-start | bytes 1179656 | tf_op jit(solution)/shard_map/ppermute | solution.py:449
  175.9 8.7 %collective-permute-start.29 = (bf16[1536,128]{1,0:T(8,128)(2,1)S(1)}, bf16[1536,128]{1,0:T(8,128)(2,1)S(1)}, u32[]{:S(2)}, u32[]{:S(2)}) collective-permute-start(bf16[1536,128]{1,0:T(8,128)(2,1)S(1)} %collective-permute-done.27.refs_2_), channel_id=1, source_target_pairs={{0,1},{1,0},{2,3},{3,2},{4,5},{5,4},{6,7},{7,6},{8,9},{9,8},{10,11... | collective-permute-start | bytes 1179656 | tf_op jit(solution)/shard_map/ppermute | solution.py:449
  176.4 8.2 %collective-permute-start.32 = (bf16[1024,128]{1,0:T(8,128)(2,1)S(1)}, bf16[1024,128]{1,0:T(8,128)(2,1)S(1)}, u32[]{:S(2)}, u32[]{:S(2)}) collective-permute-start(bf16[1024,128]{1,0:T(8,128)(2,1)S(1)} %get-tuple-element.126.refs_4_), channel_id=1, source_target_pairs={{0,1},{1,0},{2,3},{3,2},{4,5},{5,4},{6,7},{7,6},{8,9},{9,8},{10,11... | collective-permute-start | bytes 786440 | tf_op jit(solution)/shard_map/ppermute | solution.py:449
  182.5 2.1 %collective-permute-start.34 = (bf16[1024,128]{1,0:T(8,128)(2,1)S(1)}, bf16[1024,128]{1,0:T(8,128)(2,1)S(1)}, u32[]{:S(2)}, u32[]{:S(2)}) collective-permute-start(bf16[1024,128]{1,0:T(8,128)(2,1)S(1)} %collective-permute-done.33.refs_6_), channel_id=1, source_target_pairs={{0,1},{1,0},{2,3},{3,2},{4,5},{5,4},{6,7},{7,6},{8,9},{9,8},{10,11... | collective-permute-start | bytes 786440 | tf_op jit(solution)/shard_map/ppermute | solution.py:449
  182.5 5.9 %collective-permute-start.30 = (bf16[512,128]{1,0:T(8,128)(2,1)S(1)}, bf16[512,128]{1,0:T(8,128)(2,1)S(1)}, u32[]{:S(2)}, u32[]{:S(2)}) collective-permute-start(bf16[512,128]{1,0:T(8,128)(2,1)S(1)} %get-tuple-element.127.refs_4_), channel_id=1, source_target_pairs={{0,1},{1,0},{2,3},{3,2},{4,5},{5,4},{6,7},{7,6},{8,9},{9,8},{10,11... | collective-permute-start | bytes 393224 | tf_op jit(solution)/shard_map/ppermute | solution.py:449
  183.0 5.4 %collective-permute-start.31 = (bf16[512,128]{1,0:T(8,128)(2,1)S(1)}, bf16[512,128]{1,0:T(8,128)(2,1)S(1)}, u32[]{:S(2)}, u32[]{:S(2)}) collective-permute-start(bf16[512,128]{1,0:T(8,128)(2,1)S(1)} %get-tuple-element.127.refs_4_), channel_id=1, source_target_pairs={{0,2},{1,3},{2,0},{3,1},{4,6},{5,7},{6,4},{7,5},{8,10},{9,11},{10,... | collective-permute-start | bytes 393224 | tf_op jit(solution)/shard_map/ppermute | solution.py:449
  188.4 1.3 collective-permute-start.35

commit v7 on v6

--- a/solution.py
+++ b/solution.py
@@ -509,7 +509,7 @@
     d1, y2, z2, v2, g0 = over_y(z1), over_y(k2_), over_z(k2_), across(v2), across(s0)
     m0 = home_call(*home[:2], after(q0, t0), p0)
     p1 = (k1, y1, z1, d1)
-    (s1,) = guest_call(*guest[:2], after(v1, m0[1], v2), p1)
+    (s1,) = guest_call(*guest[:2], after(v1, m0[1]), p1)
     t1, y2, z2, v2, g0, k3_, v3 = together(s1, y2, z2, v2, g0, k3, q3)
 
     d2, y3, z3, v3, g1 = over_y(z2), over_y(k3_), over_z(k3_), across(v3), across(s1)

time: 192 us -> 189 us (0.984)
  waiting for transfers between devices: 96.3 us -> 93 us
    ppermute x21, waiting for transfers between devices: 82.1 us -> 79.2 us  [swap(): lax.ppermute(value, 'seq', [(i, i ^ distance) for i in range(shards)])]
  transfers between devices with their start and end apart: 36 -> 36, of which waited for: 14 -> 16; matrix products, arithmetic and copies ran while one was open for 6% -> 6% of each run, Pallas kernels for 23% -> 23%
where the time goes in v7:
time: 189 us
  waiting for transfers between devices  93 us (49%)
  Pallas kernels  45.5 us (24%)
  starting transfers between devices  34.5 us (18%)
  local copies, waits for them, and re-layouts  9.37 us (5%)
  other arithmetic  6.31 us (3%)
    ppermute x21, waiting for transfers between devices, swap(): lax.ppermute(value, 'seq', [(i, i ^ distance) for i in range(shards)])  79.2 us
    ppermute x21, starting transfers between devices, swap(): lax.ppermute(value, 'seq', [(i, i ^ distance) for i in range(shards)])  26 us
    pallas_call x4, Pallas kernels, guest_call(): pl.pallas_call(functools.partial(guest_kernel, parts, len(pieces)), out_s...  14.6 us
    pallas_call x4, Pallas kernels, home_call(): pl.pallas_call(functools.partial(home_kernel, parts, len(pieces)), out_sh...  14.6 us
    ppermute x15, waiting for transfers between devices, hop(): lax.ppermute(value, 'head', [(i, i ^ distance) for i in range(groups)])  13.8 us
    ppermute x15, starting transfers between devices, hop(): lax.ppermute(value, 'head', [(i, i ^ distance) for i in range(groups)])  8.51 us
    pallas_call x2, Pallas kernels, last_terms(): pl.pallas_call(functools.partial(last_terms_kernel, len(pieces) // 2), gr...  6 us
    pallas_call x1, Pallas kernels, first_terms(): pl.pallas_call(functools.partial(first_terms_kernel, len(pieces) // 2), o...  5.39 us
  transfers between devices with their start and end apart: 36, of which 16 were waited for; matrix products, arithmetic and copies ran while one was open for 6% of the time, Pallas kernels for 23%

profile of v7, /device:TPU:0, one launch (start us, length us, event | category | flops | bytes accessed | tf_op | source)
XLA Modules:
  0.0 188.9 jit_solution(5527700079437541364)
XLA Ops:
  0.0 1.3 slice.24.refs_0_
  1.3 3.1 %collective-permute-start.1 = (bf16[2,1536,128]{2,1,0:T(8,128)(2,1)S(1)}, bf16[2,1536,128]{2,1,0:T(8,128)(2,1)}, u32[]{:S(2)}, u32[]{:S(2)}) collective-permute-start(bf16[2,1536,128]{2,1,0:T(8,128)(2,1)S(1)} %slice.24.refs_0_), channel_id=1, source_target_pairs={{0,8},{4,12},{8,0},{12,4},{16,24},{20,28},{24,16},{28,20},{1,9},{5... | collective-permute-start | bytes 2359304 | tf_op jit(solution)/shard_map/ppermute | solution.py:441
  4.4 1.5 collective-permute-start
  6.8 0.9 constant_dynamic-slice_fusion
  10.0 1.0 select_reduce_fusion
  15.1 1.2 fusion.14
  18.2 3.8 %collective-permute-done.1.refs_2_ = bf16[2,1536,128]{2,1,0:T(8,128)(2,1)} collective-permute-done((bf16[2,1536,128]{2,1,0:T(8,128)(2,1)S(1)}, bf16[2,1536,128]{2,1,0:T(8,128)(2,1)}, u32[]{:S(2)}, u32[]{:S(2)}) %collective-permute-start.1) | collective-permute-done | bytes 786464 | tf_op jit(solution)/shard_map/ppermute | solution.py:441
  22.0 1.5 collective-permute-done.refs_1_
  23.5 1.5 collective-permute-start.3
  25.9 2.7 %collective-permute-start.2 = (bf16[1536,128]{1,0:T(8,128)(2,1)}, bf16[1536,128]{1,0:T(8,128)(2,1)}, u32[]{:S(2)}, u32[]{:S(2)}) collective-permute-start(bf16[1536,128]{1,0:T(8,128)(2,1)} %get-tuple-element.70.q_ref), channel_id=1, source_target_pairs={{0,16},{4,20},{8,24},{12,28},{16,0},{20,4},{24,8},{28,12},{1,17},{... | collective-permute-start | bytes 1179656 | tf_op jit(solution)/shard_map/ppermute | solution.py:441
  28.8 2.2 %copy-done = bf16[2048,1024]{1,0:T(8,128)(2,1)S(1)} copy-done((bf16[2048,1024]{1,0:T(8,128)(2,1)S(1)}, bf16[2048,1024]{1,0:T(8,128)(2,1)}, u32[]{:S(2)}) %copy-start) | copy-done | bytes 4194328
  31.4 20.6 %collective-permute-done.2.q_ref = bf16[1536,128]{1,0:T(8,128)(2,1)} collective-permute-done((bf16[1536,128]{1,0:T(8,128)(2,1)}, bf16[1536,128]{1,0:T(8,128)(2,1)}, u32[]{:S(2)}, u32[]{:S(2)}) %collective-permute-start.2) | collective-permute-done | bytes 393248 | tf_op jit(solution)/shard_map/ppermute | solution.py:441
  52.1 4.7 %guest_attention.4 = bf16[1632,128]{1,0:T(8,128)(2,1)S(1)} custom-call(s32[192]{0:T(256)S(1)} %reshape.155.starts_ref, f32[24,512]{1,0:T(8,128)S(1)} %copy-done.3, bf16[1536,128]{1,0:T(8,128)(2,1)} %collective-permute-done.2.q_ref, bf16[2,1536,128]{2,1,0:T(8,128)(2,1)S(1)} %slice.24.refs_0_, bf16[2,1536,128]{2,1,0:T(8,128)(2,1)} %collective-permute-done.refs_1_, ...), custom_call_target="tpu_custom_call" | custom-call | flops 115000000 | tf_op jit(solution)/shard_map/guest_attention/pallas_call | solution.py:220
  56.7 1.2 collective-permute-done.6.q_ref
  58.0 1.8 collective-permute-done.5.refs_2_
  59.8 3.3 %collective-permute-start.7 = (bf16[2,1536,128]{2,1,0:T(8,128)(2,1)}, bf16[2,1536,128]{2,1,0:T(8,128)(2,1)S(1)}, u32[]{:S(2)}, u32[]{:S(2)}) collective-permute-start(bf16[2,1536,128]{2,1,0:T(8,128)(2,1)} %collective-permute-done.5.refs_2_), channel_id=1, source_target_pairs={{0,4},{4,0},{8,12},{12,8},{16,20},{20,16},{24,28},{28,24},{1,5},{5... | collective-permute-start | bytes 2359304 | tf_op jit(solution)/shard_map/ppermute | solution.py:441
  64.4 3.1 %collective-permute-start.11 = (bf16[1632,128]{1,0:T(8,128)(2,1)S(1)}, bf16[1632,128]{1,0:T(8,128)(2,1)S(1)}, u32[]{:S(2)}, u32[]{:S(2)}) collective-permute-start(bf16[1632,128]{1,0:T(8,128)(2,1)S(1)} %guest_attention.4), channel_id=1, source_target_pairs={{0,16},{4,20},{8,24},{12,28},{16,0},{20,4},{24,8},{28,12},{1,17},{... | collective-permute-start | bytes 1253384 | tf_op jit(solution)/shard_map/ppermute | solution.py:441
  67.6 4.6 %home_attention.4 = (f32[1536,128]{1,0:T(8,128)S(1)}, f32[1,32,128]{2,1,0:T(8,128)S(1)}) custom-call(s32[192]{0:T(256)S(1)} %reshape.152.starts_ref, f32[24,512]{1,0:T(8,128)S(1)} %copy-done.2, bf16[1536,128]{1,0:T(8,128)(2,1)} %get-tuple-element.70.q_ref, bf16[2,1536,128]{2,1,0:T(8,128)(2,1)S(1)} %slice.24.refs_0_, ...), custom_call_target="tpu_custom_call" | custom-call | tf_op jit(solution)/shard_map/home_attention/pallas_call | solution.py:242
  72.2 9.5 %collective-permute-done.7.refs_3_ = bf16[2,1536,128]{2,1,0:T(8,128)(2,1)S(1)} collective-permute-done((bf16[2,1536,128]{2,1,0:T(8,128)(2,1)}, bf16[2,1536,128]{2,1,0:T(8,128)(2,1)S(1)}, u32[]{:S(2)}, u32[]{:S(2)}) %collective-permute-start.7) | collective-permute-done | bytes 786464 | tf_op jit(solution)/shard_map/ppermute | solution.py:441
  81.7 4.4 %guest_attention.5 = bf16[1632,128]{1,0:T(8,128)(2,1)S(1)} custom-call(s32[192]{0:T(256)S(1)} %reshape.155.starts_ref, f32[24,512]{1,0:T(8,128)S(1)} %copy-done.3, bf16[1536,128]{1,0:T(8,128)(2,1)} %collective-permute-done.6.q_ref, bf16[2,1536,128]{2,1,0:T(8,128)(2,1)S(1)} %get-tuple-element.73.refs_0_, ...), custom_call_target="tpu_custom_call" | custom-call | flops 115000000 | tf_op jit(solution)/shard_map/guest_attention/pallas_call | solution.py:220
  86.2 18.4 %collective-permute-done.10.q_ref = bf16[1536,128]{1,0:T(8,128)(2,1)S(1)} collective-permute-done((bf16[1536,128]{1,0:T(8,128)(2,1)S(1)}, bf16[1536,128]{1,0:T(8,128)(2,1)S(1)}, u32[]{:S(2)}, u32[]{:S(2)}) %collective-permute-start.10) | collective-permute-done | bytes 393248 | tf_op jit(solution)/shard_map/ppermute | solution.py:441
  104.6 2.7 %collective-permute-start.13 = (bf16[2,1536,128]{2,1,0:T(8,128)(2,1)S(1)}, bf16[2,1536,128]{2,1,0:T(8,128)(2,1)S(1)}, u32[]{:S(2)}, u32[]{:S(2)}) collective-permute-start(bf16[2,1536,128]{2,1,0:T(8,128)(2,1)S(1)} %collective-permute-done.9.refs_2_), channel_id=1, source_target_pairs={{0,4},{4,0},{8,12},{12,8},{16,20},{20,16},{24,28},{28,24},{1,5},{5... | collective-permute-start | bytes 2359304 | tf_op jit(solution)/shard_map/ppermute | solution.py:441
  107.3 3.6 %collective-permute-start.15 = (bf16[2,1536,128]{2,1,0:T(8,128)(2,1)S(1)}, bf16[2,1536,128]{2,1,0:T(8,128)(2,1)S(1)}, u32[]{:S(2)}, u32[]{:S(2)}) collective-permute-start(bf16[2,1536,128]{2,1,0:T(8,128)(2,1)S(1)} %get-tuple-element.98.refs_0_), channel_id=1, source_target_pairs={{0,8},{4,12},{8,0},{12,4},{16,24},{20,28},{24,16},{28,20},{1,9},{5... | collective-permute-start | bytes 2359304 | tf_op jit(solution)/shard_map/ppermute | solution.py:441
  111.0 4.4 %home_attention.5 = (f32[1536,128]{1,0:T(8,128)S(1)}, f32[1,32,128]{2,1,0:T(8,128)S(1)}) custom-call(s32[192]{0:T(256)S(1)} %reshape.152.starts_ref, f32[24,512]{1,0:T(8,128)S(1)} %copy-done.2, bf16[1536,128]{1,0:T(8,128)(2,1)} %get-tuple-element.74.q_ref, bf16[2,1536,128]{2,1,0:T(8,128)(2,1)S(1)} %get-tuple-element.73.refs_0_, ...), custom_call_target="tpu_custom_call" | custom-call | tf_op jit(solution)/shard_map/home_attention/pallas_call | solution.py:242
  115.4 1.0 merge_halves.4.refs_0_
  116.4 8.9 %collective-permute-done.12.q_ref = bf16[1536,128]{1,0:T(8,128)(2,1)S(1)} collective-permute-done((bf16[1536,128]{1,0:T(8,128)(2,1)S(1)}, bf16[1536,128]{1,0:T(8,128)(2,1)S(1)}, u32[]{:S(2)}, u32[]{:S(2)}) %collective-permute-start.12) | collective-permute-done | bytes 393248 | tf_op jit(solution)/shard_map/ppermute | solution.py:441
  125.3 1.5 collective-permute-start.17
  126.8 2.8 %guest_attention.6 = bf16[1632,128]{1,0:T(8,128)(2,1)S(1)} custom-call(s32[192]{0:T(256)S(1)} %reshape.155.starts_ref, f32[24,512]{1,0:T(8,128)S(1)} %copy-done.3, bf16[1536,128]{1,0:T(8,128)(2,1)S(1)} %collective-permute-done.10.q_ref, bf16[2,1536,128]{2,1,0:T(8,128)(2,1)S(1)} %get-tuple-element.90.refs_0_, ...), custom_call_target="tpu_custom_call" | custom-call | flops 115000000 | tf_op jit(solution)/shard_map/guest_attention/pallas_call | solution.py:220
  129.6 7.2 %collective-permute-done.17.refs_2_ = bf16[1536,128]{1,0:T(8,128)(2,1)S(1)} collective-permute-done((bf16[1536,128]{1,0:T(8,128)(2,1)S(1)}, bf16[1536,128]{1,0:T(8,128)(2,1)S(1)}, u32[]{:S(2)}, u32[]{:S(2)}) %collective-permute-start.17) | collective-permute-done | bytes 393248 | tf_op jit(solution)/shard_map/ppermute | solution.py:449
  136.8 7.5 %collective-permute-done.16.message_ref = bf16[1632,128]{1,0:T(8,128)(2,1)S(1)} collective-permute-done((bf16[1632,128]{1,0:T(8,128)(2,1)S(1)}, bf16[1632,128]{1,0:T(8,128)(2,1)S(1)}, u32[]{:S(2)}, u32[]{:S(2)}) %collective-permute-start.16) | collective-permute-done | bytes 417824 | tf_op jit(solution)/shard_map/ppermute | solution.py:441
  144.9 1.3 collective-permute-start.19
  146.2 2.7 %home_attention.6 = (f32[1536,128]{1,0:T(8,128)S(1)}, f32[1,32,128]{2,1,0:T(8,128)S(1)}) custom-call(s32[192]{0:T(256)S(1)} %reshape.152.starts_ref, f32[24,512]{1,0:T(8,128)S(1)} %copy-done.2, bf16[1536,128]{1,0:T(8,128)(2,1)S(1)} %copy-done.1, bf16[2,1536,128]{2,1,0:T(8,128)(2,1)S(1)} %get-tuple-element.90.refs_0_, ...), custom_call_target="tpu_custom_call" | custom-call | tf_op jit(solution)/shard_map/home_attention/pallas_call | solution.py:242
  149.0 1.0 merge_halves.5.refs_4_
  149.9 2.2 %collective-permute-start.23 = (bf16[1536,128]{1,0:T(8,128)(2,1)S(1)}, bf16[1536,128]{1,0:T(8,128)(2,1)S(1)}, u32[]{:S(2)}, u32[]{:S(2)}) collective-permute-start(bf16[1536,128]{1,0:T(8,128)(2,1)S(1)} %merge_halves.5.refs_4_), channel_id=1, source_target_pairs={{0,2},{1,3},{2,0},{3,1},{4,6},{5,7},{6,4},{7,5},{8,10},{9,11},{10,... | collective-permute-start | bytes 1179656 | tf_op jit(solution)/shard_map/ppermute | solution.py:449
  152.6 1.8 collective-permute-done.19.refs_3_
  154.4 2.8 %guest_attention.7 = bf16[1632,128]{1,0:T(8,128)(2,1)S(1)} custom-call(s32[192]{0:T(256)S(1)} %reshape.157.starts_ref, f32[24,512]{1,0:T(8,128)S(1)} %copy-done.3, bf16[1536,128]{1,0:T(8,128)(2,1)S(1)} %collective-permute-done.12.q_ref, bf16[2,1536,128]{2,1,0:T(8,128)(2,1)S(1)} %get-tuple-element.98.refs_0_, ...), custom_call_target="tpu_custom_call" | custom-call | flops 115000000 | tf_op jit(solution)/shard_map/guest_attention/pallas_call | solution.py:220
  158.0 2.0 %collective-permute-done.20.refs_4_ = bf16[2,768,128]{2,1,0:T(8,128)(2,1)S(1)} collective-permute-done((bf16[2,768,128]{2,1,0:T(8,128)(2,1)S(1)}, bf16[2,768,128]{2,1,0:T(8,128)(2,1)S(1)}, u32[]{:S(2)}, u32[]{:S(2)}) %collective-permute-start.20) | collective-permute-done | bytes 393248 | tf_op jit(solution)/shard_map/ppermute | solution.py:441
  159.9 2.9 %home_attention.7 = (f32[1536,128]{1,0:T(8,128)S(1)}, f32[1,32,128]{2,1,0:T(8,128)S(1)}) custom-call(s32[192]{0:T(256)S(1)} %reshape.154.starts_ref, f32[24,512]{1,0:T(8,128)S(1)} %copy-done.2, bf16[1536,128]{1,0:T(8,128)(2,1)S(1)} %get-tuple-element.112.q_ref, bf16[2,1536,128]{2,1,0:T(8,128)(2,1)S(1)} %get-tuple-element.98.refs_0_, ...), custom_call_target="tpu_custom_call" | custom-call | tf_op jit(solution)/shard_map/home_attention/pallas_call | solution.py:242
  162.9 1.0 merge_halves.6.refs_0_
  164.0 5.4 %first_terms.1.sum_ref = f32[1536,1024]{1,0:T(8,128)S(1)} custom-call(bf16[1024,1024]{1,0:T(8,128)(2,1)S(1)} %bitcast.5, bf16[1536,128]{1,0:T(8,128)(2,1)S(1)} %merge_halves.4.refs_0_, bf16[1536,128]{1,0:T(8,128)(2,1)S(1)} %collective-permute-done.18.refs_1_, bf16[1536,128]{1,0:T(8,128)(2,1)S(1)} %collective-permute-done.17.refs_2_, ...), custom_call_target="tpu_custom_call" | custom-call | tf_op jit(solution)/shard_map/first_terms/pallas_call | solution.py:329
  169.4 2.0 %collective-permute-done.28.message_ref = bf16[1632,128]{1,0:T(8,128)(2,1)S(1)} collective-permute-done((bf16[1632,128]{1,0:T(8,128)(2,1)S(1)}, bf16[1632,128]{1,0:T(8,128)(2,1)S(1)}, u32[]{:S(2)}, u32[]{:S(2)}) %collective-permute-start.28) | collective-permute-done | bytes 417824 | tf_op jit(solution)/shard_map/ppermute | solution.py:441
  171.4 1.0 merge_halves.7
  172.3 1.2 collective-permute-start.33
  174.6 4.7 %collective-permute-done.33.refs_6_ = bf16[1024,128]{1,0:T(8,128)(2,1)S(1)} collective-permute-done((bf16[1024,128]{1,0:T(8,128)(2,1)S(1)}, bf16[1024,128]{1,0:T(8,128)(2,1)S(1)}, u32[]{:S(2)}, u32[]{:S(2)}) %collective-permute-start.33) | collective-permute-done | bytes 262176 | tf_op jit(solution)/shard_map/ppermute | solution.py:449
  179.8 1.8 collective-permute-start.31
  181.6 3.8 %last_terms.2.refs_8_ = bf16[1536,1024]{1,0:T(8,128)(2,1)} custom-call(bf16[1024,1024]{1,0:T(8,128)(2,1)S(1)} %bitcast.6, f32[1536,1024]{1,0:T(8,128)S(1)} %first_terms.1.sum_ref, bf16[1536,128]{1,0:T(8,128)(2,1)S(1)} %merge_halves.6.refs_0_, bf16[1536,128]{1,0:T(8,128)(2,1)S(1)} %collective-permute-done.26.refs_1_, ...), custom_call_target="tpu_custom_call" | custom-call | flops 4600000000 | tf_op jit(solution)/shard_map/last_terms/pallas_call | solution.py:285
  185.4 1.3 collective-permute-done.35.refs_7_
  186.7 2.2 %last_terms.3 = bf16[1536,1024]{1,0:T(8,128)(2,1)} custom-call(bf16[1024,1024]{1,0:T(8,128)(2,1)S(1)} %bitcast.7, f32[1536,1024]{1,0:T(8,128)S(1)} %first_terms.1.sum_ref, bf16[1536,128]{1,0:T(8,128)(2,1)S(1)} %merge_halves.6.refs_0_, bf16[1536,128]{1,0:T(8,128)(2,1)S(1)} %collective-permute-done.26.refs_1_, ...), custom_call_target="tpu_custom_call", output_to_operand_aliasing={{}: (10, {})} | custom-call | flops 4600000000 | tf_op jit(solution)/shard_map/last_terms/pallas_call | solution.py:285
  (104 shorter events, 15.8 us)
Async XLA Ops:
  0.0 15.1 %copy-start.6 = (bf16[1536,512]{1,0:T(8,128)(2,1)S(1)}, bf16[1536,512]{1,0:T(8,128)(2,1)}, u32[]{:S(2)}) copy-start(bf16[1536,512]{1,0:T(8,128)(2,1)} %param.5) | copy-start | bytes 4718596
  1.3 20.7 %collective-permute-start.1 = (bf16[2,1536,128]{2,1,0:T(8,128)(2,1)S(1)}, bf16[2,1536,128]{2,1,0:T(8,128)(2,1)}, u32[]{:S(2)}, u32[]{:S(2)}) collective-permute-start(bf16[2,1536,128]{2,1,0:T(8,128)(2,1)S(1)} %slice.24.refs_0_), channel_id=1, source_target_pairs={{0,8},{4,12},{8,0},{12,4},{16,24},{20,28},{24,16},{28,20},{1,9},{5... | collective-permute-start | bytes 2359304 | tf_op jit(solution)/shard_map/ppermute | solution.py:441
  4.4 19.1 %collective-permute-start = (bf16[2,1536,128]{2,1,0:T(8,128)(2,1)S(1)}, bf16[2,1536,128]{2,1,0:T(8,128)(2,1)}, u32[]{:S(2)}, u32[]{:S(2)}) collective-permute-start(bf16[2,1536,128]{2,1,0:T(8,128)(2,1)S(1)} %slice.24.refs_0_), channel_id=1, source_target_pairs={{0,4},{4,0},{8,12},{12,8},{16,20},{20,16},{24,28},{28,24},{1,5},{5... | collective-permute-start | bytes 2359304 | tf_op jit(solution)/shard_map/ppermute | solution.py:441
  15.1 2.7 %copy-start.5 = (bf16[2,1536,512]{2,1,0:T(8,128)(2,1)S(1)}, bf16[2,1536,512]{2,1,0:T(8,128)(2,1)}, u32[]{:S(2)}) copy-start(bf16[2,1536,512]{2,1,0:T(8,128)(2,1)} %param.6) | copy-start | bytes 9437188
  23.5 28.6 %collective-permute-start.3 = (bf16[2,1536,128]{2,1,0:T(8,128)(2,1)}, bf16[2,1536,128]{2,1,0:T(8,128)(2,1)}, u32[]{:S(2)}, u32[]{:S(2)}) collective-permute-start(bf16[2,1536,128]{2,1,0:T(8,128)(2,1)} %collective-permute-done.1.refs_2_), channel_id=1, source_target_pairs={{0,4},{4,0},{8,12},{12,8},{16,20},{20,16},{24,28},{28,24},{1,5},{5... | collective-permute-start | bytes 2359304 | tf_op jit(solution)/shard_map/ppermute | solution.py:441
  25.0 34.8 %collective-permute-start.5 = (bf16[2,1536,128]{2,1,0:T(8,128)(2,1)S(1)}, bf16[2,1536,128]{2,1,0:T(8,128)(2,1)}, u32[]{:S(2)}, u32[]{:S(2)}) collective-permute-start(bf16[2,1536,128]{2,1,0:T(8,128)(2,1)S(1)} %get-tuple-element.73.refs_0_), channel_id=1, source_target_pairs={{0,8},{4,12},{8,0},{12,4},{16,24},{20,28},{24,16},{28,20},{1,9},{5... | collective-permute-start | bytes 2359304 | tf_op jit(solution)/shard_map/ppermute | solution.py:441
  25.5 34.3 %collective-permute-start.4 = (bf16[2,1536,128]{2,1,0:T(8,128)(2,1)S(1)}, bf16[2,1536,128]{2,1,0:T(8,128)(2,1)}, u32[]{:S(2)}, u32[]{:S(2)}) collective-permute-start(bf16[2,1536,128]{2,1,0:T(8,128)(2,1)S(1)} %get-tuple-element.73.refs_0_), channel_id=1, source_target_pairs={{0,4},{4,0},{8,12},{12,8},{16,20},{20,16},{24,28},{28,24},{1,5},{5... | collective-permute-start | bytes 2359304 | tf_op jit(solution)/shard_map/ppermute | solution.py:441
  25.9 26.2 %collective-permute-start.2 = (bf16[1536,128]{1,0:T(8,128)(2,1)}, bf16[1536,128]{1,0:T(8,128)(2,1)}, u32[]{:S(2)}, u32[]{:S(2)}) collective-permute-start(bf16[1536,128]{1,0:T(8,128)(2,1)} %get-tuple-element.70.q_ref), channel_id=1, source_target_pairs={{0,16},{4,20},{8,24},{12,28},{16,0},{20,4},{24,8},{28,12},{1,17},{... | collective-permute-start | bytes 1179656 | tf_op jit(solution)/shard_map/ppermute | solution.py:441
  28.6 29.4 %collective-permute-start.6 = (bf16[1536,128]{1,0:T(8,128)(2,1)}, bf16[1536,128]{1,0:T(8,128)(2,1)}, u32[]{:S(2)}, u32[]{:S(2)}) collective-permute-start(bf16[1536,128]{1,0:T(8,128)(2,1)} %get-tuple-element.74.q_ref), channel_id=1, source_target_pairs={{0,16},{4,20},{8,24},{12,28},{16,0},{20,4},{24,8},{28,12},{1,17},{... | collective-permute-start | bytes 1179656 | tf_op jit(solution)/shard_map/ppermute | solution.py:441
  28.8 2.2 %copy-start = (bf16[2048,1024]{1,0:T(8,128)(2,1)S(1)}, bf16[2048,1024]{1,0:T(8,128)(2,1)}, u32[]{:S(2)}) copy-start(bf16[2048,1024]{1,0:T(8,128)(2,1)} %param.9) | copy-start | bytes 12582916
  31.0 21.0 %copy-start.3 = (f32[24,512]{1,0:T(8,128)S(1)}, f32[24,512]{1,0:T(8,128)}, u32[]{:S(2)}) copy-start(f32[24,512]{1,0:T(8,128)} %reshape.156.bias_ref) | copy-start | bytes 147460
  31.0 36.5 %copy-start.1 = (bf16[1536,128]{1,0:T(8,128)(2,1)S(1)}, bf16[1536,128]{1,0:T(8,128)(2,1)}, u32[]{:S(2)}) copy-start(bf16[1536,128]{1,0:T(8,128)(2,1)} %get-tuple-element.91.q_ref) | copy-start | bytes 1179652
  31.0 36.6 %copy-start.2 = (f32[24,512]{1,0:T(8,128)S(1)}, f32[24,512]{1,0:T(8,128)}, u32[]{:S(2)}) copy-start(f32[24,512]{1,0:T(8,128)} %reshape.153.bias_ref) | copy-start | bytes 147460
  59.8 21.9 %collective-permute-start.7 = (bf16[2,1536,128]{2,1,0:T(8,128)(2,1)}, bf16[2,1536,128]{2,1,0:T(8,128)(2,1)S(1)}, u32[]{:S(2)}, u32[]{:S(2)}) collective-permute-start(bf16[2,1536,128]{2,1,0:T(8,128)(2,1)} %collective-permute-done.5.refs_2_), channel_id=1, source_target_pairs={{0,4},{4,0},{8,12},{12,8},{16,20},{20,16},{24,28},{28,24},{1,5},{5... | collective-permute-start | bytes 2359304 | tf_op jit(solution)/shard_map/ppermute | solution.py:441
  63.1 41.5 %collective-permute-start.9 = (bf16[2,1536,128]{2,1,0:T(8,128)(2,1)S(1)}, bf16[2,1536,128]{2,1,0:T(8,128)(2,1)S(1)}, u32[]{:S(2)}, u32[]{:S(2)}) collective-permute-start(bf16[2,1536,128]{2,1,0:T(8,128)(2,1)S(1)} %get-tuple-element.90.refs_0_), channel_id=1, source_target_pairs={{0,8},{4,12},{8,0},{12,4},{16,24},{20,28},{24,16},{28,20},{1,9},{5... | collective-permute-start | bytes 2359304 | tf_op jit(solution)/shard_map/ppermute | solution.py:441
  63.7 40.9 %collective-permute-start.8 = (bf16[2,1536,128]{2,1,0:T(8,128)(2,1)S(1)}, bf16[2,1536,128]{2,1,0:T(8,128)(2,1)S(1)}, u32[]{:S(2)}, u32[]{:S(2)}) collective-permute-start(bf16[2,1536,128]{2,1,0:T(8,128)(2,1)S(1)} %get-tuple-element.90.refs_0_), channel_id=1, source_target_pairs={{0,4},{4,0},{8,12},{12,8},{16,20},{20,16},{24,28},{28,24},{1,5},{5... | collective-permute-start | bytes 2359304 | tf_op jit(solution)/shard_map/ppermute | solution.py:441
  64.4 40.2 %collective-permute-start.11 = (bf16[1632,128]{1,0:T(8,128)(2,1)S(1)}, bf16[1632,128]{1,0:T(8,128)(2,1)S(1)}, u32[]{:S(2)}, u32[]{:S(2)}) collective-permute-start(bf16[1632,128]{1,0:T(8,128)(2,1)S(1)} %guest_attention.4), channel_id=1, source_target_pairs={{0,16},{4,20},{8,24},{12,28},{16,0},{20,4},{24,8},{28,12},{1,17},{... | collective-permute-start | bytes 1253384 | tf_op jit(solution)/shard_map/ppermute | solution.py:441
  67.6 37.0 %collective-permute-start.10 = (bf16[1536,128]{1,0:T(8,128)(2,1)S(1)}, bf16[1536,128]{1,0:T(8,128)(2,1)S(1)}, u32[]{:S(2)}, u32[]{:S(2)}) collective-permute-start(bf16[1536,128]{1,0:T(8,128)(2,1)S(1)} %copy-done.1), channel_id=1, source_target_pairs={{0,16},{4,20},{8,24},{12,28},{16,0},{20,4},{24,8},{28,12},{1,17},{... | collective-permute-start | bytes 1179656 | tf_op jit(solution)/shard_map/ppermute | solution.py:441
  104.6 20.7 %collective-permute-start.13 = (bf16[2,1536,128]{2,1,0:T(8,128)(2,1)S(1)}, bf16[2,1536,128]{2,1,0:T(8,128)(2,1)S(1)}, u32[]{:S(2)}, u32[]{:S(2)}) collective-permute-start(bf16[2,1536,128]{2,1,0:T(8,128)(2,1)S(1)} %collective-permute-done.9.refs_2_), channel_id=1, source_target_pairs={{0,4},{4,0},{8,12},{12,8},{16,20},{20,16},{24,28},{28,24},{1,5},{5... | collective-permute-start | bytes 2359304 | tf_op jit(solution)/shard_map/ppermute | solution.py:441
  107.3 18.0 %collective-permute-start.12 = (bf16[1536,128]{1,0:T(8,128)(2,1)S(1)}, bf16[1536,128]{1,0:T(8,128)(2,1)S(1)}, u32[]{:S(2)}, u32[]{:S(2)}) collective-permute-start(bf16[1536,128]{1,0:T(8,128)(2,1)S(1)} %get-tuple-element.112.q_ref), channel_id=1, source_target_pairs={{0,16},{4,20},{8,24},{12,28},{16,0},{20,4},{24,8},{28,12},{1,17},{... | collective-permute-start | bytes 1179656 | tf_op jit(solution)/shard_map/ppermute | solution.py:441
  107.3 37.0 %collective-permute-start.15 = (bf16[2,1536,128]{2,1,0:T(8,128)(2,1)S(1)}, bf16[2,1536,128]{2,1,0:T(8,128)(2,1)S(1)}, u32[]{:S(2)}, u32[]{:S(2)}) collective-permute-start(bf16[2,1536,128]{2,1,0:T(8,128)(2,1)S(1)} %get-tuple-element.98.refs_0_), channel_id=1, source_target_pairs={{0,8},{4,12},{8,0},{12,4},{16,24},{20,28},{24,16},{28,20},{1,9},{5... | collective-permute-start | bytes 2359304 | tf_op jit(solution)/shard_map/ppermute | solution.py:441
  110.8 33.5 %collective-permute-start.14 = (bf16[2,1536,128]{2,1,0:T(8,128)(2,1)S(1)}, bf16[2,1536,128]{2,1,0:T(8,128)(2,1)S(1)}, u32[]{:S(2)}, u32[]{:S(2)}) collective-permute-start(bf16[2,1536,128]{2,1,0:T(8,128)(2,1)S(1)} %get-tuple-element.98.refs_0_), channel_id=1, source_target_pairs={{0,4},{4,0},{8,12},{12,8},{16,20},{20,16},{24,28},{28,24},{1,5},{5... | collective-permute-start | bytes 2359304 | tf_op jit(solution)/shard_map/ppermute | solution.py:441
  110.9 33.4 %collective-permute-start.16 = (bf16[1632,128]{1,0:T(8,128)(2,1)S(1)}, bf16[1632,128]{1,0:T(8,128)(2,1)S(1)}, u32[]{:S(2)}, u32[]{:S(2)}) collective-permute-start(bf16[1632,128]{1,0:T(8,128)(2,1)S(1)} %guest_attention.5), channel_id=1, source_target_pairs={{0,16},{4,20},{8,24},{12,28},{16,0},{20,4},{24,8},{28,12},{1,17},{... | collective-permute-start | bytes 1253384 | tf_op jit(solution)/shard_map/ppermute | solution.py:441
  115.4 28.9 %copy-start.4 = (s32[24]{0:T(128)S(1)}, s32[24]{0:T(128)}, u32[]{:S(2)}) copy-start(s32[24]{0:T(128)} %select_reduce_fusion.2.order_ref) | copy-start | bytes 292
  125.3 4.3 %collective-permute-start.18 = (bf16[1536,128]{1,0:T(8,128)(2,1)S(1)}, bf16[1536,128]{1,0:T(8,128)(2,1)S(1)}, u32[]{:S(2)}, u32[]{:S(2)}) collective-permute-start(bf16[1536,128]{1,0:T(8,128)(2,1)S(1)} %merge_halves.4.refs_0_), channel_id=1, source_target_pairs={{0,1},{1,0},{2,3},{3,2},{4,5},{5,4},{6,7},{7,6},{8,9},{9,8},{10,11... | collective-permute-start | bytes 1179656 | tf_op jit(solution)/shard_map/ppermute | solution.py:449
  125.3 11.5 %collective-permute-start.17 = (bf16[1536,128]{1,0:T(8,128)(2,1)S(1)}, bf16[1536,128]{1,0:T(8,128)(2,1)S(1)}, u32[]{:S(2)}, u32[]{:S(2)}) collective-permute-start(bf16[1536,128]{1,0:T(8,128)(2,1)S(1)} %merge_halves.4.refs_0_), channel_id=1, source_target_pairs={{0,2},{1,3},{2,0},{3,1},{4,6},{5,7},{6,4},{7,5},{8,10},{9,11},{10,... | collective-permute-start | bytes 1179656 | tf_op jit(solution)/shard_map/ppermute | solution.py:449
  129.6 27.7 %collective-permute-start.25 = (bf16[1632,128]{1,0:T(8,128)(2,1)S(1)}, bf16[1632,128]{1,0:T(8,128)(2,1)S(1)}, u32[]{:S(2)}, u32[]{:S(2)}) collective-permute-start(bf16[1632,128]{1,0:T(8,128)(2,1)S(1)} %guest_attention.6), channel_id=1, source_target_pairs={{0,16},{4,20},{8,24},{12,28},{16,0},{20,4},{24,8},{28,12},{1,17},{... | collective-permute-start | bytes 1253384 | tf_op jit(solution)/shard_map/ppermute | solution.py:441
  144.9 9.5 %collective-permute-start.19 = (bf16[2,768,128]{2,1,0:T(8,128)(2,1)S(1)}, bf16[2,768,128]{2,1,0:T(8,128)(2,1)S(1)}, u32[]{:S(2)}, u32[]{:S(2)}) collective-permute-start(bf16[2,768,128]{2,1,0:T(8,128)(2,1)S(1)} %get-tuple-element.111), channel_id=1, source_target_pairs={{0,4},{4,0},{8,12},{12,8},{16,20},{20,16},{24,28},{28,24},{1,5},{5... | collective-permute-start | bytes 1179656 | tf_op jit(solution)/shard_map/ppermute | solution.py:441
  149.9 8.0 %collective-permute-start.23 = (bf16[1536,128]{1,0:T(8,128)(2,1)S(1)}, bf16[1536,128]{1,0:T(8,128)(2,1)S(1)}, u32[]{:S(2)}, u32[]{:S(2)}) collective-permute-start(bf16[1536,128]{1,0:T(8,128)(2,1)S(1)} %merge_halves.5.refs_4_), channel_id=1, source_target_pairs={{0,2},{1,3},{2,0},{3,1},{4,6},{5,7},{6,4},{7,5},{8,10},{9,11},{10,... | collective-permute-start | bytes 1179656 | tf_op jit(solution)/shard_map/ppermute | solution.py:449
  152.2 7.8 %collective-permute-start.20 = (bf16[2,768,128]{2,1,0:T(8,128)(2,1)S(1)}, bf16[2,768,128]{2,1,0:T(8,128)(2,1)S(1)}, u32[]{:S(2)}, u32[]{:S(2)}) collective-permute-start(bf16[2,768,128]{2,1,0:T(8,128)(2,1)S(1)} %get-tuple-element.113), channel_id=1, source_target_pairs={{0,4},{4,0},{8,12},{12,8},{16,20},{20,16},{24,28},{28,24},{1,5},{5... | collective-permute-start | bytes 1179656 | tf_op jit(solution)/shard_map/ppermute | solution.py:441
  157.2 14.1 %collective-permute-start.28 = (bf16[1632,128]{1,0:T(8,128)(2,1)S(1)}, bf16[1632,128]{1,0:T(8,128)(2,1)S(1)}, u32[]{:S(2)}, u32[]{:S(2)}) collective-permute-start(bf16[1632,128]{1,0:T(8,128)(2,1)S(1)} %guest_attention.7), channel_id=1, source_target_pairs={{0,16},{4,20},{8,24},{12,28},{16,0},{20,4},{24,8},{28,12},{1,17},{... | collective-permute-start | bytes 1253384 | tf_op jit(solution)/shard_map/ppermute | solution.py:441
  157.3 6.6 %collective-permute-start.22 = (bf16[1536,128]{1,0:T(8,128)(2,1)S(1)}, bf16[1536,128]{1,0:T(8,128)(2,1)S(1)}, u32[]{:S(2)}, u32[]{:S(2)}) collective-permute-start(bf16[1536,128]{1,0:T(8,128)(2,1)S(1)} %merge_halves.5.refs_4_), channel_id=1, source_target_pairs={{0,1},{1,0},{2,3},{3,2},{4,5},{5,4},{6,7},{7,6},{8,9},{9,8},{10,11... | collective-permute-start | bytes 1179656 | tf_op jit(solution)/shard_map/ppermute | solution.py:449
  157.4 6.6 %collective-permute-start.21 = (bf16[1536,128]{1,0:T(8,128)(2,1)S(1)}, bf16[1536,128]{1,0:T(8,128)(2,1)S(1)}, u32[]{:S(2)}, u32[]{:S(2)}) collective-permute-start(bf16[1536,128]{1,0:T(8,128)(2,1)S(1)} %collective-permute-done.17.refs_2_), channel_id=1, source_target_pairs={{0,1},{1,0},{2,3},{3,2},{4,5},{5,4},{6,7},{7,6},{8,9},{9,8},{10,11... | collective-permute-start | bytes 1179656 | tf_op jit(solution)/shard_map/ppermute | solution.py:449
  157.9 6.0 %collective-permute-start.24 = (bf16[1536,128]{1,0:T(8,128)(2,1)S(1)}, bf16[1536,128]{1,0:T(8,128)(2,1)S(1)}, u32[]{:S(2)}, u32[]{:S(2)}) collective-permute-start(bf16[1536,128]{1,0:T(8,128)(2,1)S(1)} %collective-permute-done.23.refs_6_), channel_id=1, source_target_pairs={{0,1},{1,0},{2,3},{3,2},{4,5},{5,4},{6,7},{7,6},{8,9},{9,8},{10,11... | collective-permute-start | bytes 1179656 | tf_op jit(solution)/shard_map/ppermute | solution.py:449
  163.8 10.3 %collective-permute-start.27 = (bf16[1536,128]{1,0:T(8,128)(2,1)S(1)}, bf16[1536,128]{1,0:T(8,128)(2,1)S(1)}, u32[]{:S(2)}, u32[]{:S(2)}) collective-permute-start(bf16[1536,128]{1,0:T(8,128)(2,1)S(1)} %merge_halves.6.refs_0_), channel_id=1, source_target_pairs={{0,2},{1,3},{2,0},{3,1},{4,6},{5,7},{6,4},{7,5},{8,10},{9,11},{10,... | collective-permute-start | bytes 1179656 | tf_op jit(solution)/shard_map/ppermute | solution.py:449
  172.3 7.0 %collective-permute-start.33 = (bf16[1024,128]{1,0:T(8,128)(2,1)S(1)}, bf16[1024,128]{1,0:T(8,128)(2,1)S(1)}, u32[]{:S(2)}, u32[]{:S(2)}) collective-permute-start(bf16[1024,128]{1,0:T(8,128)(2,1)S(1)} %get-tuple-element.126.refs_4_), channel_id=1, source_target_pairs={{0,2},{1,3},{2,0},{3,1},{4,6},{5,7},{6,4},{7,5},{8,10},{9,11},{10,... | collective-permute-start | bytes 786440 | tf_op jit(solution)/shard_map/ppermute | solution.py:449
  173.6 6.2 %collective-permute-start.26 = (bf16[1536,128]{1,0:T(8,128)(2,1)S(1)}, bf16[1536,128]{1,0:T(8,128)(2,1)S(1)}, u32[]{:S(2)}, u32[]{:S(2)}) collective-permute-start(bf16[1536,128]{1,0:T(8,128)(2,1)S(1)} %merge_halves.6.refs_0_), channel_id=1, source_target_pairs={{0,1},{1,0},{2,3},{3,2},{4,5},{5,4},{6,7},{7,6},{8,9},{9,8},{10,11... | collective-permute-start | bytes 1179656 | tf_op jit(solution)/shard_map/ppermute | solution.py:449
  174.1 7.4 %collective-permute-start.29 = (bf16[1536,128]{1,0:T(8,128)(2,1)S(1)}, bf16[1536,128]{1,0:T(8,128)(2,1)S(1)}, u32[]{:S(2)}, u32[]{:S(2)}) collective-permute-start(bf16[1536,128]{1,0:T(8,128)(2,1)S(1)} %collective-permute-done.27.refs_2_), channel_id=1, source_target_pairs={{0,1},{1,0},{2,3},{3,2},{4,5},{5,4},{6,7},{7,6},{8,9},{9,8},{10,11... | collective-permute-start | bytes 1179656 | tf_op jit(solution)/shard_map/ppermute | solution.py:449
  174.1 7.4 %collective-permute-start.32 = (bf16[1024,128]{1,0:T(8,128)(2,1)S(1)}, bf16[1024,128]{1,0:T(8,128)(2,1)S(1)}, u32[]{:S(2)}, u32[]{:S(2)}) collective-permute-start(bf16[1024,128]{1,0:T(8,128)(2,1)S(1)} %get-tuple-element.126.refs_4_), channel_id=1, source_target_pairs={{0,1},{1,0},{2,3},{3,2},{4,5},{5,4},{6,7},{7,6},{8,9},{9,8},{10,11... | collective-permute-start | bytes 786440 | tf_op jit(solution)/shard_map/ppermute | solution.py:449
  179.3 2.3 %collective-permute-start.34 = (bf16[1024,128]{1,0:T(8,128)(2,1)S(1)}, bf16[1024,128]{1,0:T(8,128)(2,1)S(1)}, u32[]{:S(2)}, u32[]{:S(2)}) collective-permute-start(bf16[1024,128]{1,0:T(8,128)(2,1)S(1)} %collective-permute-done.33.refs_6_), channel_id=1, source_target_pairs={{0,1},{1,0},{2,3},{3,2},{4,5},{5,4},{6,7},{7,6},{8,9},{9,8},{10,11... | collective-permute-start | bytes 786440 | tf_op jit(solution)/shard_map/ppermute | solution.py:449
  179.3 6.1 %collective-permute-start.30 = (bf16[512,128]{1,0:T(8,128)(2,1)S(1)}, bf16[512,128]{1,0:T(8,128)(2,1)S(1)}, u32[]{:S(2)}, u32[]{:S(2)}) collective-permute-start(bf16[512,128]{1,0:T(8,128)(2,1)S(1)} %get-tuple-element.127.refs_4_), channel_id=1, source_target_pairs={{0,1},{1,0},{2,3},{3,2},{4,5},{5,4},{6,7},{7,6},{8,9},{9,8},{10,11... | collective-permute-start | bytes 393224 | tf_op jit(solution)/shard_map/ppermute | solution.py:449
  179.8 5.5 %collective-permute-start.31 = (bf16[512,128]{1,0:T(8,128)(2,1)S(1)}, bf16[512,128]{1,0:T(8,128)(2,1)S(1)}, u32[]{:S(2)}, u32[]{:S(2)}) collective-permute-start(bf16[512,128]{1,0:T(8,128)(2,1)S(1)} %get-tuple-element.127.refs_4_), channel_id=1, source_target_pairs={{0,2},{1,3},{2,0},{3,1},{4,6},{5,7},{6,4},{7,5},{8,10},{9,11},{10,... | collective-permute-start | bytes 393224 | tf_op jit(solution)/shard_map/ppermute | solution.py:449
  185.3 1.3 collective-permute-start.35

commit v8 on v7

--- a/solution.py
+++ b/solution.py
@@ -456,7 +456,7 @@
 UNROLL = 12
 GUEST_US = 0.1
 PROJECT_US = 4
-UPPER_TILES = 4
+UPPER_TILES = 5
 
 
 def halves_body(queries, keys_values, global_ids, rand_ids, out_weight):

time: 189 us -> 191 us (1.011)
  no operation moved by 1% of the time
where the time goes in v8:
time: 191 us; the launch traced here: 190 us
  waiting for transfers between devices  94.3 us (49%)
  Pallas kernels  45.5 us (24%)
  starting transfers between devices  34.5 us (18%)
  local copies, waits for them, and re-layouts  9.37 us (5%)
  other arithmetic  6.31 us (3%)
    ppermute x21, waiting for transfers between devices, swap(): lax.ppermute(value, 'seq', [(i, i ^ distance) for i in range(shards)])  79.2 us
    ppermute x21, starting transfers between devices, swap(): lax.ppermute(value, 'seq', [(i, i ^ distance) for i in range(shards)])  26 us
    ppermute x15, waiting for transfers between devices, hop(): lax.ppermute(value, 'head', [(i, i ^ distance) for i in range(groups)])  15.1 us
    pallas_call x4, Pallas kernels, guest_call(): pl.pallas_call(functools.partial(guest_kernel, parts, len(pieces)), out_s...  14.6 us
    pallas_call x4, Pallas kernels, home_call(): pl.pallas_call(functools.partial(home_kernel, parts, len(pieces)), out_sh...  14.6 us
    ppermute x15, starting transfers between devices, hop(): lax.ppermute(value, 'head', [(i, i ^ distance) for i in range(groups)])  8.51 us
    pallas_call x2, Pallas kernels, last_terms(): pl.pallas_call(functools.partial(last_terms_kernel, len(pieces) // 2), gr...  6.06 us
    pallas_call x1, Pallas kernels, first_terms(): pl.pallas_call(functools.partial(first_terms_kernel, len(pieces) // 2), o...  5.39 us
  transfers between devices with their start and end apart: 36, of which 16 were waited for; matrix products, arithmetic and copies ran while one was open for 6% of the time, Pallas kernels for 23%

profile of v8, /device:TPU:0, one launch (start us, length us, event | category | flops | bytes accessed | tf_op | source)
XLA Modules:
  0.0 190.3 jit_solution(17868853548850501171)
XLA Ops:
  0.0 1.3 slice.24.refs_0_
  1.3 3.1 %collective-permute-start.1 = (bf16[2,1536,128]{2,1,0:T(8,128)(2,1)S(1)}, bf16[2,1536,128]{2,1,0:T(8,128)(2,1)}, u32[]{:S(2)}, u32[]{:S(2)}) collective-permute-start(bf16[2,1536,128]{2,1,0:T(8,128)(2,1)S(1)} %slice.24.refs_0_), channel_id=1, source_target_pairs={{0,8},{4,12},{8,0},{12,4},{16,24},{20,28},{24,16},{28,20},{1,9},{5... | collective-permute-start | bytes 2359304 | tf_op jit(solution)/shard_map/ppermute | solution.py:441
  4.4 1.5 collective-permute-start
  6.8 0.9 constant_dynamic-slice_fusion
  10.0 1.0 select_reduce_fusion
  15.1 1.2 fusion.14
  18.2 3.8 %collective-permute-done.1.refs_2_ = bf16[2,1536,128]{2,1,0:T(8,128)(2,1)} collective-permute-done((bf16[2,1536,128]{2,1,0:T(8,128)(2,1)S(1)}, bf16[2,1536,128]{2,1,0:T(8,128)(2,1)}, u32[]{:S(2)}, u32[]{:S(2)}) %collective-permute-start.1) | collective-permute-done | bytes 786464 | tf_op jit(solution)/shard_map/ppermute | solution.py:441
  22.0 1.5 collective-permute-done.refs_1_
  23.5 1.5 collective-permute-start.3
  25.9 2.7 %collective-permute-start.2 = (bf16[1536,128]{1,0:T(8,128)(2,1)}, bf16[1536,128]{1,0:T(8,128)(2,1)}, u32[]{:S(2)}, u32[]{:S(2)}) collective-permute-start(bf16[1536,128]{1,0:T(8,128)(2,1)} %get-tuple-element.70.q_ref), channel_id=1, source_target_pairs={{0,16},{4,20},{8,24},{12,28},{16,0},{20,4},{24,8},{28,12},{1,17},{... | collective-permute-start | bytes 1179656 | tf_op jit(solution)/shard_map/ppermute | solution.py:441
  28.8 2.2 %copy-done = bf16[2048,1024]{1,0:T(8,128)(2,1)S(1)} copy-done((bf16[2048,1024]{1,0:T(8,128)(2,1)S(1)}, bf16[2048,1024]{1,0:T(8,128)(2,1)}, u32[]{:S(2)}) %copy-start) | copy-done | bytes 4194328
  31.4 20.6 %collective-permute-done.2.q_ref = bf16[1536,128]{1,0:T(8,128)(2,1)} collective-permute-done((bf16[1536,128]{1,0:T(8,128)(2,1)}, bf16[1536,128]{1,0:T(8,128)(2,1)}, u32[]{:S(2)}, u32[]{:S(2)}) %collective-permute-start.2) | collective-permute-done | bytes 393248 | tf_op jit(solution)/shard_map/ppermute | solution.py:441
  52.1 4.7 %guest_attention.4 = bf16[1632,128]{1,0:T(8,128)(2,1)S(1)} custom-call(s32[192]{0:T(256)S(1)} %reshape.155.starts_ref, f32[24,512]{1,0:T(8,128)S(1)} %copy-done.3, bf16[1536,128]{1,0:T(8,128)(2,1)} %collective-permute-done.2.q_ref, bf16[2,1536,128]{2,1,0:T(8,128)(2,1)S(1)} %slice.24.refs_0_, bf16[2,1536,128]{2,1,0:T(8,128)(2,1)} %collective-permute-done.refs_1_, ...), custom_call_target="tpu_custom_call" | custom-call | flops 115000000 | tf_op jit(solution)/shard_map/guest_attention/pallas_call | solution.py:220
  56.7 1.2 collective-permute-done.6.q_ref
  58.0 1.8 collective-permute-done.5.refs_2_
  59.8 3.3 %collective-permute-start.7 = (bf16[2,1536,128]{2,1,0:T(8,128)(2,1)}, bf16[2,1536,128]{2,1,0:T(8,128)(2,1)S(1)}, u32[]{:S(2)}, u32[]{:S(2)}) collective-permute-start(bf16[2,1536,128]{2,1,0:T(8,128)(2,1)} %collective-permute-done.5.refs_2_), channel_id=1, source_target_pairs={{0,4},{4,0},{8,12},{12,8},{16,20},{20,16},{24,28},{28,24},{1,5},{5... | collective-permute-start | bytes 2359304 | tf_op jit(solution)/shard_map/ppermute | solution.py:441
  64.4 3.1 %collective-permute-start.11 = (bf16[1632,128]{1,0:T(8,128)(2,1)S(1)}, bf16[1632,128]{1,0:T(8,128)(2,1)S(1)}, u32[]{:S(2)}, u32[]{:S(2)}) collective-permute-start(bf16[1632,128]{1,0:T(8,128)(2,1)S(1)} %guest_attention.4), channel_id=1, source_target_pairs={{0,16},{4,20},{8,24},{12,28},{16,0},{20,4},{24,8},{28,12},{1,17},{... | collective-permute-start | bytes 1253384 | tf_op jit(solution)/shard_map/ppermute | solution.py:441
  67.6 4.6 %home_attention.4 = (f32[1536,128]{1,0:T(8,128)S(1)}, f32[1,32,128]{2,1,0:T(8,128)S(1)}) custom-call(s32[192]{0:T(256)S(1)} %reshape.152.starts_ref, f32[24,512]{1,0:T(8,128)S(1)} %copy-done.2, bf16[1536,128]{1,0:T(8,128)(2,1)} %get-tuple-element.70.q_ref, bf16[2,1536,128]{2,1,0:T(8,128)(2,1)S(1)} %slice.24.refs_0_, ...), custom_call_target="tpu_custom_call" | custom-call | tf_op jit(solution)/shard_map/home_attention/pallas_call | solution.py:242
  72.2 9.5 %collective-permute-done.7.refs_3_ = bf16[2,1536,128]{2,1,0:T(8,128)(2,1)S(1)} collective-permute-done((bf16[2,1536,128]{2,1,0:T(8,128)(2,1)}, bf16[2,1536,128]{2,1,0:T(8,128)(2,1)S(1)}, u32[]{:S(2)}, u32[]{:S(2)}) %collective-permute-start.7) | collective-permute-done | bytes 786464 | tf_op jit(solution)/shard_map/ppermute | solution.py:441
  81.7 4.4 %guest_attention.5 = bf16[1632,128]{1,0:T(8,128)(2,1)S(1)} custom-call(s32[192]{0:T(256)S(1)} %reshape.155.starts_ref, f32[24,512]{1,0:T(8,128)S(1)} %copy-done.3, bf16[1536,128]{1,0:T(8,128)(2,1)} %collective-permute-done.6.q_ref, bf16[2,1536,128]{2,1,0:T(8,128)(2,1)S(1)} %get-tuple-element.73.refs_0_, ...), custom_call_target="tpu_custom_call" | custom-call | flops 115000000 | tf_op jit(solution)/shard_map/guest_attention/pallas_call | solution.py:220
  86.2 18.4 %collective-permute-done.10.q_ref = bf16[1536,128]{1,0:T(8,128)(2,1)S(1)} collective-permute-done((bf16[1536,128]{1,0:T(8,128)(2,1)S(1)}, bf16[1536,128]{1,0:T(8,128)(2,1)S(1)}, u32[]{:S(2)}, u32[]{:S(2)}) %collective-permute-start.10) | collective-permute-done | bytes 393248 | tf_op jit(solution)/shard_map/ppermute | solution.py:441
  104.6 2.7 %collective-permute-start.13 = (bf16[2,1536,128]{2,1,0:T(8,128)(2,1)S(1)}, bf16[2,1536,128]{2,1,0:T(8,128)(2,1)S(1)}, u32[]{:S(2)}, u32[]{:S(2)}) collective-permute-start(bf16[2,1536,128]{2,1,0:T(8,128)(2,1)S(1)} %collective-permute-done.9.refs_2_), channel_id=1, source_target_pairs={{0,4},{4,0},{8,12},{12,8},{16,20},{20,16},{24,28},{28,24},{1,5},{5... | collective-permute-start | bytes 2359304 | tf_op jit(solution)/shard_map/ppermute | solution.py:441
  107.3 3.6 %collective-permute-start.15 = (bf16[2,1536,128]{2,1,0:T(8,128)(2,1)S(1)}, bf16[2,1536,128]{2,1,0:T(8,128)(2,1)S(1)}, u32[]{:S(2)}, u32[]{:S(2)}) collective-permute-start(bf16[2,1536,128]{2,1,0:T(8,128)(2,1)S(1)} %get-tuple-element.98.refs_0_), channel_id=1, source_target_pairs={{0,8},{4,12},{8,0},{12,4},{16,24},{20,28},{24,16},{28,20},{1,9},{5... | collective-permute-start | bytes 2359304 | tf_op jit(solution)/shard_map/ppermute | solution.py:441
  111.0 4.4 %home_attention.5 = (f32[1536,128]{1,0:T(8,128)S(1)}, f32[1,32,128]{2,1,0:T(8,128)S(1)}) custom-call(s32[192]{0:T(256)S(1)} %reshape.152.starts_ref, f32[24,512]{1,0:T(8,128)S(1)} %copy-done.2, bf16[1536,128]{1,0:T(8,128)(2,1)} %get-tuple-element.74.q_ref, bf16[2,1536,128]{2,1,0:T(8,128)(2,1)S(1)} %get-tuple-element.73.refs_0_, ...), custom_call_target="tpu_custom_call" | custom-call | tf_op jit(solution)/shard_map/home_attention/pallas_call | solution.py:242
  115.4 1.0 merge_halves.4.refs_0_
  116.4 8.9 %collective-permute-done.12.q_ref = bf16[1536,128]{1,0:T(8,128)(2,1)S(1)} collective-permute-done((bf16[1536,128]{1,0:T(8,128)(2,1)S(1)}, bf16[1536,128]{1,0:T(8,128)(2,1)S(1)}, u32[]{:S(2)}, u32[]{:S(2)}) %collective-permute-start.12) | collective-permute-done | bytes 393248 | tf_op jit(solution)/shard_map/ppermute | solution.py:441
  125.3 1.5 collective-permute-start.17
  126.8 2.8 %guest_attention.6 = bf16[1632,128]{1,0:T(8,128)(2,1)S(1)} custom-call(s32[192]{0:T(256)S(1)} %reshape.155.starts_ref, f32[24,512]{1,0:T(8,128)S(1)} %copy-done.3, bf16[1536,128]{1,0:T(8,128)(2,1)S(1)} %collective-permute-done.10.q_ref, bf16[2,1536,128]{2,1,0:T(8,128)(2,1)S(1)} %get-tuple-element.90.refs_0_, ...), custom_call_target="tpu_custom_call" | custom-call | flops 115000000 | tf_op jit(solution)/shard_map/guest_attention/pallas_call | solution.py:220
  129.6 7.2 %collective-permute-done.17.refs_2_ = bf16[1536,128]{1,0:T(8,128)(2,1)S(1)} collective-permute-done((bf16[1536,128]{1,0:T(8,128)(2,1)S(1)}, bf16[1536,128]{1,0:T(8,128)(2,1)S(1)}, u32[]{:S(2)}, u32[]{:S(2)}) %collective-permute-start.17) | collective-permute-done | bytes 393248 | tf_op jit(solution)/shard_map/ppermute | solution.py:449
  136.8 7.5 %collective-permute-done.16.message_ref = bf16[1632,128]{1,0:T(8,128)(2,1)S(1)} collective-permute-done((bf16[1632,128]{1,0:T(8,128)(2,1)S(1)}, bf16[1632,128]{1,0:T(8,128)(2,1)S(1)}, u32[]{:S(2)}, u32[]{:S(2)}) %collective-permute-start.16) | collective-permute-done | bytes 417824 | tf_op jit(solution)/shard_map/ppermute | solution.py:441
  144.9 1.3 collective-permute-start.19
  146.2 2.7 %home_attention.6 = (f32[1536,128]{1,0:T(8,128)S(1)}, f32[1,32,128]{2,1,0:T(8,128)S(1)}) custom-call(s32[192]{0:T(256)S(1)} %reshape.152.starts_ref, f32[24,512]{1,0:T(8,128)S(1)} %copy-done.2, bf16[1536,128]{1,0:T(8,128)(2,1)S(1)} %copy-done.1, bf16[2,1536,128]{2,1,0:T(8,128)(2,1)S(1)} %get-tuple-element.90.refs_0_, ...), custom_call_target="tpu_custom_call" | custom-call | tf_op jit(solution)/shard_map/home_attention/pallas_call | solution.py:242
  149.0 1.0 merge_halves.5.refs_4_
  149.9 2.2 %collective-permute-start.23 = (bf16[1536,128]{1,0:T(8,128)(2,1)S(1)}, bf16[1536,128]{1,0:T(8,128)(2,1)S(1)}, u32[]{:S(2)}, u32[]{:S(2)}) collective-permute-start(bf16[1536,128]{1,0:T(8,128)(2,1)S(1)} %merge_halves.5.refs_4_), channel_id=1, source_target_pairs={{0,2},{1,3},{2,0},{3,1},{4,6},{5,7},{6,4},{7,5},{8,10},{9,11},{10,... | collective-permute-start | bytes 1179656 | tf_op jit(solution)/shard_map/ppermute | solution.py:449
  152.6 1.8 collective-permute-done.19.refs_3_
  154.4 2.8 %guest_attention.7 = bf16[1632,128]{1,0:T(8,128)(2,1)S(1)} custom-call(s32[192]{0:T(256)S(1)} %reshape.157.starts_ref, f32[24,512]{1,0:T(8,128)S(1)} %copy-done.3, bf16[1536,128]{1,0:T(8,128)(2,1)S(1)} %collective-permute-done.12.q_ref, bf16[2,1536,128]{2,1,0:T(8,128)(2,1)S(1)} %get-tuple-element.98.refs_0_, ...), custom_call_target="tpu_custom_call" | custom-call | flops 115000000 | tf_op jit(solution)/shard_map/guest_attention/pallas_call | solution.py:220
  158.0 2.0 %collective-permute-done.20.refs_4_ = bf16[2,768,128]{2,1,0:T(8,128)(2,1)S(1)} collective-permute-done((bf16[2,768,128]{2,1,0:T(8,128)(2,1)S(1)}, bf16[2,768,128]{2,1,0:T(8,128)(2,1)S(1)}, u32[]{:S(2)}, u32[]{:S(2)}) %collective-permute-start.20) | collective-permute-done | bytes 393248 | tf_op jit(solution)/shard_map/ppermute | solution.py:441
  159.9 2.9 %home_attention.7 = (f32[1536,128]{1,0:T(8,128)S(1)}, f32[1,32,128]{2,1,0:T(8,128)S(1)}) custom-call(s32[192]{0:T(256)S(1)} %reshape.154.starts_ref, f32[24,512]{1,0:T(8,128)S(1)} %copy-done.2, bf16[1536,128]{1,0:T(8,128)(2,1)S(1)} %get-tuple-element.112.q_ref, bf16[2,1536,128]{2,1,0:T(8,128)(2,1)S(1)} %get-tuple-element.98.refs_0_, ...), custom_call_target="tpu_custom_call" | custom-call | tf_op jit(solution)/shard_map/home_attention/pallas_call | solution.py:242
  162.9 1.0 merge_halves.6.refs_0_
  164.0 5.4 %first_terms.1.sum_ref = f32[1536,1024]{1,0:T(8,128)S(1)} custom-call(bf16[1024,1024]{1,0:T(8,128)(2,1)S(1)} %bitcast.5, bf16[1536,128]{1,0:T(8,128)(2,1)S(1)} %merge_halves.4.refs_0_, bf16[1536,128]{1,0:T(8,128)(2,1)S(1)} %collective-permute-done.18.refs_1_, bf16[1536,128]{1,0:T(8,128)(2,1)S(1)} %collective-permute-done.17.refs_2_, ...), custom_call_target="tpu_custom_call" | custom-call | tf_op jit(solution)/shard_map/first_terms/pallas_call | solution.py:329
  169.4 2.0 %collective-permute-done.28.message_ref = bf16[1632,128]{1,0:T(8,128)(2,1)S(1)} collective-permute-done((bf16[1632,128]{1,0:T(8,128)(2,1)S(1)}, bf16[1632,128]{1,0:T(8,128)(2,1)S(1)}, u32[]{:S(2)}, u32[]{:S(2)}) %collective-permute-start.28) | collective-permute-done | bytes 417824 | tf_op jit(solution)/shard_map/ppermute | solution.py:441
  171.4 0.9 merge_halves.7
  172.3 1.2 collective-permute-start.33
  174.6 6.0 %collective-permute-done.33.refs_6_ = bf16[1280,128]{1,0:T(8,128)(2,1)S(1)} collective-permute-done((bf16[1280,128]{1,0:T(8,128)(2,1)S(1)}, bf16[1280,128]{1,0:T(8,128)(2,1)S(1)}, u32[]{:S(2)}, u32[]{:S(2)}) %collective-permute-start.33) | collective-permute-done | bytes 327712 | tf_op jit(solution)/shard_map/ppermute | solution.py:449
  181.2 1.8 collective-permute-start.31
  183.0 4.5 %last_terms.2.refs_8_ = bf16[1536,1024]{1,0:T(8,128)(2,1)} custom-call(bf16[1024,1024]{1,0:T(8,128)(2,1)S(1)} %bitcast.6, f32[1536,1024]{1,0:T(8,128)S(1)} %first_terms.1.sum_ref, bf16[1536,128]{1,0:T(8,128)(2,1)S(1)} %merge_halves.6.refs_0_, bf16[1536,128]{1,0:T(8,128)(2,1)S(1)} %collective-permute-done.26.refs_1_, ...), custom_call_target="tpu_custom_call" | custom-call | flops 4600000000 | tf_op jit(solution)/shard_map/last_terms/pallas_call | solution.py:285
  187.5 1.2 collective-permute-done.35.refs_7_
  188.8 1.5 last_terms.3
  (104 shorter events, 15.8 us)
Async XLA Ops:
  0.0 15.1 %copy-start.6 = (bf16[1536,512]{1,0:T(8,128)(2,1)S(1)}, bf16[1536,512]{1,0:T(8,128)(2,1)}, u32[]{:S(2)}) copy-start(bf16[1536,512]{1,0:T(8,128)(2,1)} %param.5) | copy-start | bytes 4718596
  1.3 20.7 %collective-permute-start.1 = (bf16[2,1536,128]{2,1,0:T(8,128)(2,1)S(1)}, bf16[2,1536,128]{2,1,0:T(8,128)(2,1)}, u32[]{:S(2)}, u32[]{:S(2)}) collective-permute-start(bf16[2,1536,128]{2,1,0:T(8,128)(2,1)S(1)} %slice.24.refs_0_), channel_id=1, source_target_pairs={{0,8},{4,12},{8,0},{12,4},{16,24},{20,28},{24,16},{28,20},{1,9},{5... | collective-permute-start | bytes 2359304 | tf_op jit(solution)/shard_map/ppermute | solution.py:441
  4.4 19.1 %collective-permute-start = (bf16[2,1536,128]{2,1,0:T(8,128)(2,1)S(1)}, bf16[2,1536,128]{2,1,0:T(8,128)(2,1)}, u32[]{:S(2)}, u32[]{:S(2)}) collective-permute-start(bf16[2,1536,128]{2,1,0:T(8,128)(2,1)S(1)} %slice.24.refs_0_), channel_id=1, source_target_pairs={{0,4},{4,0},{8,12},{12,8},{16,20},{20,16},{24,28},{28,24},{1,5},{5... | collective-permute-start | bytes 2359304 | tf_op jit(solution)/shard_map/ppermute | solution.py:441
  15.1 2.7 %copy-start.5 = (bf16[2,1536,512]{2,1,0:T(8,128)(2,1)S(1)}, bf16[2,1536,512]{2,1,0:T(8,128)(2,1)}, u32[]{:S(2)}) copy-start(bf16[2,1536,512]{2,1,0:T(8,128)(2,1)} %param.6) | copy-start | bytes 9437188
  23.5 28.6 %collective-permute-start.3 = (bf16[2,1536,128]{2,1,0:T(8,128)(2,1)}, bf16[2,1536,128]{2,1,0:T(8,128)(2,1)}, u32[]{:S(2)}, u32[]{:S(2)}) collective-permute-start(bf16[2,1536,128]{2,1,0:T(8,128)(2,1)} %collective-permute-done.1.refs_2_), channel_id=1, source_target_pairs={{0,4},{4,0},{8,12},{12,8},{16,20},{20,16},{24,28},{28,24},{1,5},{5... | collective-permute-start | bytes 2359304 | tf_op jit(solution)/shard_map/ppermute | solution.py:441
  25.0 34.8 %collective-permute-start.5 = (bf16[2,1536,128]{2,1,0:T(8,128)(2,1)S(1)}, bf16[2,1536,128]{2,1,0:T(8,128)(2,1)}, u32[]{:S(2)}, u32[]{:S(2)}) collective-permute-start(bf16[2,1536,128]{2,1,0:T(8,128)(2,1)S(1)} %get-tuple-element.73.refs_0_), channel_id=1, source_target_pairs={{0,8},{4,12},{8,0},{12,4},{16,24},{20,28},{24,16},{28,20},{1,9},{5... | collective-permute-start | bytes 2359304 | tf_op jit(solution)/shard_map/ppermute | solution.py:441
  25.5 34.3 %collective-permute-start.4 = (bf16[2,1536,128]{2,1,0:T(8,128)(2,1)S(1)}, bf16[2,1536,128]{2,1,0:T(8,128)(2,1)}, u32[]{:S(2)}, u32[]{:S(2)}) collective-permute-start(bf16[2,1536,128]{2,1,0:T(8,128)(2,1)S(1)} %get-tuple-element.73.refs_0_), channel_id=1, source_target_pairs={{0,4},{4,0},{8,12},{12,8},{16,20},{20,16},{24,28},{28,24},{1,5},{5... | collective-permute-start | bytes 2359304 | tf_op jit(solution)/shard_map/ppermute | solution.py:441
  25.9 26.2 %collective-permute-start.2 = (bf16[1536,128]{1,0:T(8,128)(2,1)}, bf16[1536,128]{1,0:T(8,128)(2,1)}, u32[]{:S(2)}, u32[]{:S(2)}) collective-permute-start(bf16[1536,128]{1,0:T(8,128)(2,1)} %get-tuple-element.70.q_ref), channel_id=1, source_target_pairs={{0,16},{4,20},{8,24},{12,28},{16,0},{20,4},{24,8},{28,12},{1,17},{... | collective-permute-start | bytes 1179656 | tf_op jit(solution)/shard_map/ppermute | solution.py:441
  28.6 29.4 %collective-permute-start.6 = (bf16[1536,128]{1,0:T(8,128)(2,1)}, bf16[1536,128]{1,0:T(8,128)(2,1)}, u32[]{:S(2)}, u32[]{:S(2)}) collective-permute-start(bf16[1536,128]{1,0:T(8,128)(2,1)} %get-tuple-element.74.q_ref), channel_id=1, source_target_pairs={{0,16},{4,20},{8,24},{12,28},{16,0},{20,4},{24,8},{28,12},{1,17},{... | collective-permute-start | bytes 1179656 | tf_op jit(solution)/shard_map/ppermute | solution.py:441
  28.8 2.2 %copy-start = (bf16[2048,1024]{1,0:T(8,128)(2,1)S(1)}, bf16[2048,1024]{1,0:T(8,128)(2,1)}, u32[]{:S(2)}) copy-start(bf16[2048,1024]{1,0:T(8,128)(2,1)} %param.9) | copy-start | bytes 12582916
  31.0 21.0 %copy-start.3 = (f32[24,512]{1,0:T(8,128)S(1)}, f32[24,512]{1,0:T(8,128)}, u32[]{:S(2)}) copy-start(f32[24,512]{1,0:T(8,128)} %reshape.156.bias_ref) | copy-start | bytes 147460
  31.0 36.5 %copy-start.1 = (bf16[1536,128]{1,0:T(8,128)(2,1)S(1)}, bf16[1536,128]{1,0:T(8,128)(2,1)}, u32[]{:S(2)}) copy-start(bf16[1536,128]{1,0:T(8,128)(2,1)} %get-tuple-element.91.q_ref) | copy-start | bytes 1179652
  31.0 36.6 %copy-start.2 = (f32[24,512]{1,0:T(8,128)S(1)}, f32[24,512]{1,0:T(8,128)}, u32[]{:S(2)}) copy-start(f32[24,512]{1,0:T(8,128)} %reshape.153.bias_ref) | copy-start | bytes 147460
  59.8 21.9 %collective-permute-start.7 = (bf16[2,1536,128]{2,1,0:T(8,128)(2,1)}, bf16[2,1536,128]{2,1,0:T(8,128)(2,1)S(1)}, u32[]{:S(2)}, u32[]{:S(2)}) collective-permute-start(bf16[2,1536,128]{2,1,0:T(8,128)(2,1)} %collective-permute-done.5.refs_2_), channel_id=1, source_target_pairs={{0,4},{4,0},{8,12},{12,8},{16,20},{20,16},{24,28},{28,24},{1,5},{5... | collective-permute-start | bytes 2359304 | tf_op jit(solution)/shard_map/ppermute | solution.py:441
  63.1 41.5 %collective-permute-start.9 = (bf16[2,1536,128]{2,1,0:T(8,128)(2,1)S(1)}, bf16[2,1536,128]{2,1,0:T(8,128)(2,1)S(1)}, u32[]{:S(2)}, u32[]{:S(2)}) collective-permute-start(bf16[2,1536,128]{2,1,0:T(8,128)(2,1)S(1)} %get-tuple-element.90.refs_0_), channel_id=1, source_target_pairs={{0,8},{4,12},{8,0},{12,4},{16,24},{20,28},{24,16},{28,20},{1,9},{5... | collective-permute-start | bytes 2359304 | tf_op jit(solution)/shard_map/ppermute | solution.py:441
  63.7 40.9 %collective-permute-start.8 = (bf16[2,1536,128]{2,1,0:T(8,128)(2,1)S(1)}, bf16[2,1536,128]{2,1,0:T(8,128)(2,1)S(1)}, u32[]{:S(2)}, u32[]{:S(2)}) collective-permute-start(bf16[2,1536,128]{2,1,0:T(8,128)(2,1)S(1)} %get-tuple-element.90.refs_0_), channel_id=1, source_target_pairs={{0,4},{4,0},{8,12},{12,8},{16,20},{20,16},{24,28},{28,24},{1,5},{5... | collective-permute-start | bytes 2359304 | tf_op jit(solution)/shard_map/ppermute | solution.py:441
  64.4 40.2 %collective-permute-start.11 = (bf16[1632,128]{1,0:T(8,128)(2,1)S(1)}, bf16[1632,128]{1,0:T(8,128)(2,1)S(1)}, u32[]{:S(2)}, u32[]{:S(2)}) collective-permute-start(bf16[1632,128]{1,0:T(8,128)(2,1)S(1)} %guest_attention.4), channel_id=1, source_target_pairs={{0,16},{4,20},{8,24},{12,28},{16,0},{20,4},{24,8},{28,12},{1,17},{... | collective-permute-start | bytes 1253384 | tf_op jit(solution)/shard_map/ppermute | solution.py:441
  67.6 37.0 %collective-permute-start.10 = (bf16[1536,128]{1,0:T(8,128)(2,1)S(1)}, bf16[1536,128]{1,0:T(8,128)(2,1)S(1)}, u32[]{:S(2)}, u32[]{:S(2)}) collective-permute-start(bf16[1536,128]{1,0:T(8,128)(2,1)S(1)} %copy-done.1), channel_id=1, source_target_pairs={{0,16},{4,20},{8,24},{12,28},{16,0},{20,4},{24,8},{28,12},{1,17},{... | collective-permute-start | bytes 1179656 | tf_op jit(solution)/shard_map/ppermute | solution.py:441
  104.6 20.7 %collective-permute-start.13 = (bf16[2,1536,128]{2,1,0:T(8,128)(2,1)S(1)}, bf16[2,1536,128]{2,1,0:T(8,128)(2,1)S(1)}, u32[]{:S(2)}, u32[]{:S(2)}) collective-permute-start(bf16[2,1536,128]{2,1,0:T(8,128)(2,1)S(1)} %collective-permute-done.9.refs_2_), channel_id=1, source_target_pairs={{0,4},{4,0},{8,12},{12,8},{16,20},{20,16},{24,28},{28,24},{1,5},{5... | collective-permute-start | bytes 2359304 | tf_op jit(solution)/shard_map/ppermute | solution.py:441
  107.3 18.0 %collective-permute-start.12 = (bf16[1536,128]{1,0:T(8,128)(2,1)S(1)}, bf16[1536,128]{1,0:T(8,128)(2,1)S(1)}, u32[]{:S(2)}, u32[]{:S(2)}) collective-permute-start(bf16[1536,128]{1,0:T(8,128)(2,1)S(1)} %get-tuple-element.112.q_ref), channel_id=1, source_target_pairs={{0,16},{4,20},{8,24},{12,28},{16,0},{20,4},{24,8},{28,12},{1,17},{... | collective-permute-start | bytes 1179656 | tf_op jit(solution)/shard_map/ppermute | solution.py:441
  107.3 37.0 %collective-permute-start.15 = (bf16[2,1536,128]{2,1,0:T(8,128)(2,1)S(1)}, bf16[2,1536,128]{2,1,0:T(8,128)(2,1)S(1)}, u32[]{:S(2)}, u32[]{:S(2)}) collective-permute-start(bf16[2,1536,128]{2,1,0:T(8,128)(2,1)S(1)} %get-tuple-element.98.refs_0_), channel_id=1, source_target_pairs={{0,8},{4,12},{8,0},{12,4},{16,24},{20,28},{24,16},{28,20},{1,9},{5... | collective-permute-start | bytes 2359304 | tf_op jit(solution)/shard_map/ppermute | solution.py:441
  110.8 33.5 %collective-permute-start.14 = (bf16[2,1536,128]{2,1,0:T(8,128)(2,1)S(1)}, bf16[2,1536,128]{2,1,0:T(8,128)(2,1)S(1)}, u32[]{:S(2)}, u32[]{:S(2)}) collective-permute-start(bf16[2,1536,128]{2,1,0:T(8,128)(2,1)S(1)} %get-tuple-element.98.refs_0_), channel_id=1, source_target_pairs={{0,4},{4,0},{8,12},{12,8},{16,20},{20,16},{24,28},{28,24},{1,5},{5... | collective-permute-start | bytes 2359304 | tf_op jit(solution)/shard_map/ppermute | solution.py:441
  110.9 33.4 %collective-permute-start.16 = (bf16[1632,128]{1,0:T(8,128)(2,1)S(1)}, bf16[1632,128]{1,0:T(8,128)(2,1)S(1)}, u32[]{:S(2)}, u32[]{:S(2)}) collective-permute-start(bf16[1632,128]{1,0:T(8,128)(2,1)S(1)} %guest_attention.5), channel_id=1, source_target_pairs={{0,16},{4,20},{8,24},{12,28},{16,0},{20,4},{24,8},{28,12},{1,17},{... | collective-permute-start | bytes 1253384 | tf_op jit(solution)/shard_map/ppermute | solution.py:441
  115.4 28.9 %copy-start.4 = (s32[24]{0:T(128)S(1)}, s32[24]{0:T(128)}, u32[]{:S(2)}) copy-start(s32[24]{0:T(128)} %select_reduce_fusion.2.order_ref) | copy-start | bytes 292
  125.3 4.3 %collective-permute-start.18 = (bf16[1536,128]{1,0:T(8,128)(2,1)S(1)}, bf16[1536,128]{1,0:T(8,128)(2,1)S(1)}, u32[]{:S(2)}, u32[]{:S(2)}) collective-permute-start(bf16[1536,128]{1,0:T(8,128)(2,1)S(1)} %merge_halves.4.refs_0_), channel_id=1, source_target_pairs={{0,1},{1,0},{2,3},{3,2},{4,5},{5,4},{6,7},{7,6},{8,9},{9,8},{10,11... | collective-permute-start | bytes 1179656 | tf_op jit(solution)/shard_map/ppermute | solution.py:449
  125.3 11.5 %collective-permute-start.17 = (bf16[1536,128]{1,0:T(8,128)(2,1)S(1)}, bf16[1536,128]{1,0:T(8,128)(2,1)S(1)}, u32[]{:S(2)}, u32[]{:S(2)}) collective-permute-start(bf16[1536,128]{1,0:T(8,128)(2,1)S(1)} %merge_halves.4.refs_0_), channel_id=1, source_target_pairs={{0,2},{1,3},{2,0},{3,1},{4,6},{5,7},{6,4},{7,5},{8,10},{9,11},{10,... | collective-permute-start | bytes 1179656 | tf_op jit(solution)/shard_map/ppermute | solution.py:449
  129.6 27.7 %collective-permute-start.25 = (bf16[1632,128]{1,0:T(8,128)(2,1)S(1)}, bf16[1632,128]{1,0:T(8,128)(2,1)S(1)}, u32[]{:S(2)}, u32[]{:S(2)}) collective-permute-start(bf16[1632,128]{1,0:T(8,128)(2,1)S(1)} %guest_attention.6), channel_id=1, source_target_pairs={{0,16},{4,20},{8,24},{12,28},{16,0},{20,4},{24,8},{28,12},{1,17},{... | collective-permute-start | bytes 1253384 | tf_op jit(solution)/shard_map/ppermute | solution.py:441
  144.9 9.5 %collective-permute-start.19 = (bf16[2,768,128]{2,1,0:T(8,128)(2,1)S(1)}, bf16[2,768,128]{2,1,0:T(8,128)(2,1)S(1)}, u32[]{:S(2)}, u32[]{:S(2)}) collective-permute-start(bf16[2,768,128]{2,1,0:T(8,128)(2,1)S(1)} %get-tuple-element.111), channel_id=1, source_target_pairs={{0,4},{4,0},{8,12},{12,8},{16,20},{20,16},{24,28},{28,24},{1,5},{5... | collective-permute-start | bytes 1179656 | tf_op jit(solution)/shard_map/ppermute | solution.py:441
  149.9 8.0 %collective-permute-start.23 = (bf16[1536,128]{1,0:T(8,128)(2,1)S(1)}, bf16[1536,128]{1,0:T(8,128)(2,1)S(1)}, u32[]{:S(2)}, u32[]{:S(2)}) collective-permute-start(bf16[1536,128]{1,0:T(8,128)(2,1)S(1)} %merge_halves.5.refs_4_), channel_id=1, source_target_pairs={{0,2},{1,3},{2,0},{3,1},{4,6},{5,7},{6,4},{7,5},{8,10},{9,11},{10,... | collective-permute-start | bytes 1179656 | tf_op jit(solution)/shard_map/ppermute | solution.py:449
  152.2 7.8 %collective-permute-start.20 = (bf16[2,768,128]{2,1,0:T(8,128)(2,1)S(1)}, bf16[2,768,128]{2,1,0:T(8,128)(2,1)S(1)}, u32[]{:S(2)}, u32[]{:S(2)}) collective-permute-start(bf16[2,768,128]{2,1,0:T(8,128)(2,1)S(1)} %get-tuple-element.113), channel_id=1, source_target_pairs={{0,4},{4,0},{8,12},{12,8},{16,20},{20,16},{24,28},{28,24},{1,5},{5... | collective-permute-start | bytes 1179656 | tf_op jit(solution)/shard_map/ppermute | solution.py:441
  157.2 14.1 %collective-permute-start.28 = (bf16[1632,128]{1,0:T(8,128)(2,1)S(1)}, bf16[1632,128]{1,0:T(8,128)(2,1)S(1)}, u32[]{:S(2)}, u32[]{:S(2)}) collective-permute-start(bf16[1632,128]{1,0:T(8,128)(2,1)S(1)} %guest_attention.7), channel_id=1, source_target_pairs={{0,16},{4,20},{8,24},{12,28},{16,0},{20,4},{24,8},{28,12},{1,17},{... | collective-permute-start | bytes 1253384 | tf_op jit(solution)/shard_map/ppermute | solution.py:441
  157.3 6.6 %collective-permute-start.22 = (bf16[1536,128]{1,0:T(8,128)(2,1)S(1)}, bf16[1536,128]{1,0:T(8,128)(2,1)S(1)}, u32[]{:S(2)}, u32[]{:S(2)}) collective-permute-start(bf16[1536,128]{1,0:T(8,128)(2,1)S(1)} %merge_halves.5.refs_4_), channel_id=1, source_target_pairs={{0,1},{1,0},{2,3},{3,2},{4,5},{5,4},{6,7},{7,6},{8,9},{9,8},{10,11... | collective-permute-start | bytes 1179656 | tf_op jit(solution)/shard_map/ppermute | solution.py:449
  157.4 6.6 %collective-permute-start.21 = (bf16[1536,128]{1,0:T(8,128)(2,1)S(1)}, bf16[1536,128]{1,0:T(8,128)(2,1)S(1)}, u32[]{:S(2)}, u32[]{:S(2)}) collective-permute-start(bf16[1536,128]{1,0:T(8,128)(2,1)S(1)} %collective-permute-done.17.refs_2_), channel_id=1, source_target_pairs={{0,1},{1,0},{2,3},{3,2},{4,5},{5,4},{6,7},{7,6},{8,9},{9,8},{10,11... | collective-permute-start | bytes 1179656 | tf_op jit(solution)/shard_map/ppermute | solution.py:449
  157.9 6.0 %collective-permute-start.24 = (bf16[1536,128]{1,0:T(8,128)(2,1)S(1)}, bf16[1536,128]{1,0:T(8,128)(2,1)S(1)}, u32[]{:S(2)}, u32[]{:S(2)}) collective-permute-start(bf16[1536,128]{1,0:T(8,128)(2,1)S(1)} %collective-permute-done.23.refs_6_), channel_id=1, source_target_pairs={{0,1},{1,0},{2,3},{3,2},{4,5},{5,4},{6,7},{7,6},{8,9},{9,8},{10,11... | collective-permute-start | bytes 1179656 | tf_op jit(solution)/shard_map/ppermute | solution.py:449
  163.8 10.3 %collective-permute-start.27 = (bf16[1536,128]{1,0:T(8,128)(2,1)S(1)}, bf16[1536,128]{1,0:T(8,128)(2,1)S(1)}, u32[]{:S(2)}, u32[]{:S(2)}) collective-permute-start(bf16[1536,128]{1,0:T(8,128)(2,1)S(1)} %merge_halves.6.refs_0_), channel_id=1, source_target_pairs={{0,2},{1,3},{2,0},{3,1},{4,6},{5,7},{6,4},{7,5},{8,10},{9,11},{10,... | collective-permute-start | bytes 1179656 | tf_op jit(solution)/shard_map/ppermute | solution.py:449
  172.3 8.4 %collective-permute-start.33 = (bf16[1280,128]{1,0:T(8,128)(2,1)S(1)}, bf16[1280,128]{1,0:T(8,128)(2,1)S(1)}, u32[]{:S(2)}, u32[]{:S(2)}) collective-permute-start(bf16[1280,128]{1,0:T(8,128)(2,1)S(1)} %get-tuple-element.126.refs_4_), channel_id=1, source_target_pairs={{0,2},{1,3},{2,0},{3,1},{4,6},{5,7},{6,4},{7,5},{8,10},{9,11},{10,... | collective-permute-start | bytes 983048 | tf_op jit(solution)/shard_map/ppermute | solution.py:449
  173.6 7.7 %collective-permute-start.26 = (bf16[1536,128]{1,0:T(8,128)(2,1)S(1)}, bf16[1536,128]{1,0:T(8,128)(2,1)S(1)}, u32[]{:S(2)}, u32[]{:S(2)}) collective-permute-start(bf16[1536,128]{1,0:T(8,128)(2,1)S(1)} %merge_halves.6.refs_0_), channel_id=1, source_target_pairs={{0,1},{1,0},{2,3},{3,2},{4,5},{5,4},{6,7},{7,6},{8,9},{9,8},{10,11... | collective-permute-start | bytes 1179656 | tf_op jit(solution)/shard_map/ppermute | solution.py:449
  174.1 8.8 %collective-permute-start.29 = (bf16[1536,128]{1,0:T(8,128)(2,1)S(1)}, bf16[1536,128]{1,0:T(8,128)(2,1)S(1)}, u32[]{:S(2)}, u32[]{:S(2)}) collective-permute-start(bf16[1536,128]{1,0:T(8,128)(2,1)S(1)} %collective-permute-done.27.refs_2_), channel_id=1, source_target_pairs={{0,1},{1,0},{2,3},{3,2},{4,5},{5,4},{6,7},{7,6},{8,9},{9,8},{10,11... | collective-permute-start | bytes 1179656 | tf_op jit(solution)/shard_map/ppermute | solution.py:449
  174.1 8.8 %collective-permute-start.32 = (bf16[1280,128]{1,0:T(8,128)(2,1)S(1)}, bf16[1280,128]{1,0:T(8,128)(2,1)S(1)}, u32[]{:S(2)}, u32[]{:S(2)}) collective-permute-start(bf16[1280,128]{1,0:T(8,128)(2,1)S(1)} %get-tuple-element.126.refs_4_), channel_id=1, source_target_pairs={{0,1},{1,0},{2,3},{3,2},{4,5},{5,4},{6,7},{7,6},{8,9},{9,8},{10,11... | collective-permute-start | bytes 983048 | tf_op jit(solution)/shard_map/ppermute | solution.py:449
  180.7 2.3 %collective-permute-start.34 = (bf16[1280,128]{1,0:T(8,128)(2,1)S(1)}, bf16[1280,128]{1,0:T(8,128)(2,1)S(1)}, u32[]{:S(2)}, u32[]{:S(2)}) collective-permute-start(bf16[1280,128]{1,0:T(8,128)(2,1)S(1)} %collective-permute-done.33.refs_6_), channel_id=1, source_target_pairs={{0,1},{1,0},{2,3},{3,2},{4,5},{5,4},{6,7},{7,6},{8,9},{9,8},{10,11... | collective-permute-start | bytes 983048 | tf_op jit(solution)/shard_map/ppermute | solution.py:449
  180.7 6.8 %collective-permute-start.30 = (bf16[256,128]{1,0:T(8,128)(2,1)S(1)}, bf16[256,128]{1,0:T(8,128)(2,1)S(1)}, u32[]{:S(2)}, u32[]{:S(2)}) collective-permute-start(bf16[256,128]{1,0:T(8,128)(2,1)S(1)} %get-tuple-element.127.refs_4_), channel_id=1, source_target_pairs={{0,1},{1,0},{2,3},{3,2},{4,5},{5,4},{6,7},{7,6},{8,9},{9,8},{10,11... | collective-permute-start | bytes 196616 | tf_op jit(solution)/shard_map/ppermute | solution.py:449
  181.2 6.3 %collective-permute-start.31 = (bf16[256,128]{1,0:T(8,128)(2,1)S(1)}, bf16[256,128]{1,0:T(8,128)(2,1)S(1)}, u32[]{:S(2)}, u32[]{:S(2)}) collective-permute-start(bf16[256,128]{1,0:T(8,128)(2,1)S(1)} %get-tuple-element.127.refs_4_), channel_id=1, source_target_pairs={{0,2},{1,3},{2,0},{3,1},{4,6},{5,7},{6,4},{7,5},{8,10},{9,11},{10,... | collective-permute-start | bytes 196616 | tf_op jit(solution)/shard_map/ppermute | solution.py:449
  187.5 1.3 collective-permute-start.35
